TPU v7x, 32 devices: a whole 2x2x4 slice. The times are simulated.
32 devices in a mesh: rep: 2 (over x), shard: 16 (over z, y, core).
Axes of the slice: x: 2, y: 2, z: 4, core: 2. Of those that a mesh axis runs over, the one named last changes fastest.
Arguments:
- inputs: bfloat16 [4096, 1024], P(('rep', 'shard')), may hold values from -6 to 6
- ff_in: bfloat16 [1, 2, 1024, 4096], P(None, None, 'shard'), may hold values from -0.1875 to 0.1875
- ff_out: bfloat16 [1, 2, 4096, 1024], P(None, None, 'shard'), may hold values from -0.09375 to 0.09375
- ff_bias: bfloat16 [1, 2, 4096], P(None, None, 'shard'), may hold values from -3 to 3
- attn_in: bfloat16 [1, 1024, 3072], P(None, 'shard'), may hold values from -0.1875 to 0.1875
- attn_out: bfloat16 [1, 1024, 1024], P(None, 'shard'), may hold values from -1.5 to 1.5
- conv_in: bfloat16 [1, 1024, 2048], P(None, 'shard'), may hold values from -0.1875 to 0.1875
- conv_out: bfloat16 [1, 1024, 1024], P(None, 'shard'), may hold values from -0.1875 to 0.1875
- depthwise: bfloat16 [1, 31, 1024], P(None, None, 'shard'), may hold values from -1 to 1
- distance: bfloat16 [1, 73, 64], replicated, may hold values from -4 to 4
- vectors: bfloat16 [1, 16, 1024], P(None, None, 'shard'), may hold values from -0.91 to 1.61, as said below
- attn_bias: bfloat16 [1, 1024], P(None, 'shard'), may hold values from -0.8984375 to 0.8984375
- cotangent: bfloat16 [4096, 1024], P(('rep', 'shard')), may hold values from -6 to 6
Outputs:
- output: bfloat16 [4096, 1024], P(('rep', 'shard'))
- grad_input: float32 [4096, 1024], P(('rep', 'shard'))
- grad_ff_in: float32 [1, 2, 1024, 4096], P(None, None, 'shard')
- grad_ff_out: float32 [1, 2, 4096, 1024], P(None, None, 'shard')
- grad_ff_bias: float32 [1, 2, 4096], P(None, None, 'shard')
- grad_attn_in: float32 [1, 1024, 3072], P(None, 'shard')
- grad_attn_out: float32 [1, 1024, 1024], P(None, 'shard')
- grad_conv_in: float32 [1, 1024, 2048], P(None, 'shard')
- grad_conv_out: float32 [1, 1024, 1024], P(None, 'shard')
- grad_depthwise: float32 [1, 31, 1024], P(None, None, 'shard')
- grad_distance: float32 [1, 73, 64], replicated
- grad_vectors: float32 [1, 16, 1024], P(None, None, 'shard')
- grad_attn_bias: float32 [1, 1024], P(None, 'shard')
Inputs may be any that keep to these rules, and one draw needn't show every extreme that they name: `vectors`: in each layer rows 0, 3, 7, 9, 11 and 14 are gains near one and the other rows are biases.
All inputs are finite; a program needn't handle non-finite values.
Results may differ from a plain program's by a relative error of at most 0.015.
Values may be sent and summed in bfloat16 or wider, within the bound.
No kernel may reach another device: no remote copies, remote signals or barrier semaphores. Data moves between devices by JAX's collectives and lax.ppermute only.
A program may use at most 256 MiB of HBM per device.

v0:
```python
import jax
import jax.numpy as jnp
from jax import lax
from jax.sharding import PartitionSpec as P

LEFT = 64
RIGHT = 8
SPAN = 8


EPSILON = 1e-05
HIGHEST = lax.Precision.HIGHEST


def swapped(block, axis, apart):
    count = lax.axis_size(axis)
    route = []
    for low in range(count):
        high = low | 1 << apart
        if high != low and high < count:
            route += [(low, high), (high, low)]
    return lax.ppermute(block, axis, route)


def passed_along(value, axis, by):
    peers = lax.axis_size(axis)
    pairs = [(i, i + by) for i in range(peers) if 0 <= i + by < peers]
    return lax.ppermute(value, axis, pairs)


def matmul(left_side, right_side):
    return jnp.dot(left_side, right_side, preferred_element_type=jnp.float32)


def back_matmul(left_side, right_side):
    return lax.dot_general(
        left_side, right_side, (((1,), (1,)), ((), ())), preferred_element_type=jnp.float32
    )


def weight_matmul(left_side, right_side):
    return lax.dot_general(
        left_side, right_side, (((0,), (0,)), ((), ())), preferred_element_type=jnp.float32
    )


def column_sum(values):
    return jnp.sum(values.astype(jnp.float32), axis=0)


def rounded(values):
    return lax.optimization_barrier(values.astype(jnp.bfloat16)).astype(jnp.float32)


def normalize(values, gain_row, shift_row):
    center = values - jnp.mean(values, axis=-1, keepdims=True)
    spread = jnp.mean(center * center, axis=-1, keepdims=True)
    return center * lax.rsqrt(spread + EPSILON) * gain_row + shift_row


def fetch_layer(layer_id, params):
    return (
        lax.all_gather(params[0][layer_id], "shard", axis=1, tiled=True),
        lax.all_gather(params[1][layer_id], "shard", axis=1, tiled=True),
        lax.all_gather(params[2][layer_id], "shard", axis=1, tiled=True),
        lax.all_gather(params[3][layer_id], "shard", axis=0, tiled=True),
        lax.all_gather(params[4][layer_id], "shard", axis=0, tiled=True),
        lax.all_gather(params[5][layer_id], "shard", axis=0, tiled=True),
        lax.all_gather(params[6][layer_id], "shard", axis=0, tiled=True),
        lax.all_gather(params[7][layer_id], "shard", axis=1, tiled=True),
        lax.all_gather(params[8][layer_id], "shard", axis=1, tiled=True),
        lax.all_gather(params[9][layer_id], "shard", axis=0, tiled=True),
    )


def group_gather(stacked):
    position = lax.axis_index("shard")
    for bit_id in range(SPAN.bit_length() - 1):
        partner = swapped(stacked, "shard", bit_id)
        is_lower = jnp.bitwise_and(jnp.right_shift(position, bit_id), 1) == 0
        stacked = jnp.where(
            is_lower,
            jnp.concatenate([stacked, partner], axis=1),
            jnp.concatenate([partner, stacked], axis=1),
        )
    return stacked


def group_reduce(stacked):
    position = lax.axis_index("shard")
    for bit_id in reversed(range(SPAN.bit_length() - 1)):
        half_len = stacked.shape[1] // 2
        front_part = stacked[:, :half_len]
        back_part = stacked[:, half_len:]
        is_lower = jnp.bitwise_and(jnp.right_shift(position, bit_id), 1) == 0
        outgoing = jnp.where(is_lower, back_part, front_part)
        staying = jnp.where(is_lower, front_part, back_part)
        stacked = staying + swapped(outgoing.astype(jnp.bfloat16), "shard", bit_id).astype(
            outgoing.dtype
        )
    return stacked


def spread_table(bucket_table, length, offset):
    head_count, row_count, unused_width = bucket_table.shape
    full_width = 2 * length
    left_fill = jnp.broadcast_to(bucket_table[:, :, :1], (head_count, row_count, length - LEFT))
    right_fill = jnp.broadcast_to(
        bucket_table[:, :, -1:], (head_count, row_count, length - RIGHT - 1)
    )
    widened = jnp.concatenate([left_fill, bucket_table, right_fill], axis=2)
    flattened = jnp.concatenate(
        [
            widened.reshape(head_count, row_count * full_width),
            jnp.zeros((head_count, length), jnp.float32),
        ],
        axis=1,
    )
    window = lax.dynamic_slice_in_dim(flattened, length - offset, row_count * (full_width - 1), 1)
    return window.reshape(head_count, row_count, full_width - 1)[:, :, :length]


def gather_table(grad_relative, length, offset):
    head_count, row_count, unused_width = grad_relative.shape
    full_width = 2 * length
    window = jnp.pad(grad_relative, ((0, 0), (0, 0), (0, full_width - 1 - length)))
    flattened = jnp.zeros((head_count, row_count * full_width + length), jnp.float32)
    flattened = lax.dynamic_update_slice_in_dim(
        flattened, window.reshape(head_count, row_count * (full_width - 1)), length - offset, 1
    )
    widened = flattened[:, : row_count * full_width].reshape(head_count, row_count, full_width)
    middle = widened[:, :, length - LEFT : length + RIGHT + 1]
    first_col = middle[:, :, :1] + jnp.sum(widened[:, :, : length - LEFT], axis=2, keepdims=True)
    last_col = middle[:, :, -1:] + jnp.sum(
        widened[:, :, length + RIGHT + 1 :], axis=2, keepdims=True
    )
    return jnp.concatenate([first_col, middle[:, :, 1:-1], last_col], axis=2)


def attention_scores(queries, key_rows, distance, offset):
    direct = jnp.einsum("qhe,khe->hqk", queries, key_rows, preferred_element_type=jnp.float32)
    bucket_table = jnp.einsum("qhe,re->hqr", queries, distance, preferred_element_type=jnp.float32)
    return (direct + spread_table(bucket_table, key_rows.shape[0], offset)) * queries.shape[2] ** (
        -0.5
    )


def feed_forward(current, weight_in, bias_in, weight_out, bias_out, gain_row, shift_row):
    hidden = normalize(current, gain_row, shift_row).astype(jnp.bfloat16)
    upper = matmul(hidden, weight_in) + bias_in
    active = jax.nn.silu(upper).astype(jnp.bfloat16)
    return (matmul(active, weight_out) + bias_out, (hidden, upper, active))


def feed_backward(current, grad_current, weight_in, weight_out, gain_row, shift_row, saved):
    hidden, upper, active = saved
    grad_branch = (0.5 * grad_current).astype(jnp.bfloat16)
    grad_out_w = weight_matmul(active, grad_branch)
    grad_out_bias = column_sum(grad_branch)
    grad_active = back_matmul(grad_branch, weight_out)
    unused_out, pullback = jax.vjp(jax.nn.silu, upper)
    grad_upper = pullback(grad_active)[0].astype(jnp.bfloat16)
    grad_in_w = weight_matmul(hidden, grad_upper)
    grad_in_bias = column_sum(grad_upper)
    grad_hidden = back_matmul(grad_upper, weight_in)
    unused_out, pullback = jax.vjp(normalize, current, gain_row, shift_row)
    grad_norm, grad_gain, grad_shift = pullback(grad_hidden)
    return (
        grad_current + grad_norm,
        (grad_in_w, grad_out_w, grad_in_bias, grad_out_bias, grad_gain, grad_shift),
    )


def attend_forward(current, weight_mix, weight_out, out_bias, distance, vector, offset):
    row_count, model_width = current.shape
    head_count = model_width // distance.shape[1]
    hidden = normalize(current, vector[3], vector[4]).astype(jnp.bfloat16)
    mixed_rows = matmul(hidden, weight_mix)
    queries = (
        (mixed_rows[:, :model_width] + vector[5])
        .astype(jnp.bfloat16)
        .reshape(row_count, head_count, -1)
    )
    key_rows = mixed_rows[:, model_width : 2 * model_width].astype(jnp.bfloat16)
    values = (mixed_rows[:, 2 * model_width :] + vector[6]).astype(jnp.bfloat16)
    shared = group_gather(jnp.stack([key_rows, values]))
    length = shared.shape[1]
    all_keys = shared[0].reshape(length, head_count, -1)
    all_values = shared[1].reshape(length, head_count, -1)
    scores = attention_scores(queries, all_keys, distance, offset)
    row_peak = jnp.max(scores, axis=2, keepdims=True)
    log_total = row_peak + jnp.log(jnp.sum(jnp.exp(scores - row_peak), axis=2, keepdims=True))
    weights_low = jnp.exp(scores - log_total).astype(jnp.bfloat16)
    context = jnp.einsum(
        "hqk,khe->qhe", weights_low, all_values, preferred_element_type=jnp.float32
    )
    context = context.reshape(row_count, model_width).astype(jnp.bfloat16)
    return (matmul(context, weight_out) + out_bias, (hidden, queries, shared, log_total, context))


def attend_backward(current, grad_current, weight_mix, weight_out, distance, vector, offset, saved):
    hidden, queries, shared, log_total, context = saved
    row_count, model_width = current.shape
    head_count = queries.shape[1]
    length = shared.shape[1]
    factor = queries.shape[2] ** (-0.5)
    all_keys = shared[0].reshape(length, head_count, -1)
    all_values = shared[1].reshape(length, head_count, -1)
    grad_branch = grad_current.astype(jnp.bfloat16)
    grad_out_w = weight_matmul(context, grad_branch)
    grad_out_bias = column_sum(grad_branch)
    grad_context = (
        back_matmul(grad_branch, weight_out).astype(jnp.bfloat16).reshape(row_count, head_count, -1)
    )
    scores = attention_scores(queries, all_keys, distance, offset)
    probs_full = jnp.exp(scores - log_total)
    grad_probs = jnp.einsum(
        "qhe,khe->hqk", grad_context, all_values, preferred_element_type=jnp.float32
    )
    grad_values = jnp.einsum(
        "hqk,qhe->khe",
        probs_full.astype(jnp.bfloat16),
        grad_context,
        preferred_element_type=jnp.float32,
    )
    grad_scores = probs_full * (
        grad_probs - jnp.sum(grad_probs * probs_full, axis=2, keepdims=True)
    )
    grad_low = grad_scores.astype(jnp.bfloat16)
    grad_keys = (
        jnp.einsum("hqk,qhe->khe", grad_low, queries, preferred_element_type=jnp.float32) * factor
    )
    grad_queries = (
        jnp.einsum("hqk,khe->qhe", grad_low, all_keys, preferred_element_type=jnp.float32) * factor
    )
    grad_table = gather_table(grad_low.astype(jnp.float32) * factor, length, offset)
    grad_queries = grad_queries + jnp.einsum(
        "hqr,re->qhe", grad_table, distance.astype(jnp.float32), precision=HIGHEST
    )
    grad_distance = jnp.einsum(
        "hqr,qhe->re", grad_table, queries.astype(jnp.float32), precision=HIGHEST
    )
    summed = group_reduce(
        jnp.stack(
            [grad_keys.reshape(length, model_width), grad_values.reshape(length, model_width)]
        )
    )
    grad_mixed = jnp.concatenate(
        [grad_queries.reshape(row_count, model_width), summed[0], summed[1]], axis=1
    ).astype(jnp.bfloat16)
    grad_mix_w = weight_matmul(hidden, grad_mixed)
    grad_q_bias = column_sum(grad_mixed[:, :model_width])
    grad_v_bias = column_sum(grad_mixed[:, 2 * model_width :])
    grad_hidden = back_matmul(grad_mixed, weight_mix)
    unused_out, pullback = jax.vjp(normalize, current, vector[3], vector[4])
    grad_norm, grad_gain, grad_shift = pullback(grad_hidden)
    return (
        grad_current + grad_norm,
        (
            grad_mix_w,
            grad_out_w,
            grad_distance,
            grad_gain,
            grad_shift,
            grad_q_bias,
            grad_v_bias,
            grad_out_bias,
        ),
    )


def depth_mix(padded, depth):
    tap_count = depth.shape[0]
    row_count = padded.shape[0] - tap_count + 1
    summed = padded[0:row_count] * depth[0]
    for tap_id in range(1, tap_count):
        summed = summed + padded[tap_id : tap_id + row_count] * depth[tap_id]
    return summed


def conv_tail(padded, depth, gain_row, shift_row):
    return jax.nn.silu(normalize(depth_mix(padded, depth), gain_row, shift_row))


def gated_unit(doubled):
    model_width = doubled.shape[1] // 2
    return doubled[:, :model_width] * jax.nn.sigmoid(doubled[:, model_width:])


def convolve_forward(current, weight_in, depth, weight_out, vector, is_first):
    hidden = normalize(current, vector[7], vector[8]).astype(jnp.bfloat16)
    doubled = matmul(hidden, weight_in)
    glued = gated_unit(doubled).astype(jnp.bfloat16)
    tap_count = depth.shape[0]
    border = passed_along(glued[glued.shape[0] - (tap_count - 1) :], "shard", 1)
    border = jnp.where(is_first, jnp.zeros_like(border), border)
    padded = jnp.concatenate([border, glued], axis=0).astype(jnp.float32)
    rest = conv_tail(padded, depth, vector[9], vector[10]).astype(jnp.bfloat16)
    return (matmul(rest, weight_out), (hidden, doubled, padded, rest))


def convolve_backward(current, grad_current, weight_in, depth, weight_out, vector, is_last, saved):
    hidden, doubled, padded, rest = saved
    row_count = current.shape[0]
    tap_count = depth.shape[0]
    grad_branch = grad_current.astype(jnp.bfloat16)
    grad_out_w = weight_matmul(rest, grad_branch)
    grad_rest = back_matmul(grad_branch, weight_out)
    unused_out, pullback = jax.vjp(conv_tail, padded, depth, vector[9], vector[10])
    grad_padded, grad_depth, grad_gain_two, grad_shift_two = pullback(grad_rest)
    incoming = passed_along(grad_padded[: tap_count - 1].astype(jnp.bfloat16), "shard", -1).astype(
        jnp.float32
    )
    incoming = jnp.where(is_last, jnp.zeros_like(incoming), incoming)
    grad_main = grad_padded[tap_count - 1 :]
    split_at = row_count - (tap_count - 1)
    grad_glued = rounded(
        jnp.concatenate([grad_main[:split_at], grad_main[split_at:] + incoming], axis=0)
    )
    unused_out, pullback = jax.vjp(gated_unit, doubled)
    grad_doubled = pullback(grad_glued)[0].astype(jnp.bfloat16)
    grad_in_w = weight_matmul(hidden, grad_doubled)
    grad_hidden = back_matmul(grad_doubled, weight_in)
    unused_out, pullback = jax.vjp(normalize, current, vector[7], vector[8])
    grad_norm, grad_gain, grad_shift = pullback(grad_hidden)
    return (
        grad_current + grad_norm,
        (grad_in_w, grad_out_w, grad_depth, grad_gain, grad_shift, grad_gain_two, grad_shift_two),
    )


def layer_forward(current, gathered, distance, offset, is_first):
    (
        w_ff_in,
        w_ff_out,
        w_ff_bias,
        w_attn_in,
        w_attn_out,
        w_conv_in,
        w_conv_out,
        w_depth,
        w_vector,
        w_out_bias,
    ) = gathered
    vector = w_vector.astype(jnp.float32)
    bias_rows = w_ff_bias.astype(jnp.float32)
    depth = w_depth.astype(jnp.float32)
    out_bias = w_out_bias.astype(jnp.float32)
    branch, saved_first = feed_forward(
        current, w_ff_in[0], bias_rows[0], w_ff_out[0], vector[2], vector[0], vector[1]
    )
    after_first = current + 0.5 * branch
    branch, saved_attend = attend_forward(
        after_first, w_attn_in, w_attn_out, out_bias, distance, vector, offset
    )
    after_attend = after_first + branch
    branch, saved_conv = convolve_forward(
        after_attend, w_conv_in, depth, w_conv_out, vector, is_first
    )
    after_conv = after_attend + branch
    branch, saved_second = feed_forward(
        after_conv, w_ff_in[1], bias_rows[1], w_ff_out[1], vector[13], vector[11], vector[12]
    )
    after_second = after_conv + 0.5 * branch
    result = normalize(after_second, vector[14], vector[15])
    return (
        result,
        (
            after_first,
            after_attend,
            after_conv,
            after_second,
            saved_first,
            saved_attend,
            saved_conv,
            saved_second,
        ),
    )


def layer_backward(current, grad_current, gathered, distance, offset, is_first, is_last):
    (
        w_ff_in,
        w_ff_out,
        w_ff_bias,
        w_attn_in,
        w_attn_out,
        w_conv_in,
        w_conv_out,
        w_depth,
        w_vector,
        w_out_bias,
    ) = gathered
    vector = w_vector.astype(jnp.float32)
    depth = w_depth.astype(jnp.float32)
    unused_out, saved = layer_forward(current, gathered, distance, offset, is_first)
    (
        after_first,
        after_attend,
        after_conv,
        after_second,
        saved_first,
        saved_attend,
        saved_conv,
        saved_second,
    ) = saved
    unused_out, pullback = jax.vjp(normalize, after_second, vector[14], vector[15])
    grad_last, grad_final_gain, grad_final_shift = pullback(grad_current)
    grad_conv_side, second_grads = feed_backward(
        after_conv, grad_last, w_ff_in[1], w_ff_out[1], vector[11], vector[12], saved_second
    )
    grad_attend_side, conv_grads = convolve_backward(
        after_attend, grad_conv_side, w_conv_in, depth, w_conv_out, vector, is_last, saved_conv
    )
    grad_first_side, attend_grads = attend_backward(
        after_first, grad_attend_side, w_attn_in, w_attn_out, distance, vector, offset, saved_attend
    )
    grad_start, first_grads = feed_backward(
        current, grad_first_side, w_ff_in[0], w_ff_out[0], vector[0], vector[1], saved_first
    )
    vector_rows = jnp.stack(
        [
            first_grads[4],
            first_grads[5],
            first_grads[3],
            attend_grads[3],
            attend_grads[4],
            attend_grads[5],
            attend_grads[6],
            conv_grads[3],
            conv_grads[4],
            conv_grads[5],
            conv_grads[6],
            second_grads[4],
            second_grads[5],
            second_grads[3],
            grad_final_gain,
            grad_final_shift,
        ]
    )
    layer_grads = (
        jnp.stack([first_grads[0], second_grads[0]]),
        jnp.stack([first_grads[1], second_grads[1]]),
        jnp.stack([first_grads[2], second_grads[2]]),
        attend_grads[0],
        attend_grads[1],
        conv_grads[0],
        conv_grads[1],
        conv_grads[2],
        vector_rows,
        attend_grads[7],
    )
    return (grad_start, layer_grads, attend_grads[2])


def reduce_grads(layer_grads):
    pieces = (
        lax.psum_scatter(layer_grads[0], "shard", scatter_dimension=1, tiled=True),
        lax.psum_scatter(layer_grads[1], "shard", scatter_dimension=1, tiled=True),
        lax.psum_scatter(layer_grads[2], "shard", scatter_dimension=1, tiled=True),
        lax.psum_scatter(layer_grads[3], "shard", scatter_dimension=0, tiled=True),
        lax.psum_scatter(layer_grads[4], "shard", scatter_dimension=0, tiled=True),
        lax.psum_scatter(layer_grads[5], "shard", scatter_dimension=0, tiled=True),
        lax.psum_scatter(layer_grads[6], "shard", scatter_dimension=0, tiled=True),
        lax.psum_scatter(layer_grads[7], "shard", scatter_dimension=1, tiled=True),
        lax.psum_scatter(layer_grads[8], "shard", scatter_dimension=1, tiled=True),
        lax.psum_scatter(layer_grads[9], "shard", scatter_dimension=0, tiled=True),
    )
    return (
        lax.psum(pieces[0].astype(jnp.bfloat16), "rep").astype(jnp.float32),
        lax.psum(pieces[1].astype(jnp.bfloat16), "rep").astype(jnp.float32),
        lax.psum(pieces[2].astype(jnp.bfloat16), "rep").astype(jnp.float32),
        lax.psum(pieces[3].astype(jnp.bfloat16), "rep").astype(jnp.float32),
        lax.psum(pieces[4].astype(jnp.bfloat16), "rep").astype(jnp.float32),
        lax.psum(pieces[5].astype(jnp.bfloat16), "rep").astype(jnp.float32),
        lax.psum(pieces[6].astype(jnp.bfloat16), "rep").astype(jnp.float32),
        lax.psum(pieces[7].astype(jnp.bfloat16), "rep").astype(jnp.float32),
        lax.psum(pieces[8].astype(jnp.bfloat16), "rep").astype(jnp.float32),
        lax.psum(pieces[9].astype(jnp.bfloat16), "rep").astype(jnp.float32),
    )


def shards(
    inputs,
    ff_in,
    ff_out,
    ff_bias,
    attn_in,
    attn_out,
    conv_in,
    conv_out,
    depthwise,
    distance,
    vectors,
    attn_bias,
    cotangent,
):
    params = (
        ff_in,
        ff_out,
        ff_bias,
        attn_in,
        attn_out,
        conv_in,
        conv_out,
        depthwise,
        vectors,
        attn_bias,
    )
    layer_count = ff_in.shape[0]
    position = lax.axis_index("shard") % SPAN
    is_first = position == 0
    is_last = position == SPAN - 1
    offset = position * inputs.shape[0]
    current = inputs.astype(jnp.float32)
    gathered = None
    layer_id = 0
    gathered = fetch_layer(layer_id, params)
    layer_inputs = [current]
    current, unused_saved = layer_forward(current, gathered, distance[layer_id], offset, is_first)
    output = current.astype(jnp.bfloat16)
    grad_current = cotangent.astype(jnp.float32)
    reduced = [None] * layer_count
    distance_grads = [None] * layer_count
    for layer_id in reversed(range(layer_count)):
        weights_now = fetch_layer(layer_id, params)
        grad_current, layer_grads, grad_table = layer_backward(
            layer_inputs[layer_id],
            grad_current,
            weights_now,
            distance[layer_id],
            offset,
            is_first,
            is_last,
        )
        reduced[layer_id] = reduce_grads(layer_grads)
        distance_grads[layer_id] = grad_table
    grad_distance = lax.psum(jnp.stack(distance_grads), ("rep", "shard"))
    stacked = [jnp.stack([reduced[0][item_id]]) for item_id in range(10)]
    return (
        output,
        grad_current,
        stacked[0],
        stacked[1],
        stacked[2],
        stacked[3],
        stacked[4],
        stacked[5],
        stacked[6],
        stacked[7],
        grad_distance,
        stacked[8],
        stacked[9],
    )


def solution(mesh):
    in_specs = (
        P(("rep", "shard"), None),
        P(None, None, "shard", None),
        P(None, None, "shard", None),
        P(None, None, "shard"),
        P(None, "shard", None),
        P(None, "shard", None),
        P(None, "shard", None),
        P(None, "shard", None),
        P(None, None, "shard"),
        P(),
        P(None, None, "shard"),
        P(None, "shard"),
        P(("rep", "shard"), None),
    )
    out_specs = (
        P(("rep", "shard"), None),
        P(("rep", "shard"), None),
        P(None, None, "shard", None),
        P(None, None, "shard", None),
        P(None, None, "shard"),
        P(None, "shard", None),
        P(None, "shard", None),
        P(None, "shard", None),
        P(None, "shard", None),
        P(None, None, "shard"),
        P(),
        P(None, None, "shard"),
        P(None, "shard"),
    )
    return jax.shard_map(shards, mesh=mesh, in_specs=in_specs, out_specs=out_specs, check_vma=False)
```

profile of v0, /device:TPU:0, one launch (start us, length us, event | category | flops | bytes accessed | tf_op | source)
XLA Modules:
  0.0 2036.4 jit_solution(10653703667671347607)
XLA Ops:
  11.4 26.1 %all-gather = bf16[1,16,1024]{1,0,2:T(2,128)(2,1)S(1)} all-gather(bf16[1,16,64]{1,0,2:T(2,128)(2,1)S(1)} %copy.56), channel_id=2, replica_groups=mesh['rep'=2,'shard'=16] {'shard'}, dimensions={2}, use_global_device_ids=true | all-gather | bytes 34816 | tf_op jit(solution)/shard_map/all_gather | solution.py:71
  38.1 17.7 all-gather.2
  56.7 64.1 %slice_reduce_fusion.3 = (f32[1024]{0:T(1024)}, f32[1024]{0:T(1024)}, f32[1024]{0:T(1024)}, f32[1024]{0:T(1024)}, f32[1024]{0:T(1024)}, /*index=5*/f32[1024]{0:T...) fusion(f32[1,16,1024]{1,0,2:T(1,128)S(1)} %convert_element_type.267), kind=kLoop, calls=%fused_computation.134 | loop fusion | bytes 131072 | tf_op jit(solution)/shard_map/slice | solution.py:365
  120.9 20.1 all-gather.17.cloned.1.call-done
  141.0 4.7 fusion.15
  145.8 122.5 %all-gather.19.cloned.1.call-done = bf16[1,2,4096,1024]{3,2,1,0:T(8,128)(2,1)} async-done(((bf16[1,2,256,1024]{3,2,1,0:T(8,128)(2,1)}), bf16[1,2,4096,1024]{3,2,1,0:T(8,128)(2,1)}) %all-gather.19.cloned.1.call-update) | async-done | bytes 16777232 | tf_op jit(solution)/shard_map/all_gather | solution.py:64
  268.3 4.8 fusion.125
  273.4 57.3 %all-gather.21.cloned.1.call-done = bf16[1,1024,3072]{2,1,0:T(8,128)(2,1)} async-done(((bf16[1,64,3072]{2,1,0:T(8,128)(2,1)}), bf16[1,1024,3072]{2,1,0:T(8,128)(2,1)}) %all-gather.21.cloned.1.call-update) | async-done | bytes 6291472 | tf_op jit(solution)/shard_map/all_gather | solution.py:66
  330.7 3.9 fusion.12
  336.7 31.8 %all-reduce.66 = bf16[1024]{0:T(1024)(128)(2,1)S(1)} all-reduce(bf16[1024]{0:T(1024)(128)(2,1)S(1)} %dynamic-update-slice), channel_id=8, replica_groups=mesh['rep'=2,'shard'=16] {'shard'}, use_global_device_ids=true, to_apply=%add.66 | all-reduce | flops 1024 | bytes 4096
  369.3 19.0 all-gather.8
  391.1 76.8 %slice_reduce_fusion.39 = (f32[1024]{0:T(1024)}, f32[1024]{0:T(1024)}, f32[1024]{0:T(1024)}, f32[1024]{0:T(1024)}, f32[1024]{0:T(1024)}, /*index=5*/f32[1024]{0:...) fusion(f32[1,31,1024]{1,0,2:T(1,128)S(1)} %convert_element_type.270), kind=kLoop, calls=%fused_computation.170 | loop fusion | bytes 155648 | tf_op jit(solution)/shard_map/slice | solution.py:275
  468.7 3.8 broadcast_in_dim.41
  472.5 3.8 broadcast_in_dim.43
  476.3 19.6 concatenate.55
  495.9 15.6 copy.76
  514.2 6.0 pad_dynamic-slice_fusion
  520.2 24.5 %reshape.428 = f32[16,128,2047]{2,1,0:T(8,128)} reshape(f32[16,262016]{1,0:T(8,128)} %pad_dynamic-slice_fusion) | data formatting | bytes 33538048 | tf_op jit(solution)/shard_map/reshape | solution.py:120
  544.7 17.1 collective-permute-done.2
  561.9 4.4 maximum_select_fusion
  573.6 5.5 fusion.126
  587.9 3.0 fusion.19
  594.1 44.5 %slice_reduce_fusion.38 = (f32[1024]{0:T(1024)}, f32[1024]{0:T(1024)}, f32[1024]{0:T(1024)}, f32[1024]{0:T(1024)}, f32[1024]{0:T(1024)}, /*index=5*/f32[1024]{0:...) fusion(f32[1,31,1024]{1,0,2:T(1,128)S(1)} %convert_element_type.270), kind=kLoop, calls=%fused_computation.169 | loop fusion | bytes 98304 | tf_op jit(solution)/shard_map/slice | solution.py:277
  639.6 3.5 fusion.119
  648.0 4.7 fusion.14
  652.8 5.6 fusion.129
  661.2 7.5 convert_reduce_fusion
  668.8 3.6 multiply_reduce_fusion.1
  673.7 2.9 fusion.88
  677.2 3.6 multiply_reduce_fusion.2
  685.4 3.2 fusion.115
  695.0 4.8 multiply_reduce_fusion.3
  704.3 3.3 fusion.53
  709.4 5.8 multiply_reduce_fusion
  715.3 4.4 convert_multiply_fusion
  726.2 3.5 collective-permute-start.5
  729.7 11.9 pad.230
  741.6 22.0 %reshape.430 = f32[16,262016]{1,0:T(8,128)} reshape(f32[16,128,2047]{2,1,0:T(8,128)} %pad.230) | data formatting | bytes 33538048 | tf_op jit(solution)/shard_map/reshape | solution.py:129
  763.5 4.7 fusion.91
  769.6 5.2 copy-done.5
  777.6 13.2 copy.77
  791.2 8.1 convert_add_fusion
  802.8 6.1 slice_reduce_fusion
  809.0 4.0 slice_reduce_fusion.1
  813.0 15.5 collective-permute-done.6
  833.0 6.4 fusion.84
  843.3 6.0 multiply_reduce_fusion.4
  849.9 7.3 convert_reduce_fusion.1
  857.3 8.2 convolution_bitcast_fusion.3
  865.5 18.6 pad_maximum_fusion
  885.0 4.0 convolution_bitcast_fusion
  889.0 4.1 convolution_bitcast_fusion.1
  893.0 11.7 pad_maximum_fusion.1
  908.8 6.7 fusion.111
  922.8 18.7 reduce-scatter.24.cloned.1.call-done
  943.2 136.6 %reduce-scatter.20.cloned.1.call-done = f32[64,3072]{1,0:T(8,128)} async-done(((f32[1024,3072]{1,0:T(8,128)}), f32[64,3072]{1,0:T(8,128)}) %reduce-scatter.20.cloned.1.call-update) | async-done | bytes 786448 | tf_op jit(solution)/shard_map/reduce_scatter | solution.py:461
  1081.8 334.1 %reduce-scatter.16.cloned.1.call-done = f32[2,64,4096]{2,1,0:T(8,128)} async-done(((f32[2,1024,4096]{2,1,0:T(8,128)}), f32[2,64,4096]{2,1,0:T(8,128)}) %reduce-scatter.16.cloned.1.call-update) | async-done | bytes 2097168 | tf_op jit(solution)/shard_map/reduce_scatter | solution.py:458
  1418.6 333.1 %reduce-scatter.18.cloned.1.call-done = f32[2,256,1024]{2,1,0:T(8,128)} async-done(((f32[2,4096,1024]{2,1,0:T(8,128)}), f32[2,256,1024]{2,1,0:T(8,128)}) %reduce-scatter.18.cloned.1.call-update) | async-done | bytes 2097168 | tf_op jit(solution)/shard_map/reduce_scatter | solution.py:459
  1755.1 31.6 %all-reduce.67 = bf16[1024]{0:T(1024)(128)(2,1)S(1)} all-reduce(f32[1024]{0:T(1024)S(1)} %copy-done.136), channel_id=21, replica_groups=mesh['rep'=2,'shard'=16] {'shard'}, use_global_device_ids=true, to_apply=%region_98.99.clone | all-reduce | flops 1024 | bytes 6144
  1787.3 37.7 %psum.85 = f32[1,73,64]{1,2,0:T(8,128)} all-reduce(f32[1,73,64]{1,2,0:T(8,128)S(1)} %convolution_bitcast_fusion.6), channel_id=1, replica_groups=mesh['rep'=2,'shard'=16] {'rep','shard'}, use_global_device_ids=true, to_apply=%region_78.79 | all-reduce | flops 4672 | bytes 37376 | tf_op jit(solution)/shard_map/psum | solution.py:538
  1827.0 49.0 %reduce-scatter.28.cloned.1.call-done = f32[256,2]{1,0:T(8,128)} async-done(((f32[4096,2]{1,0:T(8,128)}), f32[256,2]{1,0:T(8,128)}) %reduce-scatter.28.cloned.1.call-update) | async-done | bytes 2064
  1877.0 57.2 %reduce-scatter.32.cloned.1.call-done = f32[64,16]{1,0:T(8,128)} async-done(((f32[1024,16]{1,0:T(8,128)}), f32[64,16]{1,0:T(8,128)}) %reduce-scatter.32.cloned.1.call-update) | async-done | bytes 4112
  1935.0 8.2 all-reduce.68
  1945.5 75.3 %all-reduce.72.cloned.1.call-done = (bf16[1,2,64,4096]{3,2,1,0:T(8,128)(2,1)}, bf16[1,2,256,1024]{3,2,1,0:T(8,128)(2,1)}, bf16[1,64,3072]{2,1,0:T(8,128)(2,1)}, ...) async-done(((bf16[1,2,64,4096]{3,2,1,0:T(8,128)(2,1)}, bf16[1,2,256,1024]{3,2,1,0:T(8,128)(2,1)}, ...) | async-done | bytes 3014672 | tf_op jit(solution)/shard_map/psum | solution.py:470
  (556 shorter events, 120.0 us)
Async XLA Ops:
  7.2 460.9 %copy-start = (bf16[1,73,64]{1,2,0:T(8,128)(2,1)S(1)}, bf16[1,73,64]{1,2,0:T(8,128)(2,1)}, u32[]{:S(2)}) copy-start(bf16[1,73,64]{1,2,0:T(8,128)(2,1)} %param.22) | copy-start | bytes 28036
  7.2 30.9 %copy-start.169 = (bf16[1,2,256]{2,1,0:T(2,128)(2,1)S(1)}, bf16[1,2,256]{2,1,0:T(2,128)(2,1)}, u32[]{:S(2)}) copy-start(bf16[1,2,256]{2,1,0:T(2,128)(2,1)} %param.16) | copy-start | bytes 3076
  7.2 48.5 %copy-start.27 = (bf16[128,1024]{1,0:T(8,128)(2,1)S(1)}, bf16[128,1024]{1,0:T(8,128)(2,1)}, u32[]{:S(2)}) copy-start(bf16[128,1024]{1,0:T(8,128)(2,1)} %param.13) | copy-start | bytes 786436
  7.2 133.8 %all-gather.17.cloned.1.call-start = ((), (), s32[]{:S(2)}) async-start(), calls=%async_computation.15 | async-start | bytes 17825792 | tf_op jit(solution)/shard_map/all_gather | solution.py:63
  8.0 260.4 %all-gather.19.cloned.1.call-start = ((), (), s32[]{:S(2)}) async-start(), calls=%async_computation.16 | async-start | bytes 17825792 | tf_op jit(solution)/shard_map/all_gather | solution.py:64
  8.7 322.0 %all-gather.21.cloned.1.call-start = ((), (), s32[]{:S(2)}) async-start(), calls=%async_computation.17 | async-start | bytes 6684672 | tf_op jit(solution)/shard_map/all_gather | solution.py:66
  9.4 575.9 %all-gather.23.cloned.1.call-start = ((), (), s32[]{:S(2)}) async-start(), calls=%async_computation.18 | async-start | bytes 2228224 | tf_op jit(solution)/shard_map/all_gather | solution.py:67
  10.0 577.9 %all-gather.25.cloned.1.call-start = ((), (), s32[]{:S(2)}) async-start(), calls=%async_computation.19 | async-start | bytes 4456448 | tf_op jit(solution)/shard_map/all_gather | solution.py:68
  10.6 634.6 %all-gather.27.cloned.1.call-start = ((), (), s32[]{:S(2)}) async-start(), calls=%async_computation.20 | async-start | bytes 2228224 | tf_op jit(solution)/shard_map/all_gather | solution.py:69
  55.9 85.1 %copy-start.141 = (f32[128]{0:T(128)}, f32[128]{0:T(128)S(1)}, u32[]{:S(2)}) copy-start(f32[128]{0:T(128)S(1)} %broadcast_multiply_fusion.36) | copy-start | bytes 1540
  56.1 64.8 %copy-start.170 = (f32[128]{0:T(128)}, f32[128]{0:T(128)S(1)}, u32[]{:S(2)}) copy-start(f32[128]{0:T(128)S(1)} %fusion.72) | copy-start | bytes 1540
  56.1 84.9 %copy-start.147 = (f32[128]{0:T(128)}, f32[128]{0:T(128)S(1)}, u32[]{:S(2)}) copy-start(f32[128]{0:T(128)S(1)} %fusion.96) | copy-start | bytes 1540
  120.9 24.9 %copy-start.66 = (f32[1024]{0:T(1024)}, f32[1024]{0:T(1024)S(1)}, u32[]{:S(2)}) copy-start(f32[1024]{0:T(1024)S(1)} %get-tuple-element.102) | copy-start | bytes 12292
  120.9 24.9 %copy-start.74 = (f32[1024]{0:T(1024)}, f32[1024]{0:T(1024)S(1)}, u32[]{:S(2)}) copy-start(f32[1024]{0:T(1024)S(1)} %get-tuple-element.101) | copy-start | bytes 12292
  120.9 209.8 %copy-start.56 = (f32[1024]{0:T(1024)}, f32[1024]{0:T(1024)S(1)}, u32[]{:S(2)}) copy-start(f32[1024]{0:T(1024)S(1)} %get-tuple-element.99) | copy-start | bytes 12292
  120.9 209.8 %copy-start.59 = (f32[1024]{0:T(1024)}, f32[1024]{0:T(1024)S(1)}, u32[]{:S(2)}) copy-start(f32[1024]{0:T(1024)S(1)} %get-tuple-element.98) | copy-start | bytes 12292
  145.8 127.3 %copy-start.39 = (f32[128,4096]{1,0:T(8,128)}, f32[128,4096]{1,0:T(8,128)S(1)}, u32[]{:S(2)}) copy-start(f32[128,4096]{1,0:T(8,128)S(1)} %fusion.15) | copy-start | bytes 6291460
  273.1 61.4 %copy-start.16 = (f32[128,1024]{1,0:T(8,128)}, f32[128,1024]{1,0:T(8,128)S(1)}, u32[]{:S(2)}) copy-start(f32[128,1024]{1,0:T(8,128)S(1)} %get-tuple-element.217) | copy-start | bytes 1572868
  273.2 61.4 %copy-start.112 = (f32[128]{0:T(128)}, f32[128]{0:T(128)S(1)}, u32[]{:S(2)}) copy-start(f32[128]{0:T(128)S(1)} %broadcast_multiply_fusion.35) | copy-start | bytes 1540
  273.4 57.3 %copy-start.172 = (f32[128]{0:T(128)}, f32[128]{0:T(128)S(1)}, u32[]{:S(2)}) copy-start(f32[128]{0:T(128)S(1)} %multiply_reduce_fusion.44) | copy-start | bytes 1540
  273.4 61.2 %copy-start.143 = (f32[128]{0:T(128)}, f32[128]{0:T(128)S(1)}, u32[]{:S(2)}) copy-start(f32[128]{0:T(128)S(1)} %fusion.97) | copy-start | bytes 1540
  330.7 38.5 %copy-start.151 = (bf16[1,31,64]{2,1,0:T(8,128)(2,1)S(1)}, bf16[1,31,64]{2,1,0:T(8,128)(2,1)}, u32[]{:S(2)}) copy-start(bf16[1,31,64]{2,1,0:T(8,128)(2,1)} %param.21) | copy-start | bytes 11908
  334.8 54.0 %collective-permute-start = (bf16[2,128,1024]{2,1,0:T(8,128)(2,1)S(1)}, bf16[2,128,1024]{2,1,0:T(8,128)(2,1)S(1)}, u32[]{:S(2)}, u32[]{:S(2)}) collective-permute-start(bf16[2,128,1024]{2,1,0:T(8,128)(2,1)S(1)} %pad_maximum_fusion.5), channel_id=1, source_target_pairs={{0,1},{1,0},{2,3},{3,2},{4,5},{5,4},{6,7},{7,6},{8,9},{9,8},{10,11... | collective-permute-start | bytes 1572872 | tf_op jit(solution)/shard_map/ppermute | solution.py:22
  335.2 584.4 %reduce-scatter.26.cloned.1.call-start = ((), (), s32[]{:S(2)}) async-start(), calls=%async_computation.14 | async-start | bytes 4456448 | tf_op jit(solution)/shard_map/reduce_scatter | solution.py:464
  389.3 78.5 %copy-start.37 = (bf16[2,256,1024]{2,1,0:T(8,128)(2,1)}, bf16[2,256,1024]{2,1,0:T(8,128)(2,1)S(1)}, u32[]{:S(2)}) copy-start(bf16[2,256,1024]{2,1,0:T(8,128)(2,1)S(1)} %maximum_select_fusion.2) | copy-start | bytes 3145732
  389.3 122.2 %collective-permute-start.1 = (bf16[2,256,1024]{2,1,0:T(8,128)(2,1)S(1)}, bf16[2,256,1024]{2,1,0:T(8,128)(2,1)}, u32[]{:S(2)}, u32[]{:S(2)}) collective-permute-start(bf16[2,256,1024]{2,1,0:T(8,128)(2,1)S(1)} %maximum_select_fusion.2), channel_id=1, source_target_pairs={{0,2},{2,0},{1,3},{3,1},{4,6},{6,4},{5,7},{7,5},{8,10},{10,8},{9,1... | collective-permute-start | bytes 3145736 | tf_op jit(solution)/shard_map/ppermute | solution.py:22
  468.0 251.7 %copy-start.35 = (bf16[128,1024]{0,1:T(8,128)(2,1)}, bf16[128,1024]{0,1:T(8,128)(2,1)S(1)}, u32[]{:S(2)}) copy-start(bf16[128,1024]{0,1:T(8,128)(2,1)S(1)} %copy.58) | copy-start | bytes 786436
  495.9 15.7 copy-start.38
  514.1 47.7 %collective-permute-start.2 = (bf16[2,512,1024]{2,1,0:T(8,128)(2,1)S(1)}, bf16[2,512,1024]{2,1,0:T(8,128)(2,1)}, u32[]{:S(2)}, u32[]{:S(2)}) collective-permute-start(bf16[2,512,1024]{2,1,0:T(8,128)(2,1)S(1)} %maximum_select_fusion.1), channel_id=1, source_target_pairs={{0,4},{4,0},{1,5},{5,1},{2,6},{6,2},{3,7},{7,3},{8,12},{12,8},{9,1... | collective-permute-start | bytes 6291464 | tf_op jit(solution)/shard_map/ppermute | solution.py:22
  592.8 45.8 %collective-permute-start.3 = (bf16[30,1024]{1,0:T(8,128)(2,1)S(1)}, bf16[30,1024]{1,0:T(8,128)(2,1)S(1)}, u32[]{:S(2)}, u32[]{:S(2)}) collective-permute-start(bf16[30,1024]{1,0:T(8,128)(2,1)S(1)} %slice.710), channel_id=1, source_target_pairs={{0,1},{1,2},{2,3},{3,4},{4,5},{5,6},{6,7},{7,8},{8,9},{9,10},{10,1... | collective-permute-start | bytes 184328 | tf_op jit(solution)/shard_map/ppermute | solution.py:28
  639.6 42.5 %copy-start.1 = (f32[158,1024]{1,0:T(8,128)}, f32[158,1024]{1,0:T(8,128)S(1)}, u32[]{:S(2)}) copy-start(f32[158,1024]{1,0:T(8,128)S(1)} %maximum_convert_fusion) | copy-start | bytes 1941508
  647.7 24.7 %copy-start.29 = (f32[128,1024]{1,0:T(8,128)}, f32[128,1024]{1,0:T(8,128)S(1)}, u32[]{:S(2)}) copy-start(f32[128,1024]{1,0:T(8,128)S(1)} %get-tuple-element.223) | copy-start | bytes 1572868
  647.7 24.7 %copy-start.152 = (f32[128]{0:T(128)}, f32[128]{0:T(128)S(1)}, u32[]{:S(2)}) copy-start(f32[128]{0:T(128)S(1)} %broadcast_multiply_fusion.32) | copy-start | bytes 1540
  647.9 24.5 %copy-start.154 = (f32[128]{0:T(128)}, f32[128]{0:T(128)S(1)}, u32[]{:S(2)}) copy-start(f32[128]{0:T(128)S(1)} %fusion.100) | copy-start | bytes 1540
  652.7 8.4 copy-start.41
  652.8 15.9 slice-start.2
  652.8 15.9 slice-start.3
  676.6 244.6 %reduce-scatter.22.cloned.1.call-start = ((), (), s32[]{:S(2)}) async-start(), calls=%async_computation.12 | async-start | bytes 4456448 | tf_op jit(solution)/shard_map/reduce_scatter | solution.py:462
  685.4 9.6 copy-start.63
  685.4 9.6 copy-start.115
  685.4 9.6 copy-start.146
  688.6 3.9 collective-permute-start.4
  704.2 237.3 %reduce-scatter.24.cloned.1.call-start = ((), (), s32[]{:S(2)}) async-start(), calls=%async_computation.13 | async-start | bytes 8912896 | tf_op jit(solution)/shard_map/reduce_scatter | solution.py:463
  726.2 64.9 %collective-permute-start.5 = (bf16[2,512,1024]{1,2,0:T(8,128)(2,1)}, bf16[2,512,1024]{1,2,0:T(8,128)(2,1)}, u32[]{:S(2)}, u32[]{:S(2)}) collective-permute-start(bf16[2,512,1024]{1,2,0:T(8,128)(2,1)} %select_convert_fusion), channel_id=1, source_target_pairs={{0,4},{4,0},{1,5},{5,1},{2,6},{6,2},{3,7},{7,3},{8,12},{12,8},{9,1... | collective-permute-start | bytes 6291464 | tf_op jit(solution)/shard_map/ppermute | solution.py:22
  741.6 22.0 %copy-start.32 = (f32[128,1024]{1,0:T(8,128)S(1)}, f32[128,1024]{1,0:T(8,128)}, u32[]{:S(2)}) copy-start(f32[128,1024]{1,0:T(8,128)} %copy-done.31) | copy-start | bytes 1572868
  741.6 22.0 %copy-start.71 = (f32[1024]{0:T(1024)S(1)}, f32[1024]{0:T(1024)}, u32[]{:S(2)}) copy-start(f32[1024]{0:T(1024)} %get-tuple-element.94) | copy-start | bytes 12292
  768.2 311.6 %reduce-scatter.20.cloned.1.call-start = ((), (), s32[]{:S(2)}) async-start(), calls=%async_computation.11 | async-start | bytes 13369344 | tf_op jit(solution)/shard_map/reduce_scatter | solution.py:461
  777.6 13.6 copy-start.9
  790.8 9.8 copy-start.4
  800.6 27.9 %collective-permute-start.6 = (bf16[2,256,1024]{1,2,0:T(8,128)(2,1)}, bf16[2,256,1024]{1,2,0:T(8,128)(2,1)}, u32[]{:S(2)}, u32[]{:S(2)}) collective-permute-start(bf16[2,256,1024]{1,2,0:T(8,128)(2,1)} %select_convert_fusion.1), channel_id=1, source_target_pairs={{0,2},{2,0},{1,3},{3,1},{4,6},{6,4},{5,7},{7,5},{8,10},{10,8},{9,1... | collective-permute-start | bytes 3145736 | tf_op jit(solution)/shard_map/ppermute | solution.py:22
  802.4 29.5 %copy-start.45 = (f32[16,128,71]{1,2,0:T(8,128)}, f32[16,128,71]{1,2,0:T(8,128)S(1)}, u32[]{:S(2)}) copy-start(f32[16,128,71]{1,2,0:T(8,128)S(1)} %copy.74) | copy-start | bytes 1744900
  808.9 19.6 copy-start.12
  813.0 17.3 copy-start.7
  813.0 17.3 copy-start.14
  830.2 2.2 collective-permute-start.7
  839.5 576.5 %reduce-scatter.16.cloned.1.call-start = ((), (), s32[]{:S(2)}) async-start(), calls=%async_computation.9 | async-start | bytes 35651584 | tf_op jit(solution)/shard_map/reduce_scatter | solution.py:458
  884.1 867.7 %reduce-scatter.18.cloned.1.call-start = ((), (), s32[]{:S(2)}) async-start(), calls=%async_computation.10 | async-start | bytes 35651584 | tf_op jit(solution)/shard_map/reduce_scatter | solution.py:459
  905.0 920.1 %reduce-scatter.30.cloned.1.call-start = ((), (), s32[]{:S(2)}) async-start(), calls=%async_computation.22 | async-start | bytes 557056
  908.5 967.5 %reduce-scatter.28.cloned.1.call-start = ((), (), s32[]{:S(2)}) async-start(), calls=%async_computation.21 | async-start | bytes 2228224
  918.0 1016.2 %reduce-scatter.32.cloned.1.call-start = ((), (), s32[]{:S(2)}) async-start(), calls=%async_computation.23 | async-start | bytes 557056
  919.5 1101.3 %all-reduce.72.cloned.1.call-start = ((), (), s32[]{:S(2)}) async-start(), calls=%async_computation.24 | async-start | bytes 6029312 | tf_op jit(solution)/shard_map/psum | solution.py:470
  1081.8 673.4 %copy-start.136 = (f32[1024]{0:T(1024)S(1)}, f32[1024]{0:T(1024)}, u32[]{:S(2)}) copy-start(f32[1024]{0:T(1024)} %get-tuple-element.146) | copy-start | bytes 12292
  1081.8 705.0 %copy-start.36 = (bf16[128,1024]{0,1:T(8,128)(2,1)S(1)}, bf16[128,1024]{0,1:T(8,128)(2,1)}, u32[]{:S(2)}) copy-start(bf16[128,1024]{0,1:T(8,128)(2,1)} %copy-done.35) | copy-start | bytes 786436
  1081.8 705.0 %copy-start.46 = (f32[16,128,71]{1,2,0:T(8,128)S(1)}, f32[16,128,71]{1,2,0:T(8,128)}, u32[]{:S(2)}) copy-start(f32[16,128,71]{1,2,0:T(8,128)} %copy-done.45) | copy-start | bytes 1744900
  (145 other events, 502.3 us)
Sparse Core Ops, SparseCore 0:
  10.2 130.7 all-gather.16
  143.2 125.0 all-gather.18
  270.6 60.0 all-gather.20
  332.7 39.9 all-gather.22
  374.7 58.1 all-gather.24
  434.9 42.5 all-gather.26
  676.7 76.4 reduce-scatter.25
  757.6 76.2 reduce-scatter.21
  837.9 103.4 reduce-scatter.23
  945.4 134.4 reduce-scatter.19
  1084.1 331.7 reduce-scatter.15
  1420.0 331.6 reduce-scatter.17
  1755.8 54.8 reduce-scatter.29
  1815.4 60.6 reduce-scatter.27
  1879.4 54.7 reduce-scatter.31
  1938.0 82.7 all-reduce.71
where the time goes:
time: 2050 us; the launch traced here: 2040 us
  waiting for transfers between devices  1240 us (60%)
  local copies, waits for them, and re-layouts  349 us (17%)
  blocking collectives  172 us (8%)
  matrix products  129 us (6%)
  other arithmetic  116 us (6%)
    reduce_scatter x1, waiting for transfers between devices, reduce_grads(): lax.psum_scatter(layer_grads[0], 'shard', scatter_dimension=1, tiled=True)  334 us
    reduce_scatter x1, waiting for transfers between devices, reduce_grads(): lax.psum_scatter(layer_grads[1], 'shard', scatter_dimension=1, tiled=True)  333 us
    reduce_scatter x1, waiting for transfers between devices, reduce_grads(): lax.psum_scatter(layer_grads[3], 'shard', scatter_dimension=0, tiled=True)  137 us
    all_gather x1, waiting for transfers between devices, fetch_layer(): lax.all_gather(params[1][layer_id], 'shard', axis=1, tiled=True)  123 us
    unnamed x19, waiting for transfers between devices  110 us
    slice x1, local copies, waits for them, and re-layouts, depth_mix(): summed = padded[0:row_count] * depth[0]  76.8 us
    psum x1, waiting for transfers between devices, reduce_grads(): lax.psum(pieces[0].astype(jnp.bfloat16), 'rep').astype(jnp.float32)  75.3 us
    slice x1, local copies, waits for them, and re-layouts, layer_forward(): result = normalize(after_second, vector[14], vector[15])  64.1 us
  transfers between devices with their start and end apart: 24, of which 13 were waited for; matrix products, arithmetic and copies ran while one was open for 26% of the time, Pallas kernels for 0%

commit v1 on v0

v1 whole, which is shorter than its diff:
```python
import functools

import jax
import jax.numpy as jnp
from jax import lax
from jax.experimental import pallas as pl
from jax.experimental.pallas import tpu as pltpu
from jax.sharding import PartitionSpec as P

LEFT = 64
RIGHT = 8
SPAN = 8
QUAD = 4
EPSILON = 1e-05
BF = jnp.bfloat16
F32 = jnp.float32
MIB = 1 << 20


def dot_nn(left, right):
    return jnp.dot(left, right, preferred_element_type=F32)


def dot_nt(left, right):
    return lax.dot_general(left, right, (((1,), (1,)), ((), ())), preferred_element_type=F32)


def dot_tn(left, right):
    return lax.dot_general(left, right, (((0,), (0,)), ((), ())), preferred_element_type=F32)


def column_sum(values):
    return jnp.sum(values.astype(F32), axis=0, keepdims=True)


def standard(values):
    center = values - jnp.mean(values, axis=-1, keepdims=True)
    scale = lax.rsqrt(jnp.mean(center * center, axis=-1, keepdims=True) + EPSILON)
    return center * scale, scale


def norm_back(values, gain, grad):
    unit, scale = standard(values)
    inner = grad * gain
    first = jnp.mean(inner, axis=-1, keepdims=True)
    second = jnp.mean(inner * unit, axis=-1, keepdims=True)
    return scale * (inner - first - unit * second), column_sum(grad * unit), column_sum(grad)


def logistic(values):
    return 1.0 / (1.0 + jnp.exp(-values))


def silu_slope(values):
    gate = logistic(values)
    return gate * (1.0 + values * (1.0 - gate))


def vmem(count):
    return [pl.BlockSpec(memory_space=pltpu.VMEM)] * count


def shape_of(rows, columns, dtype):
    return jax.ShapeDtypeStruct((rows, columns), dtype)


def kernel_call(body, name, outs, operands, scalars=0, scratch=(), flops=0):
    moved = sum(item.size * item.dtype.itemsize for item in (*operands[scalars:], *outs))
    return pl.pallas_call(
        body,
        in_specs=[pl.BlockSpec(memory_space=pltpu.SMEM)] * scalars
        + vmem(len(operands) - scalars),
        out_specs=vmem(len(outs)),
        out_shape=list(outs),
        scratch_shapes=list(scratch),
        compiler_params=pltpu.CompilerParams(vmem_limit_bytes=48 * MIB),
        cost_estimate=pl.CostEstimate(flops=flops, bytes_accessed=moved, transcendentals=0),
        name=name,
    )(*operands)


def fused(body, name, outs, *operands, flops=0):
    def kernel(*refs):
        results = body(*[ref[...] for ref in refs[: len(operands)]])
        for ref, value in zip(refs[len(operands) :], results):
            ref[...] = value.astype(ref.dtype)

    return kernel_call(kernel, name, outs, operands, flops=flops)


def flipped(value, mask):
    total = lax.axis_size("rep") * lax.axis_size("shard")
    return lax.ppermute(value, ("rep", "shard"), [(i, i ^ mask) for i in range(total)])


def ordered(pieces, position, name):
    rows, columns = pieces[0].shape

    def kernel(spot, *refs):
        for step, ref in enumerate(refs[:-1]):
            target = pl.multiple_of((spot[0] ^ step) * rows, rows)
            refs[-1][pl.ds(target, rows), :] = ref[...]

    out = shape_of(rows * len(pieces), columns, pieces[0].dtype)
    return kernel_call(kernel, name, [out], (position, *pieces), scalars=1)[0]


def group_gather(value, masks):
    first, second, core = masks
    half = value.shape[0] // 2
    via_first = flipped(value, first)
    via_second = flipped(value, second)
    cross = jnp.concatenate(
        [flipped(via_first[:half], second), flipped(via_second[half:], first)], axis=0
    )
    near = [value, via_first, via_second, cross]
    return near, [flipped(item, core) for item in near]


def group_reduce(kept, sent, masks):
    first, second, core = masks
    rows = kept.shape[0] // 4
    half = rows // 2
    swapped = flipped(sent, core)

    def corner(kept_part, swapped_part):
        total = kept_part[...] + swapped_part[...].astype(F32)
        return total[:half], total[half:]

    low, high = fused(
        corner,
        "reduce_corner",
        [shape_of(half, kept.shape[1], BF)] * 2,
        kept[3 * rows :],
        swapped[3 * rows :],
    )
    low, high = flipped(low, first), flipped(high, second)

    def sides(kept_part, swapped_part, low_part, high_part):
        total = kept_part + swapped_part.astype(F32)
        via_first, via_second = total[rows : 2 * rows], total[2 * rows :]
        via_first = jnp.concatenate(
            [via_first[:half], via_first[half:] + high_part.astype(F32)], axis=0
        )
        via_second = jnp.concatenate(
            [via_second[:half] + low_part.astype(F32), via_second[half:]], axis=0
        )
        return total[:rows], via_first, via_second

    own, via_first, via_second = fused(
        sides,
        "reduce_sides",
        [shape_of(rows, kept.shape[1], dtype) for dtype in (F32, BF, BF)],
        kept[: 3 * rows],
        swapped[: 3 * rows],
        low,
        high,
    )
    return own, flipped(via_first, first), flipped(via_second, second)


def joined(parts):
    return parts[0] + parts[1].astype(F32) + parts[2].astype(F32)


def feed_half(pieces, weight_in, bias, weight_out, norm_rows, out_dtype):
    rows = sum(item.shape[0] for item in pieces)
    width, inner = weight_in.shape
    count = len(pieces)

    def body(*values):
        hidden = jnp.concatenate(values[:count], axis=0)
        w_in, b_in, w_out, gain, shift = values[count:]
        if norm_rows is not None:
            unit, unused_scale = standard(hidden.astype(F32))
            hidden = (unit * gain + shift).astype(BF)
        upper = dot_nn(hidden, w_in) + b_in
        active = (upper * logistic(upper)).astype(BF)
        return hidden, upper, active, dot_nn(active, w_out)

    gain, shift = (bias[:, :8], bias[:, :8]) if norm_rows is None else norm_rows
    return fused(
        body,
        "feed_forward",
        [
            shape_of(rows, width, BF),
            shape_of(rows, inner, F32),
            shape_of(rows, inner, BF),
            shape_of(rows, width, out_dtype),
        ],
        *pieces,
        weight_in,
        bias,
        weight_out,
        gain,
        shift,
        flops=4 * rows * width * inner,
    )


def feed(blocks, weight_in, bias, weight_out, norm_rows, masks):
    near, far = blocks
    saved_far = feed_half(far, weight_in, bias, weight_out, norm_rows, BF)
    saved_near = feed_half(near, weight_in, bias, weight_out, norm_rows, F32)
    parts = group_reduce(saved_near[3], saved_far[3], masks)
    return parts, (saved_near[:3], saved_far[:3])


def feed_back_half(pieces, saved, weight_in, weight_out, out_dtype):
    upper = saved[1]
    rows, inner = upper.shape
    width = weight_in.shape[0]
    count = len(pieces)

    def body(*values):
        branch = jnp.concatenate(values[:count], axis=0)
        before, w_in, w_out = values[count:]
        slope = (dot_nt(branch, w_out) * silu_slope(before)).astype(BF)
        return branch, slope, column_sum(slope), dot_nt(slope, w_in)

    return fused(
        body,
        "feed_backward",
        [
            shape_of(rows, width, BF),
            shape_of(rows, inner, BF),
            shape_of(1, inner, F32),
            shape_of(rows, width, out_dtype),
        ],
        *pieces,
        upper,
        weight_in,
        weight_out,
        flops=4 * rows * width * inner,
    )


def token_product(left, right, position, places, name):
    rows, columns = left[0].shape[1], right[0].shape[1]
    extent = rows // places

    def kernel(spot, left_near, left_far, right_near, right_far, *refs):
        total = refs[-1]
        total[...] = dot_tn(left_near[...], right_near[...])
        total[...] += dot_tn(left_far[...], right_far[...])
        for step, ref in enumerate(refs[:-1]):
            source = pl.multiple_of((spot[0] ^ step) * extent, extent)
            ref[...] = total[pl.ds(source, extent), :].astype(ref.dtype)

    outs = [shape_of(extent, columns, F32)] + [shape_of(extent, columns, BF)] * (places - 1)
    return kernel_call(
        kernel,
        name,
        outs,
        (position, *left, *right),
        scalars=1,
        scratch=[pltpu.VMEM((rows, columns), F32)],
        flops=4 * left[0].shape[0] * rows * columns,
    )


def feed_back(blocks, saved, weight_in, weight_out, masks, plane, planes):
    saved_near, saved_far = saved
    far = feed_back_half(blocks[1], saved_far, weight_in, weight_out, BF)
    near = feed_back_half(blocks[0], saved_near, weight_in, weight_out, F32)
    parts = group_reduce(near[3], far[3], masks)
    grad_out = token_product(
        (saved_near[2], saved_far[2]), (near[0], far[0]), plane, planes, "feed_out_weight"
    )
    grad_in = token_product(
        (saved_near[0], saved_far[0]), (near[1], far[1]), plane, planes, "feed_in_weight"
    )
    return parts, grad_in, grad_out, near[2] + far[2]


def feed_weights(weight_in, weight_out, place):
    rows, hidden = weight_in.shape
    half = weight_out.shape[0] // 2
    columns = weight_in.reshape(rows, place.planes, QUAD, 2, half)
    columns = lax.dynamic_index_in_dim(columns, place.rep, 3, keepdims=False)
    columns = columns.transpose(2, 0, 1, 3).reshape(QUAD, rows, place.planes * half)

    def for_member(step):
        return lax.dynamic_index_in_dim(columns, place.quad ^ step, 0, keepdims=False)

    pieces = [for_member(0)] + [flipped(for_member(step), step) for step in range(1, QUAD)]
    piece_in = ordered(pieces, place.quad_spot, "order_columns")
    piece_out = lax.dynamic_slice_in_dim(weight_out, place.rep * half, half, 0)
    steps = range(1, place.planes)
    pieces_in = [piece_in] + [flipped(piece_in, QUAD * step) for step in steps]
    pieces_out = [piece_out] + [flipped(piece_out, QUAD * step) for step in steps]
    return (
        ordered(pieces_in, place.plane_spot, "order_feed_in"),
        ordered(pieces_out, place.plane_spot, "order_feed_out"),
    )


def plane_sum(pieces, name):
    arrived = [flipped(item, QUAD * step) for step, item in enumerate(pieces) if step]

    def body(*values):
        return (sum((item.astype(F32) for item in values[1:]), values[0]),)

    return fused(body, name, [shape_of(*pieces[0].shape, BF)], pieces[0], *arrived)[0]


def feed_weight_grads(grad_in, grad_out, place):
    low_out = plane_sum(grad_out, "sum_feed_out")
    other = flipped(low_out, place.shards)
    is_first = place.rep == 0
    total_out = jnp.concatenate(
        [jnp.where(is_first, low_out, other), jnp.where(is_first, other, low_out)], axis=0
    ).astype(F32)

    low_in = plane_sum(grad_in, "sum_feed_in")
    rows = low_in.shape[0] // QUAD
    blocks = low_in.reshape(QUAD, rows, low_in.shape[1])

    def for_member(step):
        return lax.dynamic_index_in_dim(blocks, place.quad ^ step, 0, keepdims=False)

    pieces = [for_member(0)] + [flipped(for_member(step), step) for step in range(1, QUAD)]
    mine = ordered(pieces, place.quad_spot, "order_grad_in")
    theirs = flipped(mine, place.shards)
    both = jnp.stack([jnp.where(is_first, mine, theirs), jnp.where(is_first, theirs, mine)])
    both = both.reshape(2, QUAD, rows, place.planes, -1).transpose(2, 3, 1, 0, 4)
    return both.reshape(rows, -1).astype(F32), total_out


def score_block(query, keys, table, bias, place, rows, length):
    scores = dot_nt(query, keys)
    spread = dot_nt(query, table)
    band = pltpu.roll(spread, 0, axis=1, stride=1, stride_axis=0)
    column = lax.broadcasted_iota(jnp.int32, (rows, length + 2 * rows), 1)
    bias[...] = jnp.where(column < place, spread[:, :1], spread[:, -1:])
    bias[:, pl.ds(place, 3 * rows)] = band[:, rows:]
    return scores + bias[:, rows : rows + length]


def place_rows(source, columns, target, position, rows):
    for step in range(SPAN):
        spot = pl.ds(pl.multiple_of((position ^ step) * rows, rows), rows)
        target[spot, :] = source[step * rows : (step + 1) * rows, columns]


def split_rows(value, kept, sent, rows):
    for index, step in enumerate((0, 4, 2, 6)):
        target = slice(index * rows, (index + 1) * rows)
        kept[target, :] = value[step * rows : (step + 1) * rows]
        sent[target, :] = value[(step + 1) * rows : (step + 2) * rows].astype(BF)


def join_pieces(refs, target, rows):
    for step, ref in enumerate(refs):
        target[step * rows : (step + 1) * rows, :] = ref[...]


def attend_kernel(*refs):
    spot, pieces, rest = refs[0], refs[1 : 1 + SPAN], refs[1 + SPAN :]
    (weight_in, bias_in, weight_out, table, hidden, mixed, context, peaks, kept, sent) = rest[:10]
    keys, values, bias = rest[10:]
    length, width = context.shape
    rows = length // SPAN
    head = table.shape[1] // 2
    position = spot[0]
    join_pieces(pieces, hidden, rows)
    mixed[...] = (dot_nn(hidden[...], weight_in[...]) + bias_in[...]).astype(BF)
    place_rows(mixed, slice(width, 2 * width), keys, position, rows)
    place_rows(mixed, slice(2 * width, 3 * width), values, position, rows)
    lane = lax.broadcasted_iota(jnp.int32, (rows, width), 1)

    def block(index, carry):
        place = pl.multiple_of(index * rows, rows)
        own = pl.ds(pl.multiple_of((position ^ index) * rows, rows), rows)
        query = mixed[own, :width] * jnp.asarray(head**-0.5, BF)
        results, logs = [], []
        for which in range(2):
            mine = lane // head == which
            part = jnp.where(mine, query, jnp.zeros_like(query))
            scores = score_block(part, keys[...], table[...], bias, place, rows, length)
            top = jnp.max(scores, axis=1, keepdims=True)
            powers = jnp.exp(scores - top)
            total = jnp.sum(powers, axis=1, keepdims=True)
            weights = (powers * (1.0 / total)).astype(BF)
            results.append(dot_nn(weights, values[...]))
            logs.append(top + jnp.log(total))
        context[own, :] = jnp.where(lane < head, results[0], results[1]).astype(BF)
        peaks[own, :] = jnp.where(lane < head, logs[0], logs[1])
        return carry

    lax.fori_loop(0, SPAN, block, 0)
    split_rows(dot_nn(context[...], weight_out[...]), kept, sent, rows)


def attend_back_kernel(*refs):
    spot, pieces, rest = refs[0], refs[1 : 1 + SPAN], refs[1 + SPAN :]
    (mixed, table, peaks, weight_in, weight_out) = rest[:5]
    (branch, grad_mixed, grad_table, far, kept, sent) = rest[5:11]
    keys, values, bias, grad_context, grad_keys, grad_values, slopes = rest[11:]
    length, width = grad_context.shape
    rows = length // SPAN
    head = table.shape[1] // 2
    position = spot[0]
    join_pieces(pieces, branch, rows)
    grad_context[...] = dot_nt(branch[...], weight_out[...]).astype(BF)
    place_rows(mixed, slice(width, 2 * width), keys, position, rows)
    place_rows(mixed, slice(2 * width, 3 * width), values, position, rows)
    grad_keys[...] = jnp.zeros_like(grad_keys)
    grad_values[...] = jnp.zeros_like(grad_values)
    grad_table[...] = jnp.zeros_like(grad_table)
    far[...] = jnp.zeros_like(far)
    lane = lax.broadcasted_iota(jnp.int32, (rows, width), 1)
    padded = lax.broadcasted_iota(jnp.int32, (rows, length + 2 * rows), 1)
    factor = head**-0.5
    slopes[:, :rows] = jnp.zeros((rows, rows), F32)
    slopes[:, rows + length :] = jnp.zeros((rows, rows), F32)
    mirror = (
        lax.broadcasted_iota(jnp.int32, (rows, rows), 0)
        + lax.broadcasted_iota(jnp.int32, (rows, rows), 1)
        == rows - 1
    ).astype(BF)

    def block(index, carry):
        place = pl.multiple_of(index * rows, rows)
        own = pl.ds(pl.multiple_of((position ^ index) * rows, rows), rows)
        query = mixed[own, :width] * jnp.asarray(factor, BF)
        results = []
        for which in range(2):
            mine = lane // head == which
            part = jnp.where(mine, query, jnp.zeros_like(query))
            scores = score_block(part, keys[...], table[...], bias, place, rows, length)
            incoming = grad_context[own, :]
            incoming = jnp.where(mine, incoming, jnp.zeros_like(incoming))
            logs = peaks[own, which * head : which * head + 1]
            probs = jnp.exp(scores - logs)
            grad_probs = dot_nt(incoming, values[...])
            shared = jnp.sum(grad_probs * probs, axis=1, keepdims=True)
            grad_low = (probs * (grad_probs - shared)).astype(BF)
            grad_values[...] += dot_tn(probs.astype(BF), incoming)
            grad_keys[...] += dot_tn(grad_low, part)
            slopes[:, rows : rows + length] = grad_low.astype(F32)
            window = slopes[:, pl.ds(place, 3 * rows)]
            whole = slopes[...]
            early = jnp.sum(jnp.where(padded < place, whole, 0.0), axis=1, keepdims=True)
            late = jnp.sum(
                jnp.where(padded >= place + 3 * rows, whole, 0.0), axis=1, keepdims=True
            )
            window = jnp.concatenate(
                [jnp.zeros((rows, rows), F32), dot_nn(mirror, window.astype(BF))], axis=1
            )
            window = pltpu.roll(
                window, 3 * rows + 1, axis=1, stride=1, stride_axis=0
            ).astype(BF)
            grad_table[...] += dot_tn(window, dot_nn(mirror, part).astype(BF))
            part_wide = part.astype(F32)
            far[0:1, :] += jnp.sum(early * part_wide, axis=0, keepdims=True)
            far[1:2, :] += jnp.sum(late * part_wide, axis=0, keepdims=True)
            close = jnp.dot(
                mirror.astype(F32),
                dot_nn(window, table[...]),
                preferred_element_type=F32,
                precision=lax.Precision.HIGHEST,
            )
            results.append(
                dot_nn(grad_low, keys[...])
                + close
                + early * table[0:1, :].astype(F32)
                + late * table[4 * rows - 1 :, :].astype(F32)
            )
        grad_mixed[own, :width] = (
            jnp.where(lane < head, results[0], results[1]) * factor
        ).astype(BF)
        return carry

    lax.fori_loop(0, SPAN, block, 0)
    for step in range(SPAN):
        source = pl.ds(pl.multiple_of((position ^ step) * rows, rows), rows)
        target = slice(step * rows, (step + 1) * rows)
        grad_mixed[target, width : 2 * width] = grad_keys[source, :].astype(BF)
        grad_mixed[target, 2 * width :] = grad_values[source, :].astype(BF)
    split_rows(dot_nt(grad_mixed[...], weight_in[...]), kept, sent, rows)


def in_steps(blocks):
    near, far = blocks
    return [near[0], far[0], near[2], far[2], near[1], far[1], near[3], far[3]]


def attend(blocks, weight_in, bias_in, weight_out, table, place):
    pieces = in_steps(blocks)
    rows, model = pieces[0].shape
    length, width = SPAN * rows, weight_out.shape[0]
    outs = [
        shape_of(length, model, BF),
        shape_of(length, 3 * width, BF),
        shape_of(length, width, BF),
        shape_of(length, width, F32),
        shape_of(length // 2, model, F32),
        shape_of(length // 2, model, BF),
    ]
    hidden, mixed, context, peaks, kept, sent = kernel_call(
        attend_kernel,
        "attend_forward",
        outs,
        (place.span_spot, *pieces, weight_in, bias_in, weight_out, table),
        scalars=1,
        scratch=[
            pltpu.VMEM((length, width), BF),
            pltpu.VMEM((length, width), BF),
            pltpu.VMEM((rows, length + 2 * rows), F32),
        ],
        flops=12 * length * length * width,
    )
    return group_reduce(kept, sent, place.span_masks), (hidden, mixed, context, peaks)


def attend_back(blocks, saved, weight_in, weight_out, table, place):
    hidden, mixed, context, peaks = saved
    pieces = in_steps(blocks)
    rows, model = pieces[0].shape
    length, width = SPAN * rows, weight_out.shape[0]
    outs = [
        shape_of(length, model, BF),
        shape_of(length, 3 * width, BF),
        shape_of(4 * rows, width, F32),
        shape_of(8, width, F32),
        shape_of(length // 2, model, F32),
        shape_of(length // 2, model, BF),
    ]
    branch, grad_mixed, grad_table, far, kept, sent = kernel_call(
        attend_back_kernel,
        "attend_backward",
        outs,
        (place.span_spot, *pieces, mixed, table, peaks, weight_in, weight_out),
        scalars=1,
        scratch=[
            pltpu.VMEM((length, width), BF),
            pltpu.VMEM((length, width), BF),
            pltpu.VMEM((rows, length + 2 * rows), F32),
            pltpu.VMEM((length, width), BF),
            pltpu.VMEM((length, width), F32),
            pltpu.VMEM((length, width), F32),
            pltpu.VMEM((rows, length + 2 * rows), F32),
        ],
        flops=24 * length * length * width,
    )
    parts = group_reduce(kept, sent, place.span_masks)

    def weights(hidden_rows, mixed_grad, context_rows, branch_rows):
        return (
            dot_tn(hidden_rows, mixed_grad),
            dot_tn(context_rows, branch_rows),
            column_sum(mixed_grad),
        )

    grad_in, grad_out, sums = fused(
        weights,
        "attend_weights",
        [shape_of(model, 3 * width, F32), shape_of(width, model, F32), shape_of(1, 3 * width, F32)],
        hidden,
        grad_mixed,
        context,
        branch,
        flops=8 * length * model * width,
    )
    return parts, grad_in, grad_out, sums, distance_gradient(grad_table, far, rows)


def wide_table(distance, rows):
    index = jnp.clip(jnp.arange(4 * rows) - rows - LEFT, 0, LEFT + RIGHT)
    low = distance[index]
    return jnp.concatenate([low, low], axis=1)


def distance_gradient(grad_table, far, rows):
    first = rows + LEFT
    last = first + LEFT + RIGHT
    head = grad_table.shape[1] // 2
    low = jnp.sum(grad_table[: first + 1], axis=0) + far[0]
    high = jnp.sum(grad_table[last:], axis=0) + far[1]
    total = jnp.concatenate([low[None], grad_table[first + 1 : last], high[None]], axis=0)
    return total[:, :head] + total[:, head:]


def whole_heads(weight_out, head):
    return weight_out.shape[0] % head == 0


def attend_weights(weight_in, weight_out, head, place):
    rows, model = weight_in.shape[0], weight_out.shape[1]
    heads = model // head
    per_device = heads // SPAN
    if not whole_heads(weight_out, head):
        whole = lax.all_gather(weight_in, "shard", axis=0, tiled=True)
        whole = whole.reshape(model, 3, heads, head)
        mine = lax.dynamic_slice_in_dim(whole, place.member * per_device, per_device, 2)
        out = lax.all_gather(weight_out, "shard", axis=0, tiled=True)
        width = per_device * head
        out = lax.dynamic_slice_in_dim(out, place.member * width, width, 0)
        return mine.reshape(model, 3 * width), out
    blocks = weight_in.reshape(rows, 3, per_device, SPAN, head)
    blocks = blocks.transpose(3, 0, 1, 2, 4).reshape(SPAN, rows, 3 * per_device * head)

    def for_member(step):
        return lax.dynamic_index_in_dim(blocks, place.member ^ step, 0, keepdims=False)

    pieces = [for_member(0)] + [flipped(for_member(step), step) for step in range(1, SPAN)]
    group = ordered(pieces, place.span_spot, "order_attend_group")
    steps = range(1, place.shards // SPAN)
    pieces = [group] + [flipped(group, SPAN * step) for step in steps]
    outs = [weight_out] + [flipped(weight_out, SPAN * step) for step in steps]
    return (
        ordered(pieces, place.group_spot, "order_attend_in"),
        ordered(outs, place.group_spot, "order_attend_out"),
    )


def head_row(row, head, place, aligned):
    heads = row.shape[0] // head
    if aligned:
        row = row.reshape(-1, SPAN, head)
        row = lax.dynamic_index_in_dim(row, place.member, 1, keepdims=False)
        return row.reshape(1, -1)
    row = row.reshape(SPAN, -1)
    return lax.dynamic_slice_in_dim(row, place.member, 1, 0)


def head_spread(row, model, head, place, aligned):
    if aligned:
        whole = jnp.zeros((model // head // SPAN, SPAN, head), F32)
        block = row.reshape(-1, 1, head)
        return lax.dynamic_update_slice_in_dim(whole, block, place.member, 1).reshape(1, model)
    whole = jnp.zeros((SPAN, model // SPAN), F32)
    return lax.dynamic_update_slice_in_dim(whole, row, place.member, 0).reshape(1, model)


def attend_weight_grads(grad_in, grad_out, head, place, rows, aligned):
    model = grad_out.shape[1]
    heads = model // head
    per_device = heads // SPAN
    if not aligned:
        whole = jnp.zeros((model, 3, heads, head), F32)
        whole = lax.dynamic_update_slice_in_dim(
            whole, grad_in.reshape(model, 3, per_device, head), place.member * per_device, 2
        )
        whole = lax.psum_scatter(
            whole.reshape(model, 3 * model), "shard", scatter_dimension=0, tiled=True
        )
        out = jnp.zeros((model, model), F32)
        out = lax.dynamic_update_slice_in_dim(out, grad_out, place.member * per_device * head, 0)
        out = lax.psum_scatter(out, "shard", scatter_dimension=0, tiled=True)
        return rep_sum(whole, place), rep_sum(out, place)
    groups = place.shards // SPAN
    extent_in, extent_out = model // groups, grad_out.shape[0] // groups

    def for_group(value, extent, step):
        return lax.dynamic_slice_in_dim(value, (place.group ^ step) * extent, extent, 0)

    sum_in = for_group(grad_in, extent_in, 0)
    sum_out = for_group(grad_out, extent_out, 0)
    for step in range(1, groups):
        arrived = flipped(for_group(grad_in, extent_in, step).astype(BF), SPAN * step)
        sum_in = sum_in + arrived.astype(F32)
        arrived = flipped(for_group(grad_out, extent_out, step).astype(BF), SPAN * step)
        sum_out = sum_out + arrived.astype(F32)
    blocks = sum_in.astype(BF).reshape(SPAN, rows, -1)

    def for_member(step):
        return lax.dynamic_index_in_dim(blocks, place.member ^ step, 0, keepdims=False)

    pieces = [for_member(0)] + [flipped(for_member(step), step) for step in range(1, SPAN)]
    mine = rep_sum(ordered(pieces, place.span_spot, "order_attend_grad"), place)
    mine = mine.reshape(SPAN, rows, 3, per_device, head).transpose(1, 2, 3, 0, 4)
    return mine.reshape(rows, 3 * model), rep_sum(sum_out, place)


def rep_sum(value, place):
    low = value.astype(BF)
    return low.astype(F32) + flipped(low, place.shards).astype(F32)


def tap_rows(padded, depth, rows, offset):
    total = padded[offset : offset + rows, :] * depth[0:1, :]
    for tap in range(1, depth.shape[0]):
        total = total + padded[offset + tap : offset + tap + rows, :] * depth[tap : tap + 1, :]
    return total


def convolve_start(parts, before, out_bias, gain, shift, weight_in):
    rows, model = before.shape

    def body(own, via_first, via_second, base, bias, gain_row, shift_row, w_in):
        current = base + joined((own, via_first, via_second)) + bias
        unit, unused_scale = standard(current)
        hidden = (unit * gain_row + shift_row).astype(BF)
        doubled = dot_nn(hidden, w_in)
        return current, hidden, doubled, doubled[:, :model] * logistic(doubled[:, model:])

    return fused(
        body,
        "convolve_start",
        [
            shape_of(rows, model, F32),
            shape_of(rows, model, BF),
            shape_of(rows, 2 * model, F32),
            shape_of(rows, model, BF),
        ],
        *parts,
        before,
        out_bias,
        gain,
        shift,
        weight_in,
        flops=4 * rows * model * model,
    )


LANES = 128


def convolve_finish(glued, border, depth, norm_two, weight_out, before, norm_next):
    rows, model = before.shape
    edge = border.shape[0]
    taps = depth.shape[0]

    def kernel(
        glued_ref, border_ref, depth_ref, gain, shift, w_out, base, gain_next, shift_next,
        mixed_ref, rest_ref, current_ref, hidden_ref, padded,
    ):
        padded[:edge, :] = border_ref[...].astype(F32)
        padded[edge:, :] = glued_ref[...].astype(F32)
        for column in range(0, model, LANES):
            lanes = slice(column, column + LANES)
            total = jnp.zeros((rows, LANES), F32)
            for tap in range(taps):
                start = edge - taps + 1 + tap
                total += padded[start : start + rows, lanes] * depth_ref[tap : tap + 1, lanes]
            mixed_ref[:, lanes] = total
        unit, unused_scale = standard(mixed_ref[...])
        upper = unit * gain[...] + shift[...]
        rest = (upper * logistic(upper)).astype(BF)
        rest_ref[...] = rest
        current = base[...] + dot_nn(rest, w_out[...])
        current_ref[...] = current
        unit, unused_scale = standard(current)
        hidden_ref[...] = (unit * gain_next[...] + shift_next[...]).astype(BF)

    return kernel_call(
        kernel,
        "convolve_finish",
        [shape_of(rows, model, dtype) for dtype in (F32, BF, F32, BF)],
        (glued, border, depth, *norm_two, weight_out, before, *norm_next),
        scratch=[pltpu.VMEM((edge + rows, model), F32)],
        flops=2 * rows * model * model,
    )


def convolve_back_start(parts, grad, after, gain_next, mixed, depth, norm_two, weight_out, glued,
                        border):
    rows, model = after.shape
    edge = border.shape[0]
    taps = depth.shape[0]

    def kernel(
        own, via_first, via_second, grad_ref, after_ref, gain_next_ref, mixed_ref, depth_ref,
        gain, shift, w_out, glued_ref, border_ref,
        grad_out, branch_ref, main_ref, halo_ref, sums, grad_depth, padded, spread,
    ):
        incoming = own[...] + via_first[...].astype(F32) + via_second[...].astype(F32)
        slope, sum_gain, sum_shift = norm_back(after_ref[...], gain_next_ref[...], incoming)
        current = grad_ref[...] + slope
        grad_out[...] = current
        branch = current.astype(BF)
        branch_ref[...] = branch
        unit, scale = standard(mixed_ref[...])
        upper = unit * gain[...] + shift[...]
        grad_upper = dot_nt(branch, w_out[...]) * silu_slope(upper)
        inner = grad_upper * gain[...]
        first = jnp.mean(inner, axis=-1, keepdims=True)
        second = jnp.mean(inner * unit, axis=-1, keepdims=True)
        padded[:edge, :] = border_ref[...].astype(F32)
        padded[edge:, :] = glued_ref[...].astype(F32)
        spread[:edge, :] = jnp.zeros((edge, model), F32)
        spread[edge : edge + rows, :] = scale * (inner - first - unit * second)
        spread[edge + rows :, :] = jnp.zeros((edge, model), F32)
        sums[0:1, :] = sum_gain
        sums[1:2, :] = sum_shift
        sums[2:3, :] = column_sum(grad_upper * unit)
        sums[3:4, :] = column_sum(grad_upper)
        sums[4:, :] = jnp.zeros((4, model), F32)
        grad_depth[taps:, :] = jnp.zeros((grad_depth.shape[0] - taps, model), F32)
        for column in range(0, model, LANES):
            lanes = slice(column, column + LANES)
            total = jnp.zeros((rows + edge, LANES), F32)
            center = spread[edge : edge + rows, lanes]
            for tap in range(taps):
                start = edge - taps + 1 + tap
                grad_depth[tap : tap + 1, lanes] = jnp.sum(
                    center * padded[start : start + rows, lanes], axis=0, keepdims=True
                )
                begin = taps - 1 - tap
                total += (
                    spread[begin : begin + rows + edge, lanes] * depth_ref[tap : tap + 1, lanes]
                )
            halo_ref[:, lanes] = total[:edge].astype(BF)
            main_ref[:, lanes] = total[edge:]

    return kernel_call(
        kernel,
        "convolve_back_start",
        [
            shape_of(rows, model, F32),
            shape_of(rows, model, BF),
            shape_of(rows, model, F32),
            shape_of(edge, model, BF),
            shape_of(8, model, F32),
            shape_of(-(-taps // 8) * 8 + 8, model, F32),
        ],
        (*parts, grad, after, gain_next, mixed, depth, *norm_two, weight_out, glued, border),
        scratch=[
            pltpu.VMEM((edge + rows, model), F32),
            pltpu.VMEM((rows + 2 * edge, model), F32),
        ],
        flops=2 * rows * model * model,
    )


def convolve_back_finish(main, incoming, doubled, weight_in, before, gain, grad):
    rows, model = before.shape
    edge = incoming.shape[0]

    def body(main_rows, late, both, w_in, base, gain_row, grad_rows):
        glued = jnp.concatenate(
            [main_rows[: rows - edge], main_rows[rows - edge :] + late.astype(F32)], axis=0
        )
        glued = glued.astype(BF).astype(F32)
        gate = logistic(both[:, model:])
        slope = jnp.concatenate(
            [glued * gate, glued * both[:, :model] * gate * (1.0 - gate)], axis=1
        ).astype(BF)
        inner, sum_gain, sum_shift = norm_back(base, gain_row, dot_nt(slope, w_in))
        current = grad_rows + inner
        branch = current.astype(BF)
        sums = jnp.concatenate(
            [sum_gain, sum_shift, column_sum(branch), jnp.zeros((5, model), F32)], axis=0
        )
        return current, branch, slope, sums

    return fused(
        body,
        "convolve_back_finish",
        [
            shape_of(rows, model, F32),
            shape_of(rows, model, BF),
            shape_of(rows, 2 * model, BF),
            shape_of(8, model, F32),
        ],
        main,
        incoming,
        doubled,
        weight_in,
        before,
        gain,
        grad,
        flops=4 * rows * model * model,
    )


def convolve_weight_grads(hidden, slope, rest, branch, place):
    model = hidden.shape[1]

    def body(hidden_rows, slope_rows, rest_rows, branch_rows):
        return dot_tn(hidden_rows, slope_rows), dot_tn(rest_rows, branch_rows)

    grad_in, grad_out = fused(
        body,
        "convolve_weights",
        [shape_of(model, 2 * model, BF), shape_of(model, model, BF)],
        hidden,
        slope,
        rest,
        branch,
        flops=6 * hidden.shape[0] * model * model,
    )
    return tuple(
        rep_sum(lax.psum_scatter(item, "shard", scatter_dimension=0, tiled=True), place)
        for item in (grad_in, grad_out)
    )


def feed_to_attend(parts, before, bias, norm_next):
    rows, model = before.shape

    def body(own, via_first, via_second, base, bias_row, gain, shift):
        current = base.astype(F32) + 0.5 * (joined((own, via_first, via_second)) + bias_row)
        unit, unused_scale = standard(current)
        return current, unit * gain + shift

    outs = [shape_of(rows, model, F32), shape_of(rows, model, BF)]
    return fused(body, "feed_to_attend", outs, *parts, before, bias, *norm_next)


def turn_around(parts, before, bias, norm_last, cotangent):
    rows, model = before.shape

    def body(own, via_first, via_second, base, bias_row, gain, shift, grad):
        current = base + 0.5 * (joined((own, via_first, via_second)) + bias_row)
        unit, unused_scale = standard(current)
        slope, sum_gain, sum_shift = norm_back(current, gain, grad.astype(F32))
        branch = (0.5 * slope).astype(BF)
        sums = jnp.concatenate(
            [sum_gain, sum_shift, column_sum(branch), jnp.zeros((5, model), F32)], axis=0
        )
        return unit * gain + shift, slope, branch, sums

    outs = [
        shape_of(rows, model, BF),
        shape_of(rows, model, F32),
        shape_of(rows, model, BF),
        shape_of(8, model, F32),
    ]
    return fused(body, "turn_around", outs, *parts, before, bias, *norm_last, cotangent)


def attend_to_feed_back(parts, grad, before, gain):
    rows, model = before.shape

    def body(own, via_first, via_second, grad_rows, base, gain_row):
        incoming = joined((own, via_first, via_second))
        slope, sum_gain, sum_shift = norm_back(base, gain_row, incoming)
        current = grad_rows + slope
        branch = (0.5 * current).astype(BF)
        sums = jnp.concatenate(
            [sum_gain, sum_shift, column_sum(branch), jnp.zeros((5, model), F32)], axis=0
        )
        return current, branch, sums

    outs = [shape_of(rows, model, F32), shape_of(rows, model, BF), shape_of(8, model, F32)]
    return fused(body, "attend_to_feed_back", outs, *parts, grad, before, gain)


def last_step(parts, grad, before, gain):
    rows, model = before.shape

    def body(own, via_first, via_second, grad_rows, base, gain_row):
        incoming = joined((own, via_first, via_second))
        slope, sum_gain, sum_shift = norm_back(base.astype(F32), gain_row, incoming)
        sums = jnp.concatenate([sum_gain, sum_shift, jnp.zeros((6, model), F32)], axis=0)
        return grad_rows + slope, sums

    outs = [shape_of(rows, model, F32), shape_of(8, model, F32)]
    return fused(body, "last_step", outs, *parts, grad, before, gain)


def shard_gather(value, place):
    gathered = value[None]
    for bit in range(place.shards.bit_length() - 1):
        arrived = flipped(gathered, 1 << bit)
        low = jnp.bitwise_and(jnp.right_shift(place.shard, bit), 1) == 0
        gathered = jnp.concatenate(
            [jnp.where(low, gathered, arrived), jnp.where(low, arrived, gathered)], axis=0
        )
    return gathered


def shard_reduce(value, place):
    for bit in range(place.shards.bit_length() - 1):
        pairs = value.reshape(value.shape[0] // 2, 2, *value.shape[1:])
        low = jnp.bitwise_and(jnp.right_shift(place.shard, bit), 1) == 0
        staying = jnp.where(low, pairs[:, 0], pairs[:, 1])
        leaving = jnp.where(low, pairs[:, 1], pairs[:, 0])
        value = staying + flipped(leaving, 1 << bit)
    value = value[0]
    return value + flipped(value, place.shards)


def sum_everywhere(value, place):
    for bit in range((2 * place.shards).bit_length() - 1):
        value = value + flipped(value, 1 << bit)
    return value


class Place:
    def __init__(self):
        self.shards = lax.axis_size("shard")
        self.planes = self.shards // QUAD
        self.rep = lax.axis_index("rep")
        self.shard = lax.axis_index("shard")
        self.quad = self.shard % QUAD
        self.plane = self.shard // QUAD
        self.member = self.shard % SPAN
        self.group = self.shard // SPAN
        self.quad_spot = self.quad.reshape(1)
        self.plane_spot = self.plane.reshape(1)
        self.span_spot = self.member.reshape(1)
        self.group_spot = self.group.reshape(1)
        self.feed_masks = (self.shards, 2, 1)
        self.span_masks = (4, 2, 1)


def along(value, by, place):
    count = place.shards
    route = [(i, i + by) for i in range(count) if 0 <= i + by < count]
    return lax.ppermute(value, "shard", route)


def shards(
    inputs,
    ff_in,
    ff_out,
    ff_bias,
    attn_in,
    attn_out,
    conv_in,
    conv_out,
    depthwise,
    distance,
    vectors,
    attn_bias,
    cotangent,
):
    place = Place()
    rows, model = inputs.shape
    head = distance.shape[2]
    taps = depthwise.shape[1]
    edge = -(-(taps - 1) // 16) * 16
    unit = model // place.shards
    half = ff_out.shape[2] // 2
    aligned = whole_heads(attn_out[0], head)
    bias_rows = ff_bias.shape[2] // unit

    blocks = group_gather(inputs, place.feed_masks)
    small = jnp.concatenate(
        [vectors[0], attn_bias, depthwise[0], ff_bias[0].reshape(2 * bias_rows, unit)], axis=0
    )
    small = shard_gather(small, place)
    count = vectors.shape[1]
    wide = small[:, : count + 1 + taps].transpose(1, 0, 2).reshape(-1, model).astype(F32)
    vector = [wide[index : index + 1] for index in range(count)]
    out_bias = wide[count : count + 1]
    depth = wide[count + 1 :]
    feed_bias = small[:, count + 1 + taps :].reshape(place.planes, QUAD, 2, 2, half)
    feed_bias = lax.dynamic_index_in_dim(feed_bias, place.quad, 1, keepdims=False)
    feed_bias = lax.dynamic_index_in_dim(feed_bias, place.rep, 2, keepdims=False)
    feed_bias = feed_bias.transpose(1, 0, 2).reshape(2, 1, -1).astype(F32)
    first_in, first_out = feed_weights(ff_in[0, 0], ff_out[0, 0], place)
    mix_in, mix_out = attend_weights(attn_in[0], attn_out[0], head, place)
    second_in, second_out = feed_weights(ff_in[0, 1], ff_out[0, 1], place)
    glue_in = lax.all_gather(conv_in[0], "shard", axis=0, tiled=True)
    glue_out = lax.all_gather(conv_out[0], "shard", axis=0, tiled=True)
    table = wide_table(distance[0], rows)
    mix_bias = jnp.concatenate(
        [
            head_row(vector[5][0], head, place, aligned),
            jnp.zeros((1, model // SPAN), F32),
            head_row(vector[6][0], head, place, aligned),
        ],
        axis=1,
    )

    parts, saved_first = feed(
        blocks, first_in, feed_bias[0], first_out, (vector[0], vector[1]), place.feed_masks
    )
    after_first, hidden = feed_to_attend(parts, inputs, vector[2], (vector[3], vector[4]))
    parts, saved_attend = attend(
        group_gather(hidden, place.span_masks), mix_in, mix_bias, mix_out, table, place
    )
    after_attend, conv_hidden, doubled, glued = convolve_start(
        parts, after_first, out_bias, vector[7], vector[8], glue_in
    )
    border = along(glued[rows - edge :], 1, place)
    border = jnp.where(place.member == 0, jnp.zeros_like(border), border)
    mixed, rest, after_conv, hidden = convolve_finish(
        glued,
        border,
        depth,
        (vector[9], vector[10]),
        glue_out,
        after_attend,
        (vector[11], vector[12]),
    )
    parts, saved_second = feed(
        group_gather(hidden, place.feed_masks),
        second_in,
        feed_bias[1],
        second_out,
        None,
        place.feed_masks,
    )
    output, grad_last, branch, last_sums = turn_around(
        parts, after_conv, vector[13], (vector[14], vector[15]), cotangent
    )

    parts, second_grad_in, second_grad_out, second_bias = feed_back(
        group_gather(branch, place.feed_masks),
        saved_second,
        second_in,
        second_out,
        place.feed_masks,
        place.plane_spot,
        place.planes,
    )
    grad_conv, conv_branch, main, halo, conv_sums, grad_depth = convolve_back_start(
        parts,
        grad_last,
        after_conv,
        vector[11],
        mixed,
        depth,
        (vector[9], vector[10]),
        glue_out,
        glued,
        border,
    )
    incoming = along(halo, -1, place)
    incoming = jnp.where(place.member == SPAN - 1, jnp.zeros_like(incoming), incoming)
    grad_attend, branch, slope, attend_sums = convolve_back_finish(
        main, incoming, doubled, glue_in, after_attend, vector[7], grad_conv
    )
    conv_grads = convolve_weight_grads(conv_hidden, slope, rest, conv_branch, place)
    parts, mix_grad_in, mix_grad_out, mix_sums, grad_distance = attend_back(
        group_gather(branch, place.span_masks), saved_attend, mix_in, mix_out, table, place
    )
    grad_first, branch, first_sums = attend_to_feed_back(
        parts, grad_attend, after_first, vector[3]
    )
    parts, first_grad_in, first_grad_out, first_bias = feed_back(
        group_gather(branch, place.feed_masks),
        saved_first,
        first_in,
        first_out,
        place.feed_masks,
        place.plane_spot,
        place.planes,
    )
    grad_input, input_sums = last_step(parts, grad_first, inputs, vector[0])

    second_grads = feed_weight_grads(second_grad_in, second_grad_out, place)
    mix_grads = attend_weight_grads(mix_grad_in, mix_grad_out, head, place, unit, aligned)
    first_grads = feed_weight_grads(first_grad_in, first_grad_out, place)
    width = mix_sums.shape[1] // 3
    vector_grads = [
        input_sums[0:2],
        first_sums[2:3],
        first_sums[0:2],
        head_spread(mix_sums[:, :width], model, head, place, aligned),
        head_spread(mix_sums[:, 2 * width :], model, head, place, aligned),
        attend_sums[0:2],
        conv_sums[2:4],
        conv_sums[0:2],
        last_sums[2:3],
        last_sums[0:2],
        attend_sums[2:3],
        grad_depth[:taps],
    ]
    wide_grads = jnp.concatenate(vector_grads, axis=0)
    wide_grads = wide_grads.reshape(-1, place.shards, unit).transpose(1, 0, 2)
    bias_grads = jnp.zeros((place.planes, QUAD, 2, 2, half), F32)
    bias_pair = jnp.stack([first_bias, second_bias]).reshape(2, place.planes, half)
    bias_grads = lax.dynamic_update_slice(
        bias_grads,
        bias_pair.transpose(1, 0, 2)[:, None, :, None, :],
        (0, place.quad, 0, place.rep, 0),
    ).reshape(place.shards, 2 * bias_rows, unit)
    small_grads = shard_reduce(jnp.concatenate([wide_grads, bias_grads], axis=1), place)
    return (
        output,
        grad_input,
        jnp.stack([first_grads[0], second_grads[0]])[None],
        jnp.stack([first_grads[1], second_grads[1]])[None],
        small_grads[count + 1 + taps :].reshape(1, 2, -1),
        mix_grads[0][None],
        mix_grads[1][None],
        conv_grads[0][None],
        conv_grads[1][None],
        small_grads[count + 1 : count + 1 + taps][None],
        sum_everywhere(grad_distance, place)[None],
        small_grads[:count][None],
        small_grads[count : count + 1],
    )


def solution(mesh):
    in_specs = (
        P(("rep", "shard"), None),
        P(None, None, "shard", None),
        P(None, None, "shard", None),
        P(None, None, "shard"),
        P(None, "shard", None),
        P(None, "shard", None),
        P(None, "shard", None),
        P(None, "shard", None),
        P(None, None, "shard"),
        P(),
        P(None, None, "shard"),
        P(None, "shard"),
        P(("rep", "shard"), None),
    )
    out_specs = (
        P(("rep", "shard"), None),
        P(("rep", "shard"), None),
        P(None, None, "shard", None),
        P(None, None, "shard", None),
        P(None, None, "shard"),
        P(None, "shard", None),
        P(None, "shard", None),
        P(None, "shard", None),
        P(None, "shard", None),
        P(None, None, "shard"),
        P(),
        P(None, None, "shard"),
        P(None, "shard"),
    )
    return jax.shard_map(shards, mesh=mesh, in_specs=in_specs, out_specs=out_specs, check_vma=False)
```

time: 2050 us -> 743 us (0.36)
  waiting for transfers between devices: 1240 us -> 237 us
  local copies, waits for them, and re-layouts: 349 us -> 155 us
  starting transfers between devices: 9.88 us -> 183 us
  blocking collectives: 172 us -> 0 us
  matrix products: 129 us -> 0 us
  Pallas kernels: 0 us -> 123 us
  other arithmetic: 116 us -> 18.8 us
    reduce_scatter x6 -> x2, waiting for transfers between devices: 823 us -> 0.01 us  [convolve_weight_grads(): lax.psum_scatter(item, 'shard', scatter_dimension=0, tiled=True)]
    ppermute x8 -> x156, waiting for transfers between devices: 35.2 us -> 236 us  [the longest x154 234 us: flipped(): lax.ppermute(value, ('rep', 'shard'), [(i, i ^ mask) for i in range(total)])]
    all_gather x6 -> x2, waiting for transfers between devices: 200 us -> 0.01 us  [the longest x1 0.01 us: shards(): glue_in = lax.all_gather(conv_in[0], 'shard', axis=0, tiled=True)]
    ppermute x8 -> x156, starting transfers between devices: 8.25 us -> 183 us  [the longest x154 179 us: flipped(): lax.ppermute(value, ('rep', 'shard'), [(i, i ^ mask) for i in range(total)])]
    slice x14 -> x73, local copies, waits for them, and re-layouts: 195 us -> 47.2 us  [the longest x15 10.3 us: shards(): vector = [wide[index:index + 1] for index in range(count)]]
    dot_general x33 -> x0, matrix products: 129 us -> none  [the longest x8 42.9 us: back_matmul(): lax.dot_general(left_side, right_side, (((1,), (1,)), ((), ())), preferre...]
    pallas_call x0 -> x52, Pallas kernels: none -> 123 us  [kernel_call(): pl.pallas_call(body, in_specs=[pl.BlockSpec(memory_space=pltpu.SMEM)] * s...]
    unnamed x19 -> x4, waiting for transfers between devices: 110 us -> 0.73 us
  transfers between devices with their start and end apart: 24 -> 160, of which waited for: 13 -> 58; matrix products, arithmetic and copies ran while one was open for 26% -> 15% of each run, Pallas kernels for 0% -> 13%
where the time goes in v1:
time: 743 us; the launch traced here: 734 us
  waiting for transfers between devices  237 us (32%)
  starting transfers between devices  183 us (25%)
  local copies, waits for them, and re-layouts  155 us (21%)
  Pallas kernels  123 us (17%)
  other arithmetic  18.8 us (3%)
  between operations  16.6 us (2%)
    ppermute x154, waiting for transfers between devices, flipped(): lax.ppermute(value, ('rep', 'shard'), [(i, i ^ mask) for i in range(total)])  234 us
    ppermute x154, starting transfers between devices, flipped(): lax.ppermute(value, ('rep', 'shard'), [(i, i ^ mask) for i in range(total)])  179 us
    pallas_call x52, Pallas kernels, kernel_call(): pl.pallas_call(body, in_specs=[pl.BlockSpec(memory_space=pltpu.SMEM)] * s...  123 us
    unnamed x343, local copies, waits for them, and re-layouts  65.8 us
  transfers between devices with their start and end apart: 160, of which 58 were waited for; matrix products, arithmetic and copies ran while one was open for 15% of the time, Pallas kernels for 13%

profile of v1, /device:TPU:0, one launch (start us, length us, event | category | flops | bytes accessed | tf_op | source)
XLA Modules:
  0.0 734.3 jit_solution(2886613847769149342)
XLA Ops:
  10.0 2.6 collective-permute-start.1
  23.6 3.6 collective-permute-done.12
  34.5 16.7 %collective-permute-done.13 = bf16[8,56,64]{2,1,0:T(8,128)(2,1)S(1)} collective-permute-done((bf16[8,56,64]{2,1,0:T(8,128)(2,1)S(1)}, bf16[8,56,64]{2,1,0:T(8,128)(2,1)S(1)}, u32[]{:S(2)}, u32[]{:S(2)}) %collective-permute-start.13) | collective-permute-done | bytes 57376 | tf_op jit(solution)/shard_map/ppermute | solution.py:93
  59.1 3.3 collective-permute-done.2
  65.6 17.9 %collective-permute-done.15.refs_2_ = bf16[128,1024]{1,0:T(8,128)(2,1)S(1)} collective-permute-done((bf16[128,1024]{1,0:T(8,128)(2,1)S(1)}, bf16[128,1024]{1,0:T(8,128)(2,1)S(1)}, u32[]{:S(2)}, u32[]{:S(2)}) %collective-permute-start.15) | collective-permute-done | bytes 262176 | tf_op jit(solution)/shard_map/ppermute | solution.py:93
  84.0 17.1 %collective-permute-done.8.refs_2_ = bf16[256,512]{1,0:T(8,128)(2,1)S(1)} collective-permute-done((bf16[256,512]{1,0:T(8,128)(2,1)S(1)}, bf16[256,512]{1,0:T(8,128)(2,1)S(1)}, u32[]{:S(2)}, u32[]{:S(2)}) %collective-permute-start.8) | collective-permute-done | bytes 262176 | tf_op jit(solution)/shard_map/ppermute | solution.py:93
  103.0 3.5 feed_forward.5
  110.1 4.3 feed_forward.4
  128.1 4.6 collective-permute-done.24.refs_1_
  136.6 2.4 reshape_squeeze.20
  142.5 2.5 collective-permute-start.38
  145.9 2.4 collective-permute-start.37
  156.1 3.8 collective-permute-start.42
  163.9 11.3 %collective-permute-done.42.refs_1_ = bf16[64,1024]{1,0:T(8,128)(2,1)S(1)} collective-permute-done((bf16[64,1024]{1,0:T(8,128)(2,1)S(1)}, bf16[64,1024]{1,0:T(8,128)(2,1)S(1)}, u32[]{:S(2)}, u32[]{:S(2)}) %collective-permute-start.42) | collective-permute-done | bytes 131104 | tf_op jit(solution)/shard_map/ppermute | solution.py:93
  176.3 6.6 collective-permute-done.41.refs_1_
  183.0 16.9 %attend_forward.1 = (bf16[1024,1024]{1,0:T(8,128)(2,1)}, bf16[1024,384]{1,0:T(8,128)(2,1)S(1)}, bf16[1024,128]{1,0:T(8,128)(2,1)S(1)}, f32[1024,128]{1,0:T(8,128...) custom-call(s32[1]{0:T(128)} %bitcast.spot.refs_0_, bf16[128,1024]{1,0:T(8,128)(2,1)} %get-tuple-element.144.refs_1_, ...), custom_call_target="tpu_custom_call" | custom-call | flops 1610612736 | bytes 10094080 | tf_op jit(solution)/shard_map/attend_forward/pallas_call | solution.py:69
  205.2 3.9 collective-permute-done.44.refs_2_
  212.7 4.9 collective-permute-done.46.refs_1_
  222.4 3.2 convolve_start.1
  240.7 3.4 convolve_finish.1
  247.5 5.3 collective-permute-done.50.refs_2_
  258.2 3.1 collective-permute-done.55.refs_3_
  261.3 3.2 collective-permute-start.61
  269.7 2.7 collective-permute-done.61.refs_3_
  272.4 10.2 %collective-permute-start.56 = (bf16[256,512]{1,0:T(8,128)(2,1)S(1)}, bf16[256,512]{1,0:T(8,128)(2,1)S(1)}, u32[]{:S(2)}, u32[]{:S(2)}) collective-permute-start(bf16[256,512]{1,0:T(8,128)(2,1)S(1)} %order_columns.3.refs_0_), channel_id=1, source_target_pairs={{0,4},{1,5},{2,6},{3,7},{4,0},{5,1},{6,2},{7,3},{8,12},{9,13},{10,... | collective-permute-start | bytes 786440 | tf_op jit(solution)/shard_map/ppermute | solution.py:93
  282.6 16.3 %collective-permute-done.60.refs_2_ = bf16[128,1024]{1,0:T(8,128)(2,1)S(1)} collective-permute-done((bf16[128,1024]{1,0:T(8,128)(2,1)S(1)}, bf16[128,1024]{1,0:T(8,128)(2,1)S(1)}, u32[]{:S(2)}, u32[]{:S(2)}) %collective-permute-start.60) | collective-permute-done | bytes 262176 | tf_op jit(solution)/shard_map/ppermute | solution.py:93
  300.0 10.1 %collective-permute-done.57.refs_2_ = bf16[256,512]{1,0:T(8,128)(2,1)S(1)} collective-permute-done((bf16[256,512]{1,0:T(8,128)(2,1)S(1)}, bf16[256,512]{1,0:T(8,128)(2,1)S(1)}, u32[]{:S(2)}, u32[]{:S(2)}) %collective-permute-start.57) | collective-permute-done | bytes 262176 | tf_op jit(solution)/shard_map/ppermute | solution.py:93
  311.7 2.7 feed_forward.7
  316.6 2.7 feed_forward.6
  324.2 3.6 collective-permute-done.67.refs_2_
  346.9 4.5 collective-permute-done.71.refs_1_
  356.4 2.8 collective-permute-done.74
  360.9 2.9 feed_backward.5
  365.8 3.3 feed_backward.4
  373.0 3.7 collective-permute-done.80.refs_2_
  378.9 5.7 collective-permute-done.82.via_first
  385.8 9.9 %convolve_back_start.1 = (f32[128,1024]{1,0:T(8,128)S(1)}, bf16[128,1024]{1,0:T(8,128)(2,1)S(1)}, f32[128,1024]{1,0:T(8,128)S(1)}, bf16[32,1024]{1,0:T(8,128)(2,...) custom-call(f32[128,1024]{1,0:T(8,128)S(1)} %get-tuple-element.172.own, ...), custom_call_target="tpu_custom_call" | custom-call | flops 268435456 | bytes 6758400 | tf_op jit(solution)/shard_map/convolve_back_start/pallas_call | solution.py:69
  405.9 4.7 convolve_back_finish.1
  411.5 4.1 convolve_weights.1
  435.9 8.1 %collective-permute-done.119.refs_2_ = bf16[256,512]{1,0:T(8,128)(2,1)S(1)} collective-permute-done((bf16[256,512]{1,0:T(8,128)(2,1)}, bf16[256,512]{1,0:T(8,128)(2,1)S(1)}, u32[]{:S(2)}, u32[]{:S(2)}) %collective-permute-start.119) | collective-permute-done | bytes 262176 | tf_op jit(solution)/shard_map/ppermute | solution.py:93
  444.0 2.7 collective-permute-start.131
  448.7 24.2 %collective-permute-start.91 = (bf16[64,1024]{1,0:T(8,128)(2,1)S(1)}, bf16[64,1024]{1,0:T(8,128)(2,1)S(1)}, u32[]{:S(2)}, u32[]{:S(2)}) collective-permute-start(bf16[64,1024]{1,0:T(8,128)(2,1)S(1)} %slice.499), channel_id=1, source_target_pairs={{0,4},{1,5},{2,6},{3,7},{4,0},{5,1},{6,2},{7,3},{8,12},{9,13},{10,... | collective-permute-start | bytes 393224 | tf_op jit(solution)/shard_map/ppermute | solution.py:93
  474.2 3.2 collective-permute-done.91
  492.5 28.2 %attend_backward.1 = (bf16[1024,1024]{1,0:T(8,128)(2,1)}, bf16[1024,384]{1,0:T(8,128)(2,1)S(1)}, f32[512,128]{1,0:T(8,128)S(1)}, f32[8,128]{1,0:T(8,128)S(1)}, f...) custom-call(s32[1]{0:T(128)} %bitcast.spot.refs_0_, bf16[128,1024]{1,0:T(8,128)(2,1)} %get-tuple-element.181.refs_1_, ...), custom_call_target="tpu_custom_call" | custom-call | flops 3221225472 | bytes 10883072 | tf_op jit(solution)/shard_map/attend_backward/pallas_call | solution.py:69
  535.2 2.4 collective-permute-done.94.refs_2_
  541.0 3.3 attend_weights.1
  544.3 2.2 collective-permute-done.96.refs_1_
  551.5 3.6 collective-permute-start.138
  557.5 12.9 %collective-permute-done.153 = f32[73,64]{1,0:T(8,128)S(1)} collective-permute-done((f32[73,64]{1,0:T(8,128)S(1)}, f32[73,64]{1,0:T(8,128)S(1)}, u32[]{:S(2)}, u32[]{:S(2)}) %collective-permute-start.153) | collective-permute-done | bytes 18720 | tf_op jit(solution)/shard_map/ppermute | solution.py:93
  571.3 2.9 collective-permute-start.147
  574.5 17.9 %collective-permute-done.154 = f32[73,64]{1,0:T(8,128)S(1)} collective-permute-done((f32[73,64]{1,0:T(8,128)S(1)}, f32[73,64]{1,0:T(8,128)S(1)}, u32[]{:S(2)}, u32[]{:S(2)}) %collective-permute-start.154) | collective-permute-done | bytes 18720 | tf_op jit(solution)/shard_map/ppermute | solution.py:93
  597.0 2.2 collective-permute-start.144
  600.8 4.0 feed_backward.7
  624.3 2.9 feed_backward.6
  628.2 2.2 feed_in_weight.2
  631.1 3.4 collective-permute-start.112
  637.9 2.7 broadcast_in_dim_reshape.3
  651.0 2.2 feed_out_weight.2
  653.2 3.6 collective-permute-start.126
  666.1 9.6 %collective-permute-done.126.refs_2_ = bf16[128,1024]{1,0:T(8,128)(2,1)} collective-permute-done((bf16[128,1024]{1,0:T(8,128)(2,1)}, bf16[128,1024]{1,0:T(8,128)(2,1)}, u32[]{:S(2)}, u32[]{:S(2)}) %collective-permute-start.126) | collective-permute-done | bytes 262176 | tf_op jit(solution)/shard_map/ppermute | solution.py:93
  689.9 4.3 concatenate.140
  699.1 2.7 collective-permute-done.134
  701.9 5.8 collective-permute-start.135
  723.0 2.5 collective-permute-done.149
  (855 shorter events, 321.8 us)
Async XLA Ops:
  7.2 212.3 %all-gather.5.cloned.1.call-start = ((), (), s32[]{:S(2)}) async-start(), calls=%async_computation.4 | async-start | bytes 4456448 | tf_op jit(solution)/shard_map/all_gather | solution.py:1049
  7.9 229.0 %all-gather.7.cloned.1.call-start = ((), (), s32[]{:S(2)}) async-start(), calls=%async_computation.5 | async-start | bytes 2228224 | tf_op jit(solution)/shard_map/all_gather | solution.py:1050
  10.0 41.4 %collective-permute-start.1 = (bf16[128,1024]{1,0:T(8,128)(2,1)}, bf16[128,1024]{1,0:T(8,128)(2,1)}, u32[]{:S(2)}, u32[]{:S(2)}) collective-permute-start(bf16[128,1024]{1,0:T(8,128)(2,1)} %refs_4_.1), channel_id=1, source_target_pairs={{0,2},{1,3},{2,0},{3,1},{4,6},{5,7},{6,4},{7,5},{8,10},{9,11},{10,... | collective-permute-start | bytes 786440 | tf_op jit(solution)/shard_map/ppermute | solution.py:93
  19.1 13.4 %collective-permute-start.4 = (bf16[64,512]{1,0:T(8,128)(2,1)S(1)}, bf16[64,512]{1,0:T(8,128)(2,1)S(1)}, u32[]{:S(2)}, u32[]{:S(2)}) collective-permute-start(bf16[64,512]{1,0:T(8,128)(2,1)S(1)} %get-tuple-element.374), channel_id=1, source_target_pairs={{0,1},{1,0},{2,3},{3,2},{4,5},{5,4},{6,7},{7,6},{8,9},{9,8},{10,11... | collective-permute-start | bytes 196616 | tf_op jit(solution)/shard_map/ppermute | solution.py:93
  27.2 24.0 %collective-permute-start.13 = (bf16[8,56,64]{2,1,0:T(8,128)(2,1)S(1)}, bf16[8,56,64]{2,1,0:T(8,128)(2,1)S(1)}, u32[]{:S(2)}, u32[]{:S(2)}) collective-permute-start(bf16[8,56,64]{2,1,0:T(8,128)(2,1)S(1)} %pad_maximum_fusion.3), channel_id=1, source_target_pairs={{0,8},{1,9},{2,10},{3,11},{4,12},{5,13},{6,14},{7,15},{8,0},{9,1},... | collective-permute-start | bytes 172040 | tf_op jit(solution)/shard_map/ppermute | solution.py:93
  29.0 24.8 %collective-permute-start = (bf16[128,1024]{1,0:T(8,128)(2,1)S(1)}, bf16[128,1024]{1,0:T(8,128)(2,1)}, u32[]{:S(2)}, u32[]{:S(2)}) collective-permute-start(bf16[128,1024]{1,0:T(8,128)(2,1)S(1)} %copy-done.12), channel_id=1, source_target_pairs={{0,16},{1,17},{2,18},{3,19},{4,20},{5,21},{6,22},{7,23},{8,24},{9,... | collective-permute-start | bytes 786440 | tf_op jit(solution)/shard_map/ppermute | solution.py:93
  30.6 35.0 %collective-permute-start.16 = (bf16[128,1024]{1,0:T(8,128)(2,1)S(1)}, bf16[128,1024]{1,0:T(8,128)(2,1)S(1)}, u32[]{:S(2)}, u32[]{:S(2)}) collective-permute-start(bf16[128,1024]{1,0:T(8,128)(2,1)S(1)} %dynamic-slice_bitcast_fusion.1.refs_0_), channel_id=1, source_target_pairs={{0,12},{1,13},{2,14},{3,15},{4,8},{5,9},{6,10},{7,11},{8,4},{9,5},... | collective-permute-start | bytes 786440 | tf_op jit(solution)/shard_map/ppermute | solution.py:93
  32.4 51.0 %collective-permute-start.15 = (bf16[128,1024]{1,0:T(8,128)(2,1)S(1)}, bf16[128,1024]{1,0:T(8,128)(2,1)S(1)}, u32[]{:S(2)}, u32[]{:S(2)}) collective-permute-start(bf16[128,1024]{1,0:T(8,128)(2,1)S(1)} %dynamic-slice_bitcast_fusion.1.refs_0_), channel_id=1, source_target_pairs={{0,8},{1,9},{2,10},{3,11},{4,12},{5,13},{6,14},{7,15},{8,0},{9,1},... | collective-permute-start | bytes 786440 | tf_op jit(solution)/shard_map/ppermute | solution.py:93
  51.1 32.3 %collective-permute-start.14 = (bf16[128,1024]{1,0:T(8,128)(2,1)S(1)}, bf16[128,1024]{1,0:T(8,128)(2,1)S(1)}, u32[]{:S(2)}, u32[]{:S(2)}) collective-permute-start(bf16[128,1024]{1,0:T(8,128)(2,1)S(1)} %dynamic-slice_bitcast_fusion.1.refs_0_), channel_id=1, source_target_pairs={{0,4},{1,5},{2,6},{3,7},{4,0},{5,1},{6,2},{7,3},{8,12},{9,13},{10,... | collective-permute-start | bytes 786440 | tf_op jit(solution)/shard_map/ppermute | solution.py:93
  57.8 25.7 %collective-permute-start.9 = (bf16[256,512]{1,0:T(8,128)(2,1)S(1)}, bf16[256,512]{1,0:T(8,128)(2,1)S(1)}, u32[]{:S(2)}, u32[]{:S(2)}) collective-permute-start(bf16[256,512]{1,0:T(8,128)(2,1)S(1)} %order_columns.2.refs_0_), channel_id=1, source_target_pairs={{0,12},{1,13},{2,14},{3,15},{4,8},{5,9},{6,10},{7,11},{8,4},{9,5},... | collective-permute-start | bytes 786440 | tf_op jit(solution)/shard_map/ppermute | solution.py:93
  62.4 38.7 %collective-permute-start.8 = (bf16[256,512]{1,0:T(8,128)(2,1)S(1)}, bf16[256,512]{1,0:T(8,128)(2,1)S(1)}, u32[]{:S(2)}, u32[]{:S(2)}) collective-permute-start(bf16[256,512]{1,0:T(8,128)(2,1)S(1)} %order_columns.2.refs_0_), channel_id=1, source_target_pairs={{0,8},{1,9},{2,10},{3,11},{4,12},{5,13},{6,14},{7,15},{8,0},{9,1},... | collective-permute-start | bytes 786440 | tf_op jit(solution)/shard_map/ppermute | solution.py:93
  65.6 37.4 %collective-permute-start.17 = (bf16[128,1024]{1,0:T(8,128)(2,1)S(1)}, bf16[128,1024]{1,0:T(8,128)(2,1)}, u32[]{:S(2)}, u32[]{:S(2)}) collective-permute-start(bf16[128,1024]{1,0:T(8,128)(2,1)S(1)} %copy-done.12), channel_id=1, source_target_pairs={{0,1},{1,0},{2,3},{3,2},{4,5},{5,4},{6,7},{7,6},{8,9},{9,8},{10,11... | collective-permute-start | bytes 786440 | tf_op jit(solution)/shard_map/ppermute | solution.py:93
  83.5 19.4 %collective-permute-start.7 = (bf16[256,512]{1,0:T(8,128)(2,1)S(1)}, bf16[256,512]{1,0:T(8,128)(2,1)S(1)}, u32[]{:S(2)}, u32[]{:S(2)}) collective-permute-start(bf16[256,512]{1,0:T(8,128)(2,1)S(1)} %order_columns.2.refs_0_), channel_id=1, source_target_pairs={{0,4},{1,5},{2,6},{3,7},{4,0},{5,1},{6,2},{7,3},{8,12},{9,13},{10,... | collective-permute-start | bytes 786440 | tf_op jit(solution)/shard_map/ppermute | solution.py:93
  83.5 19.5 %collective-permute-start.19 = (bf16[128,1024]{1,0:T(8,128)(2,1)}, bf16[128,1024]{1,0:T(8,128)(2,1)}, u32[]{:S(2)}, u32[]{:S(2)}) collective-permute-start(bf16[128,1024]{1,0:T(8,128)(2,1)} %collective-permute-done.1.refs_2_), channel_id=1, source_target_pairs={{0,1},{1,0},{2,3},{3,2},{4,5},{5,4},{6,7},{7,6},{8,9},{9,8},{10,11... | collective-permute-start | bytes 786440 | tf_op jit(solution)/shard_map/ppermute | solution.py:93
  83.5 19.5 %collective-permute-start.18 = (bf16[128,1024]{1,0:T(8,128)(2,1)}, bf16[128,1024]{1,0:T(8,128)(2,1)}, u32[]{:S(2)}, u32[]{:S(2)}) collective-permute-start(bf16[128,1024]{1,0:T(8,128)(2,1)} %collective-permute-done.refs_1_), channel_id=1, source_target_pairs={{0,1},{1,0},{2,3},{3,2},{4,5},{5,4},{6,7},{7,6},{8,9},{9,8},{10,11... | collective-permute-start | bytes 786440 | tf_op jit(solution)/shard_map/ppermute | solution.py:93
  109.9 550.2 %reduce-scatter.5.cloned.1.call-start = ((), (), s32[]{:S(2)}) async-start(), calls=%async_computation.3 | async-start | bytes 2228224 | tf_op jit(solution)/shard_map/reduce_scatter | solution.py:886
  135.1 14.8 %collective-permute-start.27 = (bf16[128,1024]{1,0:T(8,128)(2,1)}, bf16[128,1024]{1,0:T(8,128)(2,1)}, u32[]{:S(2)}, u32[]{:S(2)}) collective-permute-start(bf16[128,1024]{1,0:T(8,128)(2,1)} %get-tuple-element.144.refs_1_), channel_id=1, source_target_pairs={{0,2},{1,3},{2,0},{3,1},{4,6},{5,7},{6,4},{7,5},{8,10},{9,11},{10,... | collective-permute-start | bytes 786440 | tf_op jit(solution)/shard_map/ppermute | solution.py:93
  156.1 19.1 %collective-permute-start.42 = (bf16[64,1024]{1,0:T(8,128)(2,1)S(1)}, bf16[64,1024]{1,0:T(8,128)(2,1)S(1)}, u32[]{:S(2)}, u32[]{:S(2)}) collective-permute-start(bf16[64,1024]{1,0:T(8,128)(2,1)S(1)} %bitcast.262), channel_id=1, source_target_pairs={{0,8},{1,9},{2,10},{3,11},{4,12},{5,13},{6,14},{7,15},{8,0},{9,1},... | collective-permute-start | bytes 393224 | tf_op jit(solution)/shard_map/ppermute | solution.py:93
  159.9 22.9 %collective-permute-start.41 = (bf16[512,384]{1,0:T(8,128)(2,1)S(1)}, bf16[512,384]{1,0:T(8,128)(2,1)S(1)}, u32[]{:S(2)}, u32[]{:S(2)}) collective-permute-start(bf16[512,384]{1,0:T(8,128)(2,1)S(1)} %order_attend_group.1.refs_0_), channel_id=1, source_target_pairs={{0,8},{1,9},{2,10},{3,11},{4,12},{5,13},{6,14},{7,15},{8,0},{9,1},... | collective-permute-start | bytes 1179656 | tf_op jit(solution)/shard_map/ppermute | solution.py:93
  160.2 22.7 %collective-permute-start.26 = (bf16[128,1024]{1,0:T(8,128)(2,1)}, bf16[128,1024]{1,0:T(8,128)(2,1)}, u32[]{:S(2)}, u32[]{:S(2)}) collective-permute-start(bf16[128,1024]{1,0:T(8,128)(2,1)} %get-tuple-element.144.refs_1_), channel_id=1, source_target_pairs={{0,1},{1,0},{2,3},{3,2},{4,5},{5,4},{6,7},{7,6},{8,9},{9,8},{10,11... | collective-permute-start | bytes 786440 | tf_op jit(solution)/shard_map/ppermute | solution.py:93
  160.3 22.7 %collective-permute-start.30 = (bf16[128,1024]{1,0:T(8,128)(2,1)S(1)}, bf16[128,1024]{1,0:T(8,128)(2,1)}, u32[]{:S(2)}, u32[]{:S(2)}) collective-permute-start(bf16[128,1024]{1,0:T(8,128)(2,1)S(1)} %collective-permute-done.29.refs_5_), channel_id=1, source_target_pairs={{0,1},{1,0},{2,3},{3,2},{4,5},{5,4},{6,7},{7,6},{8,9},{9,8},{10,11... | collective-permute-start | bytes 786440 | tf_op jit(solution)/shard_map/ppermute | solution.py:93
  162.3 20.6 %collective-permute-start.28 = (bf16[128,1024]{1,0:T(8,128)(2,1)}, bf16[128,1024]{1,0:T(8,128)(2,1)}, u32[]{:S(2)}, u32[]{:S(2)}) collective-permute-start(bf16[128,1024]{1,0:T(8,128)(2,1)} %collective-permute-done.27.refs_3_), channel_id=1, source_target_pairs={{0,1},{1,0},{2,3},{3,2},{4,5},{5,4},{6,7},{7,6},{8,9},{9,8},{10,11... | collective-permute-start | bytes 786440 | tf_op jit(solution)/shard_map/ppermute | solution.py:93
  252.8 14.3 %collective-permute-start.52 = (bf16[64,1024]{1,0:T(8,128)(2,1)S(1)}, bf16[64,1024]{1,0:T(8,128)(2,1)S(1)}, u32[]{:S(2)}, u32[]{:S(2)}) collective-permute-start(bf16[64,1024]{1,0:T(8,128)(2,1)S(1)} %slice.486), channel_id=1, source_target_pairs={{0,16},{1,17},{2,18},{3,19},{4,20},{5,21},{6,22},{7,23},{8,24},{9,... | collective-permute-start | bytes 393224 | tf_op jit(solution)/shard_map/ppermute | solution.py:93
  254.3 14.7 %collective-permute-start.51 = (bf16[64,1024]{1,0:T(8,128)(2,1)S(1)}, bf16[64,1024]{1,0:T(8,128)(2,1)S(1)}, u32[]{:S(2)}, u32[]{:S(2)}) collective-permute-start(bf16[64,1024]{1,0:T(8,128)(2,1)S(1)} %slice.485), channel_id=1, source_target_pairs={{0,2},{1,3},{2,0},{3,1},{4,6},{5,7},{6,4},{7,5},{8,10},{9,11},{10,... | collective-permute-start | bytes 393224 | tf_op jit(solution)/shard_map/ppermute | solution.py:93
  264.4 34.5 %collective-permute-start.60 = (bf16[128,1024]{1,0:T(8,128)(2,1)S(1)}, bf16[128,1024]{1,0:T(8,128)(2,1)S(1)}, u32[]{:S(2)}, u32[]{:S(2)}) collective-permute-start(bf16[128,1024]{1,0:T(8,128)(2,1)S(1)} %dynamic-slice_bitcast_fusion.refs_0_), channel_id=1, source_target_pairs={{0,8},{1,9},{2,10},{3,11},{4,12},{5,13},{6,14},{7,15},{8,0},{9,1},... | collective-permute-start | bytes 786440 | tf_op jit(solution)/shard_map/ppermute | solution.py:93
  266.1 33.5 %collective-permute-start.59 = (bf16[128,1024]{1,0:T(8,128)(2,1)S(1)}, bf16[128,1024]{1,0:T(8,128)(2,1)S(1)}, u32[]{:S(2)}, u32[]{:S(2)}) collective-permute-start(bf16[128,1024]{1,0:T(8,128)(2,1)S(1)} %dynamic-slice_bitcast_fusion.refs_0_), channel_id=1, source_target_pairs={{0,4},{1,5},{2,6},{3,7},{4,0},{5,1},{6,2},{7,3},{8,12},{9,13},{10,... | collective-permute-start | bytes 786440 | tf_op jit(solution)/shard_map/ppermute | solution.py:93
  267.1 32.5 %collective-permute-start.58 = (bf16[256,512]{1,0:T(8,128)(2,1)S(1)}, bf16[256,512]{1,0:T(8,128)(2,1)S(1)}, u32[]{:S(2)}, u32[]{:S(2)}) collective-permute-start(bf16[256,512]{1,0:T(8,128)(2,1)S(1)} %order_columns.3.refs_0_), channel_id=1, source_target_pairs={{0,12},{1,13},{2,14},{3,15},{4,8},{5,9},{6,10},{7,11},{8,4},{9,5},... | collective-permute-start | bytes 786440 | tf_op jit(solution)/shard_map/ppermute | solution.py:93
  268.9 41.2 %collective-permute-start.57 = (bf16[256,512]{1,0:T(8,128)(2,1)S(1)}, bf16[256,512]{1,0:T(8,128)(2,1)S(1)}, u32[]{:S(2)}, u32[]{:S(2)}) collective-permute-start(bf16[256,512]{1,0:T(8,128)(2,1)S(1)} %order_columns.3.refs_0_), channel_id=1, source_target_pairs={{0,8},{1,9},{2,10},{3,11},{4,12},{5,13},{6,14},{7,15},{8,0},{9,1},... | collective-permute-start | bytes 786440 | tf_op jit(solution)/shard_map/ppermute | solution.py:93
  272.4 39.0 %collective-permute-start.56 = (bf16[256,512]{1,0:T(8,128)(2,1)S(1)}, bf16[256,512]{1,0:T(8,128)(2,1)S(1)}, u32[]{:S(2)}, u32[]{:S(2)}) collective-permute-start(bf16[256,512]{1,0:T(8,128)(2,1)S(1)} %order_columns.3.refs_0_), channel_id=1, source_target_pairs={{0,4},{1,5},{2,6},{3,7},{4,0},{5,1},{6,2},{7,3},{8,12},{9,13},{10,... | collective-permute-start | bytes 786440 | tf_op jit(solution)/shard_map/ppermute | solution.py:93
  415.6 303.2 %reduce-scatter.3.cloned.1.call-start = ((), (), s32[]{:S(2)}) async-start(), calls=%async_computation.2 | async-start | bytes 4456448 | tf_op jit(solution)/shard_map/reduce_scatter | solution.py:886
  420.7 15.1 %collective-permute-start.118 = (bf16[256,512]{1,0:T(8,128)(2,1)S(1)}, bf16[256,512]{1,0:T(8,128)(2,1)S(1)}, u32[]{:S(2)}, u32[]{:S(2)}) collective-permute-start(bf16[256,512]{1,0:T(8,128)(2,1)S(1)} %get-tuple-element.217), channel_id=1, source_target_pairs={{0,4},{1,5},{2,6},{3,7},{4,0},{5,1},{6,2},{7,3},{8,12},{9,13},{10,... | collective-permute-start | bytes 786440 | tf_op jit(solution)/shard_map/ppermute | solution.py:93
  422.3 21.6 %collective-permute-start.119 = (bf16[256,512]{1,0:T(8,128)(2,1)}, bf16[256,512]{1,0:T(8,128)(2,1)S(1)}, u32[]{:S(2)}, u32[]{:S(2)}) collective-permute-start(bf16[256,512]{1,0:T(8,128)(2,1)} %get-tuple-element.218), channel_id=1, source_target_pairs={{0,8},{1,9},{2,10},{3,11},{4,12},{5,13},{6,14},{7,15},{8,0},{9,1},... | collective-permute-start | bytes 786440 | tf_op jit(solution)/shard_map/ppermute | solution.py:93
  423.7 20.3 %collective-permute-start.120 = (bf16[256,512]{1,0:T(8,128)(2,1)}, bf16[256,512]{1,0:T(8,128)(2,1)}, u32[]{:S(2)}, u32[]{:S(2)}) collective-permute-start(bf16[256,512]{1,0:T(8,128)(2,1)} %get-tuple-element.219), channel_id=1, source_target_pairs={{0,12},{1,13},{2,14},{3,15},{4,8},{5,9},{6,10},{7,11},{8,4},{9,5},... | collective-permute-start | bytes 786440 | tf_op jit(solution)/shard_map/ppermute | solution.py:93
  425.1 22.6 %collective-permute-start.86 = (bf16[128,1024]{1,0:T(8,128)(2,1)}, bf16[128,1024]{1,0:T(8,128)(2,1)}, u32[]{:S(2)}, u32[]{:S(2)}) collective-permute-start(bf16[128,1024]{1,0:T(8,128)(2,1)} %get-tuple-element.181.refs_1_), channel_id=1, source_target_pairs={{0,2},{1,3},{2,0},{3,1},{4,6},{5,7},{6,4},{7,5},{8,10},{9,11},{10,... | collective-permute-start | bytes 786440 | tf_op jit(solution)/shard_map/ppermute | solution.py:93
  427.2 46.4 %collective-permute-start.90 = (bf16[64,1024]{1,0:T(8,128)(2,1)S(1)}, bf16[64,1024]{1,0:T(8,128)(2,1)S(1)}, u32[]{:S(2)}, u32[]{:S(2)}) collective-permute-start(bf16[64,1024]{1,0:T(8,128)(2,1)S(1)} %slice.498), channel_id=1, source_target_pairs={{0,2},{1,3},{2,0},{3,1},{4,6},{5,7},{6,4},{7,5},{8,10},{9,11},{10,... | collective-permute-start | bytes 393224 | tf_op jit(solution)/shard_map/ppermute | solution.py:93
  435.9 42.9 %collective-permute-start.129 = (bf16[128,1024]{1,0:T(8,128)(2,1)S(1)}, bf16[128,1024]{1,0:T(8,128)(2,1)S(1)}, u32[]{:S(2)}, u32[]{:S(2)}) collective-permute-start(bf16[128,1024]{1,0:T(8,128)(2,1)S(1)} %get-tuple-element.233), channel_id=1, source_target_pairs={{0,4},{1,5},{2,6},{3,7},{4,0},{5,1},{6,2},{7,3},{8,12},{9,13},{10,... | collective-permute-start | bytes 786440 | tf_op jit(solution)/shard_map/ppermute | solution.py:93
  444.0 34.8 %collective-permute-start.130 = (bf16[128,1024]{1,0:T(8,128)(2,1)S(1)}, bf16[128,1024]{1,0:T(8,128)(2,1)S(1)}, u32[]{:S(2)}, u32[]{:S(2)}) collective-permute-start(bf16[128,1024]{1,0:T(8,128)(2,1)S(1)} %get-tuple-element.234), channel_id=1, source_target_pairs={{0,8},{1,9},{2,10},{3,11},{4,12},{5,13},{6,14},{7,15},{8,0},{9,1},... | collective-permute-start | bytes 786440 | tf_op jit(solution)/shard_map/ppermute | solution.py:93
  444.0 36.0 %collective-permute-start.131 = (bf16[128,1024]{1,0:T(8,128)(2,1)S(1)}, bf16[128,1024]{1,0:T(8,128)(2,1)S(1)}, u32[]{:S(2)}, u32[]{:S(2)}) collective-permute-start(bf16[128,1024]{1,0:T(8,128)(2,1)S(1)} %get-tuple-element.235), channel_id=1, source_target_pairs={{0,12},{1,13},{2,14},{3,15},{4,8},{5,9},{6,10},{7,11},{8,4},{9,5},... | collective-permute-start | bytes 786440 | tf_op jit(solution)/shard_map/ppermute | solution.py:93
  448.7 28.7 %collective-permute-start.91 = (bf16[64,1024]{1,0:T(8,128)(2,1)S(1)}, bf16[64,1024]{1,0:T(8,128)(2,1)S(1)}, u32[]{:S(2)}, u32[]{:S(2)}) collective-permute-start(bf16[64,1024]{1,0:T(8,128)(2,1)S(1)} %slice.499), channel_id=1, source_target_pairs={{0,4},{1,5},{2,6},{3,7},{4,0},{5,1},{6,2},{7,3},{8,12},{9,13},{10,... | collective-permute-start | bytes 393224 | tf_op jit(solution)/shard_map/ppermute | solution.py:93
  479.5 12.9 %collective-permute-start.89 = (bf16[128,1024]{1,0:T(8,128)(2,1)}, bf16[128,1024]{1,0:T(8,128)(2,1)}, u32[]{:S(2)}, u32[]{:S(2)}) collective-permute-start(bf16[128,1024]{1,0:T(8,128)(2,1)} %collective-permute-done.88.refs_5_), channel_id=1, source_target_pairs={{0,1},{1,0},{2,3},{3,2},{4,5},{5,4},{6,7},{7,6},{8,9},{9,8},{10,11... | collective-permute-start | bytes 786440 | tf_op jit(solution)/shard_map/ppermute | solution.py:93
  489.4 31.3 %collective-permute-start.132 = (bf16[128,1024]{1,0:T(8,128)(2,1)S(1)}, bf16[128,1024]{1,0:T(8,128)(2,1)S(1)}, u32[]{:S(2)}, u32[]{:S(2)}) collective-permute-start(bf16[128,1024]{1,0:T(8,128)(2,1)S(1)} %sum_feed_out.3), channel_id=1, source_target_pairs={{0,16},{1,17},{2,18},{3,19},{4,20},{5,21},{6,22},{7,23},{8,24},{9,... | collective-permute-start | bytes 786440 | tf_op jit(solution)/shard_map/ppermute | solution.py:93
  491.0 30.6 %collective-permute-start.124 = (bf16[256,512]{1,0:T(8,128)(2,1)S(1)}, bf16[256,512]{1,0:T(8,128)(2,1)S(1)}, u32[]{:S(2)}, u32[]{:S(2)}) collective-permute-start(bf16[256,512]{1,0:T(8,128)(2,1)S(1)} %order_grad_in.3), channel_id=1, source_target_pairs={{0,16},{1,17},{2,18},{3,19},{4,20},{5,21},{6,22},{7,23},{8,24},{9,... | collective-permute-start | bytes 786440 | tf_op jit(solution)/shard_map/ppermute | solution.py:93
  547.4 23.0 %collective-permute-start.99 = (bf16[128,1024]{1,0:T(8,128)(2,1)S(1)}, bf16[128,1024]{1,0:T(8,128)(2,1)S(1)}, u32[]{:S(2)}, u32[]{:S(2)}) collective-permute-start(bf16[128,1024]{1,0:T(8,128)(2,1)S(1)} %get-tuple-element.192.refs_0_), channel_id=1, source_target_pairs={{0,2},{1,3},{2,0},{3,1},{4,6},{5,7},{6,4},{7,5},{8,10},{9,11},{10,... | collective-permute-start | bytes 786440 | tf_op jit(solution)/shard_map/ppermute | solution.py:93
  551.5 42.5 %collective-permute-start.138 = (bf16[512,384]{1,0:T(8,128)(2,1)}, bf16[512,384]{1,0:T(8,128)(2,1)}, u32[]{:S(2)}, u32[]{:S(2)}) collective-permute-start(bf16[512,384]{1,0:T(8,128)(2,1)} %dynamic-slice_convert_fusion), channel_id=1, source_target_pairs={{0,8},{1,9},{2,10},{3,11},{4,12},{5,13},{6,14},{7,15},{8,0},{9,1},... | collective-permute-start | bytes 1179656 | tf_op jit(solution)/shard_map/ppermute | solution.py:93
  555.2 15.2 %collective-permute-start.153 = (f32[73,64]{1,0:T(8,128)S(1)}, f32[73,64]{1,0:T(8,128)S(1)}, u32[]{:S(2)}, u32[]{:S(2)}) collective-permute-start(f32[73,64]{1,0:T(8,128)S(1)} %add.237), channel_id=1, source_target_pairs={{0,4},{1,5},{2,6},{3,7},{4,0},{5,1},{6,2},{7,3},{8,12},{9,13},{10,... | collective-permute-start | bytes 56072 | tf_op jit(solution)/shard_map/ppermute | solution.py:93
  556.1 36.3 %collective-permute-start.100 = (bf16[64,1024]{1,0:T(8,128)(2,1)S(1)}, bf16[64,1024]{1,0:T(8,128)(2,1)S(1)}, u32[]{:S(2)}, u32[]{:S(2)}) collective-permute-start(bf16[64,1024]{1,0:T(8,128)(2,1)S(1)} %slice.502), channel_id=1, source_target_pairs={{0,2},{1,3},{2,0},{3,1},{4,6},{5,7},{6,4},{7,5},{8,10},{9,11},{10,... | collective-permute-start | bytes 393224 | tf_op jit(solution)/shard_map/ppermute | solution.py:93
  570.4 22.0 %collective-permute-start.154 = (f32[73,64]{1,0:T(8,128)S(1)}, f32[73,64]{1,0:T(8,128)S(1)}, u32[]{:S(2)}, u32[]{:S(2)}) collective-permute-start(f32[73,64]{1,0:T(8,128)S(1)} %add.238), channel_id=1, source_target_pairs={{0,8},{1,9},{2,10},{3,11},{4,12},{5,13},{6,14},{7,15},{8,0},{9,1},... | collective-permute-start | bytes 56072 | tf_op jit(solution)/shard_map/ppermute | solution.py:93
  571.1 21.9 %collective-permute-start.101 = (bf16[64,1024]{1,0:T(8,128)(2,1)}, bf16[64,1024]{1,0:T(8,128)(2,1)}, u32[]{:S(2)}, u32[]{:S(2)}) collective-permute-start(bf16[64,1024]{1,0:T(8,128)(2,1)} %slice.503), channel_id=1, source_target_pairs={{0,16},{1,17},{2,18},{3,19},{4,20},{5,21},{6,22},{7,23},{8,24},{9,... | collective-permute-start | bytes 393224 | tf_op jit(solution)/shard_map/ppermute | solution.py:93
  571.3 36.8 %collective-permute-start.147 = (bf16[64,1024]{1,0:T(8,128)(2,1)}, bf16[64,1024]{1,0:T(8,128)(2,1)}, u32[]{:S(2)}, u32[]{:S(2)}) collective-permute-start(bf16[64,1024]{1,0:T(8,128)(2,1)} %dynamic-slice_convert_fusion.1), channel_id=1, source_target_pairs={{0,8},{1,9},{2,10},{3,11},{4,12},{5,13},{6,14},{7,15},{8,0},{9,1},... | collective-permute-start | bytes 393224 | tf_op jit(solution)/shard_map/ppermute | solution.py:93
  596.9 12.8 %collective-permute-start.145 = (bf16[64,384]{1,0:T(8,128)(2,1)S(1)}, bf16[64,384]{1,0:T(8,128)(2,1)S(1)}, u32[]{:S(2)}, u32[]{:S(2)}) collective-permute-start(bf16[64,384]{1,0:T(8,128)(2,1)S(1)} %get-tuple-element.342), channel_id=1, source_target_pairs={{0,7},{1,6},{2,5},{3,4},{4,3},{5,2},{6,1},{7,0},{8,15},{9,14},{10,... | collective-permute-start | bytes 147464 | tf_op jit(solution)/shard_map/ppermute | solution.py:93
  597.0 14.2 %collective-permute-start.144 = (bf16[64,384]{1,0:T(8,128)(2,1)S(1)}, bf16[64,384]{1,0:T(8,128)(2,1)S(1)}, u32[]{:S(2)}, u32[]{:S(2)}) collective-permute-start(bf16[64,384]{1,0:T(8,128)(2,1)S(1)} %get-tuple-element.343), channel_id=1, source_target_pairs={{0,6},{1,7},{2,4},{3,5},{4,2},{5,3},{6,0},{7,1},{8,14},{9,15},{10,... | collective-permute-start | bytes 147464 | tf_op jit(solution)/shard_map/ppermute | solution.py:93
  608.1 38.2 %collective-permute-start.106 = (bf16[512,1024]{1,0:T(8,128)(2,1)}, bf16[512,1024]{1,0:T(8,128)(2,1)}, u32[]{:S(2)}, u32[]{:S(2)}) collective-permute-start(bf16[512,1024]{1,0:T(8,128)(2,1)} %get-tuple-element.196), channel_id=1, source_target_pairs={{0,1},{1,0},{2,3},{3,2},{4,5},{5,4},{6,7},{7,6},{8,9},{9,8},{10,11... | collective-permute-start | bytes 3145736 | tf_op jit(solution)/shard_map/ppermute | solution.py:93
  619.1 15.7 %collective-permute-start.146 = (bf16[512,384]{1,0:T(8,128)(2,1)S(1)}, bf16[512,384]{1,0:T(8,128)(2,1)S(1)}, u32[]{:S(2)}, u32[]{:S(2)}) collective-permute-start(bf16[512,384]{1,0:T(8,128)(2,1)S(1)} %order_attend_grad.1), channel_id=1, source_target_pairs={{0,16},{1,17},{2,18},{3,19},{4,20},{5,21},{6,22},{7,23},{8,24},{9,... | collective-permute-start | bytes 1179656 | tf_op jit(solution)/shard_map/ppermute | solution.py:93
  630.4 22.8 %collective-permute-start.111 = (bf16[256,512]{1,0:T(8,128)(2,1)}, bf16[256,512]{1,0:T(8,128)(2,1)S(1)}, u32[]{:S(2)}, u32[]{:S(2)}) collective-permute-start(bf16[256,512]{1,0:T(8,128)(2,1)} %get-tuple-element.209), channel_id=1, source_target_pairs={{0,4},{1,5},{2,6},{3,7},{4,0},{5,1},{6,2},{7,3},{8,12},{9,13},{10,... | collective-permute-start | bytes 786440 | tf_op jit(solution)/shard_map/ppermute | solution.py:93
  631.1 22.2 %collective-permute-start.112 = (bf16[256,512]{1,0:T(8,128)(2,1)}, bf16[256,512]{1,0:T(8,128)(2,1)}, u32[]{:S(2)}, u32[]{:S(2)}) collective-permute-start(bf16[256,512]{1,0:T(8,128)(2,1)} %get-tuple-element.210), channel_id=1, source_target_pairs={{0,8},{1,9},{2,10},{3,11},{4,12},{5,13},{6,14},{7,15},{8,0},{9,1},... | collective-permute-start | bytes 786440 | tf_op jit(solution)/shard_map/ppermute | solution.py:93
  634.5 22.4 %collective-permute-start.113 = (bf16[256,512]{1,0:T(8,128)(2,1)}, bf16[256,512]{1,0:T(8,128)(2,1)}, u32[]{:S(2)}, u32[]{:S(2)}) collective-permute-start(bf16[256,512]{1,0:T(8,128)(2,1)} %get-tuple-element.211), channel_id=1, source_target_pairs={{0,12},{1,13},{2,14},{3,15},{4,8},{5,9},{6,10},{7,11},{8,4},{9,5},... | collective-permute-start | bytes 786440 | tf_op jit(solution)/shard_map/ppermute | solution.py:93
  653.2 22.4 %collective-permute-start.126 = (bf16[128,1024]{1,0:T(8,128)(2,1)}, bf16[128,1024]{1,0:T(8,128)(2,1)}, u32[]{:S(2)}, u32[]{:S(2)}) collective-permute-start(bf16[128,1024]{1,0:T(8,128)(2,1)} %get-tuple-element.226), channel_id=1, source_target_pairs={{0,8},{1,9},{2,10},{3,11},{4,12},{5,13},{6,14},{7,15},{8,0},{9,1},... | collective-permute-start | bytes 786440 | tf_op jit(solution)/shard_map/ppermute | solution.py:93
  656.9 18.8 %collective-permute-start.127 = (bf16[128,1024]{1,0:T(8,128)(2,1)}, bf16[128,1024]{1,0:T(8,128)(2,1)}, u32[]{:S(2)}, u32[]{:S(2)}) collective-permute-start(bf16[128,1024]{1,0:T(8,128)(2,1)} %get-tuple-element.227), channel_id=1, source_target_pairs={{0,12},{1,13},{2,14},{3,15},{4,8},{5,9},{6,10},{7,11},{8,4},{9,5},... | collective-permute-start | bytes 786440 | tf_op jit(solution)/shard_map/ppermute | solution.py:93
  660.1 16.9 %collective-permute-start.116 = (bf16[64,512]{1,0:T(8,128)(2,1)}, bf16[64,512]{1,0:T(8,128)(2,1)S(1)}, u32[]{:S(2)}, u32[]{:S(2)}) collective-permute-start(bf16[64,512]{1,0:T(8,128)(2,1)} %get-tuple-element.360), channel_id=1, source_target_pairs={{0,3},{1,2},{2,1},{3,0},{4,7},{5,6},{6,5},{7,4},{8,11},{9,10},{10,... | collective-permute-start | bytes 196616 | tf_op jit(solution)/shard_map/ppermute | solution.py:93
  660.1 26.6 %collective-permute-start.150 = (bf16[64,1024]{1,0:T(8,128)(2,1)}, bf16[64,1024]{1,0:T(8,128)(2,1)}, u32[]{:S(2)}, u32[]{:S(2)}) collective-permute-start(bf16[64,1024]{1,0:T(8,128)(2,1)} %reduce-scatter.5.cloned.1.call-done), channel_id=1, source_target_pairs={{0,16},{1,17},{2,18},{3,19},{4,20},{5,21},{6,22},{7,23},{8,24},{9,... | collective-permute-start | bytes 393224 | tf_op jit(solution)/shard_map/ppermute | solution.py:93
  665.5 16.1 %collective-permute-start.115 = (bf16[64,512]{1,0:T(8,128)(2,1)}, bf16[64,512]{1,0:T(8,128)(2,1)S(1)}, u32[]{:S(2)}, u32[]{:S(2)}) collective-permute-start(bf16[64,512]{1,0:T(8,128)(2,1)} %get-tuple-element.361), channel_id=1, source_target_pairs={{0,2},{1,3},{2,0},{3,1},{4,6},{5,7},{6,4},{7,5},{8,10},{9,11},{10,... | collective-permute-start | bytes 196616 | tf_op jit(solution)/shard_map/ppermute | solution.py:93
  675.7 12.7 %collective-permute-start.109 = (bf16[128,1024]{1,0:T(8,128)(2,1)}, bf16[128,1024]{1,0:T(8,128)(2,1)S(1)}, u32[]{:S(2)}, u32[]{:S(2)}) collective-permute-start(bf16[128,1024]{1,0:T(8,128)(2,1)} %get-tuple-element.200), channel_id=1, source_target_pairs={{0,16},{1,17},{2,18},{3,19},{4,20},{5,21},{6,22},{7,23},{8,24},{9,... | collective-permute-start | bytes 786440 | tf_op jit(solution)/shard_map/ppermute | solution.py:93
  682.3 12.8 %collective-permute-start.128 = (bf16[128,1024]{1,0:T(8,128)(2,1)S(1)}, bf16[128,1024]{1,0:T(8,128)(2,1)}, u32[]{:S(2)}, u32[]{:S(2)}) collective-permute-start(bf16[128,1024]{1,0:T(8,128)(2,1)S(1)} %sum_feed_out.2), channel_id=1, source_target_pairs={{0,16},{1,17},{2,18},{3,19},{4,20},{5,21},{6,22},{7,23},{8,24},{9,... | collective-permute-start | bytes 786440 | tf_op jit(solution)/shard_map/ppermute | solution.py:93
  685.2 22.5 %collective-permute-start.117 = (bf16[256,512]{1,0:T(8,128)(2,1)S(1)}, bf16[256,512]{1,0:T(8,128)(2,1)}, u32[]{:S(2)}, u32[]{:S(2)}) collective-permute-start(bf16[256,512]{1,0:T(8,128)(2,1)S(1)} %order_grad_in.2), channel_id=1, source_target_pairs={{0,16},{1,17},{2,18},{3,19},{4,20},{5,21},{6,22},{7,23},{8,24},{9,... | collective-permute-start | bytes 786440 | tf_op jit(solution)/shard_map/ppermute | solution.py:93
  (263 other events, 2079.8 us)
Sparse Core Ops, SparseCore 0:
  10.2 86.2 all-gather.4
  110.0 46.5 all-gather.6
  415.7 75.2 reduce-scatter.4
  529.4 84.2 reduce-scatter.2

commit v2 on v1

v2 whole, which is shorter than its diff:
```python
import jax
import jax.numpy as jnp
from jax import lax
from jax.experimental import pallas as pl
from jax.experimental.pallas import tpu as pltpu
from jax.sharding import PartitionSpec as P

LEFT = 64
RIGHT = 8
SPAN = 8
QUAD = 4
EPSILON = 1e-05
BF = jnp.bfloat16
F32 = jnp.float32
MIB = 1 << 20


def dot_nn(left, right):
    return jnp.dot(left, right, preferred_element_type=F32)


def dot_nt(left, right):
    return lax.dot_general(left, right, (((1,), (1,)), ((), ())), preferred_element_type=F32)


def dot_tn(left, right):
    return lax.dot_general(left, right, (((0,), (0,)), ((), ())), preferred_element_type=F32)


def column_sum(values):
    return jnp.sum(values.astype(F32), axis=0, keepdims=True)


def standard(values):
    center = values - jnp.mean(values, axis=-1, keepdims=True)
    scale = lax.rsqrt(jnp.mean(center * center, axis=-1, keepdims=True) + EPSILON)
    return center * scale, scale


def norm_back(values, gain, grad):
    unit, scale = standard(values)
    inner = grad * gain
    first = jnp.mean(inner, axis=-1, keepdims=True)
    second = jnp.mean(inner * unit, axis=-1, keepdims=True)
    return scale * (inner - first - unit * second), column_sum(grad * unit), column_sum(grad)


def logistic(values):
    return 1.0 / (1.0 + jnp.exp(-values))


def silu_slope(values):
    gate = logistic(values)
    return gate * (1.0 + values * (1.0 - gate))


def vmem(count):
    return [pl.BlockSpec(memory_space=pltpu.VMEM)] * count


def shape_of(rows, columns, dtype):
    return jax.ShapeDtypeStruct((rows, columns), dtype)


def kernel_call(body, name, outs, operands, scalars=0, scratch=(), flops=0, waits=()):
    moved = sum(item.size * item.dtype.itemsize for item in (*operands[scalars:], *outs))
    count = len(operands)

    def kernel(*refs):
        body(*refs[:count], *refs[count + len(waits) :])

    return pl.pallas_call(
        kernel,
        in_specs=[pl.BlockSpec(memory_space=pltpu.SMEM)] * scalars
        + vmem(count - scalars)
        + [pl.BlockSpec(memory_space=pl.ANY)] * len(waits),
        out_specs=vmem(len(outs)),
        out_shape=list(outs),
        scratch_shapes=list(scratch),
        compiler_params=pltpu.CompilerParams(vmem_limit_bytes=40 * MIB),
        cost_estimate=pl.CostEstimate(flops=flops, bytes_accessed=moved, transcendentals=0),
        name=name,
    )(*operands, *waits)


def fused(body, name, outs, *operands, flops=0, waits=()):
    def kernel(*refs):
        results = body(*[ref[...] for ref in refs[: len(operands)]])
        for ref, value in zip(refs[len(operands) :], results):
            ref[...] = value.astype(ref.dtype)

    return kernel_call(kernel, name, outs, operands, flops=flops, waits=waits)


def flipped(value, mask):
    total = lax.axis_size("rep") * lax.axis_size("shard")
    return lax.ppermute(value, ("rep", "shard"), [(i, i ^ mask) for i in range(total)])


def square_gather(value, masks):
    first, second = masks
    return [
        value,
        flipped(value, first),
        flipped(value, second),
        flipped(value, first | second),
    ]


def square_reduce(parts, masks):
    first, second = masks
    own, via_first, via_second, cross = parts
    return [
        own,
        flipped(cross, first | second),
        flipped(via_first, first),
        flipped(via_second, second),
    ]


def joined(parts):
    return parts[0] + sum(part.astype(F32) for part in parts[1:])


def place_feed(spot, packs, w_in, w_out, unit, half):
    plane, second, core = spot[0], spot[1], spot[2]
    for step, near, ref, start in packs:
        column = (plane ^ step) * 2
        for turn in range(2):
            row = ((column + (second ^ turn)) * 2 + (core ^ near)) * unit
            source = slice(start + turn * unit, start + (turn + 1) * unit)
            w_in[pl.ds(pl.multiple_of(row, unit), unit), :] = ref[source, :]
        row = (column + (core ^ near)) * half
        source = slice(start + 2 * unit, start + 2 * unit + half)
        w_out[pl.ds(pl.multiple_of(row, half), half), :] = ref[source, :]


def pack_views(refs, place):
    planes, size = place.planes, place.pack_rows
    views = []
    if len(refs) == 2:
        for near, ref in enumerate(refs):
            views += [(step, near, ref, step * size) for step in range(planes)]
        return views
    for index, ref in enumerate(refs):
        views.append((index % planes, index // planes, ref, 0))
    return views


def feed(pieces, packs, spot, bias, wide, norm_row, masks, place, waits=()):
    rows, model = pieces[0].shape
    inner = bias.shape[1]
    count, total = len(pieces), len(pieces) * rows
    unit, half = place.unit, place.half

    def kernel(spot_ref, *refs):
        piece_refs, pack_refs = refs[:count], refs[count : count + len(packs)]
        bias_ref, wide_ref, hidden, upper, active = refs[count + len(packs) :][:5]
        outs = refs[count + len(packs) + 5 : -2]
        w_in, w_out = refs[-2:]
        place_feed(spot_ref, pack_views(pack_refs, place), w_in, w_out, unit, half)
        for index, ref in enumerate(piece_refs):
            block = ref[...]
            if norm_row is not None:
                scaled, unused_scale = standard(block.astype(F32))
                gain = wide_ref[norm_row : norm_row + 1, :]
                shift = wide_ref[norm_row + 1 : norm_row + 2, :]
                block = (scaled * gain + shift).astype(BF)
            hidden[index * rows : (index + 1) * rows, :] = block
        before = dot_nn(hidden[...], w_in[...]) + bias_ref[...]
        upper[...] = before
        active[...] = (before * logistic(before)).astype(BF)
        result = dot_nn(active[...], w_out[...])
        for index, ref in enumerate(outs):
            ref[...] = result[index * rows : (index + 1) * rows].astype(ref.dtype)

    outs = [
        shape_of(total, model, BF),
        shape_of(total, inner, F32),
        shape_of(total, inner, BF),
        shape_of(rows, model, F32),
    ] + [shape_of(rows, model, BF)] * (count - 1)
    results = kernel_call(
        kernel,
        "feed_forward",
        outs,
        (spot, *pieces, *packs, bias, wide),
        scalars=1,
        scratch=[pltpu.VMEM((model, inner), BF), pltpu.VMEM((inner, model), BF)],
        flops=4 * total * model * inner,
        waits=waits,
    )
    return square_reduce(results[3:], masks), results[:3]


def feed_back(pieces, packs, spot, saved, masks, place, waits=()):
    hidden, upper, active = saved
    rows, model = pieces[0].shape
    total, inner = upper.shape
    count = len(pieces)
    unit, half = place.unit, place.half

    def kernel(spot_ref, *refs):
        piece_refs, pack_refs = refs[:count], refs[count : count + len(packs)]
        upper_ref, branch, slope, sums = refs[count + len(packs) :][:4]
        outs = refs[count + len(packs) + 4 : -2]
        w_in, w_out = refs[-2:]
        place_feed(spot_ref, pack_views(pack_refs, place), w_in, w_out, unit, half)
        for index, ref in enumerate(piece_refs):
            branch[index * rows : (index + 1) * rows, :] = ref[...]
        grad = dot_nt(branch[...], w_out[...]) * silu_slope(upper_ref[...])
        slope[...] = grad.astype(BF)
        sums[...] = column_sum(slope[...])
        result = dot_nt(slope[...], w_in[...])
        for index, ref in enumerate(outs):
            ref[...] = result[index * rows : (index + 1) * rows].astype(ref.dtype)

    outs = [
        shape_of(total, model, BF),
        shape_of(total, inner, BF),
        shape_of(1, inner, F32),
        shape_of(rows, model, F32),
    ] + [shape_of(rows, model, BF)] * (count - 1)
    results = kernel_call(
        kernel,
        "feed_backward",
        outs,
        (spot, *pieces, *packs, upper),
        scalars=1,
        scratch=[pltpu.VMEM((model, inner), BF), pltpu.VMEM((inner, model), BF)],
        flops=4 * total * model * inner,
        waits=waits,
    )
    branch, slope, sums = results[:3]
    parts = square_reduce(results[3:], masks)
    planes, size = place.planes, place.pack_rows

    def weights(spot_ref, hidden_ref, active_ref, branch_ref, slope_ref, kept, sent, w_in, w_out):
        w_in[...] = dot_tn(hidden_ref[...], slope_ref[...])
        w_out[...] = dot_tn(active_ref[...], branch_ref[...])
        plane, second, core = spot_ref[0], spot_ref[1], spot_ref[2]
        for near, ref in enumerate((kept, sent)):
            for step in range(planes):
                column = (plane ^ step) * 2
                start = step * size
                for turn in range(2):
                    row = ((column + (second ^ turn)) * 2 + (core ^ near)) * unit
                    target = slice(start + turn * unit, start + (turn + 1) * unit)
                    source = pl.ds(pl.multiple_of(row, unit), unit)
                    ref[target, :] = w_in[source, :].astype(BF)
                row = (column + (core ^ near)) * half
                target = slice(start + 2 * unit, start + 2 * unit + half)
                ref[target, :] = w_out[pl.ds(pl.multiple_of(row, half), half), :].astype(BF)

    kept, sent = kernel_call(
        weights,
        "feed_weights",
        [shape_of(planes * size, inner, BF)] * 2,
        (spot, hidden, active, branch, slope),
        scalars=1,
        scratch=[pltpu.VMEM((model, inner), F32), pltpu.VMEM((inner, model), F32)],
        flops=4 * total * model * inner,
    )
    return parts, kept, flipped(sent, 1), sums


def feed_pack(weight_in, weight_out, place):
    rows, hidden = weight_in.shape
    half = weight_out.shape[0] // 2
    columns = weight_in.reshape(rows, place.planes, 2, 2, 2, half)
    columns = lax.dynamic_index_in_dim(columns, place.rep, 4, keepdims=False)
    own = lax.dynamic_index_in_dim(columns, place.second, 2, keepdims=False)
    other = lax.dynamic_index_in_dim(columns, 1 - place.second, 2, keepdims=False)
    own, other = (item.reshape(rows, 2 * place.planes * half) for item in (own, other))
    part_out = lax.dynamic_slice_in_dim(weight_out, place.rep * half, half, 0)
    return own, flipped(other, 2), part_out


def pack_rows(parts, waits=()):
    def body(*values):
        return (jnp.concatenate(values, axis=0),)

    rows = sum(item.shape[0] for item in parts)
    out = shape_of(rows, parts[0].shape[1], BF)
    return fused(body, "pack_rows", [out], *parts, waits=waits)[0]


def plane_bits(place):
    return range(place.planes.bit_length() - 1)


def plane_gather(pack, place):
    pieces = {0: pack}
    for bit in reversed(plane_bits(place)):
        for step in sorted(pieces):
            pieces[step | 1 << bit] = flipped(pieces[step], QUAD << bit)
    near = [pieces[step] for step in range(place.planes)]
    return near + [flipped(item, 1) for item in near]


def plane_reduce(kept, swapped, place):
    size = place.pack_rows
    planes = place.planes

    def total(kept_part, swapped_part):
        both = kept_part.astype(F32) + swapped_part.astype(F32)
        return [both[step * size : (step + 1) * size] for step in range(planes)]

    outs = [shape_of(size, kept.shape[1], F32)]
    outs += [shape_of(size, kept.shape[1], BF)] * (planes - 1)
    pieces = fused(total, "feed_core_sum", outs, kept, swapped)
    pieces = {step: [piece] for step, piece in enumerate(pieces)}
    for bit in plane_bits(place):
        for step in [step for step in sorted(pieces) if step >> bit & 1]:
            values = pieces.pop(step)
            value = values[0] if len(values) == 1 else plane_add(values)
            pieces[step ^ 1 << bit].append(flipped(value, QUAD << bit))
    return plane_add(pieces[0])


def plane_add(values):
    def body(*items):
        return (sum((item.astype(F32) for item in items[1:]), items[0].astype(F32)),)

    return fused(body, "plane_add", [shape_of(*values[0].shape, BF)], *values)[0]


def feed_grads(total, place):
    unit, half = place.unit, place.half
    arrived = flipped(total[unit : 2 * unit], 2)
    own = jnp.concatenate([total[:unit], arrived, total[2 * unit :]], axis=0)
    theirs = flipped(own, place.shards)
    is_first, is_low = place.rep == 0, place.second == 0
    first, last = jnp.where(is_first, own, theirs), jnp.where(is_first, theirs, own)
    grad_out = jnp.concatenate([first[2 * unit :], last[2 * unit :]], axis=0).astype(F32)
    sides = jnp.stack([first[: 2 * unit], last[: 2 * unit]]).reshape(2, 2, unit, -1)
    sides = jnp.where(is_low, sides, sides[:, ::-1])
    sides = sides.reshape(2, 2, unit, place.planes, 2, half).transpose(2, 3, 1, 4, 0, 5)
    return sides.reshape(unit, -1).astype(F32), grad_out


def plane_groups(place):
    return [[quad + QUAD * plane for plane in range(place.planes)] for quad in range(QUAD)]


def score_block(query, keys, table, bias, place, rows, length):
    scores = dot_nt(query, keys)
    spread = dot_nt(query, table)
    band = pltpu.roll(spread, 0, axis=1, stride=1, stride_axis=0)
    column = lax.broadcasted_iota(jnp.int32, (rows, length + 2 * rows), 1)
    bias[...] = jnp.where(column < place, spread[:, :1], spread[:, -1:])
    bias[:, pl.ds(place, 3 * rows)] = band[:, rows:]
    return scores + bias[:, rows : rows + length]


def place_rows(source, columns, target, position, rows):
    for step in range(SPAN):
        spot = pl.ds(pl.multiple_of((position ^ step) * rows, rows), rows)
        target[spot, :] = source[step * rows : (step + 1) * rows, columns]


def split_rows(value, kept, sent, rows):
    for index, step in enumerate((0, 4, 2, 6)):
        target = slice(index * rows, (index + 1) * rows)
        kept[target, :] = value[step * rows : (step + 1) * rows]
        sent[target, :] = value[(step + 1) * rows : (step + 2) * rows].astype(BF)


def join_pieces(refs, target, rows):
    for step, ref in enumerate(refs):
        target[step * rows : (step + 1) * rows, :] = ref[...]


def attend_kernel(*refs):
    spot, pieces, rest = refs[0], refs[1 : 1 + SPAN], refs[1 + SPAN :]
    (weight_in, bias_in, weight_out, table, hidden, mixed, context, peaks, kept, sent) = rest[:10]
    keys, values, bias = rest[10:]
    length, width = context.shape
    rows = length // SPAN
    head = table.shape[1] // 2
    position = spot[0]
    join_pieces(pieces, hidden, rows)
    mixed[...] = (dot_nn(hidden[...], weight_in[...]) + bias_in[...]).astype(BF)
    place_rows(mixed, slice(width, 2 * width), keys, position, rows)
    place_rows(mixed, slice(2 * width, 3 * width), values, position, rows)
    lane = lax.broadcasted_iota(jnp.int32, (rows, width), 1)

    def block(index, carry):
        place = pl.multiple_of(index * rows, rows)
        own = pl.ds(pl.multiple_of((position ^ index) * rows, rows), rows)
        query = mixed[own, :width] * jnp.asarray(head**-0.5, BF)
        results, logs = [], []
        for which in range(2):
            mine = lane // head == which
            part = jnp.where(mine, query, jnp.zeros_like(query))
            scores = score_block(part, keys[...], table[...], bias, place, rows, length)
            top = jnp.max(scores, axis=1, keepdims=True)
            powers = jnp.exp(scores - top)
            total = jnp.sum(powers, axis=1, keepdims=True)
            weights = (powers * (1.0 / total)).astype(BF)
            results.append(dot_nn(weights, values[...]))
            logs.append(top + jnp.log(total))
        context[own, :] = jnp.where(lane < head, results[0], results[1]).astype(BF)
        peaks[own, :] = jnp.where(lane < head, logs[0], logs[1])
        return carry

    lax.fori_loop(0, SPAN, block, 0)
    split_rows(dot_nn(context[...], weight_out[...]), kept, sent, rows)


def attend_back_kernel(*refs):
    spot, pieces, rest = refs[0], refs[1 : 1 + SPAN], refs[1 + SPAN :]
    (mixed, table, peaks, weight_in, weight_out) = rest[:5]
    (branch, grad_mixed, grad_table, far, kept, sent) = rest[5:11]
    keys, values, bias, grad_context, grad_keys, grad_values, slopes = rest[11:]
    length, width = grad_context.shape
    rows = length // SPAN
    head = table.shape[1] // 2
    position = spot[0]
    join_pieces(pieces, branch, rows)
    grad_context[...] = dot_nt(branch[...], weight_out[...]).astype(BF)
    place_rows(mixed, slice(width, 2 * width), keys, position, rows)
    place_rows(mixed, slice(2 * width, 3 * width), values, position, rows)
    grad_keys[...] = jnp.zeros_like(grad_keys)
    grad_values[...] = jnp.zeros_like(grad_values)
    grad_table[...] = jnp.zeros_like(grad_table)
    far[...] = jnp.zeros_like(far)
    lane = lax.broadcasted_iota(jnp.int32, (rows, width), 1)
    padded = lax.broadcasted_iota(jnp.int32, (rows, length + 2 * rows), 1)
    factor = head**-0.5
    slopes[:, :rows] = jnp.zeros((rows, rows), F32)
    slopes[:, rows + length :] = jnp.zeros((rows, rows), F32)
    mirror = (
        lax.broadcasted_iota(jnp.int32, (rows, rows), 0)
        + lax.broadcasted_iota(jnp.int32, (rows, rows), 1)
        == rows - 1
    ).astype(BF)

    def block(index, carry):
        place = pl.multiple_of(index * rows, rows)
        own = pl.ds(pl.multiple_of((position ^ index) * rows, rows), rows)
        query = mixed[own, :width] * jnp.asarray(factor, BF)
        results = []
        for which in range(2):
            mine = lane // head == which
            part = jnp.where(mine, query, jnp.zeros_like(query))
            scores = score_block(part, keys[...], table[...], bias, place, rows, length)
            incoming = grad_context[own, :]
            incoming = jnp.where(mine, incoming, jnp.zeros_like(incoming))
            logs = peaks[own, which * head : which * head + 1]
            probs = jnp.exp(scores - logs)
            grad_probs = dot_nt(incoming, values[...])
            shared = jnp.sum(grad_probs * probs, axis=1, keepdims=True)
            grad_low = (probs * (grad_probs - shared)).astype(BF)
            grad_values[...] += dot_tn(probs.astype(BF), incoming)
            grad_keys[...] += dot_tn(grad_low, part)
            slopes[:, rows : rows + length] = grad_low.astype(F32)
            window = slopes[:, pl.ds(place, 3 * rows)]
            whole = slopes[...]
            early = jnp.sum(jnp.where(padded < place, whole, 0.0), axis=1, keepdims=True)
            late = jnp.sum(
                jnp.where(padded >= place + 3 * rows, whole, 0.0), axis=1, keepdims=True
            )
            window = jnp.concatenate(
                [jnp.zeros((rows, rows), F32), dot_nn(mirror, window.astype(BF))], axis=1
            )
            window = pltpu.roll(
                window, 3 * rows + 1, axis=1, stride=1, stride_axis=0
            ).astype(BF)
            grad_table[...] += dot_tn(window, dot_nn(mirror, part).astype(BF))
            part_wide = part.astype(F32)
            far[0:1, :] += jnp.sum(early * part_wide, axis=0, keepdims=True)
            far[1:2, :] += jnp.sum(late * part_wide, axis=0, keepdims=True)
            close = jnp.dot(
                mirror.astype(F32),
                dot_nn(window, table[...]),
                preferred_element_type=F32,
                precision=lax.Precision.HIGHEST,
            )
            results.append(
                dot_nn(grad_low, keys[...])
                + close
                + early * table[0:1, :].astype(F32)
                + late * table[4 * rows - 1 :, :].astype(F32)
            )
        grad_mixed[own, :width] = (
            jnp.where(lane < head, results[0], results[1]) * factor
        ).astype(BF)
        return carry

    lax.fori_loop(0, SPAN, block, 0)
    for step in range(SPAN):
        source = pl.ds(pl.multiple_of((position ^ step) * rows, rows), rows)
        target = slice(step * rows, (step + 1) * rows)
        grad_mixed[target, width : 2 * width] = grad_keys[source, :].astype(BF)
        grad_mixed[target, 2 * width :] = grad_values[source, :].astype(BF)
    split_rows(dot_nt(grad_mixed[...], weight_in[...]), kept, sent, rows)


def group_gather(value, masks):
    near = square_gather(value, masks)
    return near, [flipped(item, 1) for item in near]


def group_reduce(kept, sent, masks):
    swapped = flipped(sent, 1)
    rows = kept.shape[0] // 4

    def body(kept_part, swapped_part):
        total = kept_part + swapped_part.astype(F32)
        return [total[index * rows : (index + 1) * rows] for index in range(4)]

    outs = [shape_of(rows, kept.shape[1], dtype) for dtype in (F32, BF, BF, BF)]
    return square_reduce(fused(body, "core_sum", outs, kept, swapped), masks)


def in_steps(blocks):
    near, far = blocks
    return [near[0], far[0], near[2], far[2], near[1], far[1], near[3], far[3]]


def attend(blocks, weight_in, bias_in, weight_out, table, place):
    pieces = in_steps(blocks)
    rows, model = pieces[0].shape
    length, width = SPAN * rows, weight_out.shape[0]
    outs = [
        shape_of(length, model, BF),
        shape_of(length, 3 * width, BF),
        shape_of(length, width, BF),
        shape_of(length, width, F32),
        shape_of(length // 2, model, F32),
        shape_of(length // 2, model, BF),
    ]
    hidden, mixed, context, peaks, kept, sent = kernel_call(
        attend_kernel,
        "attend_forward",
        outs,
        (place.span_spot, *pieces, weight_in, bias_in, weight_out, table),
        scalars=1,
        scratch=[
            pltpu.VMEM((length, width), BF),
            pltpu.VMEM((length, width), BF),
            pltpu.VMEM((rows, length + 2 * rows), F32),
        ],
        flops=48 * length * length * width,
    )
    return group_reduce(kept, sent, place.span_masks), (hidden, mixed, context, peaks)


def attend_back(blocks, saved, weight_in, weight_out, table, place, waits):
    hidden, mixed, context, peaks = saved
    pieces = in_steps(blocks)
    rows, model = pieces[0].shape
    length, width = SPAN * rows, weight_out.shape[0]
    outs = [
        shape_of(length, model, BF),
        shape_of(length, 3 * width, BF),
        shape_of(4 * rows, width, F32),
        shape_of(8, width, F32),
        shape_of(length // 2, model, F32),
        shape_of(length // 2, model, BF),
    ]
    branch, grad_mixed, grad_table, far, kept, sent = kernel_call(
        attend_back_kernel,
        "attend_backward",
        outs,
        (place.span_spot, *pieces, mixed, table, peaks, weight_in, weight_out),
        scalars=1,
        scratch=[
            pltpu.VMEM((length, width), BF),
            pltpu.VMEM((length, width), BF),
            pltpu.VMEM((rows, length + 2 * rows), F32),
            pltpu.VMEM((length, width), BF),
            pltpu.VMEM((length, width), F32),
            pltpu.VMEM((length, width), F32),
            pltpu.VMEM((rows, length + 2 * rows), F32),
        ],
        flops=96 * length * length * width,
        waits=waits,
    )
    parts = group_reduce(kept, sent, place.span_masks)

    def weights(hidden_rows, mixed_grad, context_rows, branch_rows):
        return (
            dot_tn(hidden_rows, mixed_grad),
            dot_tn(context_rows, branch_rows),
            column_sum(mixed_grad),
        )

    grad_in, grad_out, sums = fused(
        weights,
        "attend_weights",
        [shape_of(model, 3 * width, BF), shape_of(width, model, BF), shape_of(1, 3 * width, F32)],
        hidden,
        grad_mixed,
        context,
        branch,
        flops=8 * length * model * width,
    )
    return parts, grad_in, grad_out, sums, distance_gradient(grad_table, far, rows)


def wide_table(distance, rows):
    index = jnp.clip(jnp.arange(4 * rows) - rows - LEFT, 0, LEFT + RIGHT)
    low = distance[index]
    return jnp.concatenate([low, low], axis=1)


def distance_gradient(grad_table, far, rows):
    first = rows + LEFT
    last = first + LEFT + RIGHT
    head = grad_table.shape[1] // 2
    low = jnp.sum(grad_table[: first + 1], axis=0) + far[0]
    high = jnp.sum(grad_table[last:], axis=0) + far[1]
    total = jnp.concatenate([low[None], grad_table[first + 1 : last], high[None]], axis=0)
    return total[:, :head] + total[:, head:]


def whole_heads(weight_out, head):
    return weight_out.shape[0] % head == 0


def swap_if(condition, value, axis):
    return jnp.where(condition, jnp.flip(value, axis), value)


def attend_weights(weight_in, weight_out, head, place, waits):
    rows, model = weight_in.shape[0], weight_out.shape[1]
    heads = model // head
    per_device = heads // SPAN
    width = per_device * head
    if not whole_heads(weight_out, head):
        whole = lax.all_gather(weight_in, "shard", axis=0, tiled=True)
        whole = whole.reshape(model, 3, heads, head)
        mine = lax.dynamic_slice_in_dim(whole, place.member * per_device, per_device, 2)
        out = lax.all_gather(weight_out, "shard", axis=0, tiled=True)
        out = lax.dynamic_slice_in_dim(out, place.member * width, width, 0)
        return mine.reshape(model, 3 * width), out
    planes, unit = place.planes, place.unit
    groups, columns = planes // 2, 3 * width
    blocks = weight_in.reshape(rows, 3, groups, 2, 2, 2, -1)
    blocks = blocks.transpose(4, 3, 5, 0, 1, 2, 6).reshape(2, 2, 2 * rows, columns)
    own = lax.dynamic_index_in_dim(blocks, place.second, 0, keepdims=False)
    other = lax.dynamic_index_in_dim(blocks, 1 - place.second, 0, keepdims=False)
    arrived = flipped(other.reshape(4 * rows, columns), 2).reshape(own.shape)

    def arrange(spot, own_ref, arrived_ref, *outs):
        low, core = spot[0] & 1, spot[2]
        for step, out in enumerate(outs):
            for near in range(2):
                source = pl.ds(pl.multiple_of((core ^ near) * unit, unit), unit)
                for turn, ref in enumerate((own_ref, arrived_ref)):
                    start = (2 * near + turn) * unit
                    out[start : start + unit, :] = ref[low ^ step, source, :]

    near, far = kernel_call(
        arrange,
        "attend_columns",
        [shape_of(4 * unit, columns, BF)] * 2,
        (place.spot, own, arrived),
        scalars=1,
        waits=waits,
    )
    pieces = [near] + [
        flipped((near, far)[step & 1], QUAD * step) for step in range(1, planes)
    ]

    def split(*values):
        kept = jnp.concatenate([item[: 2 * unit] for item in values], axis=0)
        sent = jnp.concatenate([item[2 * unit :] for item in values], axis=0)
        return kept, sent

    kept, sent = fused(
        split, "attend_split", [shape_of(2 * planes * unit, columns, BF)] * 2, *pieces
    )
    swapped = flipped(sent, 1)
    outs = [weight_out] + [flipped(weight_out, SPAN * step) for step in range(1, groups)]

    def lay(spot, kept_ref, swapped_ref, *refs):
        plane, second, core = spot[0], spot[1], spot[2]
        w_in, w_out = refs[-2:]
        for near, ref in enumerate((kept_ref, swapped_ref)):
            for step in range(planes):
                for turn in range(2):
                    row = (((plane ^ step) * 2 + (second ^ turn)) * 2 + (core ^ near)) * unit
                    start = (2 * step + turn) * unit
                    w_in[pl.ds(pl.multiple_of(row, unit), unit), :] = ref[start : start + unit, :]
        for step, ref in enumerate(refs[:-2]):
            row = ((plane >> 1) ^ step) * unit
            w_out[pl.ds(pl.multiple_of(row, unit), unit), :] = ref[...]

    return kernel_call(
        lay,
        "attend_lay",
        [shape_of(model, columns, BF), shape_of(width, model, BF)],
        (place.spot, kept, swapped, *outs),
        scalars=1,
    )


def head_row(row, place, aligned):
    if aligned:
        row = row.reshape(-1, SPAN, place.unit)
        row = lax.dynamic_index_in_dim(row, place.member, 1, keepdims=False)
        return row.reshape(1, -1)
    row = row.reshape(SPAN, -1)
    return lax.dynamic_slice_in_dim(row, place.member, 1, 0)


def head_spread(row, model, place, aligned):
    if aligned:
        whole = jnp.zeros((place.planes // 2, SPAN, place.unit), F32)
        block = row.reshape(-1, 1, place.unit)
        return lax.dynamic_update_slice_in_dim(whole, block, place.member, 1).reshape(1, model)
    whole = jnp.zeros((SPAN, model // SPAN), F32)
    return lax.dynamic_update_slice_in_dim(whole, row, place.member, 0).reshape(1, model)


def attend_weight_grads(grad_in, grad_out, head, place, aligned):
    model = grad_out.shape[1]
    heads = model // head
    per_device = heads // SPAN
    if not aligned:
        whole = jnp.zeros((model, 3, heads, head), F32)
        whole = lax.dynamic_update_slice_in_dim(
            whole,
            grad_in.astype(F32).reshape(model, 3, per_device, head),
            place.member * per_device,
            2,
        )
        whole = lax.psum_scatter(
            whole.reshape(model, 3 * model), "shard", scatter_dimension=0, tiled=True
        )
        out = jnp.zeros((model, model), F32)
        out = lax.dynamic_update_slice_in_dim(
            out, grad_out.astype(F32), place.member * per_device * head, 0
        )
        out = lax.psum_scatter(out, "shard", scatter_dimension=0, tiled=True)
        return rep_sum(whole, place), rep_sum(out, place)
    planes, unit = place.planes, place.unit
    groups, columns = planes // 2, grad_in.shape[1]

    def lay(spot, w_in, w_out, kept, sent, *outs):
        plane, second, core = spot[0], spot[1], spot[2]
        for near, ref in enumerate((kept, sent)):
            for step in range(planes):
                for turn in range(2):
                    row = (((plane ^ step) * 2 + (second ^ turn)) * 2 + (core ^ near)) * unit
                    start = (2 * step + turn) * unit
                    ref[start : start + unit, :] = w_in[pl.ds(pl.multiple_of(row, unit), unit), :]
        for step, ref in enumerate(outs):
            row = ((plane >> 1) ^ step) * unit
            ref[...] = w_out[pl.ds(pl.multiple_of(row, unit), unit), :]

    kept, sent, *outs = kernel_call(
        lay,
        "attend_unlay",
        [shape_of(2 * planes * unit, columns, BF)] * 2 + [shape_of(unit, model, BF)] * groups,
        (place.spot, grad_in, grad_out),
        scalars=1,
    )
    swapped = flipped(sent, 1)

    def by_plane(kept_part, swapped_part):
        both = jnp.concatenate([kept_part, swapped_part], axis=1)
        return [both[2 * step * unit : 2 * (step + 1) * unit] for step in range(planes)]

    pieces = fused(
        by_plane,
        "attend_planes",
        [shape_of(2 * unit, 2 * columns, BF)] * planes,
        kept,
        swapped,
    )
    arrived = [pieces[0]] + [flipped(pieces[step], QUAD * step) for step in range(1, planes)]
    outs = [outs[0]] + [flipped(outs[step], SPAN * step) for step in range(1, groups)]

    def total(*values):
        even = sum(item.astype(F32) for item in values[:planes:2])
        odd = sum(item.astype(F32) for item in values[1:planes:2])
        both = jnp.concatenate([even, odd], axis=1)
        out = sum(item.astype(F32) for item in values[planes:])
        return both[:unit], both[unit:], out

    own, other, out = fused(
        total,
        "attend_plane_sum",
        [shape_of(unit, 4 * columns, BF)] * 2 + [shape_of(unit, model, BF)],
        *arrived,
        *outs,
    )
    whole = jnp.stack([own, flipped(other, 2)])
    whole = rep_sum(whole, place).reshape(2, unit, 2, 2, 3, groups, -1)
    whole = swap_if(place.second == 1, whole, 0)
    whole = swap_if(place.plane & 1 == 1, whole, 2)
    whole = swap_if(place.core == 1, whole, 3)
    whole = whole.transpose(1, 4, 5, 2, 0, 3, 6)
    return whole.reshape(unit, 3 * model), rep_sum(out, place)


def rep_sum(value, place):
    low = value.astype(BF)
    return low.astype(F32) + flipped(low, place.shards).astype(F32)


LANES = 128


def row(wide, index):
    return wide[index : index + 1]


def pack_columns(left, right, waits):
    def body(first, second):
        return (jnp.concatenate([first, second], axis=1),)

    out = shape_of(left.shape[0], left.shape[1] + right.shape[1], BF)
    return fused(body, "pack_columns", [out], left, right, waits=waits)[0]


def convolve_start(parts, before, wide, bias_row, weight_in):
    rows, model = before.shape

    def body(*values):
        base, small, w_in = values[4:]
        current = base + joined(values[:4]) + row(small, bias_row)
        unit, unused_scale = standard(current)
        hidden = (unit * row(small, 7) + row(small, 8)).astype(BF)
        doubled = dot_nn(hidden, w_in)
        return current, hidden, doubled, doubled[:, :model] * logistic(doubled[:, model:])

    return fused(
        body,
        "convolve_start",
        [
            shape_of(rows, model, F32),
            shape_of(rows, model, BF),
            shape_of(rows, 2 * model, F32),
            shape_of(rows, model, BF),
        ],
        *parts,
        before,
        wide,
        weight_in,
        flops=4 * rows * model * model,
    )


def convolve_finish(glued, border, wide, taps, weight_out, before):
    rows, model = before.shape
    edge = border.shape[0]

    def kernel(
        glued_ref, border_ref, small, w_out, base,
        mixed_ref, rest_ref, current_ref, hidden_ref, padded,
    ):
        padded[:edge, :] = border_ref[...].astype(F32)
        padded[edge:, :] = glued_ref[...].astype(F32)
        first, count = taps
        for column in range(0, model, LANES):
            lanes = slice(column, column + LANES)
            total = jnp.zeros((rows, LANES), F32)
            for tap in range(count):
                start = edge - count + 1 + tap
                weight = small[first + tap : first + tap + 1, lanes]
                total += padded[start : start + rows, lanes] * weight
            mixed_ref[:, lanes] = total
        unit, unused_scale = standard(mixed_ref[...])
        upper = unit * small[9:10, :] + small[10:11, :]
        rest = (upper * logistic(upper)).astype(BF)
        rest_ref[...] = rest
        current = base[...] + dot_nn(rest, w_out[...])
        current_ref[...] = current
        unit, unused_scale = standard(current)
        hidden_ref[...] = (unit * small[11:12, :] + small[12:13, :]).astype(BF)

    return kernel_call(
        kernel,
        "convolve_finish",
        [shape_of(rows, model, dtype) for dtype in (F32, BF, F32, BF)],
        (glued, border, wide, weight_out, before),
        scratch=[pltpu.VMEM((edge + rows, model), F32)],
        flops=2 * rows * model * model,
    )


def convolve_back_start(parts, grad, after, mixed, wide, taps, weight_out, glued, border, waits):
    rows, model = after.shape
    edge = border.shape[0]
    first, count = taps

    def kernel(
        own, part_one, part_two, part_three, grad_ref, after_ref, mixed_ref, small,
        w_out, glued_ref, border_ref,
        grad_out, branch_ref, main_ref, halo_ref, sums, padded, spread,
    ):
        incoming = joined((own[...], part_one[...], part_two[...], part_three[...]))
        slope, sum_gain, sum_shift = norm_back(after_ref[...], small[11:12, :], incoming)
        current = grad_ref[...] + slope
        grad_out[...] = current
        branch = current.astype(BF)
        branch_ref[...] = branch
        unit, scale = standard(mixed_ref[...])
        upper = unit * small[9:10, :] + small[10:11, :]
        grad_upper = dot_nt(branch, w_out[...]) * silu_slope(upper)
        inner = grad_upper * small[9:10, :]
        mean = jnp.mean(inner, axis=-1, keepdims=True)
        shared = jnp.mean(inner * unit, axis=-1, keepdims=True)
        padded[:edge, :] = border_ref[...].astype(F32)
        padded[edge:, :] = glued_ref[...].astype(F32)
        spread[:edge, :] = jnp.zeros((edge, model), F32)
        spread[edge : edge + rows, :] = scale * (inner - mean - unit * shared)
        spread[edge + rows :, :] = jnp.zeros((edge, model), F32)
        sums[count : count + 1, :] = column_sum(grad_upper * unit)
        sums[count + 1 : count + 2, :] = column_sum(grad_upper)
        sums[count + 2 : count + 3, :] = sum_gain
        sums[count + 3 : count + 4, :] = sum_shift
        for column in range(0, model, LANES):
            lanes = slice(column, column + LANES)
            total = jnp.zeros((rows + edge, LANES), F32)
            center = spread[edge : edge + rows, lanes]
            for tap in range(count):
                start = edge - count + 1 + tap
                sums[tap : tap + 1, lanes] = jnp.sum(
                    center * padded[start : start + rows, lanes], axis=0, keepdims=True
                )
                begin = count - 1 - tap
                weight = small[first + tap : first + tap + 1, lanes]
                total += spread[begin : begin + rows + edge, lanes] * weight
            halo_ref[:, lanes] = total[:edge].astype(BF)
            main_ref[:, lanes] = total[edge:]

    return kernel_call(
        kernel,
        "convolve_back_start",
        [
            shape_of(rows, model, F32),
            shape_of(rows, model, BF),
            shape_of(rows, model, F32),
            shape_of(edge, model, BF),
            shape_of(count + 4, model, F32),
        ],
        (*parts, grad, after, mixed, wide, weight_out, glued, border),
        scratch=[
            pltpu.VMEM((edge + rows, model), F32),
            pltpu.VMEM((rows + 2 * edge, model), F32),
        ],
        flops=2 * rows * model * model,
        waits=waits,
    )


def convolve_back_finish(main, incoming, doubled, weight_in, before, wide, grad):
    rows, model = before.shape
    edge = incoming.shape[0]

    def body(main_rows, late, both, w_in, base, small, grad_rows):
        glued = jnp.concatenate(
            [main_rows[: rows - edge], main_rows[rows - edge :] + late.astype(F32)], axis=0
        )
        glued = glued.astype(BF).astype(F32)
        gate = logistic(both[:, model:])
        slope = jnp.concatenate(
            [glued * gate, glued * both[:, :model] * gate * (1.0 - gate)], axis=1
        ).astype(BF)
        inner, sum_gain, sum_shift = norm_back(base, row(small, 7), dot_nt(slope, w_in))
        current = grad_rows + inner
        branch = current.astype(BF)
        sums = jnp.concatenate([sum_gain, sum_shift, column_sum(branch)], axis=0)
        return current, branch, slope, sums

    return fused(
        body,
        "convolve_back_finish",
        [
            shape_of(rows, model, F32),
            shape_of(rows, model, BF),
            shape_of(rows, 2 * model, BF),
            shape_of(3, model, F32),
        ],
        main,
        incoming,
        doubled,
        weight_in,
        before,
        wide,
        grad,
        flops=4 * rows * model * model,
    )


def convolve_weight_grads(hidden, slope, rest, branch, place):
    model = hidden.shape[1]

    def body(hidden_rows, slope_rows, rest_rows, branch_rows):
        both = dot_tn(hidden_rows, slope_rows), dot_tn(rest_rows, branch_rows)
        return (jnp.concatenate(both, axis=1),)

    total = fused(
        body,
        "convolve_weights",
        [shape_of(model, 3 * model, BF)],
        hidden,
        slope,
        rest,
        branch,
        flops=6 * hidden.shape[0] * model * model,
    )[0]
    total = lax.psum_scatter(total, "shard", scatter_dimension=0, tiled=True)
    total = rep_sum(total, place)
    return total[:, : 2 * model], total[:, 2 * model :]


def feed_to_attend(parts, before, wide, waits):
    rows, model = before.shape

    def body(*values):
        base, small = values[4:]
        current = base.astype(F32) + 0.5 * (joined(values[:4]) + row(small, 2))
        unit, unused_scale = standard(current)
        return current, unit * row(small, 3) + row(small, 4)

    outs = [shape_of(rows, model, F32), shape_of(rows, model, BF)]
    return fused(body, "feed_to_attend", outs, *parts, before, wide, waits=waits)


def turn_around(parts, before, wide, cotangent):
    rows, model = before.shape

    def body(*values):
        base, small, grad = values[4:]
        current = base + 0.5 * (joined(values[:4]) + row(small, 13))
        unit, unused_scale = standard(current)
        slope, sum_gain, sum_shift = norm_back(current, row(small, 14), grad.astype(F32))
        branch = (0.5 * slope).astype(BF)
        sums = jnp.concatenate([column_sum(branch), sum_gain, sum_shift], axis=0)
        return unit * row(small, 14) + row(small, 15), slope, branch, sums

    outs = [
        shape_of(rows, model, BF),
        shape_of(rows, model, F32),
        shape_of(rows, model, BF),
        shape_of(3, model, F32),
    ]
    return fused(body, "turn_around", outs, *parts, before, wide, cotangent)


def attend_to_feed_back(parts, grad, before, wide):
    rows, model = before.shape

    def body(*values):
        grad_rows, base, small = values[4:]
        slope, sum_gain, sum_shift = norm_back(base, row(small, 3), joined(values[:4]))
        current = grad_rows + slope
        branch = (0.5 * current).astype(BF)
        sums = jnp.concatenate([column_sum(branch), sum_gain, sum_shift], axis=0)
        return current, branch, sums

    outs = [shape_of(rows, model, F32), shape_of(rows, model, BF), shape_of(3, model, F32)]
    return fused(body, "attend_to_feed_back", outs, *parts, grad, before, wide)


def last_step(parts, grad, before, wide):
    rows, model = before.shape

    def body(*values):
        grad_rows, base, small = values[4:]
        slope, sum_gain, sum_shift = norm_back(
            base.astype(F32), row(small, 0), joined(values[:4])
        )
        return grad_rows + slope, jnp.concatenate([sum_gain, sum_shift], axis=0)

    outs = [shape_of(rows, model, F32), shape_of(2, model, F32)]
    return fused(body, "last_step", outs, *parts, grad, before, wide)


def shard_gather(value, place):
    gathered = value[None]
    for bit in range(place.shards.bit_length() - 1):
        arrived = flipped(gathered, 1 << bit)
        low = jnp.bitwise_and(jnp.right_shift(place.shard, bit), 1) == 0
        gathered = jnp.concatenate(
            [jnp.where(low, gathered, arrived), jnp.where(low, arrived, gathered)], axis=0
        )
    return gathered


def shard_reduce(value, place):
    both = jnp.concatenate([value, value], axis=0)
    both = lax.all_to_all(both, ("rep", "shard"), 0, 0, tiled=True)
    return jnp.sum(both, axis=0)


def sum_everywhere(value, place, delays):
    arrived = flipped(value, 1)
    for bit in range(1, (2 * place.shards).bit_length() - 1):
        waits = delays[bit - 1 : bit]
        value = fused(
            lambda own, other: (own + other,),
            "table_sum",
            [shape_of(*value.shape, F32)],
            value,
            arrived,
            waits=waits,
        )[0]
        arrived = flipped(value, 1 << bit)
    return value + arrived


class Place:
    def __init__(self, unit, half):
        self.shards = lax.axis_size("shard")
        self.planes = self.shards // QUAD
        self.unit, self.half = unit, half
        self.pack_rows = 2 * unit + half
        self.rep = lax.axis_index("rep")
        self.shard = lax.axis_index("shard")
        self.core = self.shard % 2
        self.second = self.shard // 2 % 2
        self.plane = self.shard // QUAD
        self.member = self.shard % SPAN
        self.spot = jnp.stack([self.plane, self.second, self.core])
        self.flat_spot = jnp.stack([jnp.zeros_like(self.plane), self.second, self.core])
        self.span_spot = self.member.reshape(1)
        self.feed_masks = (self.shards, 2)
        self.span_masks = (4, 2)


def along(value, by, place):
    count = place.shards
    route = [(i, i + by) for i in range(count) if 0 <= i + by < count]
    return lax.ppermute(value, "shard", route)


def shards(
    inputs,
    ff_in,
    ff_out,
    ff_bias,
    attn_in,
    attn_out,
    conv_in,
    conv_out,
    depthwise,
    distance,
    vectors,
    attn_bias,
    cotangent,
):
    rows, model = inputs.shape
    unit, half = ff_in.shape[2], ff_out.shape[2] // 2
    place = Place(unit, half)
    head = distance.shape[2]
    tap_count = depthwise.shape[1]
    edge = -(-(tap_count - 1) // 16) * 16
    aligned = whole_heads(attn_out[0], head)
    bias_rows = ff_bias.shape[2] // unit
    count = vectors.shape[1]
    taps = (count + 1, tap_count)

    small = jnp.concatenate(
        [vectors[0], attn_bias, depthwise[0], ff_bias[0].reshape(2 * bias_rows, unit)], axis=0
    )
    first_pack = pack_rows(feed_pack(ff_in[0, 0], ff_out[0, 0], place))
    first_packs = plane_gather(first_pack, place)
    pieces = square_gather(inputs, place.feed_masks)
    small = shard_gather(small, place)
    wide = small[:, : count + 1 + tap_count].transpose(1, 0, 2).reshape(-1, model).astype(F32)
    feed_bias = small[:, count + 1 + tap_count :].reshape(place.planes, 2, 2, 2, 2, half)
    feed_bias = lax.dynamic_index_in_dim(feed_bias, place.second, 1, keepdims=False)
    feed_bias = lax.dynamic_index_in_dim(feed_bias, place.rep, 3, keepdims=False)
    feed_bias = feed_bias.transpose(2, 0, 1, 3).reshape(2, 1, -1).astype(F32)
    table = wide_table(distance[0], rows)
    mix_bias = jnp.concatenate(
        [
            head_row(wide[5], place, aligned),
            jnp.zeros((1, model // SPAN), F32),
            head_row(wide[6], place, aligned),
        ],
        axis=1,
    )

    arrived = first_packs[: place.planes]
    mix_in, mix_out = attend_weights(attn_in[0], attn_out[0], head, place, arrived)
    glue = pack_columns(conv_in[0], conv_out[0], arrived)
    glue = lax.all_gather(glue, "shard", axis=0, tiled=True)
    second_pack = feed_pack(ff_in[0, 1], ff_out[0, 1], place)

    parts, saved_first = feed(
        pieces, first_packs, place.spot, feed_bias[0], wide, 0, place.feed_masks, place
    )
    second_near = lax.all_gather(
        pack_rows(second_pack, waits=saved_first[:1]),
        "shard",
        axis=0,
        tiled=True,
        axis_index_groups=plane_groups(place),
    )
    second_packs = [second_near, flipped(second_near, 1)]
    after_first, hidden = feed_to_attend(parts, inputs, wide, (mix_in,))
    parts, saved_attend = attend(
        group_gather(hidden, place.span_masks), mix_in, mix_bias, mix_out, table, place
    )
    glue_in, glue_out = glue[:, : 2 * model], glue[:, 2 * model :]
    after_attend, conv_hidden, doubled, glued = convolve_start(
        parts, after_first, wide, count, glue_in
    )
    border = along(glued[rows - edge :], 1, place)
    border = jnp.where(place.member == 0, jnp.zeros_like(border), border)
    mixed, rest, after_conv, hidden = convolve_finish(
        glued, border, wide, taps, glue_out, after_attend
    )
    pieces = square_gather(hidden, place.feed_masks)
    parts, saved_second = feed(
        pieces, second_packs, place.flat_spot, feed_bias[1], wide, None, place.feed_masks, place
    )
    output, grad_last, branch, last_sums = turn_around(parts, after_conv, wide, cotangent)

    pieces = square_gather(branch, place.feed_masks)
    parts, kept, swapped, second_bias = feed_back(
        pieces, second_packs, place.flat_spot, saved_second, place.feed_masks, place
    )
    second_total = fused(
        lambda own, other: (own.astype(F32) + other.astype(F32),),
        "feed_core_total",
        [shape_of(*kept.shape, BF)],
        kept,
        swapped,
    )[0]
    second_sum = lax.psum_scatter(
        second_total,
        "shard",
        scatter_dimension=0,
        tiled=True,
        axis_index_groups=plane_groups(place),
    )
    grad_conv, conv_branch, main, halo, conv_sums = convolve_back_start(
        parts, grad_last, after_conv, mixed, wide, taps, glue_out, glued, border, (second_total,)
    )
    incoming = along(halo, -1, place)
    incoming = jnp.where(place.member == SPAN - 1, jnp.zeros_like(incoming), incoming)
    grad_attend, branch, slope, attend_sums = convolve_back_finish(
        main, incoming, doubled, glue_in, after_attend, wide, grad_conv
    )
    conv_grads = convolve_weight_grads(conv_hidden, slope, rest, conv_branch, place)
    parts, mix_grad_in, mix_grad_out, mix_sums, grad_distance = attend_back(
        group_gather(branch, place.span_masks), saved_attend, mix_in, mix_out, table, place, ()
    )
    grad_first, branch, first_sums = attend_to_feed_back(parts, grad_attend, after_first, wide)
    pieces = square_gather(branch, place.feed_masks)
    parts, kept, swapped, first_bias = feed_back(
        pieces, first_packs, place.spot, saved_first, place.feed_masks, place
    )
    first_sum = plane_reduce(kept, swapped, place)
    grad_input, input_sums = last_step(parts, grad_first, inputs, wide)

    second_grads = feed_grads(second_sum, place)
    mix_grads = attend_weight_grads(mix_grad_in, mix_grad_out, head, place, aligned)
    first_grads = feed_grads(first_sum, place)
    width = mix_sums.shape[1] // 3
    wide_grads = jnp.concatenate(
        [
            input_sums,
            first_sums,
            head_spread(mix_sums[:, :width], model, place, aligned),
            head_spread(mix_sums[:, 2 * width :], model, place, aligned),
            attend_sums[:2],
            conv_sums[tap_count:],
            last_sums,
            attend_sums[2:],
            conv_sums[:tap_count],
        ],
        axis=0,
    )
    wide_grads = wide_grads.reshape(-1, place.shards, unit).transpose(1, 0, 2)
    bias_pair = jnp.stack([first_bias, second_bias]).reshape(2, place.planes, 2, half)
    bias_grads = lax.dynamic_update_slice(
        jnp.zeros((place.planes, 2, 2, 2, 2, half), F32),
        bias_pair.transpose(1, 2, 0, 3)[:, None, :, :, None, :],
        (0, place.second, 0, 0, place.rep, 0),
    ).reshape(place.shards, 2 * bias_rows, unit)
    small_grads = shard_reduce(jnp.concatenate([wide_grads, bias_grads], axis=1), place)
    delays = (grad_first, kept, first_sum)
    grad_distance = sum_everywhere(grad_distance, place, delays)
    return (
        output,
        grad_input,
        jnp.stack([first_grads[0], second_grads[0]])[None],
        jnp.stack([first_grads[1], second_grads[1]])[None],
        small_grads[count + 1 + tap_count :].reshape(1, 2, -1),
        mix_grads[0][None],
        mix_grads[1][None],
        conv_grads[0][None],
        conv_grads[1][None],
        small_grads[count + 1 : count + 1 + tap_count][None],
        grad_distance[None],
        small_grads[:count][None],
        small_grads[count : count + 1],
    )


def solution(mesh):
    in_specs = (
        P(("rep", "shard"), None),
        P(None, None, "shard", None),
        P(None, None, "shard", None),
        P(None, None, "shard"),
        P(None, "shard", None),
        P(None, "shard", None),
        P(None, "shard", None),
        P(None, "shard", None),
        P(None, None, "shard"),
        P(),
        P(None, None, "shard"),
        P(None, "shard"),
        P(("rep", "shard"), None),
    )
    out_specs = (
        P(("rep", "shard"), None),
        P(("rep", "shard"), None),
        P(None, None, "shard", None),
        P(None, None, "shard", None),
        P(None, None, "shard"),
        P(None, "shard", None),
        P(None, "shard", None),
        P(None, "shard", None),
        P(None, "shard", None),
        P(None, None, "shard"),
        P(),
        P(None, None, "shard"),
        P(None, "shard"),
    )
    return jax.shard_map(shards, mesh=mesh, in_specs=in_specs, out_specs=out_specs, check_vma=False)
```

time: 743 us -> 638 us (0.86)
  starting transfers between devices: 183 us -> 126 us
  local copies, waits for them, and re-layouts: 155 us -> 108 us
  Pallas kernels: 123 us -> 104 us
  waiting for transfers between devices: 237 us -> 252 us
    ppermute x154 -> x89, starting transfers between devices: 179 us -> 115 us  [flipped(): lax.ppermute(value, ('rep', 'shard'), [(i, i ^ mask) for i in range(total)])]
    slice x68 -> x15, local copies, waits for them, and re-layouts: 45.4 us -> 8.73 us  [the longest x2 4.64 us: shards(): glue_in, glue_out = (glue[:, :2 * model], glue[:, 2 * model:])]
    pallas_call x52 -> x37, Pallas kernels: 123 us -> 104 us  [kernel_call(): pl.pallas_call(kernel, in_specs=[pl.BlockSpec(memory_space=pltpu.SMEM)] *...]
    unnamed x343 -> x240, local copies, waits for them, and re-layouts: 65.8 us -> 50.2 us
    all_gather x2, waiting for transfers between devices: 0.01 us -> 8.56 us  [the longest x1 8.56 us: shards(): glue = lax.all_gather(glue, 'shard', axis=0, tiled=True)]
    ppermute x154 -> x89, waiting for transfers between devices: 234 us -> 242 us  [flipped(): lax.ppermute(value, ('rep', 'shard'), [(i, i ^ mask) for i in range(total)])]
    concatenate x26 -> x19, local copies, waits for them, and re-layouts: 17.4 us -> 10.3 us  [the longest x14 10.1 us: shards(): jnp.concatenate([input_sums, first_sums, head_spread(mix_sums[:, :width],...]
  transfers between devices with their start and end apart: 160 -> 96, of which waited for: 58 -> 44; matrix products, arithmetic and copies ran while one was open for 15% -> 13% of each run, Pallas kernels for 13% -> 14%
where the time goes in v2:
time: 638 us; the launch traced here: 626 us
  waiting for transfers between devices  252 us (39%)
  starting transfers between devices  126 us (20%)
  local copies, waits for them, and re-layouts  108 us (17%)
  Pallas kernels  104 us (16%)
  other arithmetic  20.4 us (3%)
  between operations  15.7 us (2%)
    ppermute x89, waiting for transfers between devices, flipped(): lax.ppermute(value, ('rep', 'shard'), [(i, i ^ mask) for i in range(total)])  242 us
    ppermute x89, starting transfers between devices, flipped(): lax.ppermute(value, ('rep', 'shard'), [(i, i ^ mask) for i in range(total)])  115 us
    pallas_call x37, Pallas kernels, kernel_call(): pl.pallas_call(kernel, in_specs=[pl.BlockSpec(memory_space=pltpu.SMEM)] *...  104 us
    unnamed x240, local copies, waits for them, and re-layouts  50.2 us
  transfers between devices with their start and end apart: 96, of which 44 were waited for; matrix products, arithmetic and copies ran while one was open for 13% of the time, Pallas kernels for 14%

profile of v2, /device:TPU:0, one launch (start us, length us, event | category | flops | bytes accessed | tf_op | source)
XLA Modules:
  0.0 626.2 jit_solution(15541311891987929257)
XLA Ops:
  7.2 3.0 collective-permute-start
  20.5 3.6 collective-permute-done.3.refs_1_
  30.4 8.3 %collective-permute-done.13 = bf16[4,56,64]{2,1,0:T(8,128)(2,1)S(1)} collective-permute-done((bf16[4,56,64]{2,1,0:T(8,128)(2,1)S(1)}, bf16[4,56,64]{2,1,0:T(8,128)(2,1)S(1)}, u32[]{:S(2)}, u32[]{:S(2)}) %collective-permute-start.13) | collective-permute-done | bytes 28704 | tf_op jit(solution)/shard_map/ppermute | solution.py:97
  41.4 11.8 %collective-permute-done.5.refs_7_.refs_5_.refs_4_ = bf16[256,1024]{1,0:T(8,128)(2,1)S(1)} collective-permute-done((bf16[256,1024]{1,0:T(8,128)(2,1)S(1)}, bf16[256,1024]{1,0:T(8,128)(2,1)S(1)}, u32[]{:S(2)}, u32[]{:S(2)}) %collective-permute-start.5) | collective-permute-done | bytes 524320 | tf_op jit(solution)/shard_map/ppermute | solution.py:97
  55.2 9.3 %collective-permute-done.4.refs_6_.refs_4_.refs_3_ = bf16[256,1024]{1,0:T(8,128)(2,1)S(1)} collective-permute-done((bf16[256,1024]{1,0:T(8,128)(2,1)S(1)}, bf16[256,1024]{1,0:T(8,128)(2,1)S(1)}, u32[]{:S(2)}, u32[]{:S(2)}) %collective-permute-start.4) | collective-permute-done | bytes 524320 | tf_op jit(solution)/shard_map/ppermute | solution.py:97
  64.5 9.8 %collective-permute-done.6.refs_8_.refs_6_.refs_5_ = bf16[256,1024]{1,0:T(8,128)(2,1)S(1)} collective-permute-done((bf16[256,1024]{1,0:T(8,128)(2,1)S(1)}, bf16[256,1024]{1,0:T(8,128)(2,1)S(1)}, u32[]{:S(2)}, u32[]{:S(2)}) %collective-permute-start.6) | collective-permute-done | bytes 524320 | tf_op jit(solution)/shard_map/ppermute | solution.py:97
  77.7 6.5 %collective-permute-done.2.refs_4_ = bf16[128,1024]{1,0:T(8,128)(2,1)} collective-permute-done((bf16[128,1024]{1,0:T(8,128)(2,1)S(1)}, bf16[128,1024]{1,0:T(8,128)(2,1)}, u32[]{:S(2)}, u32[]{:S(2)}) %collective-permute-start.2) | collective-permute-done | bytes 262176 | tf_op jit(solution)/shard_map/ppermute | solution.py:97
  84.7 4.9 feed_forward.2
  102.9 2.9 reshape.263
  108.6 4.7 collective-permute-done.18
  113.9 4.3 collective-permute-start.20
  118.3 15.5 %collective-permute-done.19.refs_1_ = bf16[256,384]{1,0:T(8,128)(2,1)S(1)} collective-permute-done((bf16[256,384]{1,0:T(8,128)(2,1)S(1)}, bf16[256,384]{1,0:T(8,128)(2,1)S(1)}, u32[]{:S(2)}, u32[]{:S(2)}) %collective-permute-start.19) | collective-permute-done | bytes 196640 | tf_op jit(solution)/shard_map/ppermute | solution.py:97
  133.8 6.0 collective-permute-done.20.refs_2_
  139.8 4.0 collective-permute-done.21.refs_3_
  147.5 13.5 %collective-permute-start.23 = (bf16[64,1024]{1,0:T(8,128)(2,1)S(1)}, bf16[64,1024]{1,0:T(8,128)(2,1)S(1)}, u32[]{:S(2)}, u32[]{:S(2)}) collective-permute-start(bf16[64,1024]{1,0:T(8,128)(2,1)S(1)} %bitcast.117), channel_id=1, source_target_pairs={{0,8},{1,9},{2,10},{3,11},{4,12},{5,13},{6,14},{7,15},{8,0},{9,1},... | collective-permute-start | bytes 393224 | tf_op jit(solution)/shard_map/ppermute | solution.py:97
  161.1 6.1 collective-permute-done.23.refs_4_
  170.1 4.3 collective-permute-start.27
  178.7 11.3 %collective-permute-done.27.refs_5_ = bf16[128,1024]{1,0:T(8,128)(2,1)S(1)} collective-permute-done((bf16[128,1024]{1,0:T(8,128)(2,1)S(1)}, bf16[128,1024]{1,0:T(8,128)(2,1)S(1)}, u32[]{:S(2)}, u32[]{:S(2)}) %collective-permute-start.27) | collective-permute-done | bytes 262176 | tf_op jit(solution)/shard_map/ppermute | solution.py:97
  190.7 6.0 collective-permute-done.29.refs_7_
  204.6 15.0 %attend_forward.1 = (bf16[1024,1024]{1,0:T(8,128)(2,1)S(1)}, bf16[1024,384]{1,0:T(8,128)(2,1)S(1)}, bf16[1024,128]{1,0:T(8,128)(2,1)S(1)}, f32[1024,128]{1,0:T(8...) custom-call(s32[1]{0:T(128)} %bitcast.2.refs_0_, bf16[128,1024]{1,0:T(8,128)(2,1)S(1)} %copy-done.82, ...), custom_call_target="tpu_custom_call" | custom-call | flops 6442450944 | bytes 10094080 | tf_op jit(solution)/shard_map/attend_forward/pallas_call | solution.py:72
  220.5 2.8 collective-permute-done.31.refs_1_
  227.1 8.6 %all-gather.3.cloned.1.call-done = bf16[1024,3072]{1,0:T(8,128)(2,1)} async-done(((bf16[64,3072]{1,0:T(8,128)(2,1)}), bf16[1024,3072]{1,0:T(8,128)(2,1)}) %all-gather.3.cloned.1.call-update) | async-done | bytes 6291472 | tf_op jit(solution)/shard_map/all_gather | solution.py:1186
  235.7 2.8 slice.193.refs_6_.refs_3_
  238.5 3.9 collective-permute-done.33.refs_2_
  246.7 2.9 collective-permute-start.35
  251.6 3.4 convolve_finish.1
  260.2 5.3 collective-permute-done.36.refs_2_
  265.6 7.0 %collective-permute-done.37.refs_3_ = bf16[128,1024]{1,0:T(8,128)(2,1)S(1)} collective-permute-done((bf16[128,1024]{1,0:T(8,128)(2,1)S(1)}, bf16[128,1024]{1,0:T(8,128)(2,1)S(1)}, u32[]{:S(2)}, u32[]{:S(2)}) %collective-permute-start.37) | collective-permute-done | bytes 262176 | tf_op jit(solution)/shard_map/ppermute | solution.py:97
  272.5 4.4 feed_forward.3
  280.5 6.7 %collective-permute-done.41.refs_1_ = bf16[128,1024]{1,0:T(8,128)(2,1)S(1)} collective-permute-done((bf16[128,1024]{1,0:T(8,128)(2,1)S(1)}, bf16[128,1024]{1,0:T(8,128)(2,1)S(1)}, u32[]{:S(2)}, u32[]{:S(2)}) %collective-permute-start.41) | collective-permute-done | bytes 262176 | tf_op jit(solution)/shard_map/ppermute | solution.py:97
  287.2 3.8 collective-permute-done.42.refs_2_
  296.4 5.7 collective-permute-done.44.refs_2_
  302.1 5.8 collective-permute-done.45.refs_3_
  307.9 4.7 feed_backward.2
  313.4 3.5 feed_weights.2
  317.1 4.1 collective-permute-done.50.refs_1_
  326.7 6.8 %collective-permute-done.47.refs_1_ = bf16[128,1024]{1,0:T(8,128)(2,1)S(1)} collective-permute-done((bf16[128,1024]{1,0:T(8,128)(2,1)}, bf16[128,1024]{1,0:T(8,128)(2,1)S(1)}, u32[]{:S(2)}, u32[]{:S(2)}) %collective-permute-start.47) | collective-permute-done | bytes 262176 | tf_op jit(solution)/shard_map/ppermute | solution.py:97
  333.5 4.5 collective-permute-done.48.refs_2_
  343.4 8.2 %convolve_back_start.1 = (f32[128,1024]{1,0:T(8,128)S(1)}, bf16[128,1024]{1,0:T(8,128)(2,1)S(1)}, f32[128,1024]{1,0:T(8,128)S(1)}, bf16[32,1024]{1,0:T(8,128)(2,1)}, f32[35,1024]{1,0:T(8,128)S(1)}) custom-call(f32[128,1024]{1,0:T(8,128)S(1)} %copy-done.44, bf16[128,1024]{1,0:T(8,128)(2,1)S(1)} %collective-permute-done.47.refs_1_, ...), custom_call_target="tpu_custom_call" | custom-call | flops 268435456 | bytes 7024640 | tf_op jit(solution)/shard_map/convolve_back_start/pallas_call | solution.py:72
  377.4 4.5 collective-permute-start.56
  381.8 4.3 collective-permute-done.57.refs_7_
  394.3 26.4 %attend_backward.1 = (bf16[1024,1024]{1,0:T(8,128)(2,1)S(1)}, bf16[1024,384]{1,0:T(8,128)(2,1)S(1)}, f32[512,128]{1,0:T(8,128)S(1)}, f32[8,128]{1,0:T(8,128)S(1)...) custom-call(s32[1]{0:T(128)} %bitcast.2.refs_0_, bf16[128,1024]{1,0:T(8,128)(2,1)} %get-tuple-element.163.refs_1_, ...), custom_call_target="tpu_custom_call" | custom-call | flops 12884901888 | bytes 10883072 | tf_op jit(solution)/shard_map/attend_backward/pallas_call | solution.py:72
  439.5 5.5 collective-permute-done.60.refs_1_
  445.1 5.6 collective-permute-done.61.refs_2_
  457.9 4.6 collective-permute-done.78.refs_1_
  465.6 12.4 %collective-permute-done.79.refs_2_ = bf16[128,768]{1,0:T(8,128)(2,1)S(1)} collective-permute-done((bf16[128,768]{1,0:T(8,128)(2,1)S(1)}, bf16[128,768]{1,0:T(8,128)(2,1)S(1)}, u32[]{:S(2)}, u32[]{:S(2)}) %collective-permute-start.79) | collective-permute-done | bytes 196640 | tf_op jit(solution)/shard_map/ppermute | solution.py:97
  479.8 4.8 feed_backward.3
  485.4 4.5 feed_weights.3
  493.2 3.2 collective-permute-done.84
  497.1 7.4 %collective-permute-done.83 = bf16[2,64,1536]{2,1,0:T(8,128)(2,1)} collective-permute-done((bf16[2,64,1536]{2,1,0:T(8,128)(2,1)S(1)}, bf16[2,64,1536]{2,1,0:T(8,128)(2,1)}, u32[]{:S(2)}, u32[]{:S(2)}) %collective-permute-start.83) | collective-permute-done | bytes 393248 | tf_op jit(solution)/shard_map/ppermute | solution.py:97
  506.5 3.4 reshape.274
  513.5 4.0 reverse_select_fusion.2
  521.1 2.7 collective-permute-done.67.refs_2_
  528.3 2.9 concatenate.113
  534.7 6.0 all-to-all-start
  543.6 2.8 feed_core_sum.1
  554.7 3.7 broadcast_in_dim_reshape.3
  560.9 2.8 reduce.20
  565.5 3.1 collective-permute-start.72
  572.4 16.0 %collective-permute-done.70.refs_1_ = bf16[256,1024]{1,0:T(8,128)(2,1)S(1)} collective-permute-done((bf16[256,1024]{1,0:T(8,128)(2,1)}, bf16[256,1024]{1,0:T(8,128)(2,1)S(1)}, u32[]{:S(2)}, u32[]{:S(2)}) %collective-permute-start.70) | collective-permute-done | bytes 524320 | tf_op jit(solution)/shard_map/ppermute | solution.py:97
  588.6 3.4 collective-permute-start.73
  592.1 2.8 collective-permute-done.73
  600.0 5.4 collective-permute-done.90
  611.7 6.1 collective-permute-done.85
  (542 shorter events, 216.5 us)
Async XLA Ops:
  7.2 191.3 %all-gather.5.cloned.1.call-start = ((), (), s32[]{:S(2)}) async-start(), calls=%async_computation.4 | async-start | bytes 2621440 | tf_op jit(solution)/shard_map/all_gather | solution.py:1192
  7.2 47.5 %collective-permute-start = (bf16[128,1024]{1,0:T(8,128)(2,1)}, bf16[128,1024]{1,0:T(8,128)(2,1)S(1)}, u32[]{:S(2)}, u32[]{:S(2)}) collective-permute-start(bf16[128,1024]{1,0:T(8,128)(2,1)} %refs_5_.1), channel_id=1, source_target_pairs={{0,16},{1,17},{2,18},{3,19},{4,20},{5,21},{6,22},{7,23},{8,24},{9,... | collective-permute-start | bytes 786440 | tf_op jit(solution)/shard_map/ppermute | solution.py:97
  10.2 64.2 %collective-permute-start.1 = (bf16[128,1024]{1,0:T(8,128)(2,1)}, bf16[128,1024]{1,0:T(8,128)(2,1)}, u32[]{:S(2)}, u32[]{:S(2)}) collective-permute-start(bf16[128,1024]{1,0:T(8,128)(2,1)} %refs_5_.1), channel_id=1, source_target_pairs={{0,2},{1,3},{2,0},{3,1},{4,6},{5,7},{6,4},{7,5},{8,10},{9,11},{10,... | collective-permute-start | bytes 786440 | tf_op jit(solution)/shard_map/ppermute | solution.py:97
  24.1 29.1 %collective-permute-start.5 = (bf16[256,1024]{1,0:T(8,128)(2,1)S(1)}, bf16[256,1024]{1,0:T(8,128)(2,1)S(1)}, u32[]{:S(2)}, u32[]{:S(2)}) collective-permute-start(bf16[256,1024]{1,0:T(8,128)(2,1)S(1)} %pack_rows.2.refs_5_.refs_3_.refs_2_), channel_id=1, source_target_pairs={{0,8},{1,9},{2,10},{3,11},{4,12},{5,13},{6,14},{7,15},{8,0},{9,1},... | collective-permute-start | bytes 1572872 | tf_op jit(solution)/shard_map/ppermute | solution.py:97
  26.8 11.9 %collective-permute-start.13 = (bf16[4,56,64]{2,1,0:T(8,128)(2,1)S(1)}, bf16[4,56,64]{2,1,0:T(8,128)(2,1)S(1)}, u32[]{:S(2)}, u32[]{:S(2)}) collective-permute-start(bf16[4,56,64]{2,1,0:T(8,128)(2,1)S(1)} %pad_maximum_fusion.8), channel_id=1, source_target_pairs={{0,4},{1,5},{2,6},{3,7},{4,0},{5,1},{6,2},{7,3},{8,12},{9,13},{10,... | collective-permute-start | bytes 86024 | tf_op jit(solution)/shard_map/ppermute | solution.py:97
  38.8 15.7 %collective-permute-start.14 = (bf16[8,56,64]{2,1,0:T(8,128)(2,1)S(1)}, bf16[8,56,64]{2,1,0:T(8,128)(2,1)S(1)}, u32[]{:S(2)}, u32[]{:S(2)}) collective-permute-start(bf16[8,56,64]{2,1,0:T(8,128)(2,1)S(1)} %pad_maximum_fusion.7), channel_id=1, source_target_pairs={{0,8},{1,9},{2,10},{3,11},{4,12},{5,13},{6,14},{7,15},{8,0},{9,1},... | collective-permute-start | bytes 172040 | tf_op jit(solution)/shard_map/ppermute | solution.py:97
  41.2 23.3 %collective-permute-start.4 = (bf16[256,1024]{1,0:T(8,128)(2,1)S(1)}, bf16[256,1024]{1,0:T(8,128)(2,1)S(1)}, u32[]{:S(2)}, u32[]{:S(2)}) collective-permute-start(bf16[256,1024]{1,0:T(8,128)(2,1)S(1)} %pack_rows.2.refs_5_.refs_3_.refs_2_), channel_id=1, source_target_pairs={{0,4},{1,5},{2,6},{3,7},{4,0},{5,1},{6,2},{7,3},{8,12},{9,13},{10,... | collective-permute-start | bytes 1572872 | tf_op jit(solution)/shard_map/ppermute | solution.py:97
  53.2 21.2 %collective-permute-start.6 = (bf16[256,1024]{1,0:T(8,128)(2,1)S(1)}, bf16[256,1024]{1,0:T(8,128)(2,1)S(1)}, u32[]{:S(2)}, u32[]{:S(2)}) collective-permute-start(bf16[256,1024]{1,0:T(8,128)(2,1)S(1)} %collective-permute-done.5.refs_7_.refs_5_.refs_4_), channel_id=1, source_target_pairs={{0,4},{1,5},{2,6},{3,7},{4,0},{5,1},{6,2},{7,3},{8,12},{9,13},{10,... | collective-permute-start | bytes 1572872 | tf_op jit(solution)/shard_map/ppermute | solution.py:97
  54.6 30.1 %collective-permute-start.7 = (bf16[256,1024]{1,0:T(8,128)(2,1)S(1)}, bf16[256,1024]{1,0:T(8,128)(2,1)}, u32[]{:S(2)}, u32[]{:S(2)}) collective-permute-start(bf16[256,1024]{1,0:T(8,128)(2,1)S(1)} %pack_rows.2.refs_5_.refs_3_.refs_2_), channel_id=1, source_target_pairs={{0,1},{1,0},{2,3},{3,2},{4,5},{5,4},{6,7},{7,6},{8,9},{9,8},{10,11... | collective-permute-start | bytes 1572872 | tf_op jit(solution)/shard_map/ppermute | solution.py:97
  54.7 30.0 %collective-permute-start.9 = (bf16[256,1024]{1,0:T(8,128)(2,1)S(1)}, bf16[256,1024]{1,0:T(8,128)(2,1)}, u32[]{:S(2)}, u32[]{:S(2)}) collective-permute-start(bf16[256,1024]{1,0:T(8,128)(2,1)S(1)} %collective-permute-done.5.refs_7_.refs_5_.refs_4_), channel_id=1, source_target_pairs={{0,1},{1,0},{2,3},{3,2},{4,5},{5,4},{6,7},{7,6},{8,9},{9,8},{10,11... | collective-permute-start | bytes 1572872 | tf_op jit(solution)/shard_map/ppermute | solution.py:97
  64.5 20.2 %collective-permute-start.8 = (bf16[256,1024]{1,0:T(8,128)(2,1)S(1)}, bf16[256,1024]{1,0:T(8,128)(2,1)}, u32[]{:S(2)}, u32[]{:S(2)}) collective-permute-start(bf16[256,1024]{1,0:T(8,128)(2,1)S(1)} %collective-permute-done.4.refs_6_.refs_4_.refs_3_), channel_id=1, source_target_pairs={{0,1},{1,0},{2,3},{3,2},{4,5},{5,4},{6,7},{7,6},{8,9},{9,8},{10,11... | collective-permute-start | bytes 1572872 | tf_op jit(solution)/shard_map/ppermute | solution.py:97
  96.7 139.0 %all-gather.3.cloned.1.call-start = ((), (), s32[]{:S(2)}) async-start(), calls=%async_computation.3 | async-start | bytes 6684672 | tf_op jit(solution)/shard_map/all_gather | solution.py:1186
  97.6 443.2 %reduce-scatter.3.cloned.1.call-start = ((), (), s32[]{:S(2)}) async-start(), calls=%async_computation.5 | async-start | bytes 2621440 | tf_op jit(solution)/shard_map/reduce_scatter | solution.py:1230
  113.8 20.0 %collective-permute-start.19 = (bf16[256,384]{1,0:T(8,128)(2,1)S(1)}, bf16[256,384]{1,0:T(8,128)(2,1)S(1)}, u32[]{:S(2)}, u32[]{:S(2)}) collective-permute-start(bf16[256,384]{1,0:T(8,128)(2,1)S(1)} %get-tuple-element.122), channel_id=1, source_target_pairs={{0,4},{1,5},{2,6},{3,7},{4,0},{5,1},{6,2},{7,3},{8,12},{9,13},{10,... | collective-permute-start | bytes 589832 | tf_op jit(solution)/shard_map/ppermute | solution.py:97
  113.9 25.8 %collective-permute-start.20 = (bf16[256,384]{1,0:T(8,128)(2,1)S(1)}, bf16[256,384]{1,0:T(8,128)(2,1)S(1)}, u32[]{:S(2)}, u32[]{:S(2)}) collective-permute-start(bf16[256,384]{1,0:T(8,128)(2,1)S(1)} %get-tuple-element.121.refs_0_), channel_id=1, source_target_pairs={{0,8},{1,9},{2,10},{3,11},{4,12},{5,13},{6,14},{7,15},{8,0},{9,1},... | collective-permute-start | bytes 589832 | tf_op jit(solution)/shard_map/ppermute | solution.py:97
  118.3 25.5 %collective-permute-start.21 = (bf16[256,384]{1,0:T(8,128)(2,1)S(1)}, bf16[256,384]{1,0:T(8,128)(2,1)S(1)}, u32[]{:S(2)}, u32[]{:S(2)}) collective-permute-start(bf16[256,384]{1,0:T(8,128)(2,1)S(1)} %get-tuple-element.122), channel_id=1, source_target_pairs={{0,12},{1,13},{2,14},{3,15},{4,8},{5,9},{6,10},{7,11},{8,4},{9,5},... | collective-permute-start | bytes 589832 | tf_op jit(solution)/shard_map/ppermute | solution.py:97
  143.9 23.3 %collective-permute-start.22 = (bf16[512,384]{1,0:T(8,128)(2,1)S(1)}, bf16[512,384]{1,0:T(8,128)(2,1)S(1)}, u32[]{:S(2)}, u32[]{:S(2)}) collective-permute-start(bf16[512,384]{1,0:T(8,128)(2,1)S(1)} %get-tuple-element.124), channel_id=1, source_target_pairs={{0,1},{1,0},{2,3},{3,2},{4,5},{5,4},{6,7},{7,6},{8,9},{9,8},{10,11... | collective-permute-start | bytes 1179656 | tf_op jit(solution)/shard_map/ppermute | solution.py:97
  144.0 23.8 %collective-permute-start.15 = (bf16[128,1024]{1,0:T(8,128)(2,1)S(1)}, bf16[128,1024]{1,0:T(8,128)(2,1)S(1)}, u32[]{:S(2)}, u32[]{:S(2)}) collective-permute-start(bf16[128,1024]{1,0:T(8,128)(2,1)S(1)} %copy-done.79), channel_id=1, source_target_pairs={{0,18},{1,19},{2,16},{3,17},{4,22},{5,23},{6,20},{7,21},{8,26},{9,... | collective-permute-start | bytes 786440 | tf_op jit(solution)/shard_map/ppermute | solution.py:97
  145.5 22.3 %collective-permute-start.16 = (bf16[128,1024]{1,0:T(8,128)(2,1)S(1)}, bf16[128,1024]{1,0:T(8,128)(2,1)S(1)}, u32[]{:S(2)}, u32[]{:S(2)}) collective-permute-start(bf16[128,1024]{1,0:T(8,128)(2,1)S(1)} %copy-done.77), channel_id=1, source_target_pairs={{0,16},{1,17},{2,18},{3,19},{4,20},{5,21},{6,22},{7,23},{8,24},{9,... | collective-permute-start | bytes 786440 | tf_op jit(solution)/shard_map/ppermute | solution.py:97
  147.0 20.8 %collective-permute-start.17 = (bf16[128,1024]{1,0:T(8,128)(2,1)S(1)}, bf16[128,1024]{1,0:T(8,128)(2,1)S(1)}, u32[]{:S(2)}, u32[]{:S(2)}) collective-permute-start(bf16[128,1024]{1,0:T(8,128)(2,1)S(1)} %copy-done.75), channel_id=1, source_target_pairs={{0,2},{1,3},{2,0},{3,1},{4,6},{5,7},{6,4},{7,5},{8,10},{9,11},{10,... | collective-permute-start | bytes 786440 | tf_op jit(solution)/shard_map/ppermute | solution.py:97
  147.5 19.6 %collective-permute-start.23 = (bf16[64,1024]{1,0:T(8,128)(2,1)S(1)}, bf16[64,1024]{1,0:T(8,128)(2,1)S(1)}, u32[]{:S(2)}, u32[]{:S(2)}) collective-permute-start(bf16[64,1024]{1,0:T(8,128)(2,1)S(1)} %bitcast.117), channel_id=1, source_target_pairs={{0,8},{1,9},{2,10},{3,11},{4,12},{5,13},{6,14},{7,15},{8,0},{9,1},... | collective-permute-start | bytes 393224 | tf_op jit(solution)/shard_map/ppermute | solution.py:97
  170.1 19.9 %collective-permute-start.27 = (bf16[128,1024]{1,0:T(8,128)(2,1)S(1)}, bf16[128,1024]{1,0:T(8,128)(2,1)S(1)}, u32[]{:S(2)}, u32[]{:S(2)}) collective-permute-start(bf16[128,1024]{1,0:T(8,128)(2,1)S(1)} %get-tuple-element.126.refs_1_), channel_id=1, source_target_pairs={{0,4},{1,5},{2,6},{3,7},{4,0},{5,1},{6,2},{7,3},{8,12},{9,13},{10,... | collective-permute-start | bytes 786440 | tf_op jit(solution)/shard_map/ppermute | solution.py:97
  174.4 22.3 %collective-permute-start.29 = (bf16[128,1024]{1,0:T(8,128)(2,1)S(1)}, bf16[128,1024]{1,0:T(8,128)(2,1)S(1)}, u32[]{:S(2)}, u32[]{:S(2)}) collective-permute-start(bf16[128,1024]{1,0:T(8,128)(2,1)S(1)} %get-tuple-element.126.refs_1_), channel_id=1, source_target_pairs={{0,6},{1,7},{2,4},{3,5},{4,2},{5,3},{6,0},{7,1},{8,14},{9,15},{10,... | collective-permute-start | bytes 786440 | tf_op jit(solution)/shard_map/ppermute | solution.py:97
  176.0 23.1 %collective-permute-start.24 = (bf16[128,1024]{1,0:T(8,128)(2,1)S(1)}, bf16[128,1024]{1,0:T(8,128)(2,1)S(1)}, u32[]{:S(2)}, u32[]{:S(2)}) collective-permute-start(bf16[128,1024]{1,0:T(8,128)(2,1)S(1)} %get-tuple-element.126.refs_1_), channel_id=1, source_target_pairs={{0,1},{1,0},{2,3},{3,2},{4,5},{5,4},{6,7},{7,6},{8,9},{9,8},{10,11... | collective-permute-start | bytes 786440 | tf_op jit(solution)/shard_map/ppermute | solution.py:97
  178.7 21.1 %collective-permute-start.26 = (bf16[128,1024]{1,0:T(8,128)(2,1)S(1)}, bf16[128,1024]{1,0:T(8,128)(2,1)}, u32[]{:S(2)}, u32[]{:S(2)}) collective-permute-start(bf16[128,1024]{1,0:T(8,128)(2,1)S(1)} %collective-permute-done.25.refs_3_), channel_id=1, source_target_pairs={{0,1},{1,0},{2,3},{3,2},{4,5},{5,4},{6,7},{7,6},{8,9},{9,8},{10,11... | collective-permute-start | bytes 786440 | tf_op jit(solution)/shard_map/ppermute | solution.py:97
  198.5 61.7 %collective-permute-start.40 = (bf16[1024,1024]{1,0:T(8,128)(2,1)}, bf16[1024,1024]{1,0:T(8,128)(2,1)}, u32[]{:S(2)}, u32[]{:S(2)}) collective-permute-start(bf16[1024,1024]{1,0:T(8,128)(2,1)} %all-gather.5.cloned.1.call-done.refs_5_), channel_id=1, source_target_pairs={{0,1},{1,0},{2,3},{3,2},{4,5},{5,4},{6,7},{7,6},{8,9},{9,8},{10,11... | collective-permute-start | bytes 6291464 | tf_op jit(solution)/shard_map/ppermute | solution.py:97
  223.6 15.0 %collective-permute-start.32 = (bf16[128,1024]{1,0:T(8,128)(2,1)S(1)}, bf16[128,1024]{1,0:T(8,128)(2,1)S(1)}, u32[]{:S(2)}, u32[]{:S(2)}) collective-permute-start(bf16[128,1024]{1,0:T(8,128)(2,1)S(1)} %get-tuple-element.131), channel_id=1, source_target_pairs={{0,6},{1,7},{2,4},{3,5},{4,2},{5,3},{6,0},{7,1},{8,14},{9,15},{10,... | collective-permute-start | bytes 786440 | tf_op jit(solution)/shard_map/ppermute | solution.py:97
  223.7 18.7 %collective-permute-start.33 = (bf16[128,1024]{1,0:T(8,128)(2,1)S(1)}, bf16[128,1024]{1,0:T(8,128)(2,1)S(1)}, u32[]{:S(2)}, u32[]{:S(2)}) collective-permute-start(bf16[128,1024]{1,0:T(8,128)(2,1)S(1)} %get-tuple-element.132), channel_id=1, source_target_pairs={{0,4},{1,5},{2,6},{3,7},{4,0},{5,1},{6,2},{7,3},{8,12},{9,13},{10,... | collective-permute-start | bytes 786440 | tf_op jit(solution)/shard_map/ppermute | solution.py:97
  225.5 16.9 %collective-permute-start.34 = (bf16[128,1024]{1,0:T(8,128)(2,1)S(1)}, bf16[128,1024]{1,0:T(8,128)(2,1)S(1)}, u32[]{:S(2)}, u32[]{:S(2)}) collective-permute-start(bf16[128,1024]{1,0:T(8,128)(2,1)S(1)} %get-tuple-element.133), channel_id=1, source_target_pairs={{0,2},{1,3},{2,0},{3,1},{4,6},{5,7},{6,4},{7,5},{8,10},{9,11},{10,... | collective-permute-start | bytes 786440 | tf_op jit(solution)/shard_map/ppermute | solution.py:97
  257.9 14.6 %collective-permute-start.37 = (bf16[128,1024]{1,0:T(8,128)(2,1)S(1)}, bf16[128,1024]{1,0:T(8,128)(2,1)S(1)}, u32[]{:S(2)}, u32[]{:S(2)}) collective-permute-start(bf16[128,1024]{1,0:T(8,128)(2,1)S(1)} %get-tuple-element.137.refs_1_), channel_id=1, source_target_pairs={{0,2},{1,3},{2,0},{3,1},{4,6},{5,7},{6,4},{7,5},{8,10},{9,11},{10,... | collective-permute-start | bytes 786440 | tf_op jit(solution)/shard_map/ppermute | solution.py:97
  260.1 12.4 %collective-permute-start.38 = (bf16[128,1024]{1,0:T(8,128)(2,1)S(1)}, bf16[128,1024]{1,0:T(8,128)(2,1)S(1)}, u32[]{:S(2)}, u32[]{:S(2)}) collective-permute-start(bf16[128,1024]{1,0:T(8,128)(2,1)S(1)} %get-tuple-element.137.refs_1_), channel_id=1, source_target_pairs={{0,18},{1,19},{2,16},{3,17},{4,22},{5,23},{6,20},{7,21},{8,26},{9,... | collective-permute-start | bytes 786440 | tf_op jit(solution)/shard_map/ppermute | solution.py:97
  278.5 12.5 %collective-permute-start.42 = (bf16[128,1024]{1,0:T(8,128)(2,1)S(1)}, bf16[128,1024]{1,0:T(8,128)(2,1)S(1)}, u32[]{:S(2)}, u32[]{:S(2)}) collective-permute-start(bf16[128,1024]{1,0:T(8,128)(2,1)S(1)} %get-tuple-element.141), channel_id=1, source_target_pairs={{0,16},{1,17},{2,18},{3,19},{4,20},{5,21},{6,22},{7,23},{8,24},{9,... | collective-permute-start | bytes 786440 | tf_op jit(solution)/shard_map/ppermute | solution.py:97
  294.4 13.6 %collective-permute-start.45 = (bf16[128,1024]{1,0:T(8,128)(2,1)S(1)}, bf16[128,1024]{1,0:T(8,128)(2,1)S(1)}, u32[]{:S(2)}, u32[]{:S(2)}) collective-permute-start(bf16[128,1024]{1,0:T(8,128)(2,1)S(1)} %get-tuple-element.145.refs_1_), channel_id=1, source_target_pairs={{0,2},{1,3},{2,0},{3,1},{4,6},{5,7},{6,4},{7,5},{8,10},{9,11},{10,... | collective-permute-start | bytes 786440 | tf_op jit(solution)/shard_map/ppermute | solution.py:97
  295.5 12.5 %collective-permute-start.46 = (bf16[128,1024]{1,0:T(8,128)(2,1)S(1)}, bf16[128,1024]{1,0:T(8,128)(2,1)S(1)}, u32[]{:S(2)}, u32[]{:S(2)}) collective-permute-start(bf16[128,1024]{1,0:T(8,128)(2,1)S(1)} %get-tuple-element.145.refs_1_), channel_id=1, source_target_pairs={{0,18},{1,19},{2,16},{3,17},{4,22},{5,23},{6,20},{7,21},{8,26},{9,... | collective-permute-start | bytes 786440 | tf_op jit(solution)/shard_map/ppermute | solution.py:97
  323.1 286.8 %reduce-scatter.5.cloned.1.call-start = ((), (), s32[]{:S(2)}) async-start(), calls=%async_computation.6 | async-start | bytes 6684672 | tf_op jit(solution)/shard_map/reduce_scatter | solution.py:1009
  324.6 13.3 %collective-permute-start.48 = (bf16[128,1024]{1,0:T(8,128)(2,1)}, bf16[128,1024]{1,0:T(8,128)(2,1)S(1)}, u32[]{:S(2)}, u32[]{:S(2)}) collective-permute-start(bf16[128,1024]{1,0:T(8,128)(2,1)} %copy-done.92), channel_id=1, source_target_pairs={{0,16},{1,17},{2,18},{3,19},{4,20},{5,21},{6,22},{7,23},{8,24},{9,... | collective-permute-start | bytes 786440 | tf_op jit(solution)/shard_map/ppermute | solution.py:97
  325.8 12.5 %collective-permute-start.49 = (bf16[128,1024]{1,0:T(8,128)(2,1)}, bf16[128,1024]{1,0:T(8,128)(2,1)S(1)}, u32[]{:S(2)}, u32[]{:S(2)}) collective-permute-start(bf16[128,1024]{1,0:T(8,128)(2,1)} %copy-done.91), channel_id=1, source_target_pairs={{0,2},{1,3},{2,0},{3,1},{4,6},{5,7},{6,4},{7,5},{8,10},{9,11},{10,... | collective-permute-start | bytes 786440 | tf_op jit(solution)/shard_map/ppermute | solution.py:97
  372.1 14.0 %collective-permute-start.57 = (bf16[128,1024]{1,0:T(8,128)(2,1)}, bf16[128,1024]{1,0:T(8,128)(2,1)}, u32[]{:S(2)}, u32[]{:S(2)}) collective-permute-start(bf16[128,1024]{1,0:T(8,128)(2,1)} %get-tuple-element.163.refs_1_), channel_id=1, source_target_pairs={{0,6},{1,7},{2,4},{3,5},{4,2},{5,3},{6,0},{7,1},{8,14},{9,15},{10,... | collective-permute-start | bytes 786440 | tf_op jit(solution)/shard_map/ppermute | solution.py:97
  373.5 17.5 %collective-permute-start.52 = (bf16[128,1024]{1,0:T(8,128)(2,1)}, bf16[128,1024]{1,0:T(8,128)(2,1)}, u32[]{:S(2)}, u32[]{:S(2)}) collective-permute-start(bf16[128,1024]{1,0:T(8,128)(2,1)} %get-tuple-element.163.refs_1_), channel_id=1, source_target_pairs={{0,1},{1,0},{2,3},{3,2},{4,5},{5,4},{6,7},{7,6},{8,9},{9,8},{10,11... | collective-permute-start | bytes 786440 | tf_op jit(solution)/shard_map/ppermute | solution.py:97
  374.8 16.2 %collective-permute-start.54 = (bf16[128,1024]{1,0:T(8,128)(2,1)S(1)}, bf16[128,1024]{1,0:T(8,128)(2,1)}, u32[]{:S(2)}, u32[]{:S(2)}) collective-permute-start(bf16[128,1024]{1,0:T(8,128)(2,1)S(1)} %collective-permute-done.53.refs_3_), channel_id=1, source_target_pairs={{0,1},{1,0},{2,3},{3,2},{4,5},{5,4},{6,7},{7,6},{8,9},{9,8},{10,11... | collective-permute-start | bytes 786440 | tf_op jit(solution)/shard_map/ppermute | solution.py:97
  377.4 13.6 %collective-permute-start.56 = (bf16[128,1024]{1,0:T(8,128)(2,1)}, bf16[128,1024]{1,0:T(8,128)(2,1)}, u32[]{:S(2)}, u32[]{:S(2)}) collective-permute-start(bf16[128,1024]{1,0:T(8,128)(2,1)} %collective-permute-done.55.refs_5_), channel_id=1, source_target_pairs={{0,1},{1,0},{2,3},{3,2},{4,5},{5,4},{6,7},{7,6},{8,9},{9,8},{10,11... | collective-permute-start | bytes 786440 | tf_op jit(solution)/shard_map/ppermute | solution.py:97
  425.2 13.8 %collective-permute-start.77 = (bf16[512,384]{1,0:T(8,128)(2,1)}, bf16[512,384]{1,0:T(8,128)(2,1)S(1)}, u32[]{:S(2)}, u32[]{:S(2)}) collective-permute-start(bf16[512,384]{1,0:T(8,128)(2,1)} %get-tuple-element.205), channel_id=1, source_target_pairs={{0,1},{1,0},{2,3},{3,2},{4,5},{5,4},{6,7},{7,6},{8,9},{9,8},{10,11... | collective-permute-start | bytes 1179656 | tf_op jit(solution)/shard_map/ppermute | solution.py:97
  426.6 18.4 %collective-permute-start.60 = (bf16[128,1024]{1,0:T(8,128)(2,1)}, bf16[128,1024]{1,0:T(8,128)(2,1)}, u32[]{:S(2)}, u32[]{:S(2)}) collective-permute-start(bf16[128,1024]{1,0:T(8,128)(2,1)} %get-tuple-element.169), channel_id=1, source_target_pairs={{0,6},{1,7},{2,4},{3,5},{4,2},{5,3},{6,0},{7,1},{8,14},{9,15},{10,... | collective-permute-start | bytes 786440 | tf_op jit(solution)/shard_map/ppermute | solution.py:97
  427.9 22.8 %collective-permute-start.61 = (bf16[128,1024]{1,0:T(8,128)(2,1)}, bf16[128,1024]{1,0:T(8,128)(2,1)}, u32[]{:S(2)}, u32[]{:S(2)}) collective-permute-start(bf16[128,1024]{1,0:T(8,128)(2,1)} %get-tuple-element.170), channel_id=1, source_target_pairs={{0,4},{1,5},{2,6},{3,7},{4,0},{5,1},{6,2},{7,3},{8,12},{9,13},{10,... | collective-permute-start | bytes 786440 | tf_op jit(solution)/shard_map/ppermute | solution.py:97
  428.7 22.0 %collective-permute-start.62 = (bf16[128,1024]{1,0:T(8,128)(2,1)}, bf16[128,1024]{1,0:T(8,128)(2,1)}, u32[]{:S(2)}, u32[]{:S(2)}) collective-permute-start(bf16[128,1024]{1,0:T(8,128)(2,1)} %get-tuple-element.171), channel_id=1, source_target_pairs={{0,2},{1,3},{2,0},{3,1},{4,6},{5,7},{6,4},{7,5},{8,10},{9,11},{10,... | collective-permute-start | bytes 786440 | tf_op jit(solution)/shard_map/ppermute | solution.py:97
  437.3 19.8 %collective-permute-start.81 = (bf16[64,1024]{1,0:T(8,128)(2,1)}, bf16[64,1024]{1,0:T(8,128)(2,1)S(1)}, u32[]{:S(2)}, u32[]{:S(2)}) collective-permute-start(bf16[64,1024]{1,0:T(8,128)(2,1)} %copy-done.94), channel_id=1, source_target_pairs={{0,8},{1,9},{2,10},{3,11},{4,12},{5,13},{6,14},{7,15},{8,0},{9,1},... | collective-permute-start | bytes 393224 | tf_op jit(solution)/shard_map/ppermute | solution.py:97
  439.1 23.4 %collective-permute-start.78 = (bf16[128,768]{1,0:T(8,128)(2,1)S(1)}, bf16[128,768]{1,0:T(8,128)(2,1)S(1)}, u32[]{:S(2)}, u32[]{:S(2)}) collective-permute-start(bf16[128,768]{1,0:T(8,128)(2,1)S(1)} %get-tuple-element.207), channel_id=1, source_target_pairs={{0,4},{1,5},{2,6},{3,7},{4,0},{5,1},{6,2},{7,3},{8,12},{9,13},{10,... | collective-permute-start | bytes 589832 | tf_op jit(solution)/shard_map/ppermute | solution.py:97
  453.2 26.5 %collective-permute-start.63 = (bf16[128,1024]{1,0:T(8,128)(2,1)S(1)}, bf16[128,1024]{1,0:T(8,128)(2,1)S(1)}, u32[]{:S(2)}, u32[]{:S(2)}) collective-permute-start(bf16[128,1024]{1,0:T(8,128)(2,1)S(1)} %get-tuple-element.173.refs_1_), channel_id=1, source_target_pairs={{0,16},{1,17},{2,18},{3,19},{4,20},{5,21},{6,22},{7,23},{8,24},{9,... | collective-permute-start | bytes 786440 | tf_op jit(solution)/shard_map/ppermute | solution.py:97
  454.7 25.0 %collective-permute-start.64 = (bf16[128,1024]{1,0:T(8,128)(2,1)S(1)}, bf16[128,1024]{1,0:T(8,128)(2,1)S(1)}, u32[]{:S(2)}, u32[]{:S(2)}) collective-permute-start(bf16[128,1024]{1,0:T(8,128)(2,1)S(1)} %get-tuple-element.173.refs_1_), channel_id=1, source_target_pairs={{0,2},{1,3},{2,0},{3,1},{4,6},{5,7},{6,4},{7,5},{8,10},{9,11},{10,... | collective-permute-start | bytes 786440 | tf_op jit(solution)/shard_map/ppermute | solution.py:97
  457.0 22.7 %collective-permute-start.65 = (bf16[128,1024]{1,0:T(8,128)(2,1)S(1)}, bf16[128,1024]{1,0:T(8,128)(2,1)S(1)}, u32[]{:S(2)}, u32[]{:S(2)}) collective-permute-start(bf16[128,1024]{1,0:T(8,128)(2,1)S(1)} %get-tuple-element.173.refs_1_), channel_id=1, source_target_pairs={{0,18},{1,19},{2,16},{3,17},{4,22},{5,23},{6,20},{7,21},{8,26},{9,... | collective-permute-start | bytes 786440 | tf_op jit(solution)/shard_map/ppermute | solution.py:97
  457.1 20.8 %collective-permute-start.79 = (bf16[128,768]{1,0:T(8,128)(2,1)S(1)}, bf16[128,768]{1,0:T(8,128)(2,1)S(1)}, u32[]{:S(2)}, u32[]{:S(2)}) collective-permute-start(bf16[128,768]{1,0:T(8,128)(2,1)S(1)} %get-tuple-element.208), channel_id=1, source_target_pairs={{0,8},{1,9},{2,10},{3,11},{4,12},{5,13},{6,14},{7,15},{8,0},{9,1},... | collective-permute-start | bytes 589832 | tf_op jit(solution)/shard_map/ppermute | solution.py:97
  462.5 15.4 %collective-permute-start.80 = (bf16[128,768]{1,0:T(8,128)(2,1)S(1)}, bf16[128,768]{1,0:T(8,128)(2,1)S(1)}, u32[]{:S(2)}, u32[]{:S(2)}) collective-permute-start(bf16[128,768]{1,0:T(8,128)(2,1)S(1)} %get-tuple-element.209), channel_id=1, source_target_pairs={{0,12},{1,13},{2,14},{3,15},{4,8},{5,9},{6,10},{7,11},{8,4},{9,5},... | collective-permute-start | bytes 589832 | tf_op jit(solution)/shard_map/ppermute | solution.py:97
  478.0 13.6 %collective-permute-start.82 = (bf16[64,1536]{1,0:T(8,128)(2,1)S(1)}, bf16[64,1536]{1,0:T(8,128)(2,1)S(1)}, u32[]{:S(2)}, u32[]{:S(2)}) collective-permute-start(bf16[64,1536]{1,0:T(8,128)(2,1)S(1)} %get-tuple-element.213), channel_id=1, source_target_pairs={{0,2},{1,3},{2,0},{3,1},{4,6},{5,7},{6,4},{7,5},{8,10},{9,11},{10,... | collective-permute-start | bytes 589832 | tf_op jit(solution)/shard_map/ppermute | solution.py:97
  490.0 53.6 %collective-permute-start.69 = (bf16[1024,1024]{1,0:T(8,128)(2,1)}, bf16[1024,1024]{1,0:T(8,128)(2,1)}, u32[]{:S(2)}, u32[]{:S(2)}) collective-permute-start(bf16[1024,1024]{1,0:T(8,128)(2,1)} %get-tuple-element.185), channel_id=1, source_target_pairs={{0,1},{1,0},{2,3},{3,2},{4,5},{5,4},{6,7},{7,6},{8,9},{9,8},{10,11... | collective-permute-start | bytes 6291464 | tf_op jit(solution)/shard_map/ppermute | solution.py:97
  491.7 12.8 %collective-permute-start.83 = (bf16[2,64,1536]{2,1,0:T(8,128)(2,1)S(1)}, bf16[2,64,1536]{2,1,0:T(8,128)(2,1)}, u32[]{:S(2)}, u32[]{:S(2)}) collective-permute-start(bf16[2,64,1536]{2,1,0:T(8,128)(2,1)S(1)} %pad_maximum_fusion.4), channel_id=1, source_target_pairs={{0,16},{1,17},{2,18},{3,19},{4,20},{5,21},{6,22},{7,23},{8,24},{9,... | collective-permute-start | bytes 1179656 | tf_op jit(solution)/shard_map/ppermute | solution.py:97
  492.3 56.4 %collective-permute-start.86 = (f32[73,64]{1,0:T(8,128)S(1)}, f32[73,64]{1,0:T(8,128)S(1)}, u32[]{:S(2)}, u32[]{:S(2)}) collective-permute-start(f32[73,64]{1,0:T(8,128)S(1)} %slice_add_fusion.refs_0_), channel_id=1, source_target_pairs={{0,1},{1,0},{2,3},{3,2},{4,5},{5,4},{6,7},{7,6},{8,9},{9,8},{10,11... | collective-permute-start | bytes 56072 | tf_op jit(solution)/shard_map/ppermute | solution.py:97
  511.3 12.5 %collective-permute-start.67 = (bf16[128,1024]{1,0:T(8,128)(2,1)}, bf16[128,1024]{1,0:T(8,128)(2,1)}, u32[]{:S(2)}, u32[]{:S(2)}) collective-permute-start(bf16[128,1024]{1,0:T(8,128)(2,1)} %copy-done.83), channel_id=1, source_target_pairs={{0,16},{1,17},{2,18},{3,19},{4,20},{5,21},{6,22},{7,23},{8,24},{9,... | collective-permute-start | bytes 786440 | tf_op jit(solution)/shard_map/ppermute | solution.py:97
  511.9 12.9 %collective-permute-start.68 = (bf16[128,1024]{1,0:T(8,128)(2,1)}, bf16[128,1024]{1,0:T(8,128)(2,1)}, u32[]{:S(2)}, u32[]{:S(2)}) collective-permute-start(bf16[128,1024]{1,0:T(8,128)(2,1)} %copy-done.80), channel_id=1, source_target_pairs={{0,2},{1,3},{2,0},{3,1},{4,6},{5,7},{6,4},{7,5},{8,10},{9,11},{10,... | collective-permute-start | bytes 786440 | tf_op jit(solution)/shard_map/ppermute | solution.py:97
  534.7 25.6 %all-to-all-start = ((f32[32,1,3584]{2,1,0:T(1,128)}), f32[32,1,3584]{2,1,0:T(1,128)}, u32[]{:S(2)}, u32[]{:S(2)}) async-start(f32[32,1,3584]{2,1,0:T(1,128)} %reshape.312), calls=%async_computation.1 | async-start | bytes 917504 | tf_op jit(solution)/shard_map/all_to_all | solution.py:1090
  546.4 17.8 %collective-permute-start.71 = (bf16[256,1024]{1,0:T(8,128)(2,1)}, bf16[256,1024]{1,0:T(8,128)(2,1)}, u32[]{:S(2)}, u32[]{:S(2)}) collective-permute-start(bf16[256,1024]{1,0:T(8,128)(2,1)} %get-tuple-element.189), channel_id=1, source_target_pairs={{0,4},{1,5},{2,6},{3,7},{4,0},{5,1},{6,2},{7,3},{8,12},{9,13},{10,... | collective-permute-start | bytes 1572872 | tf_op jit(solution)/shard_map/ppermute | solution.py:97
  550.8 20.1 %collective-permute-start.76 = (bf16[256,1024]{1,0:T(8,128)(2,1)}, bf16[256,1024]{1,0:T(8,128)(2,1)}, u32[]{:S(2)}, u32[]{:S(2)}) collective-permute-start(bf16[256,1024]{1,0:T(8,128)(2,1)} %pad_maximum_fusion.2), channel_id=1, source_target_pairs={{0,16},{1,17},{2,18},{3,19},{4,20},{5,21},{6,22},{7,23},{8,24},{9,... | collective-permute-start | bytes 1572872 | tf_op jit(solution)/shard_map/ppermute | solution.py:97
  558.5 33.5 %collective-permute-start.88 = (f32[73,64]{1,0:T(8,128)S(1)}, f32[73,64]{1,0:T(8,128)S(1)}, u32[]{:S(2)}, u32[]{:S(2)}) collective-permute-start(f32[73,64]{1,0:T(8,128)S(1)} %table_sum.5.refs_0_), channel_id=1, source_target_pairs={{0,4},{1,5},{2,6},{3,7},{4,0},{5,1},{6,2},{7,3},{8,12},{9,13},{10,... | collective-permute-start | bytes 56072 | tf_op jit(solution)/shard_map/ppermute | solution.py:97
  563.9 24.5 %collective-permute-start.70 = (bf16[256,1024]{1,0:T(8,128)(2,1)}, bf16[256,1024]{1,0:T(8,128)(2,1)S(1)}, u32[]{:S(2)}, u32[]{:S(2)}) collective-permute-start(bf16[256,1024]{1,0:T(8,128)(2,1)} %get-tuple-element.187), channel_id=1, source_target_pairs={{0,4},{1,5},{2,6},{3,7},{4,0},{5,1},{6,2},{7,3},{8,12},{9,13},{10,... | collective-permute-start | bytes 1572872 | tf_op jit(solution)/shard_map/ppermute | solution.py:97
  565.5 22.9 %collective-permute-start.72 = (bf16[256,1024]{1,0:T(8,128)(2,1)S(1)}, bf16[256,1024]{1,0:T(8,128)(2,1)S(1)}, u32[]{:S(2)}, u32[]{:S(2)}) collective-permute-start(bf16[256,1024]{1,0:T(8,128)(2,1)S(1)} %plane_add.2), channel_id=1, source_target_pairs={{0,8},{1,9},{2,10},{3,11},{4,12},{5,13},{6,14},{7,15},{8,0},{9,1},... | collective-permute-start | bytes 1572872 | tf_op jit(solution)/shard_map/ppermute | solution.py:97
  (150 other events, 1625.1 us)
Sparse Core Ops, SparseCore 0:
  96.8 63.1 all-gather.4
  162.3 73.3 all-gather.2
  323.2 43.6 reduce-scatter.2
  391.1 108.0 reduce-scatter.4

commit v3 on v2

--- a/solution.py
+++ b/solution.py
@@ -13,6 +13,7 @@
 BF = jnp.bfloat16
 F32 = jnp.float32
 MIB = 1 << 20
+LANES = 128
 
 
 def dot_nn(left, right):
@@ -77,7 +78,7 @@
         out_specs=vmem(len(outs)),
         out_shape=list(outs),
         scratch_shapes=list(scratch),
-        compiler_params=pltpu.CompilerParams(vmem_limit_bytes=40 * MIB),
+        compiler_params=pltpu.CompilerParams(vmem_limit_bytes=24 * MIB),
         cost_estimate=pl.CostEstimate(flops=flops, bytes_accessed=moved, transcendentals=0),
         name=name,
     )(*operands, *waits)
@@ -97,29 +98,49 @@
     return lax.ppermute(value, ("rep", "shard"), [(i, i ^ mask) for i in range(total)])
 
 
-def square_gather(value, masks):
+def square_groups(place, masks):
     first, second = masks
-    return [
-        value,
-        flipped(value, first),
-        flipped(value, second),
-        flipped(value, first | second),
-    ]
-
-
-def square_reduce(parts, masks):
+    total = 2 * place.shards
+    groups = []
+    for low in range(total):
+        if not low & (first | second):
+            groups.append([low, low | second, low | first, low | first | second])
+    return groups
+
+
+def square_exchange(blocks, masks, place):
+    groups = square_groups(place, masks)
+    return lax.all_to_all(blocks, ("rep", "shard"), 0, 0, tiled=True, axis_index_groups=groups)
+
+
+def square_spread(blocks, masks, place):
     first, second = masks
-    own, via_first, via_second, cross = parts
-    return [
-        own,
-        flipped(cross, first | second),
-        flipped(via_first, first),
-        flipped(via_second, second),
-    ]
+    rows = blocks.shape[0] // 4
+
+    def kernel(spot, source, *outs):
+        member = spot[3] * 2 + spot[1]
+        for step, ref in enumerate(outs):
+            start = pl.multiple_of((member ^ step) * rows, rows)
+            ref[...] = source[pl.ds(start, rows), :]
+
+    parts = kernel_call(
+        kernel,
+        "square_split",
+        [shape_of(rows, blocks.shape[1], BF)] * 4,
+        (place.spot, blocks),
+        scalars=1,
+    )
+    masks = (0, second, first, first | second)
+    return [parts[0]] + [flipped(part, mask) for part, mask in zip(parts[1:], masks[1:])]
+
+
+def repeated(value):
+    return jnp.concatenate([value] * 4, axis=0)
 
 
 def joined(parts):
-    return parts[0] + sum(part.astype(F32) for part in parts[1:])
+    rows = parts.shape[0] // 4
+    return sum(parts[index * rows : (index + 1) * rows].astype(F32) for index in range(4))
 
 
 def place_feed(spot, packs, w_in, w_out, unit, half):
@@ -147,92 +168,80 @@
     return views
 
 
-def feed(pieces, packs, spot, bias, wide, norm_row, masks, place, waits=()):
-    rows, model = pieces[0].shape
+def feed(blocks, packs, bias, wide, norm_row, masks, place, waits=()):
+    total, model = blocks.shape
     inner = bias.shape[1]
-    count, total = len(pieces), len(pieces) * rows
     unit, half = place.unit, place.half
+    normed = norm_row is not None
 
     def kernel(spot_ref, *refs):
-        piece_refs, pack_refs = refs[:count], refs[count : count + len(packs)]
-        bias_ref, wide_ref, hidden, upper, active = refs[count + len(packs) :][:5]
-        outs = refs[count + len(packs) + 5 : -2]
-        w_in, w_out = refs[-2:]
+        blocks_ref, pack_refs = refs[0], refs[1 : 1 + len(packs)]
+        bias_ref, wide_ref = refs[1 + len(packs) : 3 + len(packs)]
+        outs, (w_in, w_out) = refs[3 + len(packs) : -2], refs[-2:]
+        upper, active, result = outs[:3]
         place_feed(spot_ref, pack_views(pack_refs, place), w_in, w_out, unit, half)
-        for index, ref in enumerate(piece_refs):
-            block = ref[...]
-            if norm_row is not None:
-                scaled, unused_scale = standard(block.astype(F32))
-                gain = wide_ref[norm_row : norm_row + 1, :]
-                shift = wide_ref[norm_row + 1 : norm_row + 2, :]
-                block = (scaled * gain + shift).astype(BF)
-            hidden[index * rows : (index + 1) * rows, :] = block
+        hidden = blocks_ref
+        if normed:
+            hidden = outs[3]
+            scaled, unused_scale = standard(blocks_ref[...].astype(F32))
+            gain = wide_ref[norm_row : norm_row + 1, :]
+            shift = wide_ref[norm_row + 1 : norm_row + 2, :]
+            hidden[...] = (scaled * gain + shift).astype(BF)
         before = dot_nn(hidden[...], w_in[...]) + bias_ref[...]
         upper[...] = before
         active[...] = (before * logistic(before)).astype(BF)
-        result = dot_nn(active[...], w_out[...])
-        for index, ref in enumerate(outs):
-            ref[...] = result[index * rows : (index + 1) * rows].astype(ref.dtype)
+        result[...] = dot_nn(active[...], w_out[...]).astype(BF)
 
     outs = [
-        shape_of(total, model, BF),
         shape_of(total, inner, F32),
         shape_of(total, inner, BF),
-        shape_of(rows, model, F32),
-    ] + [shape_of(rows, model, BF)] * (count - 1)
+        shape_of(total, model, BF),
+    ] + [shape_of(total, model, BF)] * normed
     results = kernel_call(
         kernel,
         "feed_forward",
         outs,
-        (spot, *pieces, *packs, bias, wide),
+        (place.spot, blocks, *packs, bias, wide),
         scalars=1,
         scratch=[pltpu.VMEM((model, inner), BF), pltpu.VMEM((inner, model), BF)],
         flops=4 * total * model * inner,
         waits=waits,
     )
-    return square_reduce(results[3:], masks), results[:3]
-
-
-def feed_back(pieces, packs, spot, saved, masks, place, waits=()):
+    upper, active, result = results[:3]
+    hidden = results[3] if normed else blocks
+    return square_exchange(result, masks, place), (hidden, upper, active)
+
+
+def feed_back(branch, packs, grad_spot, saved, place, waits=()):
     hidden, upper, active = saved
-    rows, model = pieces[0].shape
     total, inner = upper.shape
-    count = len(pieces)
+    model = branch.shape[1]
     unit, half = place.unit, place.half
 
     def kernel(spot_ref, *refs):
-        piece_refs, pack_refs = refs[:count], refs[count : count + len(packs)]
-        upper_ref, branch, slope, sums = refs[count + len(packs) :][:4]
-        outs = refs[count + len(packs) + 4 : -2]
-        w_in, w_out = refs[-2:]
+        branch_ref, pack_refs = refs[0], refs[1 : 1 + len(packs)]
+        upper_ref, slope, sums, result, w_in, w_out = refs[1 + len(packs) :]
         place_feed(spot_ref, pack_views(pack_refs, place), w_in, w_out, unit, half)
-        for index, ref in enumerate(piece_refs):
-            branch[index * rows : (index + 1) * rows, :] = ref[...]
-        grad = dot_nt(branch[...], w_out[...]) * silu_slope(upper_ref[...])
+        grad = dot_nt(branch_ref[...], w_out[...]) * silu_slope(upper_ref[...])
         slope[...] = grad.astype(BF)
         sums[...] = column_sum(slope[...])
-        result = dot_nt(slope[...], w_in[...])
-        for index, ref in enumerate(outs):
-            ref[...] = result[index * rows : (index + 1) * rows].astype(ref.dtype)
+        result[...] = dot_nt(slope[...], w_in[...]).astype(BF)
 
     outs = [
-        shape_of(total, model, BF),
         shape_of(total, inner, BF),
         shape_of(1, inner, F32),
-        shape_of(rows, model, F32),
-    ] + [shape_of(rows, model, BF)] * (count - 1)
-    results = kernel_call(
+        shape_of(total, model, BF),
+    ]
+    slope, sums, result = kernel_call(
         kernel,
         "feed_backward",
         outs,
-        (spot, *pieces, *packs, upper),
+        (place.spot, branch, *packs, upper),
         scalars=1,
         scratch=[pltpu.VMEM((model, inner), BF), pltpu.VMEM((inner, model), BF)],
         flops=4 * total * model * inner,
         waits=waits,
     )
-    branch, slope, sums = results[:3]
-    parts = square_reduce(results[3:], masks)
     planes, size = place.planes, place.pack_rows
 
     def weights(spot_ref, hidden_ref, active_ref, branch_ref, slope_ref, kept, sent, w_in, w_out):
@@ -256,23 +265,55 @@
         weights,
         "feed_weights",
         [shape_of(planes * size, inner, BF)] * 2,
-        (spot, hidden, active, branch, slope),
+        (grad_spot, hidden, active, branch, slope),
         scalars=1,
         scratch=[pltpu.VMEM((model, inner), F32), pltpu.VMEM((inner, model), F32)],
         flops=4 * total * model * inner,
     )
-    return parts, kept, flipped(sent, 1), sums
-
-
-def feed_pack(weight_in, weight_out, place):
-    rows, hidden = weight_in.shape
-    half = weight_out.shape[0] // 2
-    columns = weight_in.reshape(rows, place.planes, 2, 2, 2, half)
-    columns = lax.dynamic_index_in_dim(columns, place.rep, 4, keepdims=False)
-    own = lax.dynamic_index_in_dim(columns, place.second, 2, keepdims=False)
-    other = lax.dynamic_index_in_dim(columns, 1 - place.second, 2, keepdims=False)
-    own, other = (item.reshape(rows, 2 * place.planes * half) for item in (own, other))
-    part_out = lax.dynamic_slice_in_dim(weight_out, place.rep * half, half, 0)
+    return result, kept, flipped(sent, 1), sums
+
+
+def feed_pack(ff_in, ff_out, module, place):
+    rows, hidden = ff_in.shape[2:]
+    width, model = ff_out.shape[2:]
+    half = width // 2
+    count = 2 * place.planes * half
+    if half % LANES:
+        columns = ff_in[0, module].reshape(rows, place.planes, 2, 2, 2, half)
+        columns = lax.dynamic_index_in_dim(columns, place.rep, 4, keepdims=False)
+        own = lax.dynamic_index_in_dim(columns, place.second, 2, keepdims=False)
+        other = lax.dynamic_index_in_dim(columns, 1 - place.second, 2, keepdims=False)
+        own, other = (item.reshape(rows, count) for item in (own, other))
+        part_out = lax.dynamic_slice_in_dim(ff_out[0, module], place.rep * half, half, 0)
+        return own, flipped(other, 2), part_out
+
+    def kernel(spot, in_ref, out_ref, own, other, part_out):
+        second, rep = spot[1], spot[3]
+        for turn, ref in enumerate((own, other)):
+            for index in range(2 * place.planes):
+                plane, core = index // 2, index % 2
+                start = (((plane * 2 + (second ^ turn)) * 2 + core) * 2 + rep) * half
+                source = pl.ds(pl.multiple_of(start, half), half)
+                ref[:, index * half : (index + 1) * half] = in_ref[0, 0, :, source]
+        part_out[...] = out_ref[0, 0, pl.ds(pl.multiple_of(rep * half, half), half), :]
+
+    own, other, part_out = pl.pallas_call(
+        kernel,
+        grid=(1,),
+        in_specs=[
+            pl.BlockSpec(memory_space=pltpu.SMEM),
+            pl.BlockSpec((1, 1, rows, hidden), lambda step: (0, module, 0, 0)),
+            pl.BlockSpec((1, 1, width, model), lambda step: (0, module, 0, 0)),
+        ],
+        out_specs=vmem(3),
+        out_shape=[
+            shape_of(rows, count, BF),
+            shape_of(rows, count, BF),
+            shape_of(half, model, BF),
+        ],
+        compiler_params=pltpu.CompilerParams(vmem_limit_bytes=24 * MIB),
+        name="feed_columns",
+    )(place.spot, ff_in, ff_out)
     return own, flipped(other, 2), part_out
 
 
@@ -310,12 +351,15 @@
     outs += [shape_of(size, kept.shape[1], BF)] * (planes - 1)
     pieces = fused(total, "feed_core_sum", outs, kept, swapped)
     pieces = {step: [piece] for step, piece in enumerate(pieces)}
+    early = pieces[0][0]
     for bit in plane_bits(place):
         for step in [step for step in sorted(pieces) if step >> bit & 1]:
             values = pieces.pop(step)
-            value = values[0] if len(values) == 1 else plane_add(values)
+            value = values[0]
+            if len(values) > 1:
+                value = early = plane_add(values)
             pieces[step ^ 1 << bit].append(flipped(value, QUAD << bit))
-    return plane_add(pieces[0])
+    return plane_add(pieces[0]), early
 
 
 def plane_add(values):
@@ -353,41 +397,38 @@
     return scores + bias[:, rows : rows + length]
 
 
-def place_rows(source, columns, target, position, rows):
+def place_rows(source, columns, target, core, rows):
     for step in range(SPAN):
-        spot = pl.ds(pl.multiple_of((position ^ step) * rows, rows), rows)
+        spot = pl.ds(pl.multiple_of(block_place(step, core) * rows, rows), rows)
         target[spot, :] = source[step * rows : (step + 1) * rows, columns]
 
 
-def split_rows(value, kept, sent, rows):
-    for index, step in enumerate((0, 4, 2, 6)):
-        target = slice(index * rows, (index + 1) * rows)
-        kept[target, :] = value[step * rows : (step + 1) * rows]
-        sent[target, :] = value[(step + 1) * rows : (step + 2) * rows].astype(BF)
-
-
-def join_pieces(refs, target, rows):
-    for step, ref in enumerate(refs):
-        target[step * rows : (step + 1) * rows, :] = ref[...]
+def block_place(step, core):
+    return step % 4 * 2 + (core ^ step // 4)
+
+
+def block_step(place, core):
+    return place // 2 + 4 * ((place & 1) ^ core)
 
 
 def attend_kernel(*refs):
-    spot, pieces, rest = refs[0], refs[1 : 1 + SPAN], refs[1 + SPAN :]
+    spot, near, other, rest = refs[0], refs[1], refs[2], refs[3:]
     (weight_in, bias_in, weight_out, table, hidden, mixed, context, peaks, kept, sent) = rest[:10]
     keys, values, bias = rest[10:]
     length, width = context.shape
     rows = length // SPAN
     head = table.shape[1] // 2
-    position = spot[0]
-    join_pieces(pieces, hidden, rows)
+    core = spot[2]
+    hidden[: length // 2, :] = near[...]
+    hidden[length // 2 :, :] = other[...]
     mixed[...] = (dot_nn(hidden[...], weight_in[...]) + bias_in[...]).astype(BF)
-    place_rows(mixed, slice(width, 2 * width), keys, position, rows)
-    place_rows(mixed, slice(2 * width, 3 * width), values, position, rows)
+    place_rows(mixed, slice(width, 2 * width), keys, core, rows)
+    place_rows(mixed, slice(2 * width, 3 * width), values, core, rows)
     lane = lax.broadcasted_iota(jnp.int32, (rows, width), 1)
 
     def block(index, carry):
         place = pl.multiple_of(index * rows, rows)
-        own = pl.ds(pl.multiple_of((position ^ index) * rows, rows), rows)
+        own = pl.ds(pl.multiple_of(block_step(index, core) * rows, rows), rows)
         query = mixed[own, :width] * jnp.asarray(head**-0.5, BF)
         results, logs = [], []
         for which in range(2):
@@ -405,22 +446,25 @@
         return carry
 
     lax.fori_loop(0, SPAN, block, 0)
-    split_rows(dot_nn(context[...], weight_out[...]), kept, sent, rows)
+    result = dot_nn(context[...], weight_out[...])
+    kept[...] = result[: length // 2]
+    sent[...] = result[length // 2 :].astype(BF)
 
 
 def attend_back_kernel(*refs):
-    spot, pieces, rest = refs[0], refs[1 : 1 + SPAN], refs[1 + SPAN :]
+    spot, near, other, rest = refs[0], refs[1], refs[2], refs[3:]
     (mixed, table, peaks, weight_in, weight_out) = rest[:5]
     (branch, grad_mixed, grad_table, far, kept, sent) = rest[5:11]
     keys, values, bias, grad_context, grad_keys, grad_values, slopes = rest[11:]
     length, width = grad_context.shape
     rows = length // SPAN
     head = table.shape[1] // 2
-    position = spot[0]
-    join_pieces(pieces, branch, rows)
+    core = spot[2]
+    branch[: length // 2, :] = near[...]
+    branch[length // 2 :, :] = other[...]
     grad_context[...] = dot_nt(branch[...], weight_out[...]).astype(BF)
-    place_rows(mixed, slice(width, 2 * width), keys, position, rows)
-    place_rows(mixed, slice(2 * width, 3 * width), values, position, rows)
+    place_rows(mixed, slice(width, 2 * width), keys, core, rows)
+    place_rows(mixed, slice(2 * width, 3 * width), values, core, rows)
     grad_keys[...] = jnp.zeros_like(grad_keys)
     grad_values[...] = jnp.zeros_like(grad_values)
     grad_table[...] = jnp.zeros_like(grad_table)
@@ -438,7 +482,7 @@
 
     def block(index, carry):
         place = pl.multiple_of(index * rows, rows)
-        own = pl.ds(pl.multiple_of((position ^ index) * rows, rows), rows)
+        own = pl.ds(pl.multiple_of(block_step(index, core) * rows, rows), rows)
         query = mixed[own, :width] * jnp.asarray(factor, BF)
         results = []
         for which in range(2):
@@ -490,38 +534,30 @@
 
     lax.fori_loop(0, SPAN, block, 0)
     for step in range(SPAN):
-        source = pl.ds(pl.multiple_of((position ^ step) * rows, rows), rows)
+        source = pl.ds(pl.multiple_of(block_place(step, core) * rows, rows), rows)
         target = slice(step * rows, (step + 1) * rows)
         grad_mixed[target, width : 2 * width] = grad_keys[source, :].astype(BF)
         grad_mixed[target, 2 * width :] = grad_values[source, :].astype(BF)
-    split_rows(dot_nt(grad_mixed[...], weight_in[...]), kept, sent, rows)
-
-
-def group_gather(value, masks):
-    near = square_gather(value, masks)
-    return near, [flipped(item, 1) for item in near]
-
-
-def group_reduce(kept, sent, masks):
-    swapped = flipped(sent, 1)
-    rows = kept.shape[0] // 4
-
+    result = dot_nt(grad_mixed[...], weight_in[...])
+    kept[...] = result[: length // 2]
+    sent[...] = result[length // 2 :].astype(BF)
+
+
+def group_gather(blocks, masks, place):
+    near = square_exchange(blocks, masks, place)
+    return near, flipped(near, 1)
+
+
+def group_reduce(kept, sent, masks, place):
     def body(kept_part, swapped_part):
-        total = kept_part + swapped_part.astype(F32)
-        return [total[index * rows : (index + 1) * rows] for index in range(4)]
-
-    outs = [shape_of(rows, kept.shape[1], dtype) for dtype in (F32, BF, BF, BF)]
-    return square_reduce(fused(body, "core_sum", outs, kept, swapped), masks)
-
-
-def in_steps(blocks):
-    near, far = blocks
-    return [near[0], far[0], near[2], far[2], near[1], far[1], near[3], far[3]]
+        return (kept_part + swapped_part.astype(F32),)
+
+    total = fused(body, "core_sum", [shape_of(*sent.shape, BF)], kept, flipped(sent, 1))[0]
+    return square_exchange(total, masks, place)
 
 
 def attend(blocks, weight_in, bias_in, weight_out, table, place):
-    pieces = in_steps(blocks)
-    rows, model = pieces[0].shape
+    rows, model = blocks[0].shape[0] // 4, blocks[0].shape[1]
     length, width = SPAN * rows, weight_out.shape[0]
     outs = [
         shape_of(length, model, BF),
@@ -535,7 +571,7 @@
         attend_kernel,
         "attend_forward",
         outs,
-        (place.span_spot, *pieces, weight_in, bias_in, weight_out, table),
+        (place.spot, *blocks, weight_in, bias_in, weight_out, table),
         scalars=1,
         scratch=[
             pltpu.VMEM((length, width), BF),
@@ -544,13 +580,12 @@
         ],
         flops=48 * length * length * width,
     )
-    return group_reduce(kept, sent, place.span_masks), (hidden, mixed, context, peaks)
+    return group_reduce(kept, sent, place.span_masks, place), (hidden, mixed, context, peaks)
 
 
 def attend_back(blocks, saved, weight_in, weight_out, table, place, waits):
     hidden, mixed, context, peaks = saved
-    pieces = in_steps(blocks)
-    rows, model = pieces[0].shape
+    rows, model = blocks[0].shape[0] // 4, blocks[0].shape[1]
     length, width = SPAN * rows, weight_out.shape[0]
     outs = [
         shape_of(length, model, BF),
@@ -564,7 +599,7 @@
         attend_back_kernel,
         "attend_backward",
         outs,
-        (place.span_spot, *pieces, mixed, table, peaks, weight_in, weight_out),
+        (place.spot, *blocks, mixed, table, peaks, weight_in, weight_out),
         scalars=1,
         scratch=[
             pltpu.VMEM((length, width), BF),
@@ -578,7 +613,7 @@
         flops=96 * length * length * width,
         waits=waits,
     )
-    parts = group_reduce(kept, sent, place.span_masks)
+    parts = group_reduce(kept, sent, place.span_masks, place)
 
     def weights(hidden_rows, mixed_grad, context_rows, branch_rows):
         return (
@@ -635,7 +670,8 @@
         mine = lax.dynamic_slice_in_dim(whole, place.member * per_device, per_device, 2)
         out = lax.all_gather(weight_out, "shard", axis=0, tiled=True)
         out = lax.dynamic_slice_in_dim(out, place.member * width, width, 0)
-        return mine.reshape(model, 3 * width), out
+        both = mine.reshape(model, 3 * width), out
+        return (), lambda: (both, both)
     planes, unit = place.planes, place.unit
     groups, columns = planes // 2, 3 * width
     blocks = weight_in.reshape(rows, 3, groups, 2, 2, 2, -1)
@@ -661,6 +697,16 @@
         scalars=1,
         waits=waits,
     )
+
+    def finish():
+        return attend_weights_finish(near, far, weight_out, place)
+
+    return (near, far), finish
+
+
+def attend_weights_finish(near, far, weight_out, place):
+    planes, unit, columns = place.planes, place.unit, near.shape[1]
+    groups, width, model = planes // 2, columns // 3, weight_out.shape[1]
     pieces = [near] + [
         flipped((near, far)[step & 1], QUAD * step) for step in range(1, planes)
     ]
@@ -689,13 +735,14 @@
             row = ((plane >> 1) ^ step) * unit
             w_out[pl.ds(pl.multiple_of(row, unit), unit), :] = ref[...]
 
-    return kernel_call(
+    laid = kernel_call(
         lay,
         "attend_lay",
         [shape_of(model, columns, BF), shape_of(width, model, BF)],
         (place.spot, kept, swapped, *outs),
         scalars=1,
     )
+    return laid, (kept, sent, *outs)
 
 
 def head_row(row, place, aligned):
@@ -803,9 +850,6 @@
     return low.astype(F32) + flipped(low, place.shards).astype(F32)
 
 
-LANES = 128
-
-
 def row(wide, index):
     return wide[index : index + 1]
 
@@ -818,12 +862,12 @@
     return fused(body, "pack_columns", [out], left, right, waits=waits)[0]
 
 
-def convolve_start(parts, before, wide, bias_row, weight_in):
+def convolve_start(parts, before, wide, bias_row, weight_in, waits):
     rows, model = before.shape
 
     def body(*values):
-        base, small, w_in = values[4:]
-        current = base + joined(values[:4]) + row(small, bias_row)
+        base, small, w_in = values[1:]
+        current = base + joined(values[0]) + row(small, bias_row)
         unit, unused_scale = standard(current)
         hidden = (unit * row(small, 7) + row(small, 8)).astype(BF)
         doubled = dot_nn(hidden, w_in)
@@ -838,11 +882,12 @@
             shape_of(rows, 2 * model, F32),
             shape_of(rows, model, BF),
         ],
-        *parts,
+        parts,
         before,
         wide,
         weight_in,
         flops=4 * rows * model * model,
+        waits=waits,
     )
 
 
@@ -872,12 +917,17 @@
         current = base[...] + dot_nn(rest, w_out[...])
         current_ref[...] = current
         unit, unused_scale = standard(current)
-        hidden_ref[...] = (unit * small[11:12, :] + small[12:13, :]).astype(BF)
+        hidden_ref[...] = repeated((unit * small[11:12, :] + small[12:13, :]).astype(BF))
 
     return kernel_call(
         kernel,
         "convolve_finish",
-        [shape_of(rows, model, dtype) for dtype in (F32, BF, F32, BF)],
+        [
+            shape_of(rows, model, F32),
+            shape_of(rows, model, BF),
+            shape_of(rows, model, F32),
+            shape_of(4 * rows, model, BF),
+        ],
         (glued, border, wide, weight_out, before),
         scratch=[pltpu.VMEM((edge + rows, model), F32)],
         flops=2 * rows * model * model,
@@ -890,11 +940,11 @@
     first, count = taps
 
     def kernel(
-        own, part_one, part_two, part_three, grad_ref, after_ref, mixed_ref, small,
+        parts_ref, grad_ref, after_ref, mixed_ref, small,
         w_out, glued_ref, border_ref,
         grad_out, branch_ref, main_ref, halo_ref, sums, padded, spread,
     ):
-        incoming = joined((own[...], part_one[...], part_two[...], part_three[...]))
+        incoming = joined(parts_ref[...])
         slope, sum_gain, sum_shift = norm_back(after_ref[...], small[11:12, :], incoming)
         current = grad_ref[...] + slope
         grad_out[...] = current
@@ -940,7 +990,7 @@
             shape_of(edge, model, BF),
             shape_of(count + 4, model, F32),
         ],
-        (*parts, grad, after, mixed, wide, weight_out, glued, border),
+        (parts, grad, after, mixed, wide, weight_out, glued, border),
         scratch=[
             pltpu.VMEM((edge + rows, model), F32),
             pltpu.VMEM((rows + 2 * edge, model), F32),
@@ -967,14 +1017,14 @@
         current = grad_rows + inner
         branch = current.astype(BF)
         sums = jnp.concatenate([sum_gain, sum_shift, column_sum(branch)], axis=0)
-        return current, branch, slope, sums
+        return current, repeated(branch), slope, sums
 
     return fused(
         body,
         "convolve_back_finish",
         [
             shape_of(rows, model, F32),
-            shape_of(rows, model, BF),
+            shape_of(4 * rows, model, BF),
             shape_of(rows, 2 * model, BF),
             shape_of(3, model, F32),
         ],
@@ -1015,49 +1065,50 @@
     rows, model = before.shape
 
     def body(*values):
-        base, small = values[4:]
-        current = base.astype(F32) + 0.5 * (joined(values[:4]) + row(small, 2))
+        base, small = values[1:]
+        current = base.astype(F32) + 0.5 * (joined(values[0]) + row(small, 2))
         unit, unused_scale = standard(current)
-        return current, unit * row(small, 3) + row(small, 4)
-
-    outs = [shape_of(rows, model, F32), shape_of(rows, model, BF)]
-    return fused(body, "feed_to_attend", outs, *parts, before, wide, waits=waits)
+        hidden = (unit * row(small, 3) + row(small, 4)).astype(BF)
+        return current, repeated(hidden)
+
+    outs = [shape_of(rows, model, F32), shape_of(4 * rows, model, BF)]
+    return fused(body, "feed_to_attend", outs, parts, before, wide, waits=waits)
 
 
 def turn_around(parts, before, wide, cotangent):
     rows, model = before.shape
 
     def body(*values):
-        base, small, grad = values[4:]
-        current = base + 0.5 * (joined(values[:4]) + row(small, 13))
+        base, small, grad = values[1:]
+        current = base + 0.5 * (joined(values[0]) + row(small, 13))
         unit, unused_scale = standard(current)
         slope, sum_gain, sum_shift = norm_back(current, row(small, 14), grad.astype(F32))
         branch = (0.5 * slope).astype(BF)
         sums = jnp.concatenate([column_sum(branch), sum_gain, sum_shift], axis=0)
-        return unit * row(small, 14) + row(small, 15), slope, branch, sums
+        return unit * row(small, 14) + row(small, 15), slope, repeated(branch), sums
 
     outs = [
         shape_of(rows, model, BF),
         shape_of(rows, model, F32),
-        shape_of(rows, model, BF),
+        shape_of(4 * rows, model, BF),
         shape_of(3, model, F32),
     ]
-    return fused(body, "turn_around", outs, *parts, before, wide, cotangent)
+    return fused(body, "turn_around", outs, parts, before, wide, cotangent)
 
 
 def attend_to_feed_back(parts, grad, before, wide):
     rows, model = before.shape
 
     def body(*values):
-        grad_rows, base, small = values[4:]
-        slope, sum_gain, sum_shift = norm_back(base, row(small, 3), joined(values[:4]))
+        grad_rows, base, small = values[1:]
+        slope, sum_gain, sum_shift = norm_back(base, row(small, 3), joined(values[0]))
         current = grad_rows + slope
         branch = (0.5 * current).astype(BF)
         sums = jnp.concatenate([column_sum(branch), sum_gain, sum_shift], axis=0)
-        return current, branch, sums
-
-    outs = [shape_of(rows, model, F32), shape_of(rows, model, BF), shape_of(3, model, F32)]
-    return fused(body, "attend_to_feed_back", outs, *parts, grad, before, wide)
+        return current, repeated(branch), sums
+
+    outs = [shape_of(rows, model, F32), shape_of(4 * rows, model, BF), shape_of(3, model, F32)]
+    return fused(body, "attend_to_feed_back", outs, parts, grad, before, wide)
 
 
 def last_step(parts, grad, before, wide):
@@ -1066,7 +1117,7 @@
     def body(*values):
         grad_rows, base, small = values[4:]
         slope, sum_gain, sum_shift = norm_back(
-            base.astype(F32), row(small, 0), joined(values[:4])
+            base.astype(F32), row(small, 0), sum(part.astype(F32) for part in values[:4])
         )
         return grad_rows + slope, jnp.concatenate([sum_gain, sum_shift], axis=0)
 
@@ -1075,14 +1126,8 @@
 
 
 def shard_gather(value, place):
-    gathered = value[None]
-    for bit in range(place.shards.bit_length() - 1):
-        arrived = flipped(gathered, 1 << bit)
-        low = jnp.bitwise_and(jnp.right_shift(place.shard, bit), 1) == 0
-        gathered = jnp.concatenate(
-            [jnp.where(low, gathered, arrived), jnp.where(low, arrived, gathered)], axis=0
-        )
-    return gathered
+    copies = jnp.broadcast_to(value[None], (place.shards, *value.shape))
+    return lax.all_to_all(copies, "shard", 0, 0, tiled=True)
 
 
 def shard_reduce(value, place):
@@ -1119,9 +1164,8 @@
         self.second = self.shard // 2 % 2
         self.plane = self.shard // QUAD
         self.member = self.shard % SPAN
-        self.spot = jnp.stack([self.plane, self.second, self.core])
-        self.flat_spot = jnp.stack([jnp.zeros_like(self.plane), self.second, self.core])
-        self.span_spot = self.member.reshape(1)
+        self.spot = jnp.stack([self.plane, self.second, self.core, self.rep])
+        self.flat_spot = jnp.stack([jnp.zeros_like(self.plane), self.second, self.core, self.rep])
         self.feed_masks = (self.shards, 2)
         self.span_masks = (4, 2)
 
@@ -1161,9 +1205,9 @@
     small = jnp.concatenate(
         [vectors[0], attn_bias, depthwise[0], ff_bias[0].reshape(2 * bias_rows, unit)], axis=0
     )
-    first_pack = pack_rows(feed_pack(ff_in[0, 0], ff_out[0, 0], place))
+    first_pack = pack_rows(feed_pack(ff_in, ff_out, 0, place))
     first_packs = plane_gather(first_pack, place)
-    pieces = square_gather(inputs, place.feed_masks)
+    blocks = square_exchange(repeated(inputs), place.feed_masks, place)
     small = shard_gather(small, place)
     wide = small[:, : count + 1 + tap_count].transpose(1, 0, 2).reshape(-1, model).astype(F32)
     feed_bias = small[:, count + 1 + tap_count :].reshape(place.planes, 2, 2, 2, 2, half)
@@ -1181,45 +1225,46 @@
     )
 
     arrived = first_packs[: place.planes]
-    mix_in, mix_out = attend_weights(attn_in[0], attn_out[0], head, place, arrived)
+    columns, finish_mix = attend_weights(attn_in[0], attn_out[0], head, place, arrived)
     glue = pack_columns(conv_in[0], conv_out[0], arrived)
     glue = lax.all_gather(glue, "shard", axis=0, tiled=True)
-    second_pack = feed_pack(ff_in[0, 1], ff_out[0, 1], place)
+    second_parts = feed_pack(ff_in, ff_out, 1, place)
 
     parts, saved_first = feed(
-        pieces, first_packs, place.spot, feed_bias[0], wide, 0, place.feed_masks, place
-    )
-    second_near = lax.all_gather(
-        pack_rows(second_pack, waits=saved_first[:1]),
-        "shard",
-        axis=0,
-        tiled=True,
-        axis_index_groups=plane_groups(place),
-    )
-    second_packs = [second_near, flipped(second_near, 1)]
-    after_first, hidden = feed_to_attend(parts, inputs, wide, (mix_in,))
-    parts, saved_attend = attend(
-        group_gather(hidden, place.span_masks), mix_in, mix_bias, mix_out, table, place
-    )
+        blocks,
+        first_packs,
+        feed_bias[0],
+        wide,
+        0,
+        place.feed_masks,
+        place,
+        (*columns, second_parts[1], table, mix_bias),
+    )
+    (mix_in, mix_out), ready = finish_mix()
+    after_first, hidden = feed_to_attend(parts, inputs, wide, ready)
+    second_packs = plane_gather(pack_rows(second_parts, waits=(after_first,)), place)
+    blocks = group_gather(hidden, place.span_masks, place)
+    parts, saved_attend = attend(blocks, mix_in, mix_bias, mix_out, table, place)
     glue_in, glue_out = glue[:, : 2 * model], glue[:, 2 * model :]
     after_attend, conv_hidden, doubled, glued = convolve_start(
-        parts, after_first, wide, count, glue_in
+        parts, after_first, wide, count, glue_in, second_packs[: place.planes]
     )
     border = along(glued[rows - edge :], 1, place)
     border = jnp.where(place.member == 0, jnp.zeros_like(border), border)
     mixed, rest, after_conv, hidden = convolve_finish(
         glued, border, wide, taps, glue_out, after_attend
     )
-    pieces = square_gather(hidden, place.feed_masks)
+    blocks = square_exchange(hidden, place.feed_masks, place)
     parts, saved_second = feed(
-        pieces, second_packs, place.flat_spot, feed_bias[1], wide, None, place.feed_masks, place
+        blocks, second_packs, feed_bias[1], wide, None, place.feed_masks, place
     )
     output, grad_last, branch, last_sums = turn_around(parts, after_conv, wide, cotangent)
 
-    pieces = square_gather(branch, place.feed_masks)
-    parts, kept, swapped, second_bias = feed_back(
-        pieces, second_packs, place.flat_spot, saved_second, place.feed_masks, place
-    )
+    branch = square_exchange(branch, place.feed_masks, place)
+    result, kept, swapped, second_bias = feed_back(
+        branch, second_packs, place.flat_spot, saved_second, place
+    )
+    parts = square_exchange(result, place.feed_masks, place)
     second_total = fused(
         lambda own, other: (own.astype(F32) + other.astype(F32),),
         "feed_core_total",
@@ -1244,14 +1289,21 @@
     )
     conv_grads = convolve_weight_grads(conv_hidden, slope, rest, conv_branch, place)
     parts, mix_grad_in, mix_grad_out, mix_sums, grad_distance = attend_back(
-        group_gather(branch, place.span_masks), saved_attend, mix_in, mix_out, table, place, ()
+        group_gather(branch, place.span_masks, place),
+        saved_attend,
+        mix_in,
+        mix_out,
+        table,
+        place,
+        (),
     )
     grad_first, branch, first_sums = attend_to_feed_back(parts, grad_attend, after_first, wide)
-    pieces = square_gather(branch, place.feed_masks)
-    parts, kept, swapped, first_bias = feed_back(
-        pieces, first_packs, place.spot, saved_first, place.feed_masks, place
-    )
-    first_sum = plane_reduce(kept, swapped, place)
+    branch = square_exchange(branch, place.feed_masks, place)
+    result, kept, swapped, first_bias = feed_back(
+        branch, first_packs, place.spot, saved_first, place
+    )
+    first_sum, first_step = plane_reduce(kept, swapped, place)
+    parts = square_spread(result, place.feed_masks, place)
     grad_input, input_sums = last_step(parts, grad_first, inputs, wide)
 
     second_grads = feed_grads(second_sum, place)
@@ -1280,7 +1332,7 @@
         (0, place.second, 0, 0, place.rep, 0),
     ).reshape(place.shards, 2 * bias_rows, unit)
     small_grads = shard_reduce(jnp.concatenate([wide_grads, bias_grads], axis=1), place)
-    delays = (grad_first, kept, first_sum)
+    delays = (grad_first, kept, first_step)
     grad_distance = sum_everywhere(grad_distance, place, delays)
     return (
         output,

time: 638 us -> 714 us (1.12)
  blocking collectives: 0 us -> 70.4 us
  local copies, waits for them, and re-layouts: 108 us -> 160 us
  waiting for transfers between devices: 252 us -> 205 us
  starting transfers between devices: 126 us -> 116 us
  other arithmetic: 20.4 us -> 28 us
    all_to_all x0 -> x4, blocking collectives: none -> 70.4 us  [square_exchange(): lax.all_to_all(blocks, ('rep', 'shard'), 0, 0, tiled=True, axis_index_gro...]
    ppermute x89 -> x52, waiting for transfers between devices: 242 us -> 177 us  [flipped(): lax.ppermute(value, ('rep', 'shard'), [(i, i ^ mask) for i in range(total)])]
    ppermute x89 -> x52, starting transfers between devices: 115 us -> 64.1 us  [flipped(): lax.ppermute(value, ('rep', 'shard'), [(i, i ^ mask) for i in range(total)])]
    unnamed x240 -> x334, local copies, waits for them, and re-layouts: 50.2 us -> 96.4 us
    all_to_all x0 -> x8, starting transfers between devices: none -> 34.7 us  [the longest x7 28.7 us: square_exchange(): lax.all_to_all(blocks, ('rep', 'shard'), 0, 0, tiled=True, axis_index_gro...]
    all_to_all x0 -> x8, waiting for transfers between devices: none -> 25.4 us  [the longest x7 21.6 us: square_exchange(): lax.all_to_all(blocks, ('rep', 'shard'), 0, 0, tiled=True, axis_index_gro...]
    all_gather x1, waiting for transfers between devices: 8.56 us -> 0.01 us  [shards(): glue = lax.all_gather(glue, 'shard', axis=0, tiled=True)]
    all_to_all x1, starting transfers between devices: 6.03 us -> 13.6 us  [shard_reduce(): both = lax.all_to_all(both, ('rep', 'shard'), 0, 0, tiled=True)]
  transfers between devices with their start and end apart: 96 -> 66, of which waited for: 44 -> 31; matrix products, arithmetic and copies ran while one was open for 13% -> 13% of each run, Pallas kernels for 14% -> 12%
where the time goes in v3:
time: 714 us; the launch traced here: 702 us
  waiting for transfers between devices  205 us (29%)
  local copies, waits for them, and re-layouts  160 us (22%)
  starting transfers between devices  116 us (16%)
  Pallas kernels  108 us (15%)
  blocking collectives  70.4 us (10%)
  other arithmetic  28 us (4%)
  between operations  15.8 us (2%)
    ppermute x52, waiting for transfers between devices, flipped(): lax.ppermute(value, ('rep', 'shard'), [(i, i ^ mask) for i in range(total)])  177 us
    pallas_call x38, Pallas kernels, kernel_call(): pl.pallas_call(kernel, in_specs=[pl.BlockSpec(memory_space=pltpu.SMEM)] *...  107 us
    unnamed x334, local copies, waits for them, and re-layouts  96.4 us
    all_to_all x4, blocking collectives, square_exchange(): lax.all_to_all(blocks, ('rep', 'shard'), 0, 0, tiled=True, axis_index_gro...  70.4 us
    ppermute x52, starting transfers between devices, flipped(): lax.ppermute(value, ('rep', 'shard'), [(i, i ^ mask) for i in range(total)])  64.1 us
    all_to_all x7, starting transfers between devices, square_exchange(): lax.all_to_all(blocks, ('rep', 'shard'), 0, 0, tiled=True, axis_index_gro...  28.7 us
    all_to_all x7, waiting for transfers between devices, square_exchange(): lax.all_to_all(blocks, ('rep', 'shard'), 0, 0, tiled=True, axis_index_gro...  21.6 us
  transfers between devices with their start and end apart: 66, of which 31 were waited for; matrix products, arithmetic and copies ran while one was open for 13% of the time, Pallas kernels for 12%

profile of v3, /device:TPU:0, one launch (start us, length us, event | category | flops | bytes accessed | tf_op | source)
XLA Modules:
  0.0 702.4 jit_solution(11791496295518694192)
XLA Ops:
  10.4 3.0 collective-permute-start
  13.5 3.5 collective-permute-done.refs_1_
  17.0 2.9 collective-permute-start.2
  21.5 21.0 %collective-permute-done.2.refs_5_.refs_4_ = bf16[256,1024]{1,0:T(8,128)(2,1)S(1)} collective-permute-done((bf16[256,1024]{1,0:T(8,128)(2,1)S(1)}, bf16[256,1024]{1,0:T(8,128)(2,1)S(1)}, u32[]{:S(2)}, u32[]{:S(2)}) %collective-permute-start.2) | collective-permute-done | bytes 524320 | tf_op jit(solution)/shard_map/ppermute | solution.py:98
  42.9 12.3 %collective-permute-done.3.refs_6_.refs_5_ = bf16[256,1024]{1,0:T(8,128)(2,1)S(1)} collective-permute-done((bf16[256,1024]{1,0:T(8,128)(2,1)S(1)}, bf16[256,1024]{1,0:T(8,128)(2,1)S(1)}, u32[]{:S(2)}, u32[]{:S(2)}) %collective-permute-start.3) | collective-permute-done | bytes 524320 | tf_op jit(solution)/shard_map/ppermute | solution.py:98
  59.8 2.8 copy.47
  67.9 6.0 all-to-all-start.1
  79.6 3.8 all-to-all-done.1
  83.4 3.5 all-to-all-start
  103.9 7.9 %collective-permute-done.9.refs_14_.refs_1_ = bf16[64,1024]{1,0:T(8,128)(2,1)} collective-permute-done((bf16[64,1024]{1,0:T(8,128)(2,1)}, bf16[64,1024]{1,0:T(8,128)(2,1)}, u32[]{:S(2)}, u32[]{:S(2)}) %collective-permute-start.9) | collective-permute-done | bytes 131104 | tf_op jit(solution)/shard_map/ppermute | solution.py:98
  114.6 4.7 feed_forward.2
  123.6 3.7 all-to-all-start.2
  128.7 3.0 collective-permute-start.12
  131.9 6.9 collective-permute-done.10.refs_1_
  138.9 9.6 %collective-permute-done.11.refs_2_ = bf16[256,384]{1,0:T(8,128)(2,1)S(1)} collective-permute-done((bf16[256,384]{1,0:T(8,128)(2,1)S(1)}, bf16[256,384]{1,0:T(8,128)(2,1)S(1)}, u32[]{:S(2)}, u32[]{:S(2)}) %collective-permute-start.11) | collective-permute-done | bytes 196640 | tf_op jit(solution)/shard_map/ppermute | solution.py:98
  149.3 4.5 collective-permute-done.13.refs_6_.refs_4_
  155.2 15.4 %all_to_all.131 = bf16[4,128,1024]{2,1,0:T(8,128)(2,1)S(1)} all-to-all(bf16[4,128,1024]{2,1,0:T(8,128)(2,1)S(1)} %bitcast.133), channel_id=1, replica_groups={{0,2,4,6},{1,3,5,7},{8,10,12,14},{9,11,13,15},{16,18,20,22},{17,19,21,2..., dimensions={0} | all-to-all | bytes 2097152 | tf_op jit(solution)/shard_map/all_to_all | solution.py:113
  171.1 2.7 collective-permute-done.15.refs_2_
  174.5 14.5 %attend_forward.1 = (bf16[1024,1024]{1,0:T(8,128)(2,1)S(1)}, bf16[1024,384]{1,0:T(8,128)(2,1)S(1)}, bf16[1024,128]{1,0:T(8,128)(2,1)S(1)}, f32[1024,128]{1,0:T(8...) custom-call(s32[4]{0:T(128)S(1)} %add_add_fusion.spot.refs_0_, bf16[512,1024]{1,0:T(8,128)(2,1)S(1)} %bitcast.129, ...), custom_call_target="tpu_custom_call" | custom-call | flops 6442450944 | bytes 10094080 | tf_op jit(solution)/shard_map/attend_forward/pallas_call | solution.py:73
  195.0 3.7 all-to-all-start.4
  204.0 18.4 %collective-permute-done.18.refs_6_.refs_4_ = bf16[256,1024]{1,0:T(8,128)(2,1)S(1)} collective-permute-done((bf16[256,1024]{1,0:T(8,128)(2,1)S(1)}, bf16[256,1024]{1,0:T(8,128)(2,1)S(1)}, u32[]{:S(2)}, u32[]{:S(2)}) %collective-permute-start.18) | collective-permute-done | bytes 524320 | tf_op jit(solution)/shard_map/ppermute | solution.py:98
  222.4 4.8 collective-permute-start.19
  227.2 4.9 slice.179.refs_3_
  232.1 4.1 collective-permute-done.17.refs_5_.refs_3_
  236.2 10.4 %collective-permute-done.19.refs_7_.refs_5_ = bf16[256,1024]{1,0:T(8,128)(2,1)} collective-permute-done((bf16[256,1024]{1,0:T(8,128)(2,1)S(1)}, bf16[256,1024]{1,0:T(8,128)(2,1)}, u32[]{:S(2)}, u32[]{:S(2)}) %collective-permute-start.19) | collective-permute-done | bytes 524320 | tf_op jit(solution)/shard_map/ppermute | solution.py:98
  256.9 3.4 convolve_finish.1
  263.7 6.4 all-to-all-start.5
  275.4 9.1 %all-to-all-done.5 = bf16[4,128,1024]{2,1,0:T(8,128)(2,1)} async-done(((bf16[4,128,1024]{2,1,0:T(8,128)(2,1)}), bf16[4,128,1024]{2,1,0:T(8,128)(2,1)}, u32[]{:S(2)}, u32[]{:S(2)}) %all-to-all-start.5) | async-done | bytes 1048608 | tf_op jit(solution)/shard_map/all_to_all | solution.py:113
  290.7 4.3 feed_forward.3
  297.4 17.1 %all_to_all.132 = bf16[4,128,1024]{2,1,0:T(8,128)(2,1)S(1)} all-to-all(bf16[4,128,1024]{2,1,0:T(8,128)(2,1)S(1)} %bitcast.132), channel_id=1, replica_groups={{0,2,16,18},{1,3,17,19},{4,6,20,22},{5,7,21,23},{8,10,24,26},{9,11,25,2..., dimensions={0} | all-to-all | bytes 2097152 | tf_op jit(solution)/shard_map/all_to_all | solution.py:113
  318.1 4.2 all-to-all-start.7
  322.4 12.3 %all-to-all-done.7 = bf16[4,128,1024]{2,1,0:T(8,128)(2,1)} async-done(((bf16[4,128,1024]{2,1,0:T(8,128)(2,1)}), bf16[4,128,1024]{2,1,0:T(8,128)(2,1)}, u32[]{:S(2)}, u32[]{:S(2)}) %all-to-all-start.7) | async-done | bytes 1048608 | tf_op jit(solution)/shard_map/all_to_all | solution.py:113
  342.6 4.7 feed_backward.2
  348.2 4.3 feed_weights.2
  352.7 4.1 collective-permute-done.25.refs_1_
  358.7 18.7 %all_to_all.133 = bf16[4,128,1024]{2,1,0:T(8,128)(2,1)S(1)} all-to-all(bf16[4,128,1024]{2,1,0:T(8,128)(2,1)} %bitcast.124), channel_id=1, replica_groups={{0,2,16,18},{1,3,17,19},{4,6,20,22},{5,7,21,23},{8,10,24,26},{9,11,25,2..., dimensions={0} | all-to-all | bytes 2097152 | tf_op jit(solution)/shard_map/all_to_all | solution.py:113
  377.5 8.2 %convolve_back_start.1 = (f32[128,1024]{1,0:T(8,128)S(1)}, bf16[128,1024]{1,0:T(8,128)(2,1)S(1)}, f32[128,1024]{1,0:T(8,128)S(1)}, bf16[32,1024]{1,0:T(8,128)(2,1)}, f32[35,1024]{1,0:T(8,128)S(1)}) custom-call(bf16[512,1024]{1,0:T(8,128)(2,1)S(1)} %bitcast.115, f32[128,1024]{1,0:T(8,128)S(1)} %copy-done.53, f32[128,1024]{1,0:T(8,128)S(1)} %copy-done.12, ...), custom_call_target="tpu_custom_call" | custom-call | flops 268435456 | bytes 6762496 | tf_op jit(solution)/shard_map/convolve_back_start/pallas_call | solution.py:73
  401.1 19.1 %all_to_all.134 = bf16[4,128,1024]{2,1,0:T(8,128)(2,1)S(1)} all-to-all(bf16[4,128,1024]{2,1,0:T(8,128)(2,1)S(1)} %bitcast.131), channel_id=1, replica_groups={{0,2,4,6},{1,3,5,7},{8,10,12,14},{9,11,13,15},{16,18,20,22},{17,19,21,2..., dimensions={0} | all-to-all | bytes 2097152 | tf_op jit(solution)/shard_map/all_to_all | solution.py:113
  424.2 2.6 copy-done.2
  433.4 24.7 %attend_backward.1 = (bf16[1024,1024]{1,0:T(8,128)(2,1)S(1)}, bf16[1024,384]{1,0:T(8,128)(2,1)S(1)}, f32[512,128]{1,0:T(8,128)S(1)}, f32[8,128]{1,0:T(8,128)S(1)...) custom-call(s32[4]{0:T(128)S(1)} %add_add_fusion.spot.refs_0_, bf16[512,1024]{1,0:T(8,128)(2,1)S(1)} %bitcast.127, ...), custom_call_target="tpu_custom_call" | custom-call | flops 12884901888 | bytes 10883072 | tf_op jit(solution)/shard_map/attend_backward/pallas_call | solution.py:73
  459.4 2.7 collective-permute-done.28.refs_1_
  463.3 3.6 all-to-all-start.10
  490.1 3.6 all-to-all-start.11
  511.1 9.8 %collective-permute-done.42.refs_2_ = bf16[128,768]{1,0:T(8,128)(2,1)} collective-permute-done((bf16[128,768]{1,0:T(8,128)(2,1)}, bf16[128,768]{1,0:T(8,128)(2,1)}, u32[]{:S(2)}, u32[]{:S(2)}) %collective-permute-start.42) | collective-permute-done | bytes 196640 | tf_op jit(solution)/shard_map/ppermute | solution.py:98
  525.5 3.2 collective-permute-start.45
  536.1 4.7 feed_backward.3
  543.1 4.5 feed_weights.3
  551.3 3.6 reshape.263
  554.9 3.9 reverse_select_fusion.2
  562.0 2.7 reverse_select_fusion.1
  575.8 3.8 broadcast_in_dim_reshape.3
  580.6 7.1 %collective-permute-done.30.refs_2_ = bf16[128,1024]{1,0:T(8,128)(2,1)} collective-permute-done((bf16[128,1024]{1,0:T(8,128)(2,1)}, bf16[128,1024]{1,0:T(8,128)(2,1)}, u32[]{:S(2)}, u32[]{:S(2)}) %collective-permute-start.30) | collective-permute-done | bytes 262176 | tf_op jit(solution)/shard_map/ppermute | solution.py:98
  587.7 5.5 collective-permute-done.31.refs_3_
  595.8 3.6 concatenate.101
  602.9 13.6 %all-to-all-start.12 = ((f32[32,1,3584]{2,1,0:T(1,128)}), f32[32,1,3584]{2,1,0:T(1,128)}, u32[]{:S(2)}, u32[]{:S(2)}) async-start(f32[32,1,3584]{2,1,0:T(1,128)} %reshape.308), calls=%async_computation.13 | async-start | bytes 917504 | tf_op jit(solution)/shard_map/all_to_all | solution.py:1135
  616.5 2.7 feed_core_sum.1
  626.0 12.2 %collective-permute-done.34.refs_1_ = bf16[256,1024]{1,0:T(8,128)(2,1)S(1)} collective-permute-done((bf16[256,1024]{1,0:T(8,128)(2,1)S(1)}, bf16[256,1024]{1,0:T(8,128)(2,1)S(1)}, u32[]{:S(2)}, u32[]{:S(2)}) %collective-permute-start.34) | collective-permute-done | bytes 524320 | tf_op jit(solution)/shard_map/ppermute | solution.py:98
  638.3 2.6 collective-permute-start.35
  644.1 3.5 reduce.20
  649.0 10.7 %collective-permute-done.51.refs_1_ = f32[73,64]{1,0:T(8,128)S(1)} collective-permute-done((f32[73,64]{1,0:T(8,128)S(1)}, f32[73,64]{1,0:T(8,128)S(1)}, u32[]{:S(2)}, u32[]{:S(2)}) %collective-permute-start.51) | collective-permute-done | bytes 18720 | tf_op jit(solution)/shard_map/ppermute | solution.py:98
  659.7 4.1 collective-permute-start.52
  671.8 2.8 collective-permute-done.36
  676.2 5.1 collective-permute-done.48
  682.9 7.3 %collective-permute-done.37 = bf16[256,1024]{1,0:T(8,128)(2,1)S(1)} collective-permute-done((bf16[256,1024]{1,0:T(8,128)(2,1)S(1)}, bf16[256,1024]{1,0:T(8,128)(2,1)S(1)}, u32[]{:S(2)}, u32[]{:S(2)}) %collective-permute-start.37) | collective-permute-done | bytes 524320 | tf_op jit(solution)/shard_map/ppermute | solution.py:98
  (564 shorter events, 238.4 us)
Async XLA Ops:
  7.2 220.1 %all-gather.2.cloned.1.call-start = ((), (), s32[]{:S(2)}) async-start(), calls=%async_computation.15 | async-start | bytes 6684672 | tf_op jit(solution)/shard_map/all_gather | solution.py:1230
  10.4 6.5 collective-permute-start
  17.0 25.4 %collective-permute-start.2 = (bf16[256,1024]{1,0:T(8,128)(2,1)S(1)}, bf16[256,1024]{1,0:T(8,128)(2,1)S(1)}, u32[]{:S(2)}, u32[]{:S(2)}) collective-permute-start(bf16[256,1024]{1,0:T(8,128)(2,1)S(1)} %pack_rows.2.refs_3_.refs_2_), channel_id=1, source_target_pairs={{0,8},{1,9},{2,10},{3,11},{4,12},{5,13},{6,14},{7,15},{8,0},{9,1},... | collective-permute-start | bytes 1572872 | tf_op jit(solution)/shard_map/ppermute | solution.py:98
  19.9 23.0 %collective-permute-start.1 = (bf16[256,1024]{1,0:T(8,128)(2,1)S(1)}, bf16[256,1024]{1,0:T(8,128)(2,1)S(1)}, u32[]{:S(2)}, u32[]{:S(2)}) collective-permute-start(bf16[256,1024]{1,0:T(8,128)(2,1)S(1)} %pack_rows.2.refs_3_.refs_2_), channel_id=1, source_target_pairs={{0,4},{1,5},{2,6},{3,7},{4,0},{5,1},{6,2},{7,3},{8,12},{9,13},{10,... | collective-permute-start | bytes 1572872 | tf_op jit(solution)/shard_map/ppermute | solution.py:98
  42.4 12.8 %collective-permute-start.3 = (bf16[256,1024]{1,0:T(8,128)(2,1)S(1)}, bf16[256,1024]{1,0:T(8,128)(2,1)S(1)}, u32[]{:S(2)}, u32[]{:S(2)}) collective-permute-start(bf16[256,1024]{1,0:T(8,128)(2,1)S(1)} %collective-permute-done.2.refs_5_.refs_4_), channel_id=1, source_target_pairs={{0,4},{1,5},{2,6},{3,7},{4,0},{5,1},{6,2},{7,3},{8,12},{9,13},{10,... | collective-permute-start | bytes 1572872 | tf_op jit(solution)/shard_map/ppermute | solution.py:98
  65.6 28.9 %collective-permute-start.8 = (bf16[256,384]{1,0:T(8,128)(2,1)}, bf16[256,384]{1,0:T(8,128)(2,1)}, u32[]{:S(2)}, u32[]{:S(2)}) collective-permute-start(bf16[256,384]{1,0:T(8,128)(2,1)} %bitcast.14), channel_id=1, source_target_pairs={{0,2},{1,3},{2,0},{3,1},{4,6},{5,7},{6,4},{7,5},{8,10},{9,11},{10,... | collective-permute-start | bytes 589832 | tf_op jit(solution)/shard_map/ppermute | solution.py:98
  67.9 15.5 %all-to-all-start.1 = ((bf16[16,2,1792]{2,1,0:T(2,128)(2,1)}), bf16[16,2,1792]{2,1,0:T(2,128)(2,1)}, u32[]{:S(2)}, u32[]{:S(2)}) async-start(bf16[16,2,1792]{2,1,0:T(2,128)(2,1)} %reshape.306), calls=%async_computation.1 | async-start | bytes 229376 | tf_op jit(solution)/shard_map/all_to_all | solution.py:1130
  79.2 32.5 %collective-permute-start.4 = (bf16[256,1024]{1,0:T(8,128)(2,1)S(1)}, bf16[256,1024]{1,0:T(8,128)(2,1)}, u32[]{:S(2)}, u32[]{:S(2)}) collective-permute-start(bf16[256,1024]{1,0:T(8,128)(2,1)S(1)} %pack_rows.2.refs_3_.refs_2_), channel_id=1, source_target_pairs={{0,1},{1,0},{2,3},{3,2},{4,5},{5,4},{6,7},{7,6},{8,9},{9,8},{10,11... | collective-permute-start | bytes 1572872 | tf_op jit(solution)/shard_map/ppermute | solution.py:98
  83.4 28.4 %all-to-all-start = ((bf16[4,128,1024]{2,1,0:T(8,128)(2,1)}), bf16[4,128,1024]{2,1,0:T(8,128)(2,1)S(1)}, u32[]{:S(2)}, u32[]{:S(2)}) async-start(bf16[4,128,1024]{2,1,0:T(8,128)(2,1)} %bitcast.146), calls=%async_computation | async-start | bytes 2097152 | tf_op jit(solution)/shard_map/all_to_all | solution.py:113
  93.3 18.5 %collective-permute-start.5 = (bf16[256,1024]{1,0:T(8,128)(2,1)S(1)}, bf16[256,1024]{1,0:T(8,128)(2,1)}, u32[]{:S(2)}, u32[]{:S(2)}) collective-permute-start(bf16[256,1024]{1,0:T(8,128)(2,1)S(1)} %copy-done.26), channel_id=1, source_target_pairs={{0,1},{1,0},{2,3},{3,2},{4,5},{5,4},{6,7},{7,6},{8,9},{9,8},{10,11... | collective-permute-start | bytes 1572872 | tf_op jit(solution)/shard_map/ppermute | solution.py:98
  93.4 18.4 %collective-permute-start.6 = (bf16[256,1024]{1,0:T(8,128)(2,1)S(1)}, bf16[256,1024]{1,0:T(8,128)(2,1)}, u32[]{:S(2)}, u32[]{:S(2)}) collective-permute-start(bf16[256,1024]{1,0:T(8,128)(2,1)S(1)} %copy-done.23), channel_id=1, source_target_pairs={{0,1},{1,0},{2,3},{3,2},{4,5},{5,4},{6,7},{7,6},{8,9},{9,8},{10,11... | collective-permute-start | bytes 1572872 | tf_op jit(solution)/shard_map/ppermute | solution.py:98
  93.9 17.9 %collective-permute-start.7 = (bf16[256,1024]{1,0:T(8,128)(2,1)S(1)}, bf16[256,1024]{1,0:T(8,128)(2,1)}, u32[]{:S(2)}, u32[]{:S(2)}) collective-permute-start(bf16[256,1024]{1,0:T(8,128)(2,1)S(1)} %copy-done.29), channel_id=1, source_target_pairs={{0,1},{1,0},{2,3},{3,2},{4,5},{5,4},{6,7},{7,6},{8,9},{9,8},{10,11... | collective-permute-start | bytes 1572872 | tf_op jit(solution)/shard_map/ppermute | solution.py:98
  94.6 17.2 %collective-permute-start.9 = (bf16[64,1024]{1,0:T(8,128)(2,1)}, bf16[64,1024]{1,0:T(8,128)(2,1)}, u32[]{:S(2)}, u32[]{:S(2)}) collective-permute-start(bf16[64,1024]{1,0:T(8,128)(2,1)} %copy-done.125), channel_id=1, source_target_pairs={{0,2},{1,3},{2,0},{3,1},{4,6},{5,7},{6,4},{7,5},{8,10},{9,11},{10,... | collective-permute-start | bytes 393224 | tf_op jit(solution)/shard_map/ppermute | solution.py:98
  123.6 30.2 %all-to-all-start.2 = ((bf16[4,128,1024]{2,1,0:T(8,128)(2,1)}), bf16[4,128,1024]{2,1,0:T(8,128)(2,1)S(1)}, u32[]{:S(2)}, u32[]{:S(2)}) async-start(bf16[4,128,1024]{2,1,0:T(8,128)(2,1)} %bitcast.123), calls=%async_computation.2 | async-start | bytes 2097152 | tf_op jit(solution)/shard_map/all_to_all | solution.py:113
  127.3 11.6 %collective-permute-start.10 = (bf16[256,384]{1,0:T(8,128)(2,1)S(1)}, bf16[256,384]{1,0:T(8,128)(2,1)S(1)}, u32[]{:S(2)}, u32[]{:S(2)}) collective-permute-start(bf16[256,384]{1,0:T(8,128)(2,1)S(1)} %copy-done.124), channel_id=1, source_target_pairs={{0,4},{1,5},{2,6},{3,7},{4,0},{5,1},{6,2},{7,3},{8,12},{9,13},{10,... | collective-permute-start | bytes 589832 | tf_op jit(solution)/shard_map/ppermute | solution.py:98
  128.5 20.0 %collective-permute-start.11 = (bf16[256,384]{1,0:T(8,128)(2,1)S(1)}, bf16[256,384]{1,0:T(8,128)(2,1)S(1)}, u32[]{:S(2)}, u32[]{:S(2)}) collective-permute-start(bf16[256,384]{1,0:T(8,128)(2,1)S(1)} %copy-done.87), channel_id=1, source_target_pairs={{0,8},{1,9},{2,10},{3,11},{4,12},{5,13},{6,14},{7,15},{8,0},{9,1},... | collective-permute-start | bytes 589832 | tf_op jit(solution)/shard_map/ppermute | solution.py:98
  128.7 19.8 %collective-permute-start.12 = (bf16[256,384]{1,0:T(8,128)(2,1)S(1)}, bf16[256,384]{1,0:T(8,128)(2,1)S(1)}, u32[]{:S(2)}, u32[]{:S(2)}) collective-permute-start(bf16[256,384]{1,0:T(8,128)(2,1)S(1)} %copy-done.124), channel_id=1, source_target_pairs={{0,12},{1,13},{2,14},{3,15},{4,8},{5,9},{6,10},{7,11},{8,4},{9,5},... | collective-permute-start | bytes 589832 | tf_op jit(solution)/shard_map/ppermute | solution.py:98
  131.7 22.1 %collective-permute-start.13 = (bf16[64,1024]{1,0:T(8,128)(2,1)S(1)}, bf16[64,1024]{1,0:T(8,128)(2,1)S(1)}, u32[]{:S(2)}, u32[]{:S(2)}) collective-permute-start(bf16[64,1024]{1,0:T(8,128)(2,1)S(1)} %bitcast.136), channel_id=1, source_target_pairs={{0,8},{1,9},{2,10},{3,11},{4,12},{5,13},{6,14},{7,15},{8,0},{9,1},... | collective-permute-start | bytes 393224 | tf_op jit(solution)/shard_map/ppermute | solution.py:98
  170.6 3.9 collective-permute-start.14
  170.6 3.2 collective-permute-start.15
  191.2 2.7 collective-permute-start.16
  195.0 51.7 %all-to-all-start.4 = ((bf16[4,128,1024]{2,1,0:T(8,128)(2,1)}), bf16[4,128,1024]{2,1,0:T(8,128)(2,1)S(1)}, u32[]{:S(2)}, u32[]{:S(2)}) async-start(bf16[4,128,1024]{2,1,0:T(8,128)(2,1)} %bitcast.25), calls=%async_computation.4 | async-start | bytes 2097152 | tf_op jit(solution)/shard_map/all_to_all | solution.py:113
  199.6 22.8 %collective-permute-start.18 = (bf16[256,1024]{1,0:T(8,128)(2,1)S(1)}, bf16[256,1024]{1,0:T(8,128)(2,1)S(1)}, u32[]{:S(2)}, u32[]{:S(2)}) collective-permute-start(bf16[256,1024]{1,0:T(8,128)(2,1)S(1)} %pack_rows.3.refs_4_.refs_2_), channel_id=1, source_target_pairs={{0,8},{1,9},{2,10},{3,11},{4,12},{5,13},{6,14},{7,15},{8,0},{9,1},... | collective-permute-start | bytes 1572872 | tf_op jit(solution)/shard_map/ppermute | solution.py:98
  202.1 34.2 %collective-permute-start.17 = (bf16[256,1024]{1,0:T(8,128)(2,1)S(1)}, bf16[256,1024]{1,0:T(8,128)(2,1)}, u32[]{:S(2)}, u32[]{:S(2)}) collective-permute-start(bf16[256,1024]{1,0:T(8,128)(2,1)S(1)} %pack_rows.3.refs_4_.refs_2_), channel_id=1, source_target_pairs={{0,4},{1,5},{2,6},{3,7},{4,0},{5,1},{6,2},{7,3},{8,12},{9,13},{10,... | collective-permute-start | bytes 1572872 | tf_op jit(solution)/shard_map/ppermute | solution.py:98
  222.4 24.2 %collective-permute-start.19 = (bf16[256,1024]{1,0:T(8,128)(2,1)S(1)}, bf16[256,1024]{1,0:T(8,128)(2,1)}, u32[]{:S(2)}, u32[]{:S(2)}) collective-permute-start(bf16[256,1024]{1,0:T(8,128)(2,1)S(1)} %collective-permute-done.18.refs_6_.refs_4_), channel_id=1, source_target_pairs={{0,4},{1,5},{2,6},{3,7},{4,0},{5,1},{6,2},{7,3},{8,12},{9,13},{10,... | collective-permute-start | bytes 1572872 | tf_op jit(solution)/shard_map/ppermute | solution.py:98
  253.1 3.7 collective-permute-start.20
  263.7 20.8 %all-to-all-start.5 = ((bf16[4,128,1024]{2,1,0:T(8,128)(2,1)}), bf16[4,128,1024]{2,1,0:T(8,128)(2,1)}, u32[]{:S(2)}, u32[]{:S(2)}) async-start(bf16[4,128,1024]{2,1,0:T(8,128)(2,1)} %bitcast.125), calls=%async_computation.5 | async-start | bytes 2097152 | tf_op jit(solution)/shard_map/all_to_all | solution.py:113
  270.5 3.2 collective-permute-start.23
  270.9 3.6 collective-permute-start.24
  318.1 16.7 %all-to-all-start.7 = ((bf16[4,128,1024]{2,1,0:T(8,128)(2,1)}), bf16[4,128,1024]{2,1,0:T(8,128)(2,1)}, u32[]{:S(2)}, u32[]{:S(2)}) async-start(bf16[4,128,1024]{2,1,0:T(8,128)(2,1)} %bitcast.130), calls=%async_computation.7 | async-start | bytes 2097152 | tf_op jit(solution)/shard_map/all_to_all | solution.py:113
  322.3 236.5 %reduce-scatter.3.cloned.1.call-start = ((), (), s32[]{:S(2)}) async-start(), calls=%async_computation.16 | async-start | bytes 2621440 | tf_op jit(solution)/shard_map/reduce_scatter | solution.py:1275
  352.6 4.2 collective-permute-start.25
  358.6 310.3 %reduce-scatter.5.cloned.1.call-start = ((), (), s32[]{:S(2)}) async-start(), calls=%async_computation.17 | async-start | bytes 6684672 | tf_op jit(solution)/shard_map/reduce_scatter | solution.py:1059
  388.7 3.3 collective-permute-start.26
  420.2 6.7 collective-permute-start.27
  459.4 2.7 collective-permute-start.28
  463.3 22.8 %all-to-all-start.10 = ((bf16[4,128,1024]{2,1,0:T(8,128)(2,1)}), bf16[4,128,1024]{2,1,0:T(8,128)(2,1)S(1)}, u32[]{:S(2)}, u32[]{:S(2)}) async-start(bf16[4,128,1024]{2,1,0:T(8,128)(2,1)} %bitcast.41), calls=%async_computation.10 | async-start | bytes 2097152 | tf_op jit(solution)/shard_map/all_to_all | solution.py:113
  483.8 10.6 %collective-permute-start.40 = (bf16[512,384]{1,0:T(8,128)(2,1)}, bf16[512,384]{1,0:T(8,128)(2,1)}, u32[]{:S(2)}, u32[]{:S(2)}) collective-permute-start(bf16[512,384]{1,0:T(8,128)(2,1)} %get-tuple-element.179), channel_id=1, source_target_pairs={{0,1},{1,0},{2,3},{3,2},{4,5},{5,4},{6,7},{7,6},{8,9},{9,8},{10,11... | collective-permute-start | bytes 1179656 | tf_op jit(solution)/shard_map/ppermute | solution.py:98
  484.0 25.1 %collective-permute-start.44 = (bf16[64,1024]{1,0:T(8,128)(2,1)}, bf16[64,1024]{1,0:T(8,128)(2,1)}, u32[]{:S(2)}, u32[]{:S(2)}) collective-permute-start(bf16[64,1024]{1,0:T(8,128)(2,1)} %get-tuple-element.185), channel_id=1, source_target_pairs={{0,8},{1,9},{2,10},{3,11},{4,12},{5,13},{6,14},{7,15},{8,0},{9,1},... | collective-permute-start | bytes 393224 | tf_op jit(solution)/shard_map/ppermute | solution.py:98
  490.1 44.0 %all-to-all-start.11 = ((bf16[4,128,1024]{2,1,0:T(8,128)(2,1)}), bf16[4,128,1024]{2,1,0:T(8,128)(2,1)S(1)}, u32[]{:S(2)}, u32[]{:S(2)}) async-start(bf16[4,128,1024]{2,1,0:T(8,128)(2,1)} %bitcast.121), calls=%async_computation.11 | async-start | bytes 2097152 | tf_op jit(solution)/shard_map/all_to_all | solution.py:113
  497.8 12.6 %collective-permute-start.41 = (bf16[128,768]{1,0:T(8,128)(2,1)}, bf16[128,768]{1,0:T(8,128)(2,1)S(1)}, u32[]{:S(2)}, u32[]{:S(2)}) collective-permute-start(bf16[128,768]{1,0:T(8,128)(2,1)} %get-tuple-element.181), channel_id=1, source_target_pairs={{0,4},{1,5},{2,6},{3,7},{4,0},{5,1},{6,2},{7,3},{8,12},{9,13},{10,... | collective-permute-start | bytes 589832 | tf_op jit(solution)/shard_map/ppermute | solution.py:98
  499.3 21.6 %collective-permute-start.42 = (bf16[128,768]{1,0:T(8,128)(2,1)}, bf16[128,768]{1,0:T(8,128)(2,1)}, u32[]{:S(2)}, u32[]{:S(2)}) collective-permute-start(bf16[128,768]{1,0:T(8,128)(2,1)} %get-tuple-element.182), channel_id=1, source_target_pairs={{0,8},{1,9},{2,10},{3,11},{4,12},{5,13},{6,14},{7,15},{8,0},{9,1},... | collective-permute-start | bytes 589832 | tf_op jit(solution)/shard_map/ppermute | solution.py:98
  501.7 19.2 %collective-permute-start.43 = (bf16[128,768]{1,0:T(8,128)(2,1)}, bf16[128,768]{1,0:T(8,128)(2,1)}, u32[]{:S(2)}, u32[]{:S(2)}) collective-permute-start(bf16[128,768]{1,0:T(8,128)(2,1)} %get-tuple-element.183), channel_id=1, source_target_pairs={{0,12},{1,13},{2,14},{3,15},{4,8},{5,9},{6,10},{7,11},{8,4},{9,5},... | collective-permute-start | bytes 589832 | tf_op jit(solution)/shard_map/ppermute | solution.py:98
  525.5 6.9 collective-permute-start.45
  529.4 18.2 %collective-permute-start.47 = (bf16[64,1024]{1,0:T(8,128)(2,1)}, bf16[64,1024]{1,0:T(8,128)(2,1)}, u32[]{:S(2)}, u32[]{:S(2)}) collective-permute-start(bf16[64,1024]{1,0:T(8,128)(2,1)} %get-tuple-element.188), channel_id=1, source_target_pairs={{0,16},{1,17},{2,18},{3,19},{4,20},{5,21},{6,22},{7,23},{8,24},{9,... | collective-permute-start | bytes 393224 | tf_op jit(solution)/shard_map/ppermute | solution.py:98
  533.2 16.1 %collective-permute-start.46 = (bf16[2,64,1536]{2,1,0:T(8,128)(2,1)}, bf16[2,64,1536]{2,1,0:T(8,128)(2,1)}, u32[]{:S(2)}, u32[]{:S(2)}) collective-permute-start(bf16[2,64,1536]{2,1,0:T(8,128)(2,1)} %pad_maximum_fusion.5), channel_id=1, source_target_pairs={{0,16},{1,17},{2,18},{3,19},{4,20},{5,21},{6,22},{7,23},{8,24},{9,... | collective-permute-start | bytes 1179656 | tf_op jit(solution)/shard_map/ppermute | solution.py:98
  547.6 68.9 %collective-permute-start.32 = (bf16[1024,1024]{1,0:T(8,128)(2,1)}, bf16[1024,1024]{1,0:T(8,128)(2,1)}, u32[]{:S(2)}, u32[]{:S(2)}) collective-permute-start(bf16[1024,1024]{1,0:T(8,128)(2,1)} %get-tuple-element.159), channel_id=1, source_target_pairs={{0,1},{1,0},{2,3},{3,2},{4,5},{5,4},{6,7},{7,6},{8,9},{9,8},{10,11... | collective-permute-start | bytes 6291464 | tf_op jit(solution)/shard_map/ppermute | solution.py:98
  559.9 6.3 collective-permute-start.38
  567.0 54.3 %collective-permute-start.39 = (bf16[256,1024]{1,0:T(8,128)(2,1)}, bf16[256,1024]{1,0:T(8,128)(2,1)}, u32[]{:S(2)}, u32[]{:S(2)}) collective-permute-start(bf16[256,1024]{1,0:T(8,128)(2,1)} %pad_maximum_fusion.3), channel_id=1, source_target_pairs={{0,16},{1,17},{2,18},{3,19},{4,20},{5,21},{6,22},{7,23},{8,24},{9,... | collective-permute-start | bytes 1572872 | tf_op jit(solution)/shard_map/ppermute | solution.py:98
  569.5 11.0 %collective-permute-start.29 = (bf16[128,1024]{1,0:T(8,128)(2,1)}, bf16[128,1024]{1,0:T(8,128)(2,1)}, u32[]{:S(2)}, u32[]{:S(2)}) collective-permute-start(bf16[128,1024]{1,0:T(8,128)(2,1)} %get-tuple-element.150), channel_id=1, source_target_pairs={{0,2},{1,3},{2,0},{3,1},{4,6},{5,7},{6,4},{7,5},{8,10},{9,11},{10,... | collective-permute-start | bytes 786440 | tf_op jit(solution)/shard_map/ppermute | solution.py:98
  571.3 16.4 %collective-permute-start.30 = (bf16[128,1024]{1,0:T(8,128)(2,1)}, bf16[128,1024]{1,0:T(8,128)(2,1)}, u32[]{:S(2)}, u32[]{:S(2)}) collective-permute-start(bf16[128,1024]{1,0:T(8,128)(2,1)} %get-tuple-element.151), channel_id=1, source_target_pairs={{0,16},{1,17},{2,18},{3,19},{4,20},{5,21},{6,22},{7,23},{8,24},{9,... | collective-permute-start | bytes 786440 | tf_op jit(solution)/shard_map/ppermute | solution.py:98
  572.2 21.0 %collective-permute-start.31 = (bf16[128,1024]{1,0:T(8,128)(2,1)}, bf16[128,1024]{1,0:T(8,128)(2,1)}, u32[]{:S(2)}, u32[]{:S(2)}) collective-permute-start(bf16[128,1024]{1,0:T(8,128)(2,1)} %get-tuple-element.152), channel_id=1, source_target_pairs={{0,18},{1,19},{2,16},{3,17},{4,22},{5,23},{6,20},{7,21},{8,26},{9,... | collective-permute-start | bytes 786440 | tf_op jit(solution)/shard_map/ppermute | solution.py:98
  580.6 43.5 %collective-permute-start.49 = (f32[73,64]{1,0:T(8,128)S(1)}, f32[73,64]{1,0:T(8,128)S(1)}, u32[]{:S(2)}, u32[]{:S(2)}) collective-permute-start(f32[73,64]{1,0:T(8,128)S(1)} %copy-done.88), channel_id=1, source_target_pairs={{0,1},{1,0},{2,3},{3,2},{4,5},{5,4},{6,7},{7,6},{8,9},{9,8},{10,11... | collective-permute-start | bytes 56072 | tf_op jit(solution)/shard_map/ppermute | solution.py:98
  602.9 40.7 %all-to-all-start.12 = ((f32[32,1,3584]{2,1,0:T(1,128)}), f32[32,1,3584]{2,1,0:T(1,128)}, u32[]{:S(2)}, u32[]{:S(2)}) async-start(f32[32,1,3584]{2,1,0:T(1,128)} %reshape.308), calls=%async_computation.13 | async-start | bytes 917504 | tf_op jit(solution)/shard_map/all_to_all | solution.py:1135
  619.2 19.0 %collective-permute-start.34 = (bf16[256,1024]{1,0:T(8,128)(2,1)S(1)}, bf16[256,1024]{1,0:T(8,128)(2,1)S(1)}, u32[]{:S(2)}, u32[]{:S(2)}) collective-permute-start(bf16[256,1024]{1,0:T(8,128)(2,1)S(1)} %get-tuple-element.163), channel_id=1, source_target_pairs={{0,4},{1,5},{2,6},{3,7},{4,0},{5,1},{6,2},{7,3},{8,12},{9,13},{10,... | collective-permute-start | bytes 1572872 | tf_op jit(solution)/shard_map/ppermute | solution.py:98
  624.1 16.9 %collective-permute-start.50 = (f32[73,64]{1,0:T(8,128)S(1)}, f32[73,64]{1,0:T(8,128)S(1)}, u32[]{:S(2)}, u32[]{:S(2)}) collective-permute-start(f32[73,64]{1,0:T(8,128)S(1)} %table_sum.4.refs_0_), channel_id=1, source_target_pairs={{0,2},{1,3},{2,0},{3,1},{4,6},{5,7},{6,4},{7,5},{8,10},{9,11},{10,... | collective-permute-start | bytes 56072 | tf_op jit(solution)/shard_map/ppermute | solution.py:98
  625.5 42.2 %collective-permute-start.33 = (bf16[256,1024]{1,0:T(8,128)(2,1)}, bf16[256,1024]{1,0:T(8,128)(2,1)S(1)}, u32[]{:S(2)}, u32[]{:S(2)}) collective-permute-start(bf16[256,1024]{1,0:T(8,128)(2,1)} %get-tuple-element.161), channel_id=1, source_target_pairs={{0,4},{1,5},{2,6},{3,7},{4,0},{5,1},{6,2},{7,3},{8,12},{9,13},{10,... | collective-permute-start | bytes 1572872 | tf_op jit(solution)/shard_map/ppermute | solution.py:98
  638.3 29.3 %collective-permute-start.35 = (bf16[256,1024]{1,0:T(8,128)(2,1)S(1)}, bf16[256,1024]{1,0:T(8,128)(2,1)}, u32[]{:S(2)}, u32[]{:S(2)}) collective-permute-start(bf16[256,1024]{1,0:T(8,128)(2,1)S(1)} %plane_add.2.refs_2_), channel_id=1, source_target_pairs={{0,8},{1,9},{2,10},{3,11},{4,12},{5,13},{6,14},{7,15},{8,0},{9,1},... | collective-permute-start | bytes 1572872 | tf_op jit(solution)/shard_map/ppermute | solution.py:98
  641.0 18.7 %collective-permute-start.51 = (f32[73,64]{1,0:T(8,128)S(1)}, f32[73,64]{1,0:T(8,128)S(1)}, u32[]{:S(2)}, u32[]{:S(2)}) collective-permute-start(f32[73,64]{1,0:T(8,128)S(1)} %table_sum.5.refs_0_), channel_id=1, source_target_pairs={{0,4},{1,5},{2,6},{3,7},{4,0},{5,1},{6,2},{7,3},{8,12},{9,13},{10,... | collective-permute-start | bytes 56072 | tf_op jit(solution)/shard_map/ppermute | solution.py:98
  659.7 6.5 collective-permute-start.52
  666.1 5.0 collective-permute-start.53
  668.9 12.3 %collective-permute-start.48 = (bf16[64,3072]{1,0:T(8,128)(2,1)}, bf16[64,3072]{1,0:T(8,128)(2,1)S(1)}, u32[]{:S(2)}, u32[]{:S(2)}) collective-permute-start(bf16[64,3072]{1,0:T(8,128)(2,1)} %reduce-scatter.5.cloned.1.call-done), channel_id=1, source_target_pairs={{0,16},{1,17},{2,18},{3,19},{4,20},{5,21},{6,22},{7,23},{8,24},{9,... | collective-permute-start | bytes 1179656 | tf_op jit(solution)/shard_map/ppermute | solution.py:98
  669.6 5.0 collective-permute-start.36
  674.6 15.6 %collective-permute-start.37 = (bf16[256,1024]{1,0:T(8,128)(2,1)S(1)}, bf16[256,1024]{1,0:T(8,128)(2,1)S(1)}, u32[]{:S(2)}, u32[]{:S(2)}) collective-permute-start(bf16[256,1024]{1,0:T(8,128)(2,1)S(1)} %pad_maximum_fusion.1), channel_id=1, source_target_pairs={{0,16},{1,17},{2,18},{3,19},{4,20},{5,21},{6,22},{7,23},{8,24},{9,... | collective-permute-start | bytes 1572872 | tf_op jit(solution)/shard_map/ppermute | solution.py:98
  (166 other events, 1166.1 us)
Sparse Core Ops, SparseCore 0:
  58.5 78.7 all-gather.1
  358.7 43.5 reduce-scatter.2
  427.0 107.8 reduce-scatter.4

commit v4 on v2

--- a/solution.py
+++ b/solution.py
@@ -13,6 +13,7 @@
 BF = jnp.bfloat16
 F32 = jnp.float32
 MIB = 1 << 20
+LANES = 128
 
 
 def dot_nn(left, right):
@@ -62,34 +63,50 @@
     return jax.ShapeDtypeStruct((rows, columns), dtype)
 
 
-def kernel_call(body, name, outs, operands, scalars=0, scratch=(), flops=0, waits=()):
+class Part:
+    def __init__(self, array, block, index):
+        self.array, self.block, self.index = array, block, index
+        self.shape, self.dtype = block, array.dtype
+        self.size = 1
+        for extent in block:
+            self.size *= extent
+
+
+def kernel_call(body, name, outs, operands, scalars=0, scratch=(), flops=0, limit=24):
     moved = sum(item.size * item.dtype.itemsize for item in (*operands[scalars:], *outs))
-    count = len(operands)
-
-    def kernel(*refs):
-        body(*refs[:count], *refs[count + len(waits) :])
-
+    specs = [pl.BlockSpec(memory_space=pltpu.SMEM)] * scalars
+    arrays = list(operands[:scalars])
+    for item in operands[scalars:]:
+        if isinstance(item, Part):
+            specs.append(pl.BlockSpec(item.block, lambda step, index=item.index: index))
+            arrays.append(item.array)
+        else:
+            specs += vmem(1)
+            arrays.append(item)
     return pl.pallas_call(
-        kernel,
-        in_specs=[pl.BlockSpec(memory_space=pltpu.SMEM)] * scalars
-        + vmem(count - scalars)
-        + [pl.BlockSpec(memory_space=pl.ANY)] * len(waits),
+        body,
+        grid=(1,),
+        in_specs=specs,
         out_specs=vmem(len(outs)),
         out_shape=list(outs),
         scratch_shapes=list(scratch),
-        compiler_params=pltpu.CompilerParams(vmem_limit_bytes=40 * MIB),
+        compiler_params=pltpu.CompilerParams(vmem_limit_bytes=limit * MIB),
         cost_estimate=pl.CostEstimate(flops=flops, bytes_accessed=moved, transcendentals=0),
         name=name,
-    )(*operands, *waits)
-
-
-def fused(body, name, outs, *operands, flops=0, waits=()):
+    )(*arrays)
+
+
+def fused(body, name, outs, *operands, flops=0):
     def kernel(*refs):
         results = body(*[ref[...] for ref in refs[: len(operands)]])
         for ref, value in zip(refs[len(operands) :], results):
             ref[...] = value.astype(ref.dtype)
 
-    return kernel_call(kernel, name, outs, operands, flops=flops, waits=waits)
+    return kernel_call(kernel, name, outs, operands, flops=flops)
+
+
+def tied(*values):
+    return lax.optimization_barrier(values)
 
 
 def flipped(value, mask):
@@ -122,32 +139,26 @@
     return parts[0] + sum(part.astype(F32) for part in parts[1:])
 
 
-def place_feed(spot, packs, w_in, w_out, unit, half):
+def place_feed(spot, views, w_in, w_out, unit, half):
     plane, second, core = spot[0], spot[1], spot[2]
-    for step, near, ref, start in packs:
+    for step, near, in_ref, out_ref, start in views:
         column = (plane ^ step) * 2
         for turn in range(2):
             row = ((column + (second ^ turn)) * 2 + (core ^ near)) * unit
-            source = slice(start + turn * unit, start + (turn + 1) * unit)
-            w_in[pl.ds(pl.multiple_of(row, unit), unit), :] = ref[source, :]
+            source = slice(turn * unit, (turn + 1) * unit)
+            w_in[pl.ds(pl.multiple_of(row, unit), unit), :] = in_ref[source, :]
         row = (column + (core ^ near)) * half
-        source = slice(start + 2 * unit, start + 2 * unit + half)
-        w_out[pl.ds(pl.multiple_of(row, half), half), :] = ref[source, :]
+        w_out[pl.ds(pl.multiple_of(row, half), half), :] = out_ref[start : start + half, :]
 
 
 def pack_views(refs, place):
-    planes, size = place.planes, place.pack_rows
-    views = []
-    if len(refs) == 2:
-        for near, ref in enumerate(refs):
-            views += [(step, near, ref, step * size) for step in range(planes)]
-        return views
-    for index, ref in enumerate(refs):
-        views.append((index % planes, index // planes, ref, 0))
-    return views
-
-
-def feed(pieces, packs, spot, bias, wide, norm_row, masks, place, waits=()):
+    planes, count = place.planes, 2 * place.planes
+    if len(refs) == count:
+        return [(i % planes, i // planes, ref, ref, 2 * place.unit) for i, ref in enumerate(refs)]
+    return [(i % planes, i // planes, refs[i], refs[count + i], 0) for i in range(count)]
+
+
+def feed(pieces, packs, bias, wide, norm_row, masks, place):
     rows, model = pieces[0].shape
     inner = bias.shape[1]
     count, total = len(pieces), len(pieces) * rows
@@ -184,16 +195,15 @@
         kernel,
         "feed_forward",
         outs,
-        (spot, *pieces, *packs, bias, wide),
+        (place.spot, *pieces, *packs, bias, wide),
         scalars=1,
         scratch=[pltpu.VMEM((model, inner), BF), pltpu.VMEM((inner, model), BF)],
         flops=4 * total * model * inner,
-        waits=waits,
     )
     return square_reduce(results[3:], masks), results[:3]
 
 
-def feed_back(pieces, packs, spot, saved, masks, place, waits=()):
+def feed_back(pieces, packs, saved, place):
     hidden, upper, active = saved
     rows, model = pieces[0].shape
     total, inner = upper.shape
@@ -225,97 +235,188 @@
         kernel,
         "feed_backward",
         outs,
-        (spot, *pieces, *packs, upper),
+        (place.spot, *pieces, *packs, upper),
         scalars=1,
         scratch=[pltpu.VMEM((model, inner), BF), pltpu.VMEM((inner, model), BF)],
         flops=4 * total * model * inner,
-        waits=waits,
     )
     branch, slope, sums = results[:3]
-    parts = square_reduce(results[3:], masks)
-    planes, size = place.planes, place.pack_rows
-
-    def weights(spot_ref, hidden_ref, active_ref, branch_ref, slope_ref, kept, sent, w_in, w_out):
-        w_in[...] = dot_tn(hidden_ref[...], slope_ref[...])
-        w_out[...] = dot_tn(active_ref[...], branch_ref[...])
-        plane, second, core = spot_ref[0], spot_ref[1], spot_ref[2]
+    return results[3:], branch, slope, sums
+
+
+def feed_out_grads(active, pieces, place):
+    rows, model = pieces[0].shape
+    inner = active.shape[1]
+    planes, half = place.planes, place.half
+    count = len(pieces)
+
+    def kernel(spot, active_ref, *refs):
+        total, kept, sent = refs[-1], refs[count], refs[count + 1]
+        branch = jnp.concatenate([ref[...] for ref in refs[:count]], axis=0)
+        total[...] = dot_tn(active_ref[...], branch)
         for near, ref in enumerate((kept, sent)):
             for step in range(planes):
-                column = (plane ^ step) * 2
-                start = step * size
+                row = ((spot[0] ^ step) * 2 + (spot[2] ^ near)) * half
+                source = pl.ds(pl.multiple_of(row, half), half)
+                ref[step * half : (step + 1) * half, :] = total[source, :].astype(BF)
+
+    return kernel_call(
+        kernel,
+        "feed_out_grads",
+        [shape_of(planes * half, model, BF)] * 2,
+        (place.spot, active, *pieces),
+        scalars=1,
+        scratch=[pltpu.VMEM((inner, model), F32)],
+        flops=2 * active.shape[0] * model * inner,
+    )
+
+
+def feed_in_grads(hidden, slope, place):
+    model, inner = hidden.shape[1], slope.shape[1]
+    planes, unit = place.planes, place.unit
+
+    def kernel(spot, hidden_ref, slope_ref, kept, sent, total):
+        total[...] = dot_tn(hidden_ref[...], slope_ref[...])
+        for near, ref in enumerate((kept, sent)):
+            for step in range(planes):
                 for turn in range(2):
-                    row = ((column + (second ^ turn)) * 2 + (core ^ near)) * unit
-                    target = slice(start + turn * unit, start + (turn + 1) * unit)
+                    column = (spot[0] ^ step) * 2 + (spot[1] ^ turn)
+                    row = (column * 2 + (spot[2] ^ near)) * unit
+                    start = (2 * step + turn) * unit
                     source = pl.ds(pl.multiple_of(row, unit), unit)
-                    ref[target, :] = w_in[source, :].astype(BF)
-                row = (column + (core ^ near)) * half
-                target = slice(start + 2 * unit, start + 2 * unit + half)
-                ref[target, :] = w_out[pl.ds(pl.multiple_of(row, half), half), :].astype(BF)
-
-    kept, sent = kernel_call(
-        weights,
-        "feed_weights",
-        [shape_of(planes * size, inner, BF)] * 2,
-        (spot, hidden, active, branch, slope),
+                    ref[start : start + unit, :] = total[source, :].astype(BF)
+
+    return kernel_call(
+        kernel,
+        "feed_in_grads",
+        [shape_of(2 * planes * unit, inner, BF)] * 2,
+        (place.spot, hidden, slope),
         scalars=1,
-        scratch=[pltpu.VMEM((model, inner), F32), pltpu.VMEM((inner, model), F32)],
-        flops=4 * total * model * inner,
-    )
-    return parts, kept, flipped(sent, 1), sums
-
-
-def feed_pack(weight_in, weight_out, place):
-    rows, hidden = weight_in.shape
-    half = weight_out.shape[0] // 2
-    columns = weight_in.reshape(rows, place.planes, 2, 2, 2, half)
-    columns = lax.dynamic_index_in_dim(columns, place.rep, 4, keepdims=False)
-    own = lax.dynamic_index_in_dim(columns, place.second, 2, keepdims=False)
-    other = lax.dynamic_index_in_dim(columns, 1 - place.second, 2, keepdims=False)
-    own, other = (item.reshape(rows, 2 * place.planes * half) for item in (own, other))
-    part_out = lax.dynamic_slice_in_dim(weight_out, place.rep * half, half, 0)
+        scratch=[pltpu.VMEM((model, inner), F32)],
+        flops=2 * hidden.shape[0] * model * inner,
+    )
+
+
+def plane_split(kept, swapped, place):
+    planes = place.planes
+    size = kept.shape[0] // planes
+
+    def body(kept_part, swapped_part):
+        both = kept_part.astype(F32) + swapped_part.astype(F32)
+        return [both[step * size : (step + 1) * size] for step in range(planes)]
+
+    outs = [shape_of(size, kept.shape[1], BF)] * planes
+    return fused(body, "plane_split", outs, kept, swapped)
+
+
+def plane_early(pieces, place):
+    lists = {step: [piece] for step, piece in enumerate(pieces)}
+    top = place.planes.bit_length() - 2
+    for bit in range(top):
+        for step in [step for step in sorted(lists) if step >> bit & 1]:
+            values = lists.pop(step)
+            value = values[0] if len(values) == 1 else plane_add(values)
+            lists[step ^ 1 << bit].append(flipped(value, QUAD << bit))
+    return lists
+
+
+def plane_last(value, place):
+    return flipped(value, QUAD * (place.planes // 2))
+
+
+def tied_tops(value, all_lists, place):
+    top = place.planes // 2
+    flat = [item for lists in all_lists for item in lists[top]]
+    value, *flat = tied(value, *flat)
+    flat = iter(flat)
+    return value, [[next(flat) for _ in lists[top]] for lists in all_lists]
+
+
+def tied_tops_with(value, other, lists, place):
+    top = place.planes // 2
+    value, other, *flat = tied(value, other, *lists[top])
+    return value, other, [flat]
+
+
+def plane_total(values):
+    return values[0] if len(values) == 1 else plane_add(values)
+
+
+def feed_pack(ff_in, ff_out, module, place):
+    rows, hidden = ff_in.shape[2:]
+    width, model = ff_out.shape[2:]
+    half = width // 2
+    count = 2 * place.planes * half
+    if half % LANES:
+        columns = ff_in[0, module].reshape(rows, place.planes, 2, 2, 2, half)
+        columns = lax.dynamic_index_in_dim(columns, place.rep, 4, keepdims=False)
+        own = lax.dynamic_index_in_dim(columns, place.second, 2, keepdims=False)
+        other = lax.dynamic_index_in_dim(columns, 1 - place.second, 2, keepdims=False)
+        own, other = (item.reshape(rows, count) for item in (own, other))
+        part_out = lax.dynamic_slice_in_dim(ff_out[0, module], place.rep * half, half, 0)
+        return own, flipped(other, 2), part_out
+
+    def kernel(spot, in_ref, out_ref, own, other, part_out):
+        second, rep = spot[1], spot[3]
+        for turn, ref in enumerate((own, other)):
+            for index in range(2 * place.planes):
+                plane, core = index // 2, index % 2
+                start = (((plane * 2 + (second ^ turn)) * 2 + core) * 2 + rep) * half
+                source = pl.ds(pl.multiple_of(start, half), half)
+                ref[:, index * half : (index + 1) * half] = in_ref[0, 0, :, source]
+        part_out[...] = out_ref[0, 0, pl.ds(pl.multiple_of(rep * half, half), half), :]
+
+    own, other, part_out = pl.pallas_call(
+        kernel,
+        grid=(1,),
+        in_specs=[
+            pl.BlockSpec(memory_space=pltpu.SMEM),
+            pl.BlockSpec((1, 1, rows, hidden), lambda step: (0, module, 0, 0)),
+            pl.BlockSpec((1, 1, width, model), lambda step: (0, module, 0, 0)),
+        ],
+        out_specs=vmem(3),
+        out_shape=[
+            shape_of(rows, count, BF),
+            shape_of(rows, count, BF),
+            shape_of(half, model, BF),
+        ],
+        compiler_params=pltpu.CompilerParams(vmem_limit_bytes=24 * MIB),
+        name="feed_columns",
+    )(place.spot, ff_in, ff_out)
     return own, flipped(other, 2), part_out
 
 
-def pack_rows(parts, waits=()):
+def pack_rows(parts):
     def body(*values):
         return (jnp.concatenate(values, axis=0),)
 
     rows = sum(item.shape[0] for item in parts)
     out = shape_of(rows, parts[0].shape[1], BF)
-    return fused(body, "pack_rows", [out], *parts, waits=waits)[0]
+    return fused(body, "pack_rows", [out], *parts)[0]
 
 
 def plane_bits(place):
     return range(place.planes.bit_length() - 1)
 
 
-def plane_gather(pack, place):
-    pieces = {0: pack}
+def plane_start(pack, place):
+    top = place.planes // 2
+    return [flipped(pack, QUAD * top), flipped(pack, QUAD)] if top > 1 else [flipped(pack, QUAD)]
+
+
+def plane_finish(pack, started, place):
+    pieces = {0: pack, place.planes // 2: started[0]}
+    if len(started) > 1:
+        pieces[1] = started[1]
     for bit in reversed(plane_bits(place)):
         for step in sorted(pieces):
-            pieces[step | 1 << bit] = flipped(pieces[step], QUAD << bit)
-    near = [pieces[step] for step in range(place.planes)]
-    return near + [flipped(item, 1) for item in near]
-
-
-def plane_reduce(kept, swapped, place):
-    size = place.pack_rows
-    planes = place.planes
-
-    def total(kept_part, swapped_part):
-        both = kept_part.astype(F32) + swapped_part.astype(F32)
-        return [both[step * size : (step + 1) * size] for step in range(planes)]
-
-    outs = [shape_of(size, kept.shape[1], F32)]
-    outs += [shape_of(size, kept.shape[1], BF)] * (planes - 1)
-    pieces = fused(total, "feed_core_sum", outs, kept, swapped)
-    pieces = {step: [piece] for step, piece in enumerate(pieces)}
-    for bit in plane_bits(place):
-        for step in [step for step in sorted(pieces) if step >> bit & 1]:
-            values = pieces.pop(step)
-            value = values[0] if len(values) == 1 else plane_add(values)
-            pieces[step ^ 1 << bit].append(flipped(value, QUAD << bit))
-    return plane_add(pieces[0])
+            if step % (2 << bit) == 0 and step | 1 << bit not in pieces:
+                pieces[step | 1 << bit] = flipped(pieces[step], QUAD << bit)
+    return [pieces[step] for step in range(place.planes)]
+
+
+def with_core(near):
+    return [*near, *(flipped(item, 1) for item in near)]
 
 
 def plane_add(values):
@@ -325,22 +426,55 @@
     return fused(body, "plane_add", [shape_of(*values[0].shape, BF)], *values)[0]
 
 
-def feed_grads(total, place):
+def feed_final(modules, place):
     unit, half = place.unit, place.half
-    arrived = flipped(total[unit : 2 * unit], 2)
-    own = jnp.concatenate([total[:unit], arrived, total[2 * unit :]], axis=0)
-    theirs = flipped(own, place.shards)
-    is_first, is_low = place.rep == 0, place.second == 0
-    first, last = jnp.where(is_first, own, theirs), jnp.where(is_first, theirs, own)
-    grad_out = jnp.concatenate([first[2 * unit :], last[2 * unit :]], axis=0).astype(F32)
-    sides = jnp.stack([first[: 2 * unit], last[: 2 * unit]]).reshape(2, 2, unit, -1)
-    sides = jnp.where(is_low, sides, sides[:, ::-1])
-    sides = sides.reshape(2, 2, unit, place.planes, 2, half).transpose(2, 3, 1, 4, 0, 5)
-    return sides.reshape(unit, -1).astype(F32), grad_out
-
-
-def plane_groups(place):
-    return [[quad + QUAD * plane for plane in range(place.planes)] for quad in range(QUAD)]
+    inner = modules[0][0][0].shape[1]
+    model = modules[0][2][0].shape[1]
+    planes = place.planes
+    if half % LANES:
+        grads_in, grads_out = [], []
+        for in_own, in_other, out in modules:
+            sides = jnp.stack([jnp.stack(in_own), jnp.stack(in_other)], axis=1)
+            sides = jnp.where(place.second == 0, sides, sides[:, ::-1])
+            sides = jnp.where(place.rep == 0, sides, sides[::-1])
+            sides = sides.reshape(2, 2, unit, planes, 2, half).transpose(2, 3, 1, 4, 0, 5)
+            grads_in.append(sides.reshape(unit, -1).astype(F32))
+            both = jnp.stack(out)
+            both = jnp.where(place.rep == 0, both, both[::-1])
+            grads_out.append(both.reshape(2 * half, model).astype(F32))
+        return jnp.stack(grads_in)[None], jnp.stack(grads_out)[None]
+
+    def kernel(spot, *refs):
+        grad_in, grad_out = refs[-2:]
+        second, rep = spot[1], spot[3]
+        for module in range(2):
+            own = refs[6 * module : 6 * module + 6]
+            for turn in range(2):
+                for side in range(2):
+                    piece = own[2 * turn + side][...].astype(F32)
+                    for index in range(2 * planes):
+                        plane, core = index // 2, index % 2
+                        start = (((plane * 2 + (second ^ turn)) * 2 + core) * 2 + (rep ^ side)) * half
+                        target = pl.ds(pl.multiple_of(start, half), half)
+                        grad_in[0, module, :, target] = piece[:, index * half : (index + 1) * half]
+            for side in range(2):
+                target = pl.ds(pl.multiple_of((rep ^ side) * half, half), half)
+                grad_out[0, module, target, :] = own[4 + side][...].astype(F32)
+
+    operands = [item for module in modules for pair in module for item in pair]
+    outs = [
+        jax.ShapeDtypeStruct((1, 2, unit, 4 * inner), F32),
+        jax.ShapeDtypeStruct((1, 2, 2 * half, model), F32),
+    ]
+    return kernel_call(kernel, "feed_final", outs, (place.spot, *operands), scalars=1)
+
+
+def feed_arrive(sums, place):
+    unit = place.unit
+    own = sums[0][:unit]
+    other = flipped(sums[0][unit:], 2)
+    items = [own, other, *sums[1:]]
+    return [(item, flipped(item, place.shards)) for item in items]
 
 
 def score_block(query, keys, table, bias, place, rows, length):
@@ -544,10 +678,10 @@
         ],
         flops=48 * length * length * width,
     )
-    return group_reduce(kept, sent, place.span_masks), (hidden, mixed, context, peaks)
-
-
-def attend_back(blocks, saved, weight_in, weight_out, table, place, waits):
+    return (hidden, mixed, context, peaks), kept, sent
+
+
+def attend_back(blocks, saved, weight_in, weight_out, table, place):
     hidden, mixed, context, peaks = saved
     pieces = in_steps(blocks)
     rows, model = pieces[0].shape
@@ -576,9 +710,14 @@
             pltpu.VMEM((rows, length + 2 * rows), F32),
         ],
         flops=96 * length * length * width,
-        waits=waits,
-    )
-    parts = group_reduce(kept, sent, place.span_masks)
+    )
+    return grad_mixed, kept, sent, branch, grad_table, far
+
+
+def attend_grads(saved, grad_mixed, branch, place):
+    hidden, unused_mixed, context, unused_peaks = saved
+    length, model = hidden.shape
+    width = context.shape[1]
 
     def weights(hidden_rows, mixed_grad, context_rows, branch_rows):
         return (
@@ -587,7 +726,7 @@
             column_sum(mixed_grad),
         )
 
-    grad_in, grad_out, sums = fused(
+    return fused(
         weights,
         "attend_weights",
         [shape_of(model, 3 * width, BF), shape_of(width, model, BF), shape_of(1, 3 * width, F32)],
@@ -597,7 +736,6 @@
         branch,
         flops=8 * length * model * width,
     )
-    return parts, grad_in, grad_out, sums, distance_gradient(grad_table, far, rows)
 
 
 def wide_table(distance, rows):
@@ -616,33 +754,68 @@
     return total[:, :head] + total[:, head:]
 
 
-def whole_heads(weight_out, head):
-    return weight_out.shape[0] % head == 0
-
-
-def swap_if(condition, value, axis):
-    return jnp.where(condition, jnp.flip(value, axis), value)
-
-
-def attend_weights(weight_in, weight_out, head, place, waits):
-    rows, model = weight_in.shape[0], weight_out.shape[1]
+def whole_heads(head, place):
+    return place.unit == head and 2 * place.unit == LANES and place.planes == 4
+
+
+def attend_weights_whole(weight_in, weight_out, head, place):
+    model = weight_out.shape[1]
     heads = model // head
     per_device = heads // SPAN
     width = per_device * head
-    if not whole_heads(weight_out, head):
-        whole = lax.all_gather(weight_in, "shard", axis=0, tiled=True)
-        whole = whole.reshape(model, 3, heads, head)
-        mine = lax.dynamic_slice_in_dim(whole, place.member * per_device, per_device, 2)
-        out = lax.all_gather(weight_out, "shard", axis=0, tiled=True)
-        out = lax.dynamic_slice_in_dim(out, place.member * width, width, 0)
-        return mine.reshape(model, 3 * width), out
+    whole = lax.all_gather(weight_in, "shard", axis=0, tiled=True)
+    whole = whole.reshape(model, 3, heads, head)
+    mine = lax.dynamic_slice_in_dim(whole, place.member * per_device, per_device, 2)
+    out = lax.all_gather(weight_out, "shard", axis=0, tiled=True)
+    out = lax.dynamic_slice_in_dim(out, place.member * width, width, 0)
+    return mine.reshape(model, 3 * width), out
+
+
+def attend_columns(weight_in, place):
+    rows = weight_in.shape[0]
     planes, unit = place.planes, place.unit
-    groups, columns = planes // 2, 3 * width
-    blocks = weight_in.reshape(rows, 3, groups, 2, 2, 2, -1)
-    blocks = blocks.transpose(4, 3, 5, 0, 1, 2, 6).reshape(2, 2, 2 * rows, columns)
-    own = lax.dynamic_index_in_dim(blocks, place.second, 0, keepdims=False)
-    other = lax.dynamic_index_in_dim(blocks, 1 - place.second, 0, keepdims=False)
-    arrived = flipped(other.reshape(4 * rows, columns), 2).reshape(own.shape)
+    groups, columns = planes // 2, 3 * weight_in.shape[1] // 3 // SPAN
+    if 2 * unit == LANES:
+
+        def pick(spot, whole, *outs):
+            lane = lax.broadcasted_iota(jnp.int32, (rows, LANES), 1)
+            for turn, out in enumerate(outs):
+                for low in range(2):
+                    for part in range(3):
+                        pair = []
+                        for group in range(groups):
+                            start = ((part * groups + group) * 2 + low) * 2 + (spot[1] ^ turn)
+                            source = pl.ds(pl.multiple_of(start * LANES, LANES), LANES)
+                            pair.append(whole[:, source].astype(F32))
+                        rolled = [pltpu.roll(item, unit, axis=1) for item in pair]
+                        cores = (
+                            jnp.where(lane < unit, pair[0], rolled[1]),
+                            jnp.where(lane < unit, rolled[0], pair[1]),
+                        )
+                        for core, value in enumerate(cores):
+                            out[
+                                low,
+                                core * rows : (core + 1) * rows,
+                                part * LANES : (part + 1) * LANES,
+                            ] = value.astype(BF)
+
+        own, other = kernel_call(
+            pick,
+            "attend_pick",
+            [jax.ShapeDtypeStruct((2, 2 * rows, columns), BF)] * 2,
+            (place.spot, weight_in),
+            scalars=1,
+        )
+    else:
+        blocks = weight_in.reshape(rows, 3, groups, 2, 2, 2, -1)
+        blocks = blocks.transpose(4, 3, 5, 0, 1, 2, 6).reshape(2, 2, 2 * rows, columns)
+        own = lax.dynamic_index_in_dim(blocks, place.second, 0, keepdims=False)
+        other = lax.dynamic_index_in_dim(blocks, 1 - place.second, 0, keepdims=False)
+    return own, flipped(other.reshape(4 * rows, columns), 2).reshape(own.shape)
+
+
+def attend_arrange(own, arrived, place):
+    unit, columns = place.unit, own.shape[2]
 
     def arrange(spot, own_ref, arrived_ref, *outs):
         low, core = spot[0] & 1, spot[2]
@@ -659,11 +832,26 @@
         [shape_of(4 * unit, columns, BF)] * 2,
         (place.spot, own, arrived),
         scalars=1,
-        waits=waits,
-    )
-    pieces = [near] + [
-        flipped((near, far)[step & 1], QUAD * step) for step in range(1, planes)
-    ]
+    )
+    return near, far
+
+
+def attend_weights_travel(near, far, weight_out, place):
+    size = near.shape[0]
+    both = jnp.concatenate([near, far], axis=0)
+    pieces = {0: near, 1: flipped(far, QUAD)}
+    for step in range(2, place.planes, 2):
+        arrived = flipped(both, QUAD * step)
+        pieces[step] = arrived[:size]
+        pieces[step + 1] = flipped(arrived[size:], QUAD)
+    steps = range(1, place.planes // 2)
+    outs = [weight_out] + [flipped(weight_out, SPAN * step) for step in steps]
+    return [pieces[step] for step in range(place.planes)], outs
+
+
+def attend_weights_lay(pieces, outs, place):
+    planes, unit, columns = place.planes, place.unit, pieces[0].shape[1]
+    width, model = columns // 3, outs[0].shape[1]
 
     def split(*values):
         kept = jnp.concatenate([item[: 2 * unit] for item in values], axis=0)
@@ -674,7 +862,6 @@
         split, "attend_split", [shape_of(2 * planes * unit, columns, BF)] * 2, *pieces
     )
     swapped = flipped(sent, 1)
-    outs = [weight_out] + [flipped(weight_out, SPAN * step) for step in range(1, groups)]
 
     def lay(spot, kept_ref, swapped_ref, *refs):
         plane, second, core = spot[0], spot[1], spot[2]
@@ -698,45 +885,30 @@
     )
 
 
-def head_row(row, place, aligned):
-    if aligned:
-        row = row.reshape(-1, SPAN, place.unit)
-        row = lax.dynamic_index_in_dim(row, place.member, 1, keepdims=False)
-        return row.reshape(1, -1)
-    row = row.reshape(SPAN, -1)
-    return lax.dynamic_slice_in_dim(row, place.member, 1, 0)
-
-
-def head_spread(row, model, place, aligned):
-    if aligned:
-        whole = jnp.zeros((place.planes // 2, SPAN, place.unit), F32)
-        block = row.reshape(-1, 1, place.unit)
-        return lax.dynamic_update_slice_in_dim(whole, block, place.member, 1).reshape(1, model)
-    whole = jnp.zeros((SPAN, model // SPAN), F32)
-    return lax.dynamic_update_slice_in_dim(whole, row, place.member, 0).reshape(1, model)
-
-
-def attend_weight_grads(grad_in, grad_out, head, place, aligned):
+def attend_grads_whole(grad_in, grad_out, head, place):
     model = grad_out.shape[1]
     heads = model // head
     per_device = heads // SPAN
-    if not aligned:
-        whole = jnp.zeros((model, 3, heads, head), F32)
-        whole = lax.dynamic_update_slice_in_dim(
-            whole,
-            grad_in.astype(F32).reshape(model, 3, per_device, head),
-            place.member * per_device,
-            2,
-        )
-        whole = lax.psum_scatter(
-            whole.reshape(model, 3 * model), "shard", scatter_dimension=0, tiled=True
-        )
-        out = jnp.zeros((model, model), F32)
-        out = lax.dynamic_update_slice_in_dim(
-            out, grad_out.astype(F32), place.member * per_device * head, 0
-        )
-        out = lax.psum_scatter(out, "shard", scatter_dimension=0, tiled=True)
-        return rep_sum(whole, place), rep_sum(out, place)
+    whole = jnp.zeros((model, 3, heads, head), F32)
+    whole = lax.dynamic_update_slice_in_dim(
+        whole,
+        grad_in.astype(F32).reshape(model, 3, per_device, head),
+        place.member * per_device,
+        2,
+    )
+    whole = lax.psum_scatter(
+        whole.reshape(model, 3 * model), "shard", scatter_dimension=0, tiled=True
+    )
+    out = jnp.zeros((model, model), F32)
+    out = lax.dynamic_update_slice_in_dim(
+        out, grad_out.astype(F32), place.member * per_device * head, 0
+    )
+    out = lax.psum_scatter(out, "shard", scatter_dimension=0, tiled=True)
+    return rep_sum(whole, place), rep_sum(out, place)
+
+
+def attend_grads_lay(grad_in, grad_out, place):
+    model = grad_out.shape[1]
     planes, unit = place.planes, place.unit
     groups, columns = planes // 2, grad_in.shape[1]
 
@@ -752,50 +924,103 @@
             row = ((plane >> 1) ^ step) * unit
             ref[...] = w_out[pl.ds(pl.multiple_of(row, unit), unit), :]
 
-    kept, sent, *outs = kernel_call(
+    return kernel_call(
         lay,
         "attend_unlay",
         [shape_of(2 * planes * unit, columns, BF)] * 2 + [shape_of(unit, model, BF)] * groups,
         (place.spot, grad_in, grad_out),
         scalars=1,
     )
-    swapped = flipped(sent, 1)
+
+
+def attend_grads_planes(kept, swapped, place):
+    planes, unit, columns = place.planes, place.unit, kept.shape[1]
 
     def by_plane(kept_part, swapped_part):
         both = jnp.concatenate([kept_part, swapped_part], axis=1)
-        return [both[2 * step * unit : 2 * (step + 1) * unit] for step in range(planes)]
-
-    pieces = fused(
+        pieces = [both[2 * step * unit : 2 * (step + 1) * unit] for step in range(planes)]
+        return pieces[0], jnp.concatenate([pieces[1], pieces[3]], axis=0), pieces[2]
+
+    size = 2 * unit
+    return fused(
         by_plane,
         "attend_planes",
-        [shape_of(2 * unit, 2 * columns, BF)] * planes,
+        [shape_of(count * size, 2 * columns, BF) for count in (1, 2, 1)],
         kept,
         swapped,
     )
-    arrived = [pieces[0]] + [flipped(pieces[step], QUAD * step) for step in range(1, planes)]
-    outs = [outs[0]] + [flipped(outs[step], SPAN * step) for step in range(1, groups)]
-
-    def total(*values):
-        even = sum(item.astype(F32) for item in values[:planes:2])
-        odd = sum(item.astype(F32) for item in values[1:planes:2])
+
+
+def attend_grads_relay(own, odd, even, *outs):
+    size = own.shape[0]
+    arrived = flipped(jnp.concatenate([even, odd[size:]], axis=0), 2 * QUAD)
+    outs = [outs[0]] + [flipped(outs[step], SPAN * step) for step in range(1, len(outs))]
+    return [own, odd, arrived, *outs]
+
+
+def attend_grads_sum(travelled, place):
+    unit = place.unit
+    size = 2 * unit
+    columns, model = travelled[0].shape[1] // 2, travelled[3].shape[1]
+
+    def total(own, near, far, *rest):
+        even = own.astype(F32) + far[:size].astype(F32)
+        odd = near[:size].astype(F32) + far[size:].astype(F32)
         both = jnp.concatenate([even, odd], axis=1)
-        out = sum(item.astype(F32) for item in values[planes:])
+        out = sum(item.astype(F32) for item in rest)
         return both[:unit], both[unit:], out
 
     own, other, out = fused(
         total,
         "attend_plane_sum",
         [shape_of(unit, 4 * columns, BF)] * 2 + [shape_of(unit, model, BF)],
-        *arrived,
-        *outs,
-    )
-    whole = jnp.stack([own, flipped(other, 2)])
-    whole = rep_sum(whole, place).reshape(2, unit, 2, 2, 3, groups, -1)
-    whole = swap_if(place.second == 1, whole, 0)
-    whole = swap_if(place.plane & 1 == 1, whole, 2)
-    whole = swap_if(place.core == 1, whole, 3)
-    whole = whole.transpose(1, 4, 5, 2, 0, 3, 6)
-    return whole.reshape(unit, 3 * model), rep_sum(out, place)
+        *travelled,
+    )
+    return own, other, out
+
+
+def attend_grads_arrive(sums, place):
+    own, other, out = sums
+    arrived = flipped(other, 2)
+    mine = own, arrived, out
+    return mine, tuple(flipped(item, place.shards) for item in mine)
+
+
+def attend_grads_final(mine, theirs, place):
+    unit = place.unit
+    model = mine[2].shape[1]
+    columns = mine[0].shape[1] // 4
+    groups = place.planes // 2
+
+    def kernel(spot, *refs):
+        values = [refs[i][...].astype(F32) + refs[3 + i][...].astype(F32) for i in range(3)]
+        grad_in, grad_out = refs[6:]
+        grad_out[0] = values[2]
+        lane = lax.broadcasted_iota(jnp.int32, (unit, LANES), 1)
+        low_bit, core = spot[0] & 1, spot[2]
+        for turn in range(2):
+            for low in range(2):
+                for part in range(3):
+                    blocks = []
+                    for near in range(2):
+                        start = (2 * low + near) * columns + part * LANES
+                        blocks.append(values[turn][:, start : start + LANES])
+                    first = jnp.where(core == 0, blocks[0], blocks[1])
+                    last = jnp.where(core == 0, blocks[1], blocks[0])
+                    pairs = (
+                        jnp.where(lane < unit, first, pltpu.roll(last, unit, axis=1)),
+                        jnp.where(lane < unit, pltpu.roll(first, unit, axis=1), last),
+                    )
+                    for group, value in enumerate(pairs):
+                        start = ((part * groups + group) * 2 + (low_bit ^ low)) * 2
+                        start = (start + (spot[1] ^ turn)) * LANES
+                        grad_in[0, :, pl.ds(pl.multiple_of(start, LANES), LANES)] = value
+
+    outs = [
+        jax.ShapeDtypeStruct((1, unit, 3 * model), F32),
+        jax.ShapeDtypeStruct((1, unit, model), F32),
+    ]
+    return kernel_call(kernel, "attend_final", outs, (place.spot, *mine, *theirs), scalars=1)
 
 
 def rep_sum(value, place):
@@ -803,34 +1028,97 @@
     return low.astype(F32) + flipped(low, place.shards).astype(F32)
 
 
-LANES = 128
-
-
 def row(wide, index):
     return wide[index : index + 1]
 
 
-def pack_columns(left, right, waits):
-    def body(first, second):
-        return (jnp.concatenate([first, second], axis=1),)
-
-    out = shape_of(left.shape[0], left.shape[1] + right.shape[1], BF)
-    return fused(body, "pack_columns", [out], left, right, waits=waits)[0]
-
-
-def convolve_start(parts, before, wide, bias_row, weight_in):
+def conv_pick(weight_in, weight_out, place):
+    rows, model = weight_out.shape
+    half = rows // 2
+    whole = half % 16 != 0
+    size = rows if whole else half
+
+    def pick(spot, left, right, out):
+        source = pl.ds(pl.multiple_of(spot[3] * half, half), half)
+        if whole:
+            source = slice(0, rows)
+        out[:size, :] = left[source, :model]
+        out[size : 2 * size, :] = left[source, model:]
+        out[2 * size :, :] = right[source, :]
+
+    outs = [shape_of(3 * size, model, BF)]
+    operands = (place.spot, weight_in, weight_out)
+    return kernel_call(pick, "conv_pick", outs, operands, scalars=1)[0]
+
+
+def core_groups(place):
+    return [list(range(core, place.shards, 2)) for core in range(2)]
+
+
+def conv_halved(piece, place):
+    return 6 * place.unit == 4 * piece.shape[0]
+
+
+def conv_planes(piece, place):
+    started = plane_start(piece, place)
+    return plane_finish(piece, started, place)
+
+
+def conv_square(own, masks):
+    first, second = masks
+    half = own.shape[0] // 2
+    return own, flipped(own, first), flipped(own, second), half
+
+
+def conv_relay(own, via_first, via_second, masks):
+    first, second = masks
+    half = own.shape[0] // 2
+    low, high = flipped(via_first[:half], second), flipped(via_second[half:], first)
+    near = [own, via_first, via_second, low, high]
+    return [*near, *(flipped(item, 1) for item in near)]
+
+
+def lay_conv(spot, refs, target, unit, first):
+    model = target.shape[0]
+    plane, second, core, rep = spot[0], spot[1], spot[2], spot[3]
+    size = unit if len(refs) == 1 else unit // 2
+    columns = (0, 1) if first else (2,)
+    for index, ref in enumerate(refs):
+        for local in range(ref.shape[0] // (3 * size)):
+            start = local * size
+            if len(refs) > 1:
+                kind, near = index % 5, index // 5
+                turn, side = ((0, 0), (0, 1), (1, 0), (1, 1), (1, 1))[kind]
+                step = local + (ref.shape[0] // (3 * size) if kind == 4 else 0)
+                start = (((plane ^ step) * 2 + (second ^ turn)) * 2 + (core ^ near)) * 2
+                start = pl.multiple_of((start + (rep ^ side)) * size, size)
+            for place_of, column in enumerate(columns):
+                source = (3 * local + column) * size
+                target[pl.ds(start, size), place_of * model : (place_of + 1) * model] = ref[
+                    source : source + size, :
+                ]
+
+
+def convolve_start(parts, before, wide, bias_row, weights, place):
     rows, model = before.shape
-
-    def body(*values):
-        base, small, w_in = values[4:]
-        current = base + joined(values[:4]) + row(small, bias_row)
+    count = len(weights)
+
+    def kernel(spot, *refs):
+        part_refs, (base, small), weight_refs = refs[:4], refs[4:6], refs[6 : 6 + count]
+        current_ref, hidden_ref, doubled_ref, glued_ref, w_in = refs[6 + count :]
+        lay_conv(spot, weight_refs, w_in, place.unit, True)
+        parts_now = [ref[...] for ref in part_refs]
+        current = base[...] + joined(parts_now) + small[bias_row : bias_row + 1, :]
+        current_ref[...] = current
         unit, unused_scale = standard(current)
-        hidden = (unit * row(small, 7) + row(small, 8)).astype(BF)
-        doubled = dot_nn(hidden, w_in)
-        return current, hidden, doubled, doubled[:, :model] * logistic(doubled[:, model:])
-
-    return fused(
-        body,
+        hidden = (unit * small[7:8, :] + small[8:9, :]).astype(BF)
+        hidden_ref[...] = hidden
+        doubled = dot_nn(hidden, w_in[...])
+        doubled_ref[...] = doubled
+        glued_ref[...] = (doubled[:, :model] * logistic(doubled[:, model:])).astype(BF)
+
+    return kernel_call(
+        kernel,
         "convolve_start",
         [
             shape_of(rows, model, F32),
@@ -838,22 +1126,22 @@
             shape_of(rows, 2 * model, F32),
             shape_of(rows, model, BF),
         ],
-        *parts,
-        before,
-        wide,
-        weight_in,
+        (place.spot, *parts, before, wide, *weights),
+        scalars=1,
+        scratch=[pltpu.VMEM((model, 2 * model), BF)],
+        limit=56,
         flops=4 * rows * model * model,
     )
 
 
-def convolve_finish(glued, border, wide, taps, weight_out, before):
+def convolve_finish(glued, border, wide, taps, weights, before, place):
     rows, model = before.shape
     edge = border.shape[0]
 
-    def kernel(
-        glued_ref, border_ref, small, w_out, base,
-        mixed_ref, rest_ref, current_ref, hidden_ref, padded,
-    ):
+    def kernel(spot, glued_ref, border_ref, small, base, *refs):
+        weight_refs = refs[: len(weights)]
+        mixed_ref, rest_ref, current_ref, hidden_ref, padded, w_out = refs[len(weights) :]
+        lay_conv(spot, weight_refs, w_out, place.unit, False)
         padded[:edge, :] = border_ref[...].astype(F32)
         padded[edge:, :] = glued_ref[...].astype(F32)
         first, count = taps
@@ -878,22 +1166,27 @@
         kernel,
         "convolve_finish",
         [shape_of(rows, model, dtype) for dtype in (F32, BF, F32, BF)],
-        (glued, border, wide, weight_out, before),
-        scratch=[pltpu.VMEM((edge + rows, model), F32)],
+        (place.spot, glued, border, wide, before, *weights),
+        scalars=1,
+        scratch=[pltpu.VMEM((edge + rows, model), F32), pltpu.VMEM((model, model), BF)],
+        limit=56,
         flops=2 * rows * model * model,
     )
 
 
-def convolve_back_start(parts, grad, after, mixed, wide, taps, weight_out, glued, border, waits):
+def convolve_back_start(parts, grad, after, mixed, wide, taps, weights, glued, border, place):
     rows, model = after.shape
     edge = border.shape[0]
     first, count = taps
 
     def kernel(
-        own, part_one, part_two, part_three, grad_ref, after_ref, mixed_ref, small,
-        w_out, glued_ref, border_ref,
-        grad_out, branch_ref, main_ref, halo_ref, sums, padded, spread,
+        spot, own, part_one, part_two, part_three, grad_ref, after_ref, mixed_ref, small,
+        glued_ref, border_ref, *refs,
     ):
+        weight_refs = refs[: len(weights)]
+        grad_out, branch_ref, main_ref, halo_ref, sums = refs[len(weights) : -3]
+        padded, spread, w_out = refs[-3:]
+        lay_conv(spot, weight_refs, w_out, place.unit, False)
         incoming = joined((own[...], part_one[...], part_two[...], part_three[...]))
         slope, sum_gain, sum_shift = norm_back(after_ref[...], small[11:12, :], incoming)
         current = grad_ref[...] + slope
@@ -940,37 +1233,47 @@
             shape_of(edge, model, BF),
             shape_of(count + 4, model, F32),
         ],
-        (*parts, grad, after, mixed, wide, weight_out, glued, border),
+        (
+            place.spot, *parts, grad, after, mixed, wide, glued, border,
+            *weights,
+        ),
+        scalars=1,
         scratch=[
             pltpu.VMEM((edge + rows, model), F32),
             pltpu.VMEM((rows + 2 * edge, model), F32),
+            pltpu.VMEM((model, model), BF),
         ],
+        limit=56,
         flops=2 * rows * model * model,
-        waits=waits,
-    )
-
-
-def convolve_back_finish(main, incoming, doubled, weight_in, before, wide, grad):
+    )
+
+
+def convolve_back_finish(main, incoming, doubled, weights, before, wide, grad, place):
     rows, model = before.shape
     edge = incoming.shape[0]
-
-    def body(main_rows, late, both, w_in, base, small, grad_rows):
-        glued = jnp.concatenate(
-            [main_rows[: rows - edge], main_rows[rows - edge :] + late.astype(F32)], axis=0
-        )
+    count = len(weights)
+
+    def kernel(spot, main_ref, late, both, base, small, grad_rows, *refs):
+        current_ref, branch_ref, slope_ref, sums, w_in = refs[count:]
+        lay_conv(spot, refs[:count], w_in, place.unit, True)
+        last = main_ref[rows - edge :, :] + late[...].astype(F32)
+        glued = jnp.concatenate([main_ref[: rows - edge, :], last], axis=0)
         glued = glued.astype(BF).astype(F32)
         gate = logistic(both[:, model:])
-        slope = jnp.concatenate(
-            [glued * gate, glued * both[:, :model] * gate * (1.0 - gate)], axis=1
-        ).astype(BF)
-        inner, sum_gain, sum_shift = norm_back(base, row(small, 7), dot_nt(slope, w_in))
-        current = grad_rows + inner
-        branch = current.astype(BF)
-        sums = jnp.concatenate([sum_gain, sum_shift, column_sum(branch)], axis=0)
-        return current, branch, slope, sums
-
-    return fused(
-        body,
+        slope_ref[:, :model] = (glued * gate).astype(BF)
+        slope_ref[:, model:] = (glued * both[:, :model] * gate * (1.0 - gate)).astype(BF)
+        inner, sum_gain, sum_shift = norm_back(
+            base[...], small[7:8, :], dot_nt(slope_ref[...], w_in[...])
+        )
+        current = grad_rows[...] + inner
+        current_ref[...] = current
+        branch_ref[...] = current.astype(BF)
+        sums[0:1, :] = sum_gain
+        sums[1:2, :] = sum_shift
+        sums[2:3, :] = column_sum(current.astype(BF))
+
+    return kernel_call(
+        kernel,
         "convolve_back_finish",
         [
             shape_of(rows, model, F32),
@@ -978,40 +1281,117 @@
             shape_of(rows, 2 * model, BF),
             shape_of(3, model, F32),
         ],
-        main,
-        incoming,
-        doubled,
-        weight_in,
-        before,
-        wide,
-        grad,
+        (
+            place.spot, main, incoming, doubled, before, wide, grad,
+            *weights,
+        ),
+        scalars=1,
+        scratch=[pltpu.VMEM((model, 2 * model), BF)],
+        limit=56,
         flops=4 * rows * model * model,
     )
 
 
-def convolve_weight_grads(hidden, slope, rest, branch, place):
+def conv_grads_start(hidden, slope, rest, branch, place):
     model = hidden.shape[1]
-
-    def body(hidden_rows, slope_rows, rest_rows, branch_rows):
-        both = dot_tn(hidden_rows, slope_rows), dot_tn(rest_rows, branch_rows)
-        return (jnp.concatenate(both, axis=1),)
-
-    total = fused(
-        body,
-        "convolve_weights",
-        [shape_of(model, 3 * model, BF)],
-        hidden,
-        slope,
-        rest,
-        branch,
+    unit, planes = place.unit, place.planes
+    size = unit // 2
+    halved = size % 16 == 0
+
+    def kernel(spot, hidden_ref, slope_ref, rest_ref, branch_ref, kept, sent, total):
+        total[:, : 2 * model] = dot_tn(hidden_ref[...], slope_ref[...])
+        total[:, 2 * model :] = dot_tn(rest_ref[...], branch_ref[...])
+        plane, second, core, rep = spot[0], spot[1], spot[2], spot[3]
+        for near, ref in enumerate((kept, sent)):
+            if not halved:
+                for pair in range(2 * planes):
+                    start = pl.multiple_of((pair * 2 + (core ^ near)) * unit, unit)
+                    for column in range(3):
+                        ref[(3 * pair + column) * unit : (3 * pair + column + 1) * unit, :] = total[
+                            pl.ds(start, unit), column * model : (column + 1) * model
+                        ].astype(BF)
+                continue
+            for kind, (turn, side) in enumerate(((0, 0), (0, 1), (1, 0), (1, 1))):
+                for step in range(planes):
+                    start = (((plane ^ step) * 2 + (second ^ turn)) * 2 + (core ^ near)) * 2
+                    start = pl.multiple_of((start + (rep ^ side)) * size, size)
+                    for column in range(3):
+                        target = ((kind * planes + step) * 3 + column) * size
+                        ref[target : target + size, :] = total[
+                            pl.ds(start, size), column * model : (column + 1) * model
+                        ].astype(BF)
+
+    return kernel_call(
+        kernel,
+        "conv_grads",
+        [shape_of(3 * model // 2, model, BF)] * 2,
+        (place.spot, hidden, slope, rest, branch),
+        scalars=1,
+        scratch=[pltpu.VMEM((model, 3 * model), F32)],
         flops=6 * hidden.shape[0] * model * model,
-    )[0]
-    total = lax.psum_scatter(total, "shard", scatter_dimension=0, tiled=True)
-    total = rep_sum(total, place)
-    return total[:, : 2 * model], total[:, 2 * model :]
-
-
-def feed_to_attend(parts, before, wide, waits):
+        limit=36,
+    )
+
+
+def conv_grads_split(kept, swapped, place):
+    count = 4 if place.unit // 2 % 16 == 0 else 1
+    size = kept.shape[0] // count
+
+    def body(kept_part, swapped_part):
+        total = kept_part.astype(F32) + swapped_part.astype(F32)
+        return [total[index * size : (index + 1) * size] for index in range(count)]
+
+    outs = [shape_of(size, kept.shape[1], BF)] * count
+    return list(fused(body, "conv_grads_split", outs, kept, swapped))
+
+
+def conv_grads_square(shares, masks):
+    first, second = masks
+    return [
+        shares[0],
+        flipped(shares[1], first),
+        flipped(shares[2], second),
+        flipped(shares[3], first | second),
+    ]
+
+
+def conv_grads_pieces(shares, place):
+    size = shares[0].shape[0] // place.planes
+
+    def body(*values):
+        total = sum(value.astype(F32) for value in values)
+        return [total[step * size : (step + 1) * size] for step in range(place.planes)]
+
+    outs = [shape_of(size, shares[0].shape[1], BF)] * place.planes
+    return list(fused(body, "conv_grads_pieces", outs, *shares))
+
+
+def conv_grads_whole(total, place):
+    groups = [list(range(core, place.shards, 2)) for core in range(2)]
+    mine = lax.psum_scatter(
+        total, "shard", scatter_dimension=0, tiled=True, axis_index_groups=groups
+    )
+    return rep_sum(mine, place).reshape(3, place.unit, -1)
+
+
+def conv_grads_final(mine, theirs, place):
+    size, model = mine.shape[0] // 3, mine.shape[1]
+
+    def kernel(spot, mine_ref, theirs_ref, grad_in, grad_out):
+        for turn, ref in enumerate((mine_ref, theirs_ref)):
+            target = pl.ds(pl.multiple_of((spot[3] ^ turn) * size, size), size)
+            grad_in[0, target, :model] = ref[:size, :].astype(F32)
+            grad_in[0, target, model:] = ref[size : 2 * size, :].astype(F32)
+            grad_out[0, target, :] = ref[2 * size :, :].astype(F32)
+
+    outs = [
+        jax.ShapeDtypeStruct((1, 2 * size, 2 * model), F32),
+        jax.ShapeDtypeStruct((1, 2 * size, model), F32),
+    ]
+    return kernel_call(kernel, "conv_final", outs, (place.spot, mine, theirs), scalars=1)
+
+
+def feed_to_attend(parts, before, wide):
     rows, model = before.shape
 
     def body(*values):
@@ -1021,7 +1401,7 @@
         return current, unit * row(small, 3) + row(small, 4)
 
     outs = [shape_of(rows, model, F32), shape_of(rows, model, BF)]
-    return fused(body, "feed_to_attend", outs, *parts, before, wide, waits=waits)
+    return fused(body, "feed_to_attend", outs, *parts, before, wide)
 
 
 def turn_around(parts, before, wide, cotangent):
@@ -1074,41 +1454,183 @@
     return fused(body, "last_step", outs, *parts, grad, before, wide)
 
 
+def small_unpack(gathered, counts, place):
+    rows, modules_rows = counts
+    shards, unit, half, planes = place.shards, place.unit, place.half, place.planes
+    model = shards * unit
+    if not place.aligned:
+        wide = gathered[:, :rows].transpose(1, 0, 2).reshape(rows, model).astype(F32)
+        bias = gathered[:, rows:].reshape(planes, 2, 2, 2, 2, half)
+        bias = lax.dynamic_index_in_dim(bias, place.second, 1, keepdims=False)
+        bias = lax.dynamic_index_in_dim(bias, place.rep, 3, keepdims=False)
+        bias = bias.transpose(2, 0, 1, 3).reshape(2, -1).astype(F32)
+        heads = [
+            lax.dynamic_slice_in_dim(wide[index].reshape(SPAN, -1), place.member, 1, 0)
+            for index in (5, 6)
+        ]
+        return wide, bias, jnp.concatenate([heads[0], jnp.zeros_like(heads[0]), heads[1]], axis=1)
+
+    def kernel(spot, ref, wide, bias, mix):
+        lane = lax.broadcasted_iota(jnp.int32, (1, LANES), 1)
+        second, core, rep = spot[1], spot[2], spot[3]
+        member = (spot[0] & 1) * 4 + second * 2 + core
+
+        def doubled(value):
+            return jnp.concatenate([value, value], axis=1)
+
+        for pair in range(shards // 2):
+            both = [doubled(ref[2 * pair + side].astype(F32)) for side in range(2)]
+            value = jnp.where(lane < unit, both[0], both[1])
+            wide[:, pair * LANES : (pair + 1) * LANES] = value[:rows]
+        for module in range(2):
+            for index in range(2 * planes):
+                shard = (index // 2 * 2 + second) * 2 + index % 2
+                block = doubled(ref[shard].astype(F32))
+                start = rows + (module * 2) * 2
+                options = [
+                    jnp.where(
+                        lane < unit,
+                        block[start + 2 * side : start + 2 * side + 1],
+                        block[start + 2 * side + 1 : start + 2 * side + 2],
+                    )
+                    for side in range(2)
+                ]
+                value = jnp.where(rep == 0, options[0], options[1])
+                bias[module : module + 1, index * half : (index + 1) * half] = value
+        mix[...] = jnp.zeros_like(mix)
+        pair = [doubled(ref[member + SPAN * group].astype(F32)) for group in range(2)]
+        value = jnp.where(lane < unit, pair[0], pair[1])
+        mix[:, :LANES] = value[5:6]
+        mix[:, 2 * LANES :] = value[6:7]
+
+    outs = [
+        shape_of(rows, model, F32),
+        shape_of(2, 2 * planes * half, F32),
+        shape_of(1, 3 * LANES, F32),
+    ]
+    return kernel_call(kernel, "small_unpack", outs, (place.spot, gathered), scalars=1)
+
+
 def shard_gather(value, place):
-    gathered = value[None]
-    for bit in range(place.shards.bit_length() - 1):
-        arrived = flipped(gathered, 1 << bit)
-        low = jnp.bitwise_and(jnp.right_shift(place.shard, bit), 1) == 0
-        gathered = jnp.concatenate(
-            [jnp.where(low, gathered, arrived), jnp.where(low, arrived, gathered)], axis=0
+    copies = jnp.broadcast_to(value[None], (place.shards, *value.shape))
+    return lax.all_to_all(copies, "shard", 0, 0, tiled=True)
+
+
+def small_reduce(sums, mix_sums, biases, distance, counts, place):
+    input_sums, first_sums, attend_sums, conv_sums, last_sums = sums
+    rows, taps = counts
+    unit, half, planes, shards = place.unit, place.half, place.planes, place.shards
+    model = unit * shards
+    width = mix_sums.shape[1] // 3
+    if not place.aligned:
+        heads = []
+        for start in (0, 2 * width):
+            whole = jnp.zeros((SPAN, model // SPAN), F32)
+            block = mix_sums[:, start : start + width]
+            whole = lax.dynamic_update_slice_in_dim(whole, block, place.member, 0)
+            heads.append(whole.reshape(1, model))
+        wide = jnp.concatenate(
+            [
+                input_sums, first_sums, *heads, attend_sums[:2], conv_sums[taps:], last_sums,
+                attend_sums[2:], conv_sums[:taps],
+            ],
+            axis=0,
         )
-    return gathered
-
-
-def shard_reduce(value, place):
-    both = jnp.concatenate([value, value], axis=0)
-    both = lax.all_to_all(both, ("rep", "shard"), 0, 0, tiled=True)
-    return jnp.sum(both, axis=0)
-
-
-def sum_everywhere(value, place, delays):
-    arrived = flipped(value, 1)
-    for bit in range(1, (2 * place.shards).bit_length() - 1):
-        waits = delays[bit - 1 : bit]
-        value = fused(
-            lambda own, other: (own + other,),
-            "table_sum",
-            [shape_of(*value.shape, F32)],
-            value,
-            arrived,
-            waits=waits,
-        )[0]
-        arrived = flipped(value, 1 << bit)
-    return value + arrived
+        wide = wide.reshape(-1, shards, unit).transpose(1, 0, 2)
+        pair = jnp.stack(biases).reshape(2, planes, 2, half)
+        bias = lax.dynamic_update_slice(
+            jnp.zeros((planes, 2, 2, 2, 2, half), F32),
+            pair.transpose(1, 2, 0, 3)[:, None, :, :, None, :],
+            (0, place.second, 0, 0, place.rep, 0),
+        ).reshape(shards, -1, unit)
+        both = jnp.concatenate([wide, bias], axis=1)
+        both = lax.all_to_all(
+            jnp.concatenate([both, both], axis=0), ("rep", "shard"), 0, 0, tiled=True
+        )
+        total = jnp.sum(both, axis=0)
+        for bit in range((2 * shards).bit_length() - 1):
+            distance = distance + flipped(distance, 1 << bit)
+        return total[:rows], total[rows:].reshape(2, 2 * half), distance
+    extent = -(-(rows + 8) // 8) * 8
+    table_rows = distance.shape[0]
+    fold = -(-table_rows // 16) * 8
+
+    def pack(spot, in_ref, first, attend_ref, conv, last, mix, bias_one, bias_two, table, out, wide):
+        plane, second, core, rep = spot[0], spot[1], spot[2], spot[3]
+        wide[...] = jnp.zeros_like(wide)
+        wide[0:2, :] = in_ref[...]
+        wide[2:5, :] = first[...]
+        wide[7:9, :] = attend_ref[0:2, :]
+        wide[9:13, :] = conv[taps:, :]
+        wide[13:16, :] = last[...]
+        wide[16:17, :] = attend_ref[2:3, :]
+        wide[17 : 17 + taps, :] = conv[:taps, :]
+        lane = lax.broadcasted_iota(jnp.int32, (1, LANES), 1)
+        for group in range(2):
+            start = ((group * 2 + (plane & 1)) * 2 + second) * LANES
+            target = pl.ds(pl.multiple_of(start, LANES), LANES)
+            for index, begin in ((5, 0), (6, 2 * width)):
+                value = mix[:, begin : begin + LANES]
+                moved = pltpu.roll(jnp.broadcast_to(value, (8, LANES)), unit, axis=1)[:1]
+                low = value if group == 0 else moved
+                high = moved if group == 0 else value
+                placed = jnp.where(core == 0, low, high)
+                placed = jnp.where(lane // unit == core, placed, 0.0)
+                wide[index : index + 1, target] = placed
+        for module, ref in enumerate((bias_one, bias_two)):
+            for index in range(2 * planes):
+                value = ref[:, index * half : (index + 1) * half]
+                start = pl.multiple_of((index // 2 * 2 + second) * LANES, LANES)
+                for side in range(2):
+                    line = rows + ((index % 2) * 2 + module) * 2 + side
+                    wide[line : line + 1, pl.ds(start, LANES)] = jnp.where(rep == side, value, 0.0)
+        rest = jnp.concatenate(
+            [table[fold:, :], jnp.zeros((2 * fold - table_rows, unit), F32)], axis=0
+        )
+        folded = jnp.concatenate([table[:fold, :], rest], axis=1)
+        for target in range(2 * shards):
+            pair = target % shards // 2
+            out[target, :extent, :] = wide[:, pair * LANES : (pair + 1) * LANES]
+            out[target, extent:, :] = folded
+
+    packed = kernel_call(
+        pack,
+        "small_pack",
+        [jax.ShapeDtypeStruct((2 * shards, extent + fold, LANES), F32)],
+        (place.spot, *sums, mix_sums, *biases, distance),
+        scalars=1,
+        scratch=[pltpu.VMEM((extent, model), F32)],
+    )[0]
+    packed = lax.all_to_all(packed, ("rep", "shard"), 0, 0, tiled=True)
+
+    def unpack(spot, ref, wide, bias, table):
+        total = ref[0]
+        for index in range(1, 2 * shards):
+            total = total + ref[index]
+        table[:fold, :] = total[extent:, :unit]
+        core = spot[2]
+        moved = pltpu.roll(total, unit, axis=1)
+        table[fold:, :] = moved[extent : extent + table_rows - fold, :unit]
+        wide[...] = jnp.where(core == 0, total, moved)[:rows, :unit]
+        for module in range(2):
+            for side in range(2):
+                lines = [rows + (near * 2 + module) * 2 + side for near in range(2)]
+                value = jnp.where(
+                    core == 0, total[lines[0] : lines[0] + 1], total[lines[1] : lines[1] + 1]
+                )
+                bias[module : module + 1, side * half : (side + 1) * half] = value
+
+    return kernel_call(
+        unpack,
+        "small_sum",
+        [shape_of(rows, unit, F32), shape_of(2, 2 * half, F32), shape_of(*distance.shape, F32)],
+        (place.spot, packed),
+        scalars=1,
+    )
 
 
 class Place:
-    def __init__(self, unit, half):
+    def __init__(self, unit, half, head):
         self.shards = lax.axis_size("shard")
         self.planes = self.shards // QUAD
         self.unit, self.half = unit, half
@@ -1119,9 +1641,10 @@
         self.second = self.shard // 2 % 2
         self.plane = self.shard // QUAD
         self.member = self.shard % SPAN
-        self.spot = jnp.stack([self.plane, self.second, self.core])
-        self.flat_spot = jnp.stack([jnp.zeros_like(self.plane), self.second, self.core])
+        self.spot = jnp.stack([self.plane, self.second, self.core, self.rep])
+        self.flat_spot = jnp.stack([jnp.zeros_like(self.plane), self.second, self.core, self.rep])
         self.span_spot = self.member.reshape(1)
+        self.aligned = whole_heads(head, self)
         self.feed_masks = (self.shards, 2)
         self.span_masks = (4, 2)
 
@@ -1149,150 +1672,237 @@
 ):
     rows, model = inputs.shape
     unit, half = ff_in.shape[2], ff_out.shape[2] // 2
-    place = Place(unit, half)
     head = distance.shape[2]
+    place = Place(unit, half, head)
     tap_count = depthwise.shape[1]
     edge = -(-(tap_count - 1) // 16) * 16
-    aligned = whole_heads(attn_out[0], head)
     bias_rows = ff_bias.shape[2] // unit
     count = vectors.shape[1]
     taps = (count + 1, tap_count)
-
+    wide_rows = count + 1 + tap_count
+
+    first_parts = feed_pack(ff_in, ff_out, 0, place)
     small = jnp.concatenate(
         [vectors[0], attn_bias, depthwise[0], ff_bias[0].reshape(2 * bias_rows, unit)], axis=0
     )
-    first_pack = pack_rows(feed_pack(ff_in[0, 0], ff_out[0, 0], place))
-    first_packs = plane_gather(first_pack, place)
-    pieces = square_gather(inputs, place.feed_masks)
+    first_pack = pack_rows(first_parts)
+    first_pack, current, mix_in, later_in = tied(first_pack, inputs, attn_in[0], ff_in)
+    first_far = plane_start(first_pack, place)
+    pieces = square_gather(current, place.feed_masks)
+    second_parts = feed_pack(later_in, ff_out, 1, place)
+    columns = attend_columns(mix_in, place) if place.aligned else (mix_in, mix_in)
+    (
+        first_far[0], first_far[1], small, second_in, second_other, second_out, *early
+    ) = tied(*first_far, small, *second_parts, *columns, *pieces)
+    columns, pieces = early[:2], early[2:]
     small = shard_gather(small, place)
-    wide = small[:, : count + 1 + tap_count].transpose(1, 0, 2).reshape(-1, model).astype(F32)
-    feed_bias = small[:, count + 1 + tap_count :].reshape(place.planes, 2, 2, 2, 2, half)
-    feed_bias = lax.dynamic_index_in_dim(feed_bias, place.second, 1, keepdims=False)
-    feed_bias = lax.dynamic_index_in_dim(feed_bias, place.rep, 3, keepdims=False)
-    feed_bias = feed_bias.transpose(2, 0, 1, 3).reshape(2, 1, -1).astype(F32)
+    first_near = plane_finish(first_pack, first_far, place)
+    first_packs = with_core(first_near)
+    wide, feed_bias, mix_bias = small_unpack(small, (wide_rows, 2 * bias_rows), place)
     table = wide_table(distance[0], rows)
-    mix_bias = jnp.concatenate(
-        [
-            head_row(wide[5], place, aligned),
-            jnp.zeros((1, model // SPAN), F32),
-            head_row(wide[6], place, aligned),
-        ],
-        axis=1,
-    )
-
-    arrived = first_packs[: place.planes]
-    mix_in, mix_out = attend_weights(attn_in[0], attn_out[0], head, place, arrived)
-    glue = pack_columns(conv_in[0], conv_out[0], arrived)
-    glue = lax.all_gather(glue, "shard", axis=0, tiled=True)
-    second_pack = feed_pack(ff_in[0, 1], ff_out[0, 1], place)
+    second_in = pack_rows((second_in, second_other))
+    if place.aligned:
+        columns = attend_arrange(*columns, place)
+    glue = conv_pick(conv_in[0], conv_out[0], place)
+    last = place.planes - 1
+    first_packs[last], glue, second_in, wide, mix_bias, table, *columns = tied(
+        first_packs[last], glue, second_in, wide, mix_bias, table, *columns
+    )
 
     parts, saved_first = feed(
-        pieces, first_packs, place.spot, feed_bias[0], wide, 0, place.feed_masks, place
-    )
-    second_near = lax.all_gather(
-        pack_rows(second_pack, waits=saved_first[:1]),
-        "shard",
-        axis=0,
-        tiled=True,
-        axis_index_groups=plane_groups(place),
-    )
-    second_packs = [second_near, flipped(second_near, 1)]
-    after_first, hidden = feed_to_attend(parts, inputs, wide, (mix_in,))
-    parts, saved_attend = attend(
-        group_gather(hidden, place.span_masks), mix_in, mix_bias, mix_out, table, place
-    )
-    glue_in, glue_out = glue[:, : 2 * model], glue[:, 2 * model :]
+        pieces, first_packs, feed_bias[0:1], wide, 0, place.feed_masks, place
+    )
+    if place.aligned:
+        travelled, outs = attend_weights_travel(*columns, attn_out[0], place)
+        after_first, hidden = feed_to_attend(parts, inputs, wide)
+        hidden, glue, *travelled = tied(hidden, glue, *travelled)
+        glue_planes = conv_planes(glue, place)
+        mix_in, mix_out = attend_weights_lay(travelled, outs, place)
+    else:
+        mix_in, mix_out = attend_weights_whole(attn_in[0], attn_out[0], head, place)
+        after_first, hidden = feed_to_attend(parts, inputs, wide)
+    near, far = group_gather(hidden, place.span_masks)
+    if place.aligned:
+        far[3], second_in, *glue_planes = tied(far[3], second_in, *glue_planes)
+        glue_own = pack_rows(glue_planes)
+        glue_own, via_first, via_second, unused_half = conv_square(glue_own, place.feed_masks)
+    else:
+        glue = [lax.all_gather(glue, "shard", axis=0, tiled=True)]
+        far[3], second_in = tied(far[3], second_in)
+    second_in_far = plane_start(second_in, place)
+    saved_attend, kept, sent = attend((near, far), mix_in, mix_bias, mix_out, table, place)
+    if place.aligned:
+        sent, *second_in_far, via_first, via_second = tied(
+            sent, *second_in_far, via_first, via_second
+        )
+        glue = conv_relay(glue_own, via_first, via_second, place.feed_masks)
+    else:
+        sent, *second_in_far = tied(sent, *second_in_far)
+    parts = group_reduce(kept, sent, place.span_masks)
+    parts[3], second_out, *glue = tied(parts[3], second_out, *glue)
+    second_out_far = plane_start(second_out, place)
     after_attend, conv_hidden, doubled, glued = convolve_start(
-        parts, after_first, wide, count, glue_in
+        parts, after_first, wide, count, glue, place
     )
     border = along(glued[rows - edge :], 1, place)
     border = jnp.where(place.member == 0, jnp.zeros_like(border), border)
     mixed, rest, after_conv, hidden = convolve_finish(
-        glued, border, wide, taps, glue_out, after_attend
-    )
+        glued, border, wide, taps, glue, after_attend, place
+    )
+    hidden, *second_far = tied(hidden, *second_in_far, *second_out_far)
+    second_packs = [
+        *with_core(plane_finish(second_in, second_far[:2], place)),
+        *with_core(plane_finish(second_out, second_far[2:], place)),
+    ]
     pieces = square_gather(hidden, place.feed_masks)
     parts, saved_second = feed(
-        pieces, second_packs, place.flat_spot, feed_bias[1], wide, None, place.feed_masks, place
+        pieces, second_packs, feed_bias[1:2], wide, None, place.feed_masks, place
     )
     output, grad_last, branch, last_sums = turn_around(parts, after_conv, wide, cotangent)
 
     pieces = square_gather(branch, place.feed_masks)
-    parts, kept, swapped, second_bias = feed_back(
-        pieces, second_packs, place.flat_spot, saved_second, place.feed_masks, place
-    )
-    second_total = fused(
-        lambda own, other: (own.astype(F32) + other.astype(F32),),
-        "feed_core_total",
-        [shape_of(*kept.shape, BF)],
-        kept,
-        swapped,
-    )[0]
-    second_sum = lax.psum_scatter(
-        second_total,
-        "shard",
-        scatter_dimension=0,
-        tiled=True,
-        axis_index_groups=plane_groups(place),
-    )
+    result, branch, slope, second_bias = feed_back(pieces, second_packs, saved_second, place)
+    second_grads = [
+        *feed_in_grads(saved_second[0], slope, place),
+        *feed_out_grads(saved_second[2], pieces, place),
+    ]
+    *result, second_grads[1], second_grads[3] = tied(*result, second_grads[1], second_grads[3])
+    second_grads[1], second_grads[3] = flipped(second_grads[1], 1), flipped(second_grads[3], 1)
+    parts = square_reduce(result, place.feed_masks)
+    second_split = [plane_split(*pair, place) for pair in (second_grads[:2], second_grads[2:])]
+    parts[3], *flat = tied(parts[3], *second_split[0], *second_split[1])
+    second_split = [flat[: place.planes], flat[place.planes :]]
+    second_lists = [plane_early(pieces, place) for pieces in second_split]
     grad_conv, conv_branch, main, halo, conv_sums = convolve_back_start(
-        parts, grad_last, after_conv, mixed, wide, taps, glue_out, glued, border, (second_total,)
+        parts, grad_last, after_conv, mixed, wide, taps, glue, glued, border, place
     )
     incoming = along(halo, -1, place)
+    incoming, second_tops = tied_tops(incoming, second_lists, place)
+    second_early = [lists[0] for lists in second_lists]
     incoming = jnp.where(place.member == SPAN - 1, jnp.zeros_like(incoming), incoming)
     grad_attend, branch, slope, attend_sums = convolve_back_finish(
-        main, incoming, doubled, glue_in, after_attend, wide, grad_conv
-    )
-    conv_grads = convolve_weight_grads(conv_hidden, slope, rest, conv_branch, place)
-    parts, mix_grad_in, mix_grad_out, mix_sums, grad_distance = attend_back(
-        group_gather(branch, place.span_masks), saved_attend, mix_in, mix_out, table, place, ()
-    )
+        main, incoming, doubled, glue, after_attend, wide, grad_conv, place
+    )
+    conv_kept, conv_sent = conv_grads_start(conv_hidden, slope, rest, conv_branch, place)
+    second_tops = [plane_total(values) for values in second_tops]
+    count_early = len(second_early[0])
+    branch, conv_kept, conv_sent, *flat = tied(
+        branch, conv_kept, conv_sent, *second_tops, *second_early[0], *second_early[1]
+    )
+    second_tops = flat[:2]
+    second_early = [flat[2 : 2 + count_early], flat[2 + count_early :]]
+    near, far = group_gather(branch, place.span_masks)
+    conv_shares = conv_grads_split(conv_kept, flipped(conv_sent, 1), place)
+    far[3], *flat = tied(far[3], *conv_shares, *second_tops)
+    conv_shares, second_tops = flat[:-2], flat[-2:]
+    if place.aligned:
+        conv_shares = conv_grads_square(conv_shares, place.feed_masks)
+    second_lasts = [plane_last(top, place) for top in second_tops]
+    back = attend_back((near, far), saved_attend, mix_in, mix_out, table, place)
+    grad_mixed, kept, sent, branch, grad_table, table_far = back
+    sent, *second_lasts = tied(sent, *second_lasts)
+    mix_grad_in, mix_grad_out, mix_sums = attend_grads(saved_attend, grad_mixed, branch, place)
+    second_sums = [plane_add([*own, last]) for own, last in zip(second_early, second_lasts)]
+    if place.aligned:
+        mix_kept, mix_swap, *mix_outs = attend_grads_lay(mix_grad_in, mix_grad_out, place)
+        kept, mix_swap = tied(kept, mix_swap)
+        mix_swap = flipped(mix_swap, 1)
+    parts = group_reduce(kept, sent, place.span_masks)
+    if place.aligned:
+        mix_sent = list(attend_grads_planes(mix_kept, mix_swap, place))
+        parts[1], *mix_sent = tied(parts[1], *mix_sent)
+        mix_sent[1] = flipped(mix_sent[1], QUAD)
+        parts[3], mix_sent[1], *conv_shares = tied(parts[3], mix_sent[1], *conv_shares)
+        conv_pieces = conv_grads_pieces(conv_shares, place)
+    grad_distance = distance_gradient(grad_table, table_far, rows)
     grad_first, branch, first_sums = attend_to_feed_back(parts, grad_attend, after_first, wide)
-    pieces = square_gather(branch, place.feed_masks)
-    parts, kept, swapped, first_bias = feed_back(
-        pieces, first_packs, place.spot, saved_first, place.feed_masks, place
-    )
-    first_sum = plane_reduce(kept, swapped, place)
+    if place.aligned:
+        branch, *conv_pieces = tied(branch, *conv_pieces)
+        conv_lists = plane_early(conv_pieces, place)
+        mix_sent = attend_grads_relay(*mix_sent, *mix_outs)
+        pieces = square_gather(branch, place.feed_masks)
+        pieces[3], (conv_top,) = tied_tops(pieces[3], [conv_lists], place)
+    else:
+        pieces = square_gather(branch, place.feed_masks)
+        conv_whole = conv_grads_whole(conv_shares[0], place)
+        mix_grads = attend_grads_whole(mix_grad_in, mix_grad_out, head, place)
+        mix_grads = [item[None] for item in mix_grads]
+    kept, sent = feed_out_grads(saved_first[2], pieces, place)
+    pieces[0], kept, sent = tied(pieces[0], kept, sent)
+    out_swapped = flipped(sent, 1)
+    result, branch, slope, first_bias = feed_back(pieces, first_packs, saved_first, place)
+    out_split = plane_split(kept, out_swapped, place)
+    slope, *out_split = tied(slope, *out_split)
+    out_lists = plane_early(out_split, place)
+    kept, sent = feed_in_grads(saved_first[0], slope, place)
+    kept, *result = tied(kept, *result)
+    if place.aligned:
+        kept, *mix_sent = tied(kept, *mix_sent)
+        mix_own, mix_other, mix_out_sum = attend_grads_sum(mix_sent, place)
+        conv_last = plane_last(plane_total(conv_top), place)
+    in_swapped = flipped(sent, 1)
+    in_swapped, (out_top,) = tied_tops(in_swapped, [out_lists], place)
+    out_last = plane_last(plane_total(out_top), place)
+    in_lists = plane_early(plane_split(kept, in_swapped, place), place)
+    parts = square_reduce(result, place.feed_masks)
+    second_other = flipped(second_sums[0][unit:], 2)
+    if place.aligned:
+        mix_arrived = flipped(mix_other, 2)
+        parts[3], mix_arrived, conv_last = tied(parts[3], mix_arrived, conv_last)
+        conv_mine = plane_add([*conv_lists[0], conv_last])
+    parts[3], second_other, (in_top,) = tied_tops_with(parts[3], second_other, in_lists, place)
+    in_last = plane_last(plane_total(in_top), place)
     grad_input, input_sums = last_step(parts, grad_first, inputs, wide)
 
-    second_grads = feed_grads(second_sum, place)
-    mix_grads = attend_weight_grads(mix_grad_in, mix_grad_out, head, place, aligned)
-    first_grads = feed_grads(first_sum, place)
-    width = mix_sums.shape[1] // 3
-    wide_grads = jnp.concatenate(
-        [
-            input_sums,
-            first_sums,
-            head_spread(mix_sums[:, :width], model, place, aligned),
-            head_spread(mix_sums[:, 2 * width :], model, place, aligned),
-            attend_sums[:2],
-            conv_sums[tap_count:],
-            last_sums,
-            attend_sums[2:],
-            conv_sums[:tap_count],
-        ],
-        axis=0,
-    )
-    wide_grads = wide_grads.reshape(-1, place.shards, unit).transpose(1, 0, 2)
-    bias_pair = jnp.stack([first_bias, second_bias]).reshape(2, place.planes, 2, half)
-    bias_grads = lax.dynamic_update_slice(
-        jnp.zeros((place.planes, 2, 2, 2, 2, half), F32),
-        bias_pair.transpose(1, 2, 0, 3)[:, None, :, :, None, :],
-        (0, place.second, 0, 0, place.rep, 0),
-    ).reshape(place.shards, 2 * bias_rows, unit)
-    small_grads = shard_reduce(jnp.concatenate([wide_grads, bias_grads], axis=1), place)
-    delays = (grad_first, kept, first_sum)
-    grad_distance = sum_everywhere(grad_distance, place, delays)
+    second_pack = pack_rows((second_sums[0][:unit], second_other, second_sums[1]))
+    second_theirs = flipped(second_pack, place.shards)
+    small_grads, bias_grads, grad_distance = small_reduce(
+        (input_sums, first_sums, attend_sums, conv_sums, last_sums),
+        mix_sums,
+        (first_bias, second_bias),
+        grad_distance,
+        (wide_rows, tap_count),
+        place,
+    )
+    out_sum = plane_add([*out_lists[0], out_last])
+    out_theirs = flipped(out_sum, place.shards)
+    if place.aligned:
+        mix_mine = mix_own, mix_arrived, mix_out_sum
+        mix_theirs = [flipped(item, place.shards) for item in mix_mine]
+        conv_theirs = flipped(conv_mine, place.shards)
+        mix_grads = attend_grads_final(mix_mine, mix_theirs, place)
+        conv_grads = conv_grads_final(conv_mine, conv_theirs, place)
+    else:
+        conv_grads = (
+            jnp.concatenate([conv_whole[0], conv_whole[1]], axis=1)[None],
+            conv_whole[2][None],
+        )
+    in_last, small_grads, mix_last, conv_end, second_theirs, out_theirs, *early = tied(
+        in_last,
+        small_grads,
+        mix_grads[0],
+        conv_grads[0],
+        second_theirs,
+        out_theirs,
+        *in_lists[0][1:],
+    )
+    first_mine = feed_arrive([plane_add([in_lists[0][0], *early, in_last])], place)
+    first_mine = [*first_mine, (out_sum, out_theirs)]
+    cuts = (0, unit, 2 * unit, 2 * unit + half)
+    second_mine = [
+        (second_pack[cuts[i] : cuts[i + 1]], second_theirs[cuts[i] : cuts[i + 1]])
+        for i in range(3)
+    ]
+    feed_grads = feed_final((first_mine, second_mine), place)
+    mix_grads, conv_grads = (mix_last, mix_grads[1]), (conv_end, conv_grads[1])
     return (
         output,
         grad_input,
-        jnp.stack([first_grads[0], second_grads[0]])[None],
-        jnp.stack([first_grads[1], second_grads[1]])[None],
-        small_grads[count + 1 + tap_count :].reshape(1, 2, -1),
-        mix_grads[0][None],
-        mix_grads[1][None],
-        conv_grads[0][None],
-        conv_grads[1][None],
-        small_grads[count + 1 : count + 1 + tap_count][None],
+        *feed_grads,
+        bias_grads[None],
+        *mix_grads,
+        *conv_grads,
+        small_grads[count + 1 :][None],
         grad_distance[None],
         small_grads[:count][None],
         small_grads[count : count + 1],

time: 638 us -> 597 us (0.936)
  local copies, waits for them, and re-layouts: 108 us -> 36.9 us
  waiting for transfers between devices: 252 us -> 278 us
  Pallas kernels: 104 us -> 127 us
  other arithmetic: 20.4 us -> 2.58 us
  between operations: 15.7 us -> 2.73 us
  starting transfers between devices: 126 us -> 137 us
    ppermute x89 -> x125, waiting for transfers between devices: 242 us -> 277 us  [flipped(): lax.ppermute(value, ('rep', 'shard'), [(i, i ^ mask) for i in range(total)])]
    pallas_call x37 -> x58, Pallas kernels: 104 us -> 127 us  [the longest x56 126 us: kernel_call(): pl.pallas_call(body, grid=(1,), in_specs=specs, out_specs=vmem(len(outs))...]
    unnamed x240 -> x241, local copies, waits for them, and re-layouts: 50.2 us -> 28.4 us
    ppermute x89 -> x125, starting transfers between devices: 115 us -> 127 us  [flipped(): lax.ppermute(value, ('rep', 'shard'), [(i, i ^ mask) for i in range(total)])]
    concatenate x19 -> x0, local copies, waits for them, and re-layouts: 10.3 us -> none  [the longest x14 10.1 us: shards(): jnp.concatenate([input_sums, first_sums, head_spread(mix_sums[:, :width],...]
    reshape x13 -> x0, local copies, waits for them, and re-layouts: 9.2 us -> none  [the longest x1 3.42 us: attend_weight_grads(): whole = rep_sum(whole, place).reshape(2, unit, 2, 2, 3, groups, -1)]
    all_gather x2 -> x0, waiting for transfers between devices: 8.56 us -> none  [the longest x1 8.56 us: shards(): glue = lax.all_gather(glue, 'shard', axis=0, tiled=True)]
    another operation x6 -> x0, local copies, waits for them, and re-layouts: 6.89 us -> none  [the longest x1 3.74 us: shards(): mix_grads[0][None]]
  transfers between devices with their start and end apart: 96 -> 129, of which waited for: 44 -> 49; matrix products, arithmetic and copies ran while one was open for 13% -> 2% of each run, Pallas kernels for 14% -> 16%
where the time goes in v4:
time: 597 us; the launch traced here: 585 us
  waiting for transfers between devices  278 us (47%)
  starting transfers between devices  137 us (23%)
  Pallas kernels  127 us (21%)
  local copies, waits for them, and re-layouts  36.9 us (6%)
    ppermute x125, waiting for transfers between devices, flipped(): lax.ppermute(value, ('rep', 'shard'), [(i, i ^ mask) for i in range(total)])  277 us
    ppermute x125, starting transfers between devices, flipped(): lax.ppermute(value, ('rep', 'shard'), [(i, i ^ mask) for i in range(total)])  127 us
    pallas_call x56, Pallas kernels, kernel_call(): pl.pallas_call(body, grid=(1,), in_specs=specs, out_specs=vmem(len(outs))...  126 us
    unnamed x241, local copies, waits for them, and re-layouts  28.4 us
  transfers between devices with their start and end apart: 129, of which 49 were waited for; matrix products, arithmetic and copies ran while one was open for 2% of the time, Pallas kernels for 16%

profile of v4, /device:TPU:0, one launch (start us, length us, event | category | flops | bytes accessed | tf_op | source)
XLA Modules:
  0.0 585.1 jit_solution(10333499393141958569)
XLA Ops:
  4.0 3.0 collective-permute-start
  7.0 3.5 collective-permute-done.refs_1_
  10.5 2.9 collective-permute-start.1
  20.6 3.6 collective-permute-done.3.refs_1_
  27.4 8.9 %collective-permute-done.6.refs_2_ = bf16[128,1024]{1,0:T(8,128)(2,1)S(1)} collective-permute-done((bf16[128,1024]{1,0:T(8,128)(2,1)S(1)}, bf16[128,1024]{1,0:T(8,128)(2,1)S(1)}, u32[]{:S(2)}, u32[]{:S(2)}) %collective-permute-start.6) | collective-permute-done | bytes 262176 | tf_op jit(solution)/shard_map/ppermute | solution.py:114
  39.7 4.6 all-to-all-start
  44.7 5.1 collective-permute-done.8.refs_7_
  56.5 2.7 collective-permute-start.16
  60.2 5.1 feed_forward.2
  67.3 2.5 collective-permute-start.13
  70.8 4.0 collective-permute-done.17
  77.4 4.6 collective-permute-done.14.refs_2_
  87.7 12.4 %collective-permute-done.26.refs_1_ = bf16[96,1024]{1,0:T(8,128)(2,1)S(1)} collective-permute-done((bf16[96,1024]{1,0:T(8,128)(2,1)S(1)}, bf16[96,1024]{1,0:T(8,128)(2,1)S(1)}, u32[]{:S(2)}, u32[]{:S(2)}) %collective-permute-start.26) | collective-permute-done | bytes 196640 | tf_op jit(solution)/shard_map/ppermute | solution.py:114
  103.5 8.7 %collective-permute-done.22.refs_5_ = bf16[128,1024]{1,0:T(8,128)(2,1)S(1)} collective-permute-done((bf16[128,1024]{1,0:T(8,128)(2,1)S(1)}, bf16[128,1024]{1,0:T(8,128)(2,1)S(1)}, u32[]{:S(2)}, u32[]{:S(2)}) %collective-permute-start.22) | collective-permute-done | bytes 262176 | tf_op jit(solution)/shard_map/ppermute | solution.py:114
  112.2 2.3 collective-permute-done.28.refs_3_
  124.5 15.1 %attend_forward.1 = (bf16[1024,1024]{1,0:T(8,128)(2,1)S(1)}, bf16[1024,384]{1,0:T(8,128)(2,1)S(1)}, bf16[1024,128]{1,0:T(8,128)(2,1)S(1)}, f32[1024,128]{1,0:T(8...) custom-call(s32[1]{0:T(128)} %bitcast.4.refs_0_, bf16[128,1024]{1,0:T(8,128)(2,1)S(1)} %copy-done.73, ...), custom_call_target="tpu_custom_call" | custom-call | flops 6442450944 | bytes 10094080 | tf_op jit(solution)/shard_map/attend_forward/pallas_call | solution.py:86
  144.9 8.2 %collective-permute-done.39.refs_9_.refs_3_ = bf16[192,1024]{1,0:T(8,128)(2,1)S(1)} collective-permute-done((bf16[192,1024]{1,0:T(8,128)(2,1)S(1)}, bf16[192,1024]{1,0:T(8,128)(2,1)S(1)}, u32[]{:S(2)}, u32[]{:S(2)}) %collective-permute-start.39) | collective-permute-done | bytes 393248 | tf_op jit(solution)/shard_map/ppermute | solution.py:114
  153.6 9.9 %collective-permute-done.40.refs_10_.refs_4_ = bf16[192,1024]{1,0:T(8,128)(2,1)S(1)} collective-permute-done((bf16[192,1024]{1,0:T(8,128)(2,1)S(1)}, bf16[192,1024]{1,0:T(8,128)(2,1)S(1)}, u32[]{:S(2)}, u32[]{:S(2)}) %collective-permute-start.40) | collective-permute-done | bytes 393248 | tf_op jit(solution)/shard_map/ppermute | solution.py:114
  168.6 10.4 %collective-permute-done.38.refs_3_ = bf16[128,1024]{1,0:T(8,128)(2,1)S(1)} collective-permute-done((bf16[128,1024]{1,0:T(8,128)(2,1)S(1)}, bf16[128,1024]{1,0:T(8,128)(2,1)S(1)}, u32[]{:S(2)}, u32[]{:S(2)}) %collective-permute-start.38) | collective-permute-done | bytes 262176 | tf_op jit(solution)/shard_map/ppermute | solution.py:114
  180.9 5.7 convolve_start.1
  189.0 2.2 collective-permute-start.47
  194.6 7.5 %convolve_finish.1 = (f32[128,1024]{1,0:T(8,128)}, bf16[128,1024]{1,0:T(8,128)(2,1)}, f32[128,1024]{1,0:T(8,128)}, bf16[128,1024]{1,0:T(8,128)(2,1)}) custom-call(s32[4]{0:T(128)} %copy-done.38, bf16[128,1024]{1,0:T(8,128)(2,1)} %get-tuple-element.392.glued_ref, bf16[32,1024]{1,0:T(8,128)(2,1)} %broadcast_select_fusion.1.border_ref, f32[48,1024]{1,0:T(8,128)} %copy-done.1, ...), custom_call_target="tpu_custom_call" | custom-call | flops 268435456 | bytes 8912896 | tf_op jit(solution)/shard_map/convolve_finish/pallas_call | solution.py:86
  209.3 3.8 collective-permute-done.49.refs_1_
  213.1 2.0 collective-permute-start.57
  215.2 3.3 collective-permute-done.50.refs_2_
  225.3 3.9 feed_forward.3
  232.7 6.6 %collective-permute-done.62.refs_1_ = bf16[128,1024]{1,0:T(8,128)(2,1)S(1)} collective-permute-done((bf16[128,1024]{1,0:T(8,128)(2,1)S(1)}, bf16[128,1024]{1,0:T(8,128)(2,1)S(1)}, u32[]{:S(2)}, u32[]{:S(2)}) %collective-permute-start.62) | collective-permute-done | bytes 262176 | tf_op jit(solution)/shard_map/ppermute | solution.py:114
  239.3 4.6 collective-permute-done.63.refs_2_
  249.6 5.7 collective-permute-done.65.refs_1_
  255.3 4.4 collective-permute-done.66.refs_2_
  260.6 4.2 feed_backward.2
  264.8 2.4 feed_in_grads.2
  277.3 6.6 %collective-permute-done.70.part_three = bf16[128,1024]{1,0:T(8,128)(2,1)S(1)} collective-permute-done((bf16[128,1024]{1,0:T(8,128)(2,1)S(1)}, bf16[128,1024]{1,0:T(8,128)(2,1)S(1)}, u32[]{:S(2)}, u32[]{:S(2)}) %collective-permute-start.70) | collective-permute-done | bytes 262176 | tf_op jit(solution)/shard_map/ppermute | solution.py:114
  286.7 10.6 %convolve_back_start.1 = (f32[128,1024]{1,0:T(8,128)}, bf16[128,1024]{1,0:T(8,128)(2,1)}, f32[128,1024]{1,0:T(8,128)}, bf16[32,1024]{1,0:T(8,128)(2,1)}, f32[35,1024]{1,0:T(8,128)}) custom-call(s32[4]{0:T(128)} %copy-done.38, f32[128,1024]{1,0:T(8,128)} %copy-done.13, bf16[128,1024]{1,0:T(8,128)(2,1)} %copy-done.108, bf16[128,1024]{1,0:T(8,128)(2,1)} %copy-done.109, ...), custom_call_target="tpu_custom_call" | custom-call | flops 268435456 | bytes 11218944 | tf_op jit(solution)/shard_map/convolve_back_start/pallas_call | solution.py:86
  303.4 6.7 %convolve_back_finish.1 = (f32[128,1024]{1,0:T(8,128)}, bf16[128,1024]{1,0:T(8,128)(2,1)}, bf16[128,2048]{1,0:T(8,128)(2,1)}, f32[3,1024]{1,0:T(4,128)}) custom-call(s32[4]{0:T(128)} %copy-done.38, f32[128,1024]{1,0:T(8,128)} %get-tuple-element.440.main_ref, bf16[32,1024]{1,0:T(8,128)(2,1)} %broadcast_select_fusion.late, ...), custom_call_target="tpu_custom_call" | custom-call | flops 536870912 | bytes 10498048 | tf_op jit(solution)/shard_map/convolve_back_finish/pallas_call | solution.py:86
  311.3 3.0 conv_grads.1
  314.3 2.5 collective-permute-start.85
  320.3 6.6 %collective-permute-done.83.refs_7_ = bf16[128,1024]{1,0:T(8,128)(2,1)S(1)} collective-permute-done((bf16[128,1024]{1,0:T(8,128)(2,1)S(1)}, bf16[128,1024]{1,0:T(8,128)(2,1)S(1)}, u32[]{:S(2)}, u32[]{:S(2)}) %collective-permute-start.83) | collective-permute-done | bytes 262176 | tf_op jit(solution)/shard_map/ppermute | solution.py:114
  327.4 3.4 collective-permute-done.79.refs_3_
  332.1 2.6 collective-permute-start.86
  335.2 24.4 %attend_backward.1 = (bf16[1024,1024]{1,0:T(8,128)(2,1)S(1)}, bf16[1024,384]{1,0:T(8,128)(2,1)S(1)}, f32[512,128]{1,0:T(8,128)S(1)}, f32[8,128]{1,0:T(8,128)S(1)...) custom-call(s32[1]{0:T(128)} %bitcast.4.refs_0_, bf16[128,1024]{1,0:T(8,128)(2,1)S(1)} %copy-done.80, ...), custom_call_target="tpu_custom_call" | custom-call | flops 12884901888 | bytes 10883072 | tf_op jit(solution)/shard_map/attend_backward/pallas_call | solution.py:86
  367.1 7.8 %collective-permute-done.89.refs_1_ = bf16[128,1024]{1,0:T(8,128)(2,1)S(1)} collective-permute-done((bf16[128,1024]{1,0:T(8,128)(2,1)S(1)}, bf16[128,1024]{1,0:T(8,128)(2,1)S(1)}, u32[]{:S(2)}, u32[]{:S(2)}) %collective-permute-start.89) | collective-permute-done | bytes 262176 | tf_op jit(solution)/shard_map/ppermute | solution.py:114
  376.6 3.5 collective-permute-done.94.refs_1_
  381.3 24.6 %collective-permute-done.95.refs_2_ = bf16[384,1024]{1,0:T(8,128)(2,1)S(1)} collective-permute-done((bf16[384,1024]{1,0:T(8,128)(2,1)S(1)}, bf16[384,1024]{1,0:T(8,128)(2,1)S(1)}, u32[]{:S(2)}, u32[]{:S(2)}) %collective-permute-start.95) | collective-permute-done | bytes 786464 | tf_op jit(solution)/shard_map/ppermute | solution.py:114
  405.9 5.0 collective-permute-done.92.refs_3_
  412.1 2.1 collective-permute-start.99
  416.7 4.5 collective-permute-done.100.refs_1_
  422.3 4.1 collective-permute-done.97.refs_1_
  428.6 5.0 feed_backward.3
  437.6 2.5 collective-permute-start.105
  440.7 2.5 collective-permute-start.108
  444.2 24.3 %collective-permute-done.106.refs_4_ = bf16[64,1024]{1,0:T(8,128)(2,1)S(1)} collective-permute-done((bf16[64,1024]{1,0:T(8,128)(2,1)S(1)}, bf16[64,1024]{1,0:T(8,128)(2,1)S(1)}, u32[]{:S(2)}, u32[]{:S(2)}) %collective-permute-start.106) | collective-permute-done | bytes 131104 | tf_op jit(solution)/shard_map/ppermute | solution.py:114
  474.6 11.7 %collective-permute-done.107.refs_1_ = bf16[64,1536]{1,0:T(8,128)(2,1)S(1)} collective-permute-done((bf16[64,1536]{1,0:T(8,128)(2,1)S(1)}, bf16[64,1536]{1,0:T(8,128)(2,1)S(1)}, u32[]{:S(2)}, u32[]{:S(2)}) %collective-permute-start.107) | collective-permute-done | bytes 196640 | tf_op jit(solution)/shard_map/ppermute | solution.py:114
  488.1 3.6 collective-permute-done.109.refs_1_
  495.2 3.1 all-to-all-start.1
  500.3 2.5 collective-permute-start.121
  507.4 32.8 %collective-permute-done.117.refs_1_ = bf16[96,1024]{1,0:T(8,128)(2,1)S(1)} collective-permute-done((bf16[96,1024]{1,0:T(8,128)(2,1)}, bf16[96,1024]{1,0:T(8,128)(2,1)S(1)}, u32[]{:S(2)}, u32[]{:S(2)}) %collective-permute-start.117) | collective-permute-done | bytes 196640 | tf_op jit(solution)/shard_map/ppermute | solution.py:114
  542.4 5.1 collective-permute-done.121.refs_2_
  549.2 5.1 collective-permute-done.116.refs_5_
  554.3 2.1 collective-permute-start.123
  556.4 2.3 collective-permute-start.113
  564.7 3.0 collective-permute-done.123.refs_1_
  578.7 3.0 collective-permute-done.126.refs_3_
  581.8 2.9 feed_final.1
  (526 shorter events, 179.1 us)
Async XLA Ops:
  10.5 25.7 %collective-permute-start.1 = (bf16[256,1024]{1,0:T(8,128)(2,1)S(1)}, bf16[256,1024]{1,0:T(8,128)(2,1)S(1)}, u32[]{:S(2)}, u32[]{:S(2)}) collective-permute-start(bf16[256,1024]{1,0:T(8,128)(2,1)S(1)} %pack_rows.4.refs_4_), channel_id=1, source_target_pairs={{0,8},{1,9},{2,10},{3,11},{4,12},{5,13},{6,14},{7,15},{8,0},{9,1},... | collective-permute-start | bytes 1572872 | tf_op jit(solution)/shard_map/ppermute | solution.py:114
  13.4 22.8 %collective-permute-start.2 = (bf16[256,1024]{1,0:T(8,128)(2,1)S(1)}, bf16[256,1024]{1,0:T(8,128)(2,1)}, u32[]{:S(2)}, u32[]{:S(2)}) collective-permute-start(bf16[256,1024]{1,0:T(8,128)(2,1)S(1)} %pack_rows.4.refs_4_), channel_id=1, source_target_pairs={{0,4},{1,5},{2,6},{3,7},{4,0},{5,1},{6,2},{7,3},{8,12},{9,13},{10,... | collective-permute-start | bytes 1572872 | tf_op jit(solution)/shard_map/ppermute | solution.py:114
  36.3 13.5 %collective-permute-start.8 = (bf16[256,1024]{1,0:T(8,128)(2,1)S(1)}, bf16[256,1024]{1,0:T(8,128)(2,1)}, u32[]{:S(2)}, u32[]{:S(2)}) collective-permute-start(bf16[256,1024]{1,0:T(8,128)(2,1)S(1)} %collective-permute-done.1.refs_6_), channel_id=1, source_target_pairs={{0,4},{1,5},{2,6},{3,7},{4,0},{5,1},{6,2},{7,3},{8,12},{9,13},{10,... | collective-permute-start | bytes 1572872 | tf_op jit(solution)/shard_map/ppermute | solution.py:114
  38.3 18.2 %collective-permute-start.9 = (bf16[256,1024]{1,0:T(8,128)(2,1)S(1)}, bf16[256,1024]{1,0:T(8,128)(2,1)}, u32[]{:S(2)}, u32[]{:S(2)}) collective-permute-start(bf16[256,1024]{1,0:T(8,128)(2,1)S(1)} %pack_rows.4.refs_4_), channel_id=1, source_target_pairs={{0,1},{1,0},{2,3},{3,2},{4,5},{5,4},{6,7},{7,6},{8,9},{9,8},{10,11... | collective-permute-start | bytes 1572872 | tf_op jit(solution)/shard_map/ppermute | solution.py:114
  38.4 20.8 %collective-permute-start.11 = (bf16[256,1024]{1,0:T(8,128)(2,1)S(1)}, bf16[256,1024]{1,0:T(8,128)(2,1)}, u32[]{:S(2)}, u32[]{:S(2)}) collective-permute-start(bf16[256,1024]{1,0:T(8,128)(2,1)S(1)} %collective-permute-done.1.refs_6_), channel_id=1, source_target_pairs={{0,1},{1,0},{2,3},{3,2},{4,5},{5,4},{6,7},{7,6},{8,9},{9,8},{10,11... | collective-permute-start | bytes 1572872 | tf_op jit(solution)/shard_map/ppermute | solution.py:114
  39.7 14.4 %all-to-all-start = ((bf16[16,2,1792]{2,1,0:T(2,128)(2,1)}), bf16[16,2,1792]{2,1,0:T(2,128)(2,1)S(1)}, u32[]{:S(2)}, u32[]{:S(2)}) async-start(bf16[16,2,1792]{2,1,0:T(2,128)(2,1)} %reshape.68), calls=%async_computation | async-start | bytes 229376 | tf_op jit(solution)/shard_map/all_to_all | solution.py:1516
  44.3 14.9 %collective-permute-start.10 = (bf16[256,1024]{1,0:T(8,128)(2,1)}, bf16[256,1024]{1,0:T(8,128)(2,1)}, u32[]{:S(2)}, u32[]{:S(2)}) collective-permute-start(bf16[256,1024]{1,0:T(8,128)(2,1)} %collective-permute-done.2.refs_5_), channel_id=1, source_target_pairs={{0,1},{1,0},{2,3},{3,2},{4,5},{5,4},{6,7},{7,6},{8,9},{9,8},{10,11... | collective-permute-start | bytes 1572872 | tf_op jit(solution)/shard_map/ppermute | solution.py:114
  55.1 19.8 %collective-permute-start.17 = (bf16[512,384]{1,0:T(8,128)(2,1)S(1)}, bf16[512,384]{1,0:T(8,128)(2,1)S(1)}, u32[]{:S(2)}, u32[]{:S(2)}) collective-permute-start(bf16[512,384]{1,0:T(8,128)(2,1)S(1)} %pad_maximum_fusion), channel_id=1, source_target_pairs={{0,8},{1,9},{2,10},{3,11},{4,12},{5,13},{6,14},{7,15},{8,0},{9,1},... | collective-permute-start | bytes 1179656 | tf_op jit(solution)/shard_map/ppermute | solution.py:114
  56.5 26.0 %collective-permute-start.16 = (bf16[256,384]{1,0:T(8,128)(2,1)S(1)}, bf16[256,384]{1,0:T(8,128)(2,1)S(1)}, u32[]{:S(2)}, u32[]{:S(2)}) collective-permute-start(bf16[256,384]{1,0:T(8,128)(2,1)S(1)} %get-tuple-element.350), channel_id=1, source_target_pairs={{0,4},{1,5},{2,6},{3,7},{4,0},{5,1},{6,2},{7,3},{8,12},{9,13},{10,... | collective-permute-start | bytes 589832 | tf_op jit(solution)/shard_map/ppermute | solution.py:114
  82.5 17.6 %collective-permute-start.24 = (bf16[128,1024]{1,0:T(8,128)(2,1)S(1)}, bf16[128,1024]{1,0:T(8,128)(2,1)S(1)}, u32[]{:S(2)}, u32[]{:S(2)}) collective-permute-start(bf16[128,1024]{1,0:T(8,128)(2,1)S(1)} %get-tuple-element.351.refs_1_), channel_id=1, source_target_pairs={{0,6},{1,7},{2,4},{3,5},{4,2},{5,3},{6,0},{7,1},{8,14},{9,15},{10,... | collective-permute-start | bytes 786440 | tf_op jit(solution)/shard_map/ppermute | solution.py:114
  83.7 16.4 %collective-permute-start.26 = (bf16[96,1024]{1,0:T(8,128)(2,1)S(1)}, bf16[96,1024]{1,0:T(8,128)(2,1)S(1)}, u32[]{:S(2)}, u32[]{:S(2)}) collective-permute-start(bf16[96,1024]{1,0:T(8,128)(2,1)S(1)} %conv_pick.1.refs_0_), channel_id=1, source_target_pairs={{0,4},{1,5},{2,6},{3,7},{4,0},{5,1},{6,2},{7,3},{8,12},{9,13},{10,... | collective-permute-start | bytes 589832 | tf_op jit(solution)/shard_map/ppermute | solution.py:114
  85.5 15.4 %collective-permute-start.27 = (bf16[96,1024]{1,0:T(8,128)(2,1)S(1)}, bf16[96,1024]{1,0:T(8,128)(2,1)S(1)}, u32[]{:S(2)}, u32[]{:S(2)}) collective-permute-start(bf16[96,1024]{1,0:T(8,128)(2,1)S(1)} %conv_pick.1.refs_0_), channel_id=1, source_target_pairs={{0,8},{1,9},{2,10},{3,11},{4,12},{5,13},{6,14},{7,15},{8,0},{9,1},... | collective-permute-start | bytes 589832 | tf_op jit(solution)/shard_map/ppermute | solution.py:114
  87.1 15.8 %collective-permute-start.20 = (bf16[128,1024]{1,0:T(8,128)(2,1)S(1)}, bf16[128,1024]{1,0:T(8,128)(2,1)S(1)}, u32[]{:S(2)}, u32[]{:S(2)}) collective-permute-start(bf16[128,1024]{1,0:T(8,128)(2,1)S(1)} %get-tuple-element.351.refs_1_), channel_id=1, source_target_pairs={{0,2},{1,3},{2,0},{3,1},{4,6},{5,7},{6,4},{7,5},{8,10},{9,11},{10,... | collective-permute-start | bytes 786440 | tf_op jit(solution)/shard_map/ppermute | solution.py:114
  87.6 29.1 %collective-permute-start.29 = (bf16[512,384]{1,0:T(8,128)(2,1)S(1)}, bf16[512,384]{1,0:T(8,128)(2,1)S(1)}, u32[]{:S(2)}, u32[]{:S(2)}) collective-permute-start(bf16[512,384]{1,0:T(8,128)(2,1)S(1)} %get-tuple-element.360), channel_id=1, source_target_pairs={{0,1},{1,0},{2,3},{3,2},{4,5},{5,4},{6,7},{7,6},{8,9},{9,8},{10,11... | collective-permute-start | bytes 1179656 | tf_op jit(solution)/shard_map/ppermute | solution.py:114
  100.1 14.4 %collective-permute-start.25 = (bf16[128,1024]{1,0:T(8,128)(2,1)S(1)}, bf16[128,1024]{1,0:T(8,128)(2,1)S(1)}, u32[]{:S(2)}, u32[]{:S(2)}) collective-permute-start(bf16[128,1024]{1,0:T(8,128)(2,1)S(1)} %collective-permute-done.24.refs_7_), channel_id=1, source_target_pairs={{0,1},{1,0},{2,3},{3,2},{4,5},{5,4},{6,7},{7,6},{8,9},{9,8},{10,11... | collective-permute-start | bytes 786440 | tf_op jit(solution)/shard_map/ppermute | solution.py:114
  100.8 13.7 %collective-permute-start.28 = (bf16[96,1024]{1,0:T(8,128)(2,1)S(1)}, bf16[96,1024]{1,0:T(8,128)(2,1)S(1)}, u32[]{:S(2)}, u32[]{:S(2)}) collective-permute-start(bf16[96,1024]{1,0:T(8,128)(2,1)S(1)} %collective-permute-done.27.refs_2_), channel_id=1, source_target_pairs={{0,4},{1,5},{2,6},{3,7},{4,0},{5,1},{6,2},{7,3},{8,12},{9,13},{10,... | collective-permute-start | bytes 589832 | tf_op jit(solution)/shard_map/ppermute | solution.py:114
  115.1 25.3 %collective-permute-start.33 = (bf16[384,1024]{1,0:T(8,128)(2,1)S(1)}, bf16[384,1024]{1,0:T(8,128)(2,1)}, u32[]{:S(2)}, u32[]{:S(2)}) collective-permute-start(bf16[384,1024]{1,0:T(8,128)(2,1)S(1)} %pack_rows.6.refs_6_.refs_0_), channel_id=1, source_target_pairs={{0,16},{1,17},{2,18},{3,19},{4,20},{5,21},{6,22},{7,23},{8,24},{9,... | collective-permute-start | bytes 2359304 | tf_op jit(solution)/shard_map/ppermute | solution.py:114
  116.7 23.7 %collective-permute-start.34 = (bf16[384,1024]{1,0:T(8,128)(2,1)S(1)}, bf16[384,1024]{1,0:T(8,128)(2,1)}, u32[]{:S(2)}, u32[]{:S(2)}) collective-permute-start(bf16[384,1024]{1,0:T(8,128)(2,1)S(1)} %pack_rows.6.refs_6_.refs_0_), channel_id=1, source_target_pairs={{0,2},{1,3},{2,0},{3,1},{4,6},{5,7},{6,4},{7,5},{8,10},{9,11},{10,... | collective-permute-start | bytes 2359304 | tf_op jit(solution)/shard_map/ppermute | solution.py:114
  117.8 22.6 %collective-permute-start.31 = (bf16[128,1024]{1,0:T(8,128)(2,1)}, bf16[128,1024]{1,0:T(8,128)(2,1)S(1)}, u32[]{:S(2)}, u32[]{:S(2)}) collective-permute-start(bf16[128,1024]{1,0:T(8,128)(2,1)} %pack_rows.5.refs_4_), channel_id=1, source_target_pairs={{0,8},{1,9},{2,10},{3,11},{4,12},{5,13},{6,14},{7,15},{8,0},{9,1},... | collective-permute-start | bytes 786440 | tf_op jit(solution)/shard_map/ppermute | solution.py:114
  118.4 22.0 %collective-permute-start.32 = (bf16[128,1024]{1,0:T(8,128)(2,1)}, bf16[128,1024]{1,0:T(8,128)(2,1)S(1)}, u32[]{:S(2)}, u32[]{:S(2)}) collective-permute-start(bf16[128,1024]{1,0:T(8,128)(2,1)} %pack_rows.5.refs_4_), channel_id=1, source_target_pairs={{0,4},{1,5},{2,6},{3,7},{4,0},{5,1},{6,2},{7,3},{8,12},{9,13},{10,... | collective-permute-start | bytes 786440 | tf_op jit(solution)/shard_map/ppermute | solution.py:114
  140.4 23.1 %collective-permute-start.35 = (bf16[512,1024]{1,0:T(8,128)(2,1)S(1)}, bf16[512,1024]{1,0:T(8,128)(2,1)S(1)}, u32[]{:S(2)}, u32[]{:S(2)}) collective-permute-start(bf16[512,1024]{1,0:T(8,128)(2,1)S(1)} %get-tuple-element.372), channel_id=1, source_target_pairs={{0,1},{1,0},{2,3},{3,2},{4,5},{5,4},{6,7},{7,6},{8,9},{9,8},{10,11... | collective-permute-start | bytes 3145736 | tf_op jit(solution)/shard_map/ppermute | solution.py:114
  143.4 21.7 %collective-permute-start.41 = (bf16[384,1024]{1,0:T(8,128)(2,1)S(1)}, bf16[384,1024]{1,0:T(8,128)(2,1)S(1)}, u32[]{:S(2)}, u32[]{:S(2)}) collective-permute-start(bf16[384,1024]{1,0:T(8,128)(2,1)S(1)} %pack_rows.6.refs_6_.refs_0_), channel_id=1, source_target_pairs={{0,1},{1,0},{2,3},{3,2},{4,5},{5,4},{6,7},{7,6},{8,9},{9,8},{10,11... | collective-permute-start | bytes 2359304 | tf_op jit(solution)/shard_map/ppermute | solution.py:114
  143.4 23.2 %collective-permute-start.42 = (bf16[384,1024]{1,0:T(8,128)(2,1)}, bf16[384,1024]{1,0:T(8,128)(2,1)S(1)}, u32[]{:S(2)}, u32[]{:S(2)}) collective-permute-start(bf16[384,1024]{1,0:T(8,128)(2,1)} %collective-permute-done.33.refs_7_.refs_1_), channel_id=1, source_target_pairs={{0,1},{1,0},{2,3},{3,2},{4,5},{5,4},{6,7},{7,6},{8,9},{9,8},{10,11... | collective-permute-start | bytes 2359304 | tf_op jit(solution)/shard_map/ppermute | solution.py:114
  143.9 23.3 %collective-permute-start.43 = (bf16[384,1024]{1,0:T(8,128)(2,1)}, bf16[384,1024]{1,0:T(8,128)(2,1)S(1)}, u32[]{:S(2)}, u32[]{:S(2)}) collective-permute-start(bf16[384,1024]{1,0:T(8,128)(2,1)} %collective-permute-done.34.refs_8_.refs_2_), channel_id=1, source_target_pairs={{0,1},{1,0},{2,3},{3,2},{4,5},{5,4},{6,7},{7,6},{8,9},{9,8},{10,11... | collective-permute-start | bytes 2359304 | tf_op jit(solution)/shard_map/ppermute | solution.py:114
  165.1 13.9 %collective-permute-start.38 = (bf16[128,1024]{1,0:T(8,128)(2,1)S(1)}, bf16[128,1024]{1,0:T(8,128)(2,1)S(1)}, u32[]{:S(2)}, u32[]{:S(2)}) collective-permute-start(bf16[128,1024]{1,0:T(8,128)(2,1)S(1)} %get-tuple-element.376), channel_id=1, source_target_pairs={{0,2},{1,3},{2,0},{3,1},{4,6},{5,7},{6,4},{7,5},{8,10},{9,11},{10,... | collective-permute-start | bytes 786440 | tf_op jit(solution)/shard_map/ppermute | solution.py:114
  189.0 15.0 %collective-permute-start.47 = (bf16[128,1024]{1,0:T(8,128)(2,1)S(1)}, bf16[128,1024]{1,0:T(8,128)(2,1)S(1)}, u32[]{:S(2)}, u32[]{:S(2)}) collective-permute-start(bf16[128,1024]{1,0:T(8,128)(2,1)S(1)} %copy-done.58), channel_id=1, source_target_pairs={{0,8},{1,9},{2,10},{3,11},{4,12},{5,13},{6,14},{7,15},{8,0},{9,1},... | collective-permute-start | bytes 786440 | tf_op jit(solution)/shard_map/ppermute | solution.py:114
  192.8 15.4 %collective-permute-start.53 = (bf16[128,1024]{1,0:T(8,128)(2,1)}, bf16[128,1024]{1,0:T(8,128)(2,1)S(1)}, u32[]{:S(2)}, u32[]{:S(2)}) collective-permute-start(bf16[128,1024]{1,0:T(8,128)(2,1)} %pack_rows.5.refs_4_), channel_id=1, source_target_pairs={{0,1},{1,0},{2,3},{3,2},{4,5},{5,4},{6,7},{7,6},{8,9},{9,8},{10,11... | collective-permute-start | bytes 786440 | tf_op jit(solution)/shard_map/ppermute | solution.py:114
  194.0 15.4 %collective-permute-start.58 = (bf16[128,1024]{1,0:T(8,128)(2,1)S(1)}, bf16[128,1024]{1,0:T(8,128)(2,1)S(1)}, u32[]{:S(2)}, u32[]{:S(2)}) collective-permute-start(bf16[128,1024]{1,0:T(8,128)(2,1)S(1)} %copy-done.58), channel_id=1, source_target_pairs={{0,1},{1,0},{2,3},{3,2},{4,5},{5,4},{6,7},{7,6},{8,9},{9,8},{10,11... | collective-permute-start | bytes 786440 | tf_op jit(solution)/shard_map/ppermute | solution.py:114
  269.9 13.9 %collective-permute-start.70 = (bf16[128,1024]{1,0:T(8,128)(2,1)S(1)}, bf16[128,1024]{1,0:T(8,128)(2,1)S(1)}, u32[]{:S(2)}, u32[]{:S(2)}) collective-permute-start(bf16[128,1024]{1,0:T(8,128)(2,1)S(1)} %get-tuple-element.424), channel_id=1, source_target_pairs={{0,2},{1,3},{2,0},{3,1},{4,6},{5,7},{6,4},{7,5},{8,10},{9,11},{10,... | collective-permute-start | bytes 786440 | tf_op jit(solution)/shard_map/ppermute | solution.py:114
  271.4 14.4 %collective-permute-start.68 = (bf16[128,1024]{1,0:T(8,128)(2,1)S(1)}, bf16[128,1024]{1,0:T(8,128)(2,1)S(1)}, u32[]{:S(2)}, u32[]{:S(2)}) collective-permute-start(bf16[128,1024]{1,0:T(8,128)(2,1)S(1)} %get-tuple-element.422), channel_id=1, source_target_pairs={{0,18},{1,19},{2,16},{3,17},{4,22},{5,23},{6,20},{7,21},{8,26},{9,... | collective-permute-start | bytes 786440 | tf_op jit(solution)/shard_map/ppermute | solution.py:114
  272.6 13.3 %collective-permute-start.69 = (bf16[128,1024]{1,0:T(8,128)(2,1)S(1)}, bf16[128,1024]{1,0:T(8,128)(2,1)S(1)}, u32[]{:S(2)}, u32[]{:S(2)}) collective-permute-start(bf16[128,1024]{1,0:T(8,128)(2,1)S(1)} %get-tuple-element.423), channel_id=1, source_target_pairs={{0,16},{1,17},{2,18},{3,19},{4,20},{5,21},{6,22},{7,23},{8,24},{9,... | collective-permute-start | bytes 786440 | tf_op jit(solution)/shard_map/ppermute | solution.py:114
  283.8 17.0 %collective-permute-start.74 = (bf16[128,1024]{1,0:T(8,128)(2,1)}, bf16[128,1024]{1,0:T(8,128)(2,1)S(1)}, u32[]{:S(2)}, u32[]{:S(2)}) collective-permute-start(bf16[128,1024]{1,0:T(8,128)(2,1)} %get-tuple-element.443), channel_id=1, source_target_pairs={{0,4},{1,5},{2,6},{3,7},{4,0},{5,1},{6,2},{7,3},{8,12},{9,13},{10,... | collective-permute-start | bytes 786440 | tf_op jit(solution)/shard_map/ppermute | solution.py:114
  284.8 16.1 %collective-permute-start.75 = (bf16[128,1024]{1,0:T(8,128)(2,1)}, bf16[128,1024]{1,0:T(8,128)(2,1)}, u32[]{:S(2)}, u32[]{:S(2)}) collective-permute-start(bf16[128,1024]{1,0:T(8,128)(2,1)} %get-tuple-element.445), channel_id=1, source_target_pairs={{0,4},{1,5},{2,6},{3,7},{4,0},{5,1},{6,2},{7,3},{8,12},{9,13},{10,... | collective-permute-start | bytes 786440 | tf_op jit(solution)/shard_map/ppermute | solution.py:114
  298.8 15.5 %collective-permute-start.76 = (bf16[128,1024]{1,0:T(8,128)(2,1)}, bf16[128,1024]{1,0:T(8,128)(2,1)S(1)}, u32[]{:S(2)}, u32[]{:S(2)}) collective-permute-start(bf16[128,1024]{1,0:T(8,128)(2,1)} %copy-done.83), channel_id=1, source_target_pairs={{0,4},{1,5},{2,6},{3,7},{4,0},{5,1},{6,2},{7,3},{8,12},{9,13},{10,... | collective-permute-start | bytes 786440 | tf_op jit(solution)/shard_map/ppermute | solution.py:114
  300.7 13.6 %collective-permute-start.77 = (bf16[128,1024]{1,0:T(8,128)(2,1)}, bf16[128,1024]{1,0:T(8,128)(2,1)S(1)}, u32[]{:S(2)}, u32[]{:S(2)}) collective-permute-start(bf16[128,1024]{1,0:T(8,128)(2,1)} %copy-done.86), channel_id=1, source_target_pairs={{0,4},{1,5},{2,6},{3,7},{4,0},{5,1},{6,2},{7,3},{8,12},{9,13},{10,... | collective-permute-start | bytes 786440 | tf_op jit(solution)/shard_map/ppermute | solution.py:114
  314.3 17.1 %collective-permute-start.85 = (bf16[1536,1024]{1,0:T(8,128)(2,1)S(1)}, bf16[1536,1024]{1,0:T(8,128)(2,1)S(1)}, u32[]{:S(2)}, u32[]{:S(2)}) collective-permute-start(bf16[1536,1024]{1,0:T(8,128)(2,1)S(1)} %get-tuple-element.466), channel_id=1, source_target_pairs={{0,1},{1,0},{2,3},{3,2},{4,5},{5,4},{6,7},{7,6},{8,9},{9,8},{10,11... | collective-permute-start | bytes 9437192 | tf_op jit(solution)/shard_map/ppermute | solution.py:114
  317.1 13.6 %collective-permute-start.79 = (bf16[128,1024]{1,0:T(8,128)(2,1)S(1)}, bf16[128,1024]{1,0:T(8,128)(2,1)S(1)}, u32[]{:S(2)}, u32[]{:S(2)}) collective-permute-start(bf16[128,1024]{1,0:T(8,128)(2,1)S(1)} %copy-done.80), channel_id=1, source_target_pairs={{0,2},{1,3},{2,0},{3,1},{4,6},{5,7},{6,4},{7,5},{8,10},{9,11},{10,... | collective-permute-start | bytes 786440 | tf_op jit(solution)/shard_map/ppermute | solution.py:114
  332.1 27.5 %collective-permute-start.86 = (bf16[128,1024]{1,0:T(8,128)(2,1)S(1)}, bf16[128,1024]{1,0:T(8,128)(2,1)S(1)}, u32[]{:S(2)}, u32[]{:S(2)}) collective-permute-start(bf16[128,1024]{1,0:T(8,128)(2,1)S(1)} %plane_add.10), channel_id=1, source_target_pairs={{0,8},{1,9},{2,10},{3,11},{4,12},{5,13},{6,14},{7,15},{8,0},{9,1},... | collective-permute-start | bytes 786440 | tf_op jit(solution)/shard_map/ppermute | solution.py:114
  334.7 24.9 %collective-permute-start.87 = (bf16[128,1024]{1,0:T(8,128)(2,1)S(1)}, bf16[128,1024]{1,0:T(8,128)(2,1)S(1)}, u32[]{:S(2)}, u32[]{:S(2)}) collective-permute-start(bf16[128,1024]{1,0:T(8,128)(2,1)S(1)} %plane_add.11), channel_id=1, source_target_pairs={{0,8},{1,9},{2,10},{3,11},{4,12},{5,13},{6,14},{7,15},{8,0},{9,1},... | collective-permute-start | bytes 786440 | tf_op jit(solution)/shard_map/ppermute | solution.py:114
  359.7 20.4 %collective-permute-start.94 = (bf16[384,1024]{1,0:T(8,128)(2,1)S(1)}, bf16[384,1024]{1,0:T(8,128)(2,1)S(1)}, u32[]{:S(2)}, u32[]{:S(2)}) collective-permute-start(bf16[384,1024]{1,0:T(8,128)(2,1)S(1)} %get-tuple-element.501), channel_id=1, source_target_pairs={{0,16},{1,17},{2,18},{3,19},{4,20},{5,21},{6,22},{7,23},{8,24},{9,... | collective-permute-start | bytes 2359304 | tf_op jit(solution)/shard_map/ppermute | solution.py:114
  363.1 42.8 %collective-permute-start.95 = (bf16[384,1024]{1,0:T(8,128)(2,1)S(1)}, bf16[384,1024]{1,0:T(8,128)(2,1)S(1)}, u32[]{:S(2)}, u32[]{:S(2)}) collective-permute-start(bf16[384,1024]{1,0:T(8,128)(2,1)S(1)} %get-tuple-element.502), channel_id=1, source_target_pairs={{0,2},{1,3},{2,0},{3,1},{4,6},{5,7},{6,4},{7,5},{8,10},{9,11},{10,... | collective-permute-start | bytes 2359304 | tf_op jit(solution)/shard_map/ppermute | solution.py:114
  364.5 41.4 %collective-permute-start.96 = (bf16[384,1024]{1,0:T(8,128)(2,1)S(1)}, bf16[384,1024]{1,0:T(8,128)(2,1)S(1)}, u32[]{:S(2)}, u32[]{:S(2)}) collective-permute-start(bf16[384,1024]{1,0:T(8,128)(2,1)S(1)} %get-tuple-element.503), channel_id=1, source_target_pairs={{0,18},{1,19},{2,16},{3,17},{4,22},{5,23},{6,20},{7,21},{8,26},{9,... | collective-permute-start | bytes 2359304 | tf_op jit(solution)/shard_map/ppermute | solution.py:114
  375.0 36.0 %collective-permute-start.93 = (bf16[256,768]{1,0:T(8,128)(2,1)S(1)}, bf16[256,768]{1,0:T(8,128)(2,1)S(1)}, u32[]{:S(2)}, u32[]{:S(2)}) collective-permute-start(bf16[256,768]{1,0:T(8,128)(2,1)S(1)} %get-tuple-element.499), channel_id=1, source_target_pairs={{0,4},{1,5},{2,6},{3,7},{4,0},{5,1},{6,2},{7,3},{8,12},{9,13},{10,... | collective-permute-start | bytes 1179656 | tf_op jit(solution)/shard_map/ppermute | solution.py:114
  376.2 34.8 %collective-permute-start.92 = (bf16[128,1024]{1,0:T(8,128)(2,1)S(1)}, bf16[128,1024]{1,0:T(8,128)(2,1)S(1)}, u32[]{:S(2)}, u32[]{:S(2)}) collective-permute-start(bf16[128,1024]{1,0:T(8,128)(2,1)S(1)} %get-tuple-element.498), channel_id=1, source_target_pairs={{0,2},{1,3},{2,0},{3,1},{4,6},{5,7},{6,4},{7,5},{8,10},{9,11},{10,... | collective-permute-start | bytes 786440 | tf_op jit(solution)/shard_map/ppermute | solution.py:114
  380.1 31.3 %collective-permute-start.91 = (bf16[128,1024]{1,0:T(8,128)(2,1)S(1)}, bf16[128,1024]{1,0:T(8,128)(2,1)S(1)}, u32[]{:S(2)}, u32[]{:S(2)}) collective-permute-start(bf16[128,1024]{1,0:T(8,128)(2,1)S(1)} %get-tuple-element.497), channel_id=1, source_target_pairs={{0,4},{1,5},{2,6},{3,7},{4,0},{5,1},{6,2},{7,3},{8,12},{9,13},{10,... | collective-permute-start | bytes 786440 | tf_op jit(solution)/shard_map/ppermute | solution.py:114
  436.9 35.9 %collective-permute-start.110 = (bf16[512,1024]{1,0:T(8,128)(2,1)S(1)}, bf16[512,1024]{1,0:T(8,128)(2,1)S(1)}, u32[]{:S(2)}, u32[]{:S(2)}) collective-permute-start(bf16[512,1024]{1,0:T(8,128)(2,1)S(1)} %get-tuple-element.560), channel_id=1, source_target_pairs={{0,1},{1,0},{2,3},{3,2},{4,5},{5,4},{6,7},{7,6},{8,9},{9,8},{10,11... | collective-permute-start | bytes 3145736 | tf_op jit(solution)/shard_map/ppermute | solution.py:114
  437.6 32.2 %collective-permute-start.105 = (bf16[256,768]{1,0:T(8,128)(2,1)S(1)}, bf16[256,768]{1,0:T(8,128)(2,1)S(1)}, u32[]{:S(2)}, u32[]{:S(2)}) collective-permute-start(bf16[256,768]{1,0:T(8,128)(2,1)S(1)} %pad_maximum_fusion.1), channel_id=1, source_target_pairs={{0,8},{1,9},{2,10},{3,11},{4,12},{5,13},{6,14},{7,15},{8,0},{9,1},... | collective-permute-start | bytes 1179656 | tf_op jit(solution)/shard_map/ppermute | solution.py:114
  440.1 28.4 %collective-permute-start.106 = (bf16[64,1024]{1,0:T(8,128)(2,1)S(1)}, bf16[64,1024]{1,0:T(8,128)(2,1)S(1)}, u32[]{:S(2)}, u32[]{:S(2)}) collective-permute-start(bf16[64,1024]{1,0:T(8,128)(2,1)S(1)} %get-tuple-element.546), channel_id=1, source_target_pairs={{0,8},{1,9},{2,10},{3,11},{4,12},{5,13},{6,14},{7,15},{8,0},{9,1},... | collective-permute-start | bytes 393224 | tf_op jit(solution)/shard_map/ppermute | solution.py:114
  440.7 33.6 %collective-permute-start.108 = (bf16[96,1024]{1,0:T(8,128)(2,1)S(1)}, bf16[96,1024]{1,0:T(8,128)(2,1)S(1)}, u32[]{:S(2)}, u32[]{:S(2)}) collective-permute-start(bf16[96,1024]{1,0:T(8,128)(2,1)S(1)} %plane_add.12), channel_id=1, source_target_pairs={{0,8},{1,9},{2,10},{3,11},{4,12},{5,13},{6,14},{7,15},{8,0},{9,1},... | collective-permute-start | bytes 589832 | tf_op jit(solution)/shard_map/ppermute | solution.py:114
  443.2 28.2 %collective-permute-start.111 = (bf16[128,1024]{1,0:T(8,128)(2,1)S(1)}, bf16[128,1024]{1,0:T(8,128)(2,1)S(1)}, u32[]{:S(2)}, u32[]{:S(2)}) collective-permute-start(bf16[128,1024]{1,0:T(8,128)(2,1)S(1)} %get-tuple-element.562), channel_id=1, source_target_pairs={{0,4},{1,5},{2,6},{3,7},{4,0},{5,1},{6,2},{7,3},{8,12},{9,13},{10,... | collective-permute-start | bytes 786440 | tf_op jit(solution)/shard_map/ppermute | solution.py:114
  468.5 23.2 %collective-permute-start.102 = (bf16[128,1024]{1,0:T(8,128)(2,1)S(1)}, bf16[128,1024]{1,0:T(8,128)(2,1)S(1)}, u32[]{:S(2)}, u32[]{:S(2)}) collective-permute-start(bf16[128,1024]{1,0:T(8,128)(2,1)S(1)} %get-tuple-element.538), channel_id=1, source_target_pairs={{0,18},{1,19},{2,16},{3,17},{4,22},{5,23},{6,20},{7,21},{8,26},{9,... | collective-permute-start | bytes 786440 | tf_op jit(solution)/shard_map/ppermute | solution.py:114
  469.8 21.9 %collective-permute-start.103 = (bf16[128,1024]{1,0:T(8,128)(2,1)S(1)}, bf16[128,1024]{1,0:T(8,128)(2,1)S(1)}, u32[]{:S(2)}, u32[]{:S(2)}) collective-permute-start(bf16[128,1024]{1,0:T(8,128)(2,1)S(1)} %get-tuple-element.539), channel_id=1, source_target_pairs={{0,16},{1,17},{2,18},{3,19},{4,20},{5,21},{6,22},{7,23},{8,24},{9,... | collective-permute-start | bytes 786440 | tf_op jit(solution)/shard_map/ppermute | solution.py:114
  471.4 16.7 %collective-permute-start.104 = (bf16[128,1024]{1,0:T(8,128)(2,1)S(1)}, bf16[128,1024]{1,0:T(8,128)(2,1)S(1)}, u32[]{:S(2)}, u32[]{:S(2)}) collective-permute-start(bf16[128,1024]{1,0:T(8,128)(2,1)S(1)} %get-tuple-element.540), channel_id=1, source_target_pairs={{0,2},{1,3},{2,0},{3,1},{4,6},{5,7},{6,4},{7,5},{8,10},{9,11},{10,... | collective-permute-start | bytes 786440 | tf_op jit(solution)/shard_map/ppermute | solution.py:114
  472.8 13.4 %collective-permute-start.107 = (bf16[64,1536]{1,0:T(8,128)(2,1)S(1)}, bf16[64,1536]{1,0:T(8,128)(2,1)S(1)}, u32[]{:S(2)}, u32[]{:S(2)}) collective-permute-start(bf16[64,1536]{1,0:T(8,128)(2,1)S(1)} %get-tuple-element.552), channel_id=1, source_target_pairs={{0,2},{1,3},{2,0},{3,1},{4,6},{5,7},{6,4},{7,5},{8,10},{9,11},{10,... | collective-permute-start | bytes 589832 | tf_op jit(solution)/shard_map/ppermute | solution.py:114
  474.4 17.3 %collective-permute-start.112 = (bf16[128,1024]{1,0:T(8,128)(2,1)S(1)}, bf16[128,1024]{1,0:T(8,128)(2,1)S(1)}, u32[]{:S(2)}, u32[]{:S(2)}) collective-permute-start(bf16[128,1024]{1,0:T(8,128)(2,1)S(1)} %get-tuple-element.565), channel_id=1, source_target_pairs={{0,4},{1,5},{2,6},{3,7},{4,0},{5,1},{6,2},{7,3},{8,12},{9,13},{10,... | collective-permute-start | bytes 786440 | tf_op jit(solution)/shard_map/ppermute | solution.py:114
  495.2 68.3 %all-to-all-start.1 = ((f32[32,96,128]{2,1,0:T(8,128)}), f32[32,96,128]{2,1,0:T(8,128)S(1)}, u32[]{:S(2)}, u32[]{:S(2)}) async-start(f32[32,96,128]{2,1,0:T(8,128)} %small_pack.1), calls=%async_computation.1 | async-start | bytes 3145728 | tf_op jit(solution)/shard_map/all_to_all | solution.py:1604
  498.4 43.7 %collective-permute-start.120 = (bf16[128,1024]{1,0:T(8,128)(2,1)}, bf16[128,1024]{1,0:T(8,128)(2,1)S(1)}, u32[]{:S(2)}, u32[]{:S(2)}) collective-permute-start(bf16[128,1024]{1,0:T(8,128)(2,1)} %copy-done.68), channel_id=1, source_target_pairs={{0,4},{1,5},{2,6},{3,7},{4,0},{5,1},{6,2},{7,3},{8,12},{9,13},{10,... | collective-permute-start | bytes 786440 | tf_op jit(solution)/shard_map/ppermute | solution.py:114
  500.3 47.2 %collective-permute-start.121 = (bf16[128,1024]{1,0:T(8,128)(2,1)S(1)}, bf16[128,1024]{1,0:T(8,128)(2,1)S(1)}, u32[]{:S(2)}, u32[]{:S(2)}) collective-permute-start(bf16[128,1024]{1,0:T(8,128)(2,1)S(1)} %plane_add.17), channel_id=1, source_target_pairs={{0,8},{1,9},{2,10},{3,11},{4,12},{5,13},{6,14},{7,15},{8,0},{9,1},... | collective-permute-start | bytes 786440 | tf_op jit(solution)/shard_map/ppermute | solution.py:114
  502.8 37.5 %collective-permute-start.117 = (bf16[96,1024]{1,0:T(8,128)(2,1)}, bf16[96,1024]{1,0:T(8,128)(2,1)S(1)}, u32[]{:S(2)}, u32[]{:S(2)}) collective-permute-start(bf16[96,1024]{1,0:T(8,128)(2,1)} %copy-done.89), channel_id=1, source_target_pairs={{0,4},{1,5},{2,6},{3,7},{4,0},{5,1},{6,2},{7,3},{8,12},{9,13},{10,... | collective-permute-start | bytes 589832 | tf_op jit(solution)/shard_map/ppermute | solution.py:114
  505.3 62.4 %collective-permute-start.119 = (bf16[256,1024]{1,0:T(8,128)(2,1)S(1)}, bf16[256,1024]{1,0:T(8,128)(2,1)}, u32[]{:S(2)}, u32[]{:S(2)}) collective-permute-start(bf16[256,1024]{1,0:T(8,128)(2,1)S(1)} %pack_rows.7), channel_id=1, source_target_pairs={{0,16},{1,17},{2,18},{3,19},{4,20},{5,21},{6,22},{7,23},{8,24},{9,... | collective-permute-start | bytes 1572872 | tf_op jit(solution)/shard_map/ppermute | solution.py:114
  506.9 49.6 %collective-permute-start.114 = (bf16[64,1536]{1,0:T(8,128)(2,1)S(1)}, bf16[64,1536]{1,0:T(8,128)(2,1)S(1)}, u32[]{:S(2)}, u32[]{:S(2)}) collective-permute-start(bf16[64,1536]{1,0:T(8,128)(2,1)S(1)} %copy-done.35), channel_id=1, source_target_pairs={{0,16},{1,17},{2,18},{3,19},{4,20},{5,21},{6,22},{7,23},{8,24},{9,... | collective-permute-start | bytes 589832 | tf_op jit(solution)/shard_map/ppermute | solution.py:114
  540.3 18.4 %collective-permute-start.118 = (bf16[96,1024]{1,0:T(8,128)(2,1)S(1)}, bf16[96,1024]{1,0:T(8,128)(2,1)S(1)}, u32[]{:S(2)}, u32[]{:S(2)}) collective-permute-start(bf16[96,1024]{1,0:T(8,128)(2,1)S(1)} %plane_add.15.mine_ref), channel_id=1, source_target_pairs={{0,16},{1,17},{2,18},{3,19},{4,20},{5,21},{6,22},{7,23},{8,24},{9,... | collective-permute-start | bytes 589832 | tf_op jit(solution)/shard_map/ppermute | solution.py:114
  542.2 19.5 %collective-permute-start.115 = (bf16[64,1536]{1,0:T(8,128)(2,1)S(1)}, bf16[64,1536]{1,0:T(8,128)(2,1)S(1)}, u32[]{:S(2)}, u32[]{:S(2)}) collective-permute-start(bf16[64,1536]{1,0:T(8,128)(2,1)S(1)} %copy-done.37), channel_id=1, source_target_pairs={{0,16},{1,17},{2,18},{3,19},{4,20},{5,21},{6,22},{7,23},{8,24},{9,... | collective-permute-start | bytes 589832 | tf_op jit(solution)/shard_map/ppermute | solution.py:114
  554.3 13.4 %collective-permute-start.123 = (bf16[128,1024]{1,0:T(8,128)(2,1)}, bf16[128,1024]{1,0:T(8,128)(2,1)}, u32[]{:S(2)}, u32[]{:S(2)}) collective-permute-start(bf16[128,1024]{1,0:T(8,128)(2,1)} %get-tuple-element.599), channel_id=1, source_target_pairs={{0,4},{1,5},{2,6},{3,7},{4,0},{5,1},{6,2},{7,3},{8,12},{9,13},{10,... | collective-permute-start | bytes 786440 | tf_op jit(solution)/shard_map/ppermute | solution.py:114
  (183 other events, 2443.4 us)

commit v5 on v4

--- a/solution.py
+++ b/solution.py
@@ -109,6 +109,11 @@
     return lax.optimization_barrier(values)
 
 
+def tied_lists(*lists):
+    flat = iter(tied(*[item for values in lists for item in values]))
+    return [[next(flat) for _ in values] for values in lists]
+
+
 def flipped(value, mask):
     total = lax.axis_size("rep") * lax.axis_size("shard")
     return lax.ppermute(value, ("rep", "shard"), [(i, i ^ mask) for i in range(total)])
@@ -330,12 +335,6 @@
     value, *flat = tied(value, *flat)
     flat = iter(flat)
     return value, [[next(flat) for _ in lists[top]] for lists in all_lists]
-
-
-def tied_tops_with(value, other, lists, place):
-    top = place.planes // 2
-    value, other, *flat = tied(value, other, *lists[top])
-    return value, other, [flat]
 
 
 def plane_total(values):
@@ -676,6 +675,7 @@
             pltpu.VMEM((length, width), BF),
             pltpu.VMEM((rows, length + 2 * rows), F32),
         ],
+        limit=56,
         flops=48 * length * length * width,
     )
     return (hidden, mixed, context, peaks), kept, sent
@@ -814,53 +814,63 @@
     return own, flipped(other.reshape(4 * rows, columns), 2).reshape(own.shape)
 
 
-def attend_arrange(own, arrived, place):
+def attend_arrange(own, arrived, glue, place):
     unit, columns = place.unit, own.shape[2]
-
-    def arrange(spot, own_ref, arrived_ref, *outs):
+    size = 4 * unit
+
+    def arrange(spot, own_ref, arrived_ref, glue_ref, near_out, one, two):
         low, core = spot[0] & 1, spot[2]
-        for step, out in enumerate(outs):
-            for near in range(2):
-                source = pl.ds(pl.multiple_of((core ^ near) * unit, unit), unit)
-                for turn, ref in enumerate((own_ref, arrived_ref)):
-                    start = (2 * near + turn) * unit
-                    out[start : start + unit, :] = ref[low ^ step, source, :]
-
-    near, far = kernel_call(
+        for near in range(2):
+            source = pl.ds(pl.multiple_of((core ^ near) * unit, unit), unit)
+            for turn, ref in enumerate((own_ref, arrived_ref)):
+                start = (2 * near + turn) * unit
+                mine, other = ref[low, source, :], ref[low ^ 1, source, :]
+                near_out[start : start + unit, :] = mine
+                two[start : start + unit, :] = mine
+                two[size + start : size + start + unit, :] = other
+                one[start : start + unit, :] = other
+        one[size:, :] = glue_ref[...]
+        two[2 * size :, :] = glue_ref[...]
+
+    count = glue.shape[0]
+    return kernel_call(
         arrange,
         "attend_columns",
-        [shape_of(4 * unit, columns, BF)] * 2,
-        (place.spot, own, arrived),
+        [
+            shape_of(size, columns, BF),
+            shape_of(size + count, columns, BF),
+            shape_of(2 * size + count, columns, BF),
+        ],
+        (place.spot, own, arrived, glue),
         scalars=1,
     )
-    return near, far
-
-
-def attend_weights_travel(near, far, weight_out, place):
-    size = near.shape[0]
-    both = jnp.concatenate([near, far], axis=0)
-    pieces = {0: near, 1: flipped(far, QUAD)}
-    for step in range(2, place.planes, 2):
-        arrived = flipped(both, QUAD * step)
-        pieces[step] = arrived[:size]
-        pieces[step + 1] = flipped(arrived[size:], QUAD)
-    steps = range(1, place.planes // 2)
-    outs = [weight_out] + [flipped(weight_out, SPAN * step) for step in steps]
-    return [pieces[step] for step in range(place.planes)], outs
-
-
-def attend_weights_lay(pieces, outs, place):
-    planes, unit, columns = place.planes, place.unit, pieces[0].shape[1]
+
+
+def attend_weights_split(near, glue, travelled, place):
+    unit = place.unit
+    size = 4 * unit
+    columns = near.shape[1]
+
+    def split(near_rows, glue_rows, odd, even, relayed):
+        pieces = (near_rows, odd, even, relayed)
+        kept = jnp.concatenate([item[: 2 * unit] for item in pieces], axis=0)
+        sent = jnp.concatenate([item[2 * unit : size] for item in pieces], axis=0)
+        whole = [glue_rows, odd[size:], even[2 * size :], relayed[size:]]
+        return kept, sent, jnp.concatenate(whole, axis=0)
+
+    return fused(
+        split,
+        "attend_split",
+        [shape_of(8 * unit, columns, BF)] * 2 + [shape_of(4 * glue.shape[0], columns, BF)],
+        near,
+        glue,
+        *travelled,
+    )
+
+
+def attend_weights_lay(kept, sent, outs, place):
+    planes, unit, columns = place.planes, place.unit, kept.shape[1]
     width, model = columns // 3, outs[0].shape[1]
-
-    def split(*values):
-        kept = jnp.concatenate([item[: 2 * unit] for item in values], axis=0)
-        sent = jnp.concatenate([item[2 * unit :] for item in values], axis=0)
-        return kept, sent
-
-    kept, sent = fused(
-        split, "attend_split", [shape_of(2 * planes * unit, columns, BF)] * 2, *pieces
-    )
     swapped = flipped(sent, 1)
 
     def lay(spot, kept_ref, swapped_ref, *refs):
@@ -933,39 +943,13 @@
     )
 
 
-def attend_grads_planes(kept, swapped, place):
-    planes, unit, columns = place.planes, place.unit, kept.shape[1]
-
-    def by_plane(kept_part, swapped_part):
-        both = jnp.concatenate([kept_part, swapped_part], axis=1)
-        pieces = [both[2 * step * unit : 2 * (step + 1) * unit] for step in range(planes)]
-        return pieces[0], jnp.concatenate([pieces[1], pieces[3]], axis=0), pieces[2]
-
-    size = 2 * unit
-    return fused(
-        by_plane,
-        "attend_planes",
-        [shape_of(count * size, 2 * columns, BF) for count in (1, 2, 1)],
-        kept,
-        swapped,
-    )
-
-
-def attend_grads_relay(own, odd, even, *outs):
-    size = own.shape[0]
-    arrived = flipped(jnp.concatenate([even, odd[size:]], axis=0), 2 * QUAD)
-    outs = [outs[0]] + [flipped(outs[step], SPAN * step) for step in range(1, len(outs))]
-    return [own, odd, arrived, *outs]
-
-
 def attend_grads_sum(travelled, place):
     unit = place.unit
-    size = 2 * unit
-    columns, model = travelled[0].shape[1] // 2, travelled[3].shape[1]
-
-    def total(own, near, far, *rest):
-        even = own.astype(F32) + far[:size].astype(F32)
-        odd = near[:size].astype(F32) + far[size:].astype(F32)
+    columns, model = travelled[0].shape[1] // 2, travelled[4].shape[1]
+
+    def total(own, one, two, three, *rest):
+        even = own.astype(F32) + two.astype(F32)
+        odd = one[: three.shape[0]].astype(F32) + three.astype(F32)
         both = jnp.concatenate([even, odd], axis=1)
         out = sum(item.astype(F32) for item in rest)
         return both[:unit], both[unit:], out
@@ -1032,7 +1016,18 @@
     return wide[index : index + 1]
 
 
-def conv_pick(weight_in, weight_out, place):
+def blocks_of(width, first, model):
+    low, high = (0, 2 * model) if first else (2 * model, 3 * model)
+    result = []
+    for block in range(3 * model // width):
+        begin, end = max(block * width, low), min((block + 1) * width, high)
+        if begin < end:
+            source = slice(begin - block * width, end - block * width)
+            result.append((block, source, slice(begin - low, end - low)))
+    return result
+
+
+def conv_pick(weight_in, weight_out, width, place):
     rows, model = weight_out.shape
     half = rows // 2
     whole = half % 16 != 0
@@ -1042,26 +1037,13 @@
         source = pl.ds(pl.multiple_of(spot[3] * half, half), half)
         if whole:
             source = slice(0, rows)
-        out[:size, :] = left[source, :model]
-        out[size : 2 * size, :] = left[source, model:]
-        out[2 * size :, :] = right[source, :]
-
-    outs = [shape_of(3 * size, model, BF)]
+        for ref, first in ((left, True), (right, False)):
+            for block, own, columns in blocks_of(width, first, model):
+                out[block * size : (block + 1) * size, own] = ref[source, columns]
+
+    outs = [shape_of(3 * model // width * size, width, BF)]
     operands = (place.spot, weight_in, weight_out)
     return kernel_call(pick, "conv_pick", outs, operands, scalars=1)[0]
-
-
-def core_groups(place):
-    return [list(range(core, place.shards, 2)) for core in range(2)]
-
-
-def conv_halved(piece, place):
-    return 6 * place.unit == 4 * piece.shape[0]
-
-
-def conv_planes(piece, place):
-    started = plane_start(piece, place)
-    return plane_finish(piece, started, place)
 
 
 def conv_square(own, masks):
@@ -1070,33 +1052,31 @@
     return own, flipped(own, first), flipped(own, second), half
 
 
-def conv_relay(own, via_first, via_second, masks):
+def conv_relay(via_first, via_second, masks):
     first, second = masks
-    half = own.shape[0] // 2
-    low, high = flipped(via_first[:half], second), flipped(via_second[half:], first)
-    near = [own, via_first, via_second, low, high]
-    return [*near, *(flipped(item, 1) for item in near)]
+    half = via_first.shape[0] // 2
+    return flipped(via_first[:half], second), flipped(via_second[half:], first)
 
 
 def lay_conv(spot, refs, target, unit, first):
     model = target.shape[0]
     plane, second, core, rep = spot[0], spot[1], spot[2], spot[3]
     size = unit if len(refs) == 1 else unit // 2
-    columns = (0, 1) if first else (2,)
+    width = refs[0].shape[1]
+    extent = 3 * model // width * size
+    blocks = blocks_of(width, first, model)
     for index, ref in enumerate(refs):
-        for local in range(ref.shape[0] // (3 * size)):
+        for local in range(ref.shape[0] // extent):
             start = local * size
             if len(refs) > 1:
                 kind, near = index % 5, index // 5
                 turn, side = ((0, 0), (0, 1), (1, 0), (1, 1), (1, 1))[kind]
-                step = local + (ref.shape[0] // (3 * size) if kind == 4 else 0)
+                step = local + (ref.shape[0] // extent if kind == 4 else 0)
                 start = (((plane ^ step) * 2 + (second ^ turn)) * 2 + (core ^ near)) * 2
                 start = pl.multiple_of((start + (rep ^ side)) * size, size)
-            for place_of, column in enumerate(columns):
-                source = (3 * local + column) * size
-                target[pl.ds(start, size), place_of * model : (place_of + 1) * model] = ref[
-                    source : source + size, :
-                ]
+            for block, own, columns in blocks:
+                source = local * extent + block * size
+                target[pl.ds(start, size), columns] = ref[source : source + size, own]
 
 
 def convolve_start(parts, before, wide, bias_row, weights, place):
@@ -1296,7 +1276,9 @@
     model = hidden.shape[1]
     unit, planes = place.unit, place.planes
     size = unit // 2
-    halved = size % 16 == 0
+    halved = place.aligned
+    width = 3 * model // 4 if halved else model
+    columns = range(0, 3 * model, width)
 
     def kernel(spot, hidden_ref, slope_ref, rest_ref, branch_ref, kept, sent, total):
         total[:, : 2 * model] = dot_tn(hidden_ref[...], slope_ref[...])
@@ -1306,25 +1288,26 @@
             if not halved:
                 for pair in range(2 * planes):
                     start = pl.multiple_of((pair * 2 + (core ^ near)) * unit, unit)
-                    for column in range(3):
-                        ref[(3 * pair + column) * unit : (3 * pair + column + 1) * unit, :] = total[
-                            pl.ds(start, unit), column * model : (column + 1) * model
+                    for index, column in enumerate(columns):
+                        target = (3 * pair + index) * unit
+                        ref[target : target + unit, :] = total[
+                            pl.ds(start, unit), column : column + width
                         ].astype(BF)
                 continue
             for kind, (turn, side) in enumerate(((0, 0), (0, 1), (1, 0), (1, 1))):
                 for step in range(planes):
                     start = (((plane ^ step) * 2 + (second ^ turn)) * 2 + (core ^ near)) * 2
                     start = pl.multiple_of((start + (rep ^ side)) * size, size)
-                    for column in range(3):
-                        target = ((kind * planes + step) * 3 + column) * size
+                    for index, column in enumerate(columns):
+                        target = ((kind * planes + step) * len(columns) + index) * size
                         ref[target : target + size, :] = total[
-                            pl.ds(start, size), column * model : (column + 1) * model
+                            pl.ds(start, size), column : column + width
                         ].astype(BF)
 
     return kernel_call(
         kernel,
         "conv_grads",
-        [shape_of(3 * model // 2, model, BF)] * 2,
+        [shape_of(len(columns) * model // 2, width, BF)] * 2,
         (place.spot, hidden, slope, rest, branch),
         scalars=1,
         scratch=[pltpu.VMEM((model, 3 * model), F32)],
@@ -1334,7 +1317,7 @@
 
 
 def conv_grads_split(kept, swapped, place):
-    count = 4 if place.unit // 2 % 16 == 0 else 1
+    count = 4 if place.aligned else 1
     size = kept.shape[0] // count
 
     def body(kept_part, swapped_part):
@@ -1355,15 +1338,42 @@
     ]
 
 
-def conv_grads_pieces(shares, place):
-    size = shares[0].shape[0] // place.planes
-
-    def body(*values):
-        total = sum(value.astype(F32) for value in values)
-        return [total[step * size : (step + 1) * size] for step in range(place.planes)]
-
-    outs = [shape_of(size, shares[0].shape[1], BF)] * place.planes
-    return list(fused(body, "conv_grads_pieces", outs, *shares))
+def plane_pieces(mix_kept, mix_swapped, shares, place):
+    planes, unit = place.planes, place.unit
+    rows, width = 2 * unit, shares[0].shape[1]
+    size = shares[0].shape[0] // planes
+
+    def body(kept, swapped, *values):
+        both = jnp.concatenate([kept, swapped], axis=1)
+        mix = [both[step * rows : (step + 1) * rows] for step in range(planes)]
+        total = sum(value.astype(F32) for value in values).astype(BF)
+        conv = [total[step * size : (step + 1) * size] for step in range(planes)]
+        joint = jnp.concatenate([mix[1], conv[1], conv[3]], axis=0)
+        return mix[0], mix[2], mix[3], conv[0], conv[2], joint
+
+    outs = [shape_of(rows, width, BF)] * 3 + [shape_of(size, width, BF)] * 2
+    outs += [shape_of(rows + 2 * size, width, BF)]
+    return list(fused(body, "plane_pieces", outs, mix_kept, mix_swapped, *shares))
+
+
+def conv_grads_top(own, joint):
+    size = own.shape[0]
+
+    def body(mine, arrived):
+        return (mine.astype(F32) + arrived[arrived.shape[0] - size :].astype(F32),)
+
+    return fused(body, "conv_grads_top", [shape_of(*own.shape, BF)], own, joint)[0]
+
+
+def conv_grads_sum(own, joint, last):
+    size = own.shape[0]
+
+    def body(mine, arrived, late):
+        start = arrived.shape[0] - 2 * size
+        near = arrived[start : start + size]
+        return (mine.astype(F32) + near.astype(F32) + late.astype(F32),)
+
+    return fused(body, "conv_grads_sum", [shape_of(*own.shape, BF)], own, joint, last)[0]
 
 
 def conv_grads_whole(total, place):
@@ -1375,14 +1385,16 @@
 
 
 def conv_grads_final(mine, theirs, place):
-    size, model = mine.shape[0] // 3, mine.shape[1]
+    size, width = place.unit // 2, mine.shape[1]
+    model = width * mine.shape[0] // size // 3
 
     def kernel(spot, mine_ref, theirs_ref, grad_in, grad_out):
         for turn, ref in enumerate((mine_ref, theirs_ref)):
             target = pl.ds(pl.multiple_of((spot[3] ^ turn) * size, size), size)
-            grad_in[0, target, :model] = ref[:size, :].astype(F32)
-            grad_in[0, target, model:] = ref[size : 2 * size, :].astype(F32)
-            grad_out[0, target, :] = ref[2 * size :, :].astype(F32)
+            for out, first in ((grad_in, True), (grad_out, False)):
+                for block, own, columns in blocks_of(width, first, model):
+                    value = ref[block * size : (block + 1) * size, own]
+                    out[0, target, columns] = value.astype(F32)
 
     outs = [
         jax.ShapeDtypeStruct((1, 2 * size, 2 * model), F32),
@@ -1551,9 +1563,10 @@
         for bit in range((2 * shards).bit_length() - 1):
             distance = distance + flipped(distance, 1 << bit)
         return total[:rows], total[rows:].reshape(2, 2 * half), distance
-    extent = -(-(rows + 8) // 8) * 8
+    extent = -(-(rows + 8) // 32) * 32
+    size = extent // 2
     table_rows = distance.shape[0]
-    fold = -(-table_rows // 16) * 8
+    fold = -(-table_rows // 32) * 16
 
     def pack(spot, in_ref, first, attend_ref, conv, last, mix, bias_one, bias_two, table, out, wide):
         plane, second, core, rep = spot[0], spot[1], spot[2], spot[3]
@@ -1578,25 +1591,48 @@
                 placed = jnp.where(lane // unit == core, placed, 0.0)
                 wide[index : index + 1, target] = placed
         for module, ref in enumerate((bias_one, bias_two)):
-            for index in range(2 * planes):
-                value = ref[:, index * half : (index + 1) * half]
-                start = pl.multiple_of((index // 2 * 2 + second) * LANES, LANES)
+            for index in range(planes):
+                pair = [
+                    ref[:, start * half : (start + 1) * half]
+                    for start in (2 * index, 2 * index + 1)
+                ]
+                moved = [
+                    pltpu.roll(jnp.broadcast_to(item, (8, LANES)), unit, axis=1)[:1]
+                    for item in pair
+                ]
+                halves = (
+                    jnp.where(lane < unit, pair[0], moved[1]),
+                    jnp.where(lane < unit, moved[0], pair[1]),
+                )
+                start = pl.multiple_of((index * 2 + second) * LANES, LANES)
                 for side in range(2):
-                    line = rows + ((index % 2) * 2 + module) * 2 + side
-                    wide[line : line + 1, pl.ds(start, LANES)] = jnp.where(rep == side, value, 0.0)
+                    for part, value in enumerate(halves):
+                        line = rows + (module * 2 + side) * 2 + part
+                        wide[line : line + 1, pl.ds(start, LANES)] = jnp.where(
+                            rep == side, value, 0.0
+                        )
         rest = jnp.concatenate(
             [table[fold:, :], jnp.zeros((2 * fold - table_rows, unit), F32)], axis=0
         )
         folded = jnp.concatenate([table[:fold, :], rest], axis=1)
-        for target in range(2 * shards):
-            pair = target % shards // 2
-            out[target, :extent, :] = wide[:, pair * LANES : (pair + 1) * LANES]
-            out[target, extent:, :] = folded
+        folded = folded.astype(BF)
+        wide_lane = lax.broadcasted_iota(jnp.int32, (size, LANES), 1)
+        for pair in range(shards // 2):
+            block = wide[:, pair * LANES : (pair + 1) * LANES]
+            upper, lower = block[:size], block[size:]
+            both = (
+                jnp.where(wide_lane < unit, upper, pltpu.roll(lower, unit, axis=1)),
+                jnp.where(wide_lane < unit, pltpu.roll(upper, unit, axis=1), lower),
+            )
+            for side in range(2):
+                for target in (2 * pair + side, 2 * pair + side + shards):
+                    out[target, :size, :] = both[side].astype(BF)
+                    out[target, size:, :] = folded
 
     packed = kernel_call(
         pack,
         "small_pack",
-        [jax.ShapeDtypeStruct((2 * shards, extent + fold, LANES), F32)],
+        [jax.ShapeDtypeStruct((2 * shards, size + fold, LANES), BF)],
         (place.spot, *sums, mix_sums, *biases, distance),
         scalars=1,
         scratch=[pltpu.VMEM((extent, model), F32)],
@@ -1604,21 +1640,20 @@
     packed = lax.all_to_all(packed, ("rep", "shard"), 0, 0, tiled=True)
 
     def unpack(spot, ref, wide, bias, table):
-        total = ref[0]
+        total = ref[0].astype(F32)
         for index in range(1, 2 * shards):
-            total = total + ref[index]
-        table[:fold, :] = total[extent:, :unit]
-        core = spot[2]
+            total = total + ref[index].astype(F32)
         moved = pltpu.roll(total, unit, axis=1)
-        table[fold:, :] = moved[extent : extent + table_rows - fold, :unit]
-        wide[...] = jnp.where(core == 0, total, moved)[:rows, :unit]
+        table[:fold, :] = total[size:, :unit]
+        table[fold:, :] = moved[size : size + table_rows - fold, :unit]
+        both = jnp.concatenate([total[:size, :unit], moved[:size, :unit]], axis=0)
+        wide[...] = both[:rows]
         for module in range(2):
             for side in range(2):
-                lines = [rows + (near * 2 + module) * 2 + side for near in range(2)]
-                value = jnp.where(
-                    core == 0, total[lines[0] : lines[0] + 1], total[lines[1] : lines[1] + 1]
+                line = rows + (module * 2 + side) * 2
+                bias[module : module + 1, side * half : (side + 1) * half] = jnp.concatenate(
+                    [both[line : line + 1], both[line + 1 : line + 2]], axis=1
                 )
-                bias[module : module + 1, side * half : (side + 1) * half] = value
 
     return kernel_call(
         unpack,
@@ -1696,64 +1731,71 @@
     ) = tied(*first_far, small, *second_parts, *columns, *pieces)
     columns, pieces = early[:2], early[2:]
     small = shard_gather(small, place)
+    second_pack = pack_rows((second_in, second_other, second_out))
+    glue_width = 3 * model // SPAN if place.aligned else model
+    glue = conv_pick(conv_in[0], conv_out[0], glue_width, place)
+    if place.aligned:
+        columns = attend_arrange(*columns, glue, place)
     first_near = plane_finish(first_pack, first_far, place)
+    last = place.planes - 1
+    first_near[last], small, glue, second_pack, *columns = tied(
+        first_near[last], small, glue, second_pack, *columns
+    )
     first_packs = with_core(first_near)
     wide, feed_bias, mix_bias = small_unpack(small, (wide_rows, 2 * bias_rows), place)
     table = wide_table(distance[0], rows)
-    second_in = pack_rows((second_in, second_other))
-    if place.aligned:
-        columns = attend_arrange(*columns, place)
-    glue = conv_pick(conv_in[0], conv_out[0], place)
-    last = place.planes - 1
-    first_packs[last], glue, second_in, wide, mix_bias, table, *columns = tied(
-        first_packs[last], glue, second_in, wide, mix_bias, table, *columns
-    )
+    wide, mix_bias, table, pieces[0] = tied(wide, mix_bias, table, pieces[0])
 
     parts, saved_first = feed(
         pieces, first_packs, feed_bias[0:1], wide, 0, place.feed_masks, place
     )
     if place.aligned:
-        travelled, outs = attend_weights_travel(*columns, attn_out[0], place)
-        after_first, hidden = feed_to_attend(parts, inputs, wide)
-        hidden, glue, *travelled = tied(hidden, glue, *travelled)
-        glue_planes = conv_planes(glue, place)
-        mix_in, mix_out = attend_weights_lay(travelled, outs, place)
+        mix_near, one, two = columns
+        odd, even = flipped(one, QUAD), flipped(two, 2 * QUAD)
+        parts, (odd, even, mix_out) = tied_lists(parts, (odd, even, attn_out[0]))
+        mix_outs = [mix_out, flipped(mix_out, SPAN)]
+        relayed = flipped(even[4 * unit :], QUAD)
+    after_first, hidden = feed_to_attend(parts, inputs, wide)
+    near, far = group_gather(hidden, place.span_masks)
+    if place.aligned:
+        near, far, (relayed, second_pack, mix_outs[1]) = tied_lists(
+            near, far, (relayed, second_pack, mix_outs[1])
+        )
+        mix_kept, mix_sent, glue = attend_weights_split(
+            mix_near, glue, (odd, even, relayed), place
+        )
+        mix_in, mix_out = attend_weights_lay(mix_kept, mix_sent, mix_outs, place)
+        glue, via_first, via_second, unused_half = conv_square(glue, place.feed_masks)
     else:
         mix_in, mix_out = attend_weights_whole(attn_in[0], attn_out[0], head, place)
-        after_first, hidden = feed_to_attend(parts, inputs, wide)
-    near, far = group_gather(hidden, place.span_masks)
-    if place.aligned:
-        far[3], second_in, *glue_planes = tied(far[3], second_in, *glue_planes)
-        glue_own = pack_rows(glue_planes)
-        glue_own, via_first, via_second, unused_half = conv_square(glue_own, place.feed_masks)
-    else:
         glue = [lax.all_gather(glue, "shard", axis=0, tiled=True)]
-        far[3], second_in = tied(far[3], second_in)
-    second_in_far = plane_start(second_in, place)
+        near, far, (second_pack,) = tied_lists(near, far, (second_pack,))
+    second_far = plane_start(second_pack, place)
     saved_attend, kept, sent = attend((near, far), mix_in, mix_bias, mix_out, table, place)
     if place.aligned:
-        sent, *second_in_far, via_first, via_second = tied(
-            sent, *second_in_far, via_first, via_second
+        sent, via_first, via_second = tied(sent, via_first, via_second)
+        low, high = conv_relay(via_first, via_second, place.feed_masks)
+    sent, *second_far = tied(sent, *second_far)
+    parts = group_reduce(kept, sent, place.span_masks)
+    if place.aligned:
+        parts, glue, (second_pack, *second_far) = tied_lists(
+            parts, (glue, via_first, via_second, low, high), (second_pack, *second_far)
         )
-        glue = conv_relay(glue_own, via_first, via_second, place.feed_masks)
+        glue = [*glue, *(flipped(item, 1) for item in glue)]
     else:
-        sent, *second_in_far = tied(sent, *second_in_far)
-    parts = group_reduce(kept, sent, place.span_masks)
-    parts[3], second_out, *glue = tied(parts[3], second_out, *glue)
-    second_out_far = plane_start(second_out, place)
+        parts, (second_pack, *second_far) = tied_lists(parts, (second_pack, *second_far))
+    second_near = plane_finish(second_pack, second_far, place)
     after_attend, conv_hidden, doubled, glued = convolve_start(
         parts, after_first, wide, count, glue, place
     )
     border = along(glued[rows - edge :], 1, place)
     border = jnp.where(place.member == 0, jnp.zeros_like(border), border)
+    border, *second_near = tied(border, *second_near)
+    second_packs = with_core(second_near)
     mixed, rest, after_conv, hidden = convolve_finish(
         glued, border, wide, taps, glue, after_attend, place
     )
-    hidden, *second_far = tied(hidden, *second_in_far, *second_out_far)
-    second_packs = [
-        *with_core(plane_finish(second_in, second_far[:2], place)),
-        *with_core(plane_finish(second_out, second_far[2:], place)),
-    ]
+    hidden, *second_packs = tied(hidden, *second_packs)
     pieces = square_gather(hidden, place.feed_masks)
     parts, saved_second = feed(
         pieces, second_packs, feed_bias[1:2], wide, None, place.feed_masks, place
@@ -1770,8 +1812,7 @@
     second_grads[1], second_grads[3] = flipped(second_grads[1], 1), flipped(second_grads[3], 1)
     parts = square_reduce(result, place.feed_masks)
     second_split = [plane_split(*pair, place) for pair in (second_grads[:2], second_grads[2:])]
-    parts[3], *flat = tied(parts[3], *second_split[0], *second_split[1])
-    second_split = [flat[: place.planes], flat[place.planes :]]
+    parts, *second_split = tied_lists(parts, *second_split)
     second_lists = [plane_early(pieces, place) for pieces in second_split]
     grad_conv, conv_branch, main, halo, conv_sums = convolve_back_start(
         parts, grad_last, after_conv, mixed, wide, taps, glue, glued, border, place
@@ -1793,69 +1834,99 @@
     second_early = [flat[2 : 2 + count_early], flat[2 + count_early :]]
     near, far = group_gather(branch, place.span_masks)
     conv_shares = conv_grads_split(conv_kept, flipped(conv_sent, 1), place)
-    far[3], *flat = tied(far[3], *conv_shares, *second_tops)
-    conv_shares, second_tops = flat[:-2], flat[-2:]
+    near, far, conv_shares, second_tops = tied_lists(near, far, conv_shares, second_tops)
     if place.aligned:
         conv_shares = conv_grads_square(conv_shares, place.feed_masks)
     second_lasts = [plane_last(top, place) for top in second_tops]
     back = attend_back((near, far), saved_attend, mix_in, mix_out, table, place)
     grad_mixed, kept, sent, branch, grad_table, table_far = back
-    sent, *second_lasts = tied(sent, *second_lasts)
+    (sent,), second_lasts, conv_shares = tied_lists((sent,), second_lasts, conv_shares)
     mix_grad_in, mix_grad_out, mix_sums = attend_grads(saved_attend, grad_mixed, branch, place)
     second_sums = [plane_add([*own, last]) for own, last in zip(second_early, second_lasts)]
+    second_other = flipped(second_sums[0][unit:], 2)
     if place.aligned:
         mix_kept, mix_swap, *mix_outs = attend_grads_lay(mix_grad_in, mix_grad_out, place)
         kept, mix_swap = tied(kept, mix_swap)
         mix_swap = flipped(mix_swap, 1)
+        kept, mix_swap = tied(kept, mix_swap)
+    kept, second_other = tied(kept, second_other)
+    second_pack = pack_rows((second_sums[0][:unit], second_other, second_sums[1]))
+    second_theirs = flipped(second_pack, place.shards)
     parts = group_reduce(kept, sent, place.span_masks)
     if place.aligned:
-        mix_sent = list(attend_grads_planes(mix_kept, mix_swap, place))
-        parts[1], *mix_sent = tied(parts[1], *mix_sent)
-        mix_sent[1] = flipped(mix_sent[1], QUAD)
-        parts[3], mix_sent[1], *conv_shares = tied(parts[3], mix_sent[1], *conv_shares)
-        conv_pieces = conv_grads_pieces(conv_shares, place)
+        mix_outs[1] = flipped(mix_outs[1], SPAN)
+        planed = plane_pieces(mix_kept, mix_swap, conv_shares, place)
+        parts, (second_theirs, mix_outs[1]), planed = tied_lists(
+            parts, (second_theirs, mix_outs[1]), planed
+        )
+    else:
+        parts, (second_theirs,) = tied_lists(parts, (second_theirs,))
     grad_distance = distance_gradient(grad_table, table_far, rows)
     grad_first, branch, first_sums = attend_to_feed_back(parts, grad_attend, after_first, wide)
     if place.aligned:
-        branch, *conv_pieces = tied(branch, *conv_pieces)
-        conv_lists = plane_early(conv_pieces, place)
-        mix_sent = attend_grads_relay(*mix_sent, *mix_outs)
+        (branch,), planed = tied_lists((branch,), planed)
+        mix_zero, mix_two, mix_three, conv_zero, conv_two, joint = planed
         pieces = square_gather(branch, place.feed_masks)
-        pieces[3], (conv_top,) = tied_tops(pieces[3], [conv_lists], place)
+        joint = flipped(joint, QUAD)
+        mix_two = flipped(mix_two, 2 * QUAD)
+        pieces, (mix_two, mix_three, joint) = tied_lists(pieces, (mix_two, mix_three, joint))
+        mix_three = flipped(mix_three, 3 * QUAD)
+        conv_last = plane_last(conv_grads_top(conv_two, joint), place)
     else:
         pieces = square_gather(branch, place.feed_masks)
         conv_whole = conv_grads_whole(conv_shares[0], place)
         mix_grads = attend_grads_whole(mix_grad_in, mix_grad_out, head, place)
         mix_grads = [item[None] for item in mix_grads]
     kept, sent = feed_out_grads(saved_first[2], pieces, place)
-    pieces[0], kept, sent = tied(pieces[0], kept, sent)
-    out_swapped = flipped(sent, 1)
+    out_split = plane_split(kept, flipped(sent, 1), place)
+    pieces, out_split = tied_lists(pieces, out_split)
+    out_lists = plane_early(out_split, place)
     result, branch, slope, first_bias = feed_back(pieces, first_packs, saved_first, place)
-    out_split = plane_split(kept, out_swapped, place)
-    slope, *out_split = tied(slope, *out_split)
-    out_lists = plane_early(out_split, place)
+    slope, (out_top,) = tied_tops(slope, [out_lists], place)
+    out_early = out_lists[0]
+    if place.aligned:
+        slope, conv_last = tied(slope, conv_last)
+        conv_mine = conv_grads_sum(conv_zero, joint, conv_last)
     kept, sent = feed_in_grads(saved_first[0], slope, place)
     kept, *result = tied(kept, *result)
-    if place.aligned:
-        kept, *mix_sent = tied(kept, *mix_sent)
-        mix_own, mix_other, mix_out_sum = attend_grads_sum(mix_sent, place)
-        conv_last = plane_last(plane_total(conv_top), place)
     in_swapped = flipped(sent, 1)
-    in_swapped, (out_top,) = tied_tops(in_swapped, [out_lists], place)
-    out_last = plane_last(plane_total(out_top), place)
     in_lists = plane_early(plane_split(kept, in_swapped, place), place)
     parts = square_reduce(result, place.feed_masks)
-    second_other = flipped(second_sums[0][unit:], 2)
+    out_last = plane_last(plane_total(out_top), place)
+    parts, out_early, *in_lists = tied_lists(parts, out_early, *in_lists.values())
+    in_early, in_top = in_lists[0], in_lists[-1]
+    in_last = plane_last(plane_total(in_top), place)
     if place.aligned:
+        parts[0], mix_three = tied(parts[0], mix_three)
+        mix_own, mix_other, mix_out_sum = attend_grads_sum(
+            (mix_zero, joint, mix_two, mix_three, *mix_outs), place
+        )
         mix_arrived = flipped(mix_other, 2)
-        parts[3], mix_arrived, conv_last = tied(parts[3], mix_arrived, conv_last)
-        conv_mine = plane_add([*conv_lists[0], conv_last])
-    parts[3], second_other, (in_top,) = tied_tops_with(parts[3], second_other, in_lists, place)
-    in_last = plane_last(plane_total(in_top), place)
+        mix_theirs = [flipped(mix_own, place.shards), None, flipped(mix_out_sum, place.shards)]
+        conv_theirs = flipped(conv_mine, place.shards)
     grad_input, input_sums = last_step(parts, grad_first, inputs, wide)
-
-    second_pack = pack_rows((second_sums[0][:unit], second_other, second_sums[1]))
-    second_theirs = flipped(second_pack, place.shards)
+    if place.aligned:
+        input_sums, out_last, mix_arrived = tied(input_sums, out_last, mix_arrived)
+        mix_theirs[1] = flipped(mix_arrived, place.shards)
+    out_sum = plane_add([*out_early, out_last])
+    out_theirs = flipped(out_sum, place.shards)
+    if place.aligned:
+        mix_grads = attend_grads_final((mix_own, mix_arrived, mix_out_sum), mix_theirs, place)
+        conv_grads = conv_grads_final(conv_mine, conv_theirs, place)
+    else:
+        conv_grads = (
+            jnp.concatenate([conv_whole[0], conv_whole[1]], axis=1)[None],
+            conv_whole[2][None],
+        )
+
+    (in_last, input_sums, out_theirs), mix_grads, conv_grads = tied_lists(
+        (in_last, input_sums, out_theirs), mix_grads, conv_grads
+    )
+    in_sum = plane_add([*in_early, in_last])
+    in_own, in_other = in_sum[:unit], flipped(in_sum[unit:], 2)
+    in_theirs = flipped(in_own, place.shards)
+    input_sums, in_other, in_theirs = tied(input_sums, in_other, in_theirs)
+    first_mine = [(in_own, in_theirs), (in_other, flipped(in_other, place.shards))]
     small_grads, bias_grads, grad_distance = small_reduce(
         (input_sums, first_sums, attend_sums, conv_sums, last_sums),
         mix_sums,
@@ -1864,29 +1935,6 @@
         (wide_rows, tap_count),
         place,
     )
-    out_sum = plane_add([*out_lists[0], out_last])
-    out_theirs = flipped(out_sum, place.shards)
-    if place.aligned:
-        mix_mine = mix_own, mix_arrived, mix_out_sum
-        mix_theirs = [flipped(item, place.shards) for item in mix_mine]
-        conv_theirs = flipped(conv_mine, place.shards)
-        mix_grads = attend_grads_final(mix_mine, mix_theirs, place)
-        conv_grads = conv_grads_final(conv_mine, conv_theirs, place)
-    else:
-        conv_grads = (
-            jnp.concatenate([conv_whole[0], conv_whole[1]], axis=1)[None],
-            conv_whole[2][None],
-        )
-    in_last, small_grads, mix_last, conv_end, second_theirs, out_theirs, *early = tied(
-        in_last,
-        small_grads,
-        mix_grads[0],
-        conv_grads[0],
-        second_theirs,
-        out_theirs,
-        *in_lists[0][1:],
-    )
-    first_mine = feed_arrive([plane_add([in_lists[0][0], *early, in_last])], place)
     first_mine = [*first_mine, (out_sum, out_theirs)]
     cuts = (0, unit, 2 * unit, 2 * unit + half)
     second_mine = [
@@ -1894,7 +1942,6 @@
         for i in range(3)
     ]
     feed_grads = feed_final((first_mine, second_mine), place)
-    mix_grads, conv_grads = (mix_last, mix_grads[1]), (conv_end, conv_grads[1])
     return (
         output,
         grad_input,

time: 597 us -> 526 us (0.88)
  waiting for transfers between devices: 278 us -> 232 us
  starting transfers between devices: 137 us -> 121 us
  local copies, waits for them, and re-layouts: 36.9 us -> 30.5 us
    ppermute x125 -> x114, waiting for transfers between devices: 277 us -> 218 us  [flipped(): lax.ppermute(value, ('rep', 'shard'), [(i, i ^ mask) for i in range(total)])]
    ppermute x125 -> x114, starting transfers between devices: 127 us -> 109 us  [flipped(): lax.ppermute(value, ('rep', 'shard'), [(i, i ^ mask) for i in range(total)])]
    all_to_all x1, waiting for transfers between devices: 1.56 us -> 8.33 us  [shard_gather(): return lax.all_to_all(copies, 'shard', 0, 0, tiled=True)]
    unnamed x241 -> x176, local copies, waits for them, and re-layouts: 28.4 us -> 23.6 us
    pallas_call x56 -> x54, Pallas kernels: 126 us -> 126 us  [kernel_call(): pl.pallas_call(body, grid=(1,), in_specs=specs, out_specs=vmem(len(outs))...]
  transfers between devices with their start and end apart: 129 -> 118, of which waited for: 49 -> 55; matrix products, arithmetic and copies ran while one was open for 2% -> 2% of each run, Pallas kernels for 16% -> 20%
where the time goes in v5:
time: 526 us; the launch traced here: 516 us
  waiting for transfers between devices  232 us (44%)
  Pallas kernels  127 us (24%)
  starting transfers between devices  121 us (23%)
  local copies, waits for them, and re-layouts  30.5 us (6%)
    ppermute x114, waiting for transfers between devices, flipped(): lax.ppermute(value, ('rep', 'shard'), [(i, i ^ mask) for i in range(total)])  218 us
    pallas_call x54, Pallas kernels, kernel_call(): pl.pallas_call(body, grid=(1,), in_specs=specs, out_specs=vmem(len(outs))...  126 us
    ppermute x114, starting transfers between devices, flipped(): lax.ppermute(value, ('rep', 'shard'), [(i, i ^ mask) for i in range(total)])  109 us
    unnamed x176, local copies, waits for them, and re-layouts  23.6 us
  transfers between devices with their start and end apart: 118, of which 55 were waited for; matrix products, arithmetic and copies ran while one was open for 2% of the time, Pallas kernels for 20%

profile of v5, /device:TPU:0, one launch (start us, length us, event | category | flops | bytes accessed | tf_op | source)
XLA Modules:
  0.0 515.6 jit_solution(17631544129317271310)
XLA Ops:
  3.9 3.0 collective-permute-start
  7.0 3.5 collective-permute-done.refs_1_
  10.5 2.9 collective-permute-start.1
  20.0 3.8 collective-permute-done.3.refs_1_
  26.9 8.3 %collective-permute-done.6.refs_2_ = bf16[128,1024]{1,0:T(8,128)(2,1)S(1)} collective-permute-done((bf16[128,1024]{1,0:T(8,128)(2,1)S(1)}, bf16[128,1024]{1,0:T(8,128)(2,1)S(1)}, u32[]{:S(2)}, u32[]{:S(2)}) %collective-permute-start.6) | collective-permute-done | bytes 262176 | tf_op jit(solution)/shard_map/ppermute | solution.py:119
  38.4 4.7 all-to-all-start
  46.2 8.3 %all-to-all-done = bf16[16,2,1792]{2,1,0:T(2,128)(2,1)} async-done(((bf16[16,2,1792]{2,1,0:T(2,128)(2,1)}), bf16[16,2,1792]{2,1,0:T(2,128)(2,1)}, u32[]{:S(2)}, u32[]{:S(2)}) %all-to-all-start) | async-done | bytes 114720 | tf_op jit(solution)/shard_map/all_to_all | solution.py:1528
  59.3 2.2 collective-permute-start.16
  63.4 5.2 %feed_forward.2 = (bf16[512,1024]{1,0:T(8,128)(2,1)S(1)}, f32[512,1024]{1,0:T(8,128)S(1)}, bf16[512,1024]{1,0:T(8,128)(2,1)S(1)}, f32[128,1024]{1,0:T(8,128)S(1)...) custom-call(s32[4]{0:T(128)S(1)} %pad_add_fusion.spot.spot_ref, ...), custom_call_target="tpu_custom_call" | custom-call | flops 2147483648 | bytes 10948608 | tf_op jit(solution)/shard_map/feed_forward/pallas_call | solution.py:86
  74.4 6.8 %collective-permute-done.16.refs_2_ = bf16[512,384]{1,0:T(8,128)(2,1)S(1)} collective-permute-done((bf16[512,384]{1,0:T(8,128)(2,1)}, bf16[512,384]{1,0:T(8,128)(2,1)S(1)}, u32[]{:S(2)}, u32[]{:S(2)}) %collective-permute-start.16) | collective-permute-done | bytes 393248 | tf_op jit(solution)/shard_map/ppermute | solution.py:119
  81.2 6.3 %collective-permute-done.17.refs_3_ = bf16[768,384]{1,0:T(8,128)(2,1)S(1)} collective-permute-done((bf16[768,384]{1,0:T(8,128)(2,1)S(1)}, bf16[768,384]{1,0:T(8,128)(2,1)S(1)}, u32[]{:S(2)}, u32[]{:S(2)}) %collective-permute-start.17) | collective-permute-done | bytes 589856 | tf_op jit(solution)/shard_map/ppermute | solution.py:119
  88.5 2.9 collective-permute-start.20
  94.2 8.9 %collective-permute-done.26.refs_1_ = bf16[64,1024]{1,0:T(8,128)(2,1)S(1)} collective-permute-done((bf16[64,1024]{1,0:T(8,128)(2,1)S(1)}, bf16[64,1024]{1,0:T(8,128)(2,1)S(1)}, u32[]{:S(2)}, u32[]{:S(2)}) %collective-permute-start.26) | collective-permute-done | bytes 131104 | tf_op jit(solution)/shard_map/ppermute | solution.py:119
  105.5 7.6 %collective-permute-done.25.refs_4_ = bf16[512,384]{1,0:T(8,128)(2,1)S(1)} collective-permute-done((bf16[512,384]{1,0:T(8,128)(2,1)S(1)}, bf16[512,384]{1,0:T(8,128)(2,1)S(1)}, u32[]{:S(2)}, u32[]{:S(2)}) %collective-permute-start.25) | collective-permute-done | bytes 393248 | tf_op jit(solution)/shard_map/ppermute | solution.py:119
  120.9 17.7 %attend_forward.1 = (bf16[1024,1024]{1,0:T(8,128)(2,1)}, bf16[1024,384]{1,0:T(8,128)(2,1)}, bf16[1024,128]{1,0:T(8,128)(2,1)}, f32[1024,128]{1,0:T(8,128)}, f32[...) custom-call(s32[1]{0:T(128)} %bitcast.4.refs_0_, bf16[128,1024]{1,0:T(8,128)(2,1)} %copy-done.44, ...), custom_call_target="tpu_custom_call" | custom-call | flops 6442450944 | bytes 10094080 | tf_op jit(solution)/shard_map/attend_forward/pallas_call | solution.py:86
  138.6 3.2 collective-permute-done.30.refs_6_
  152.5 8.2 %collective-permute-done.36.refs_9_.refs_3_ = bf16[512,384]{1,0:T(8,128)(2,1)S(1)} collective-permute-done((bf16[512,384]{1,0:T(8,128)(2,1)S(1)}, bf16[512,384]{1,0:T(8,128)(2,1)S(1)}, u32[]{:S(2)}, u32[]{:S(2)}) %collective-permute-start.36) | collective-permute-done | bytes 393248 | tf_op jit(solution)/shard_map/ppermute | solution.py:119
  162.5 3.3 collective-permute-done.35.refs_3_
  166.8 2.7 collective-permute-done.41.refs_14_.refs_8_
  172.5 5.8 %convolve_start.1 = (f32[128,1024]{1,0:T(8,128)}, bf16[128,1024]{1,0:T(8,128)(2,1)}, f32[128,2048]{1,0:T(8,128)}, bf16[128,1024]{1,0:T(8,128)(2,1)}) custom-call(s32[4]{0:T(128)} %copy-done.21, f32[128,1024]{1,0:T(8,128)} %copy-done.16, bf16[128,1024]{1,0:T(8,128)(2,1)} %copy-done.68, bf16[128,1024]{1,0:T(8,128)(2,1)} %copy-done.69, ...), custom_call_target="tpu_custom_call" | custom-call | flops 536870912 | bytes 10420224 | tf_op jit(solution)/shard_map/convolve_start/pallas_call | solution.py:86
  179.1 2.2 collective-permute-start.43
  185.3 7.5 %convolve_finish.1 = (f32[128,1024]{1,0:T(8,128)}, bf16[128,1024]{1,0:T(8,128)(2,1)}, f32[128,1024]{1,0:T(8,128)}, bf16[128,1024]{1,0:T(8,128)(2,1)}) custom-call(s32[4]{0:T(128)} %copy-done.21, bf16[128,1024]{1,0:T(8,128)(2,1)} %get-tuple-element.457.glued_ref, bf16[32,1024]{1,0:T(8,128)(2,1)} %broadcast_select_fusion.1.border_ref, f32[48,1024]{1,0:T(8,128)} %copy-done.1, ...), custom_call_target="tpu_custom_call" | custom-call | flops 268435456 | bytes 8912896 | tf_op jit(solution)/shard_map/convolve_finish/pallas_call | solution.py:86
  195.9 2.7 collective-permute-start.50
  199.5 5.2 %collective-permute-done.49.refs_1_ = bf16[128,1024]{1,0:T(8,128)(2,1)S(1)} collective-permute-done((bf16[128,1024]{1,0:T(8,128)(2,1)}, bf16[128,1024]{1,0:T(8,128)(2,1)S(1)}, u32[]{:S(2)}, u32[]{:S(2)}) %collective-permute-start.49) | collective-permute-done | bytes 262176 | tf_op jit(solution)/shard_map/ppermute | solution.py:119
  204.6 5.4 %collective-permute-done.50.refs_2_ = bf16[128,1024]{1,0:T(8,128)(2,1)S(1)} collective-permute-done((bf16[128,1024]{1,0:T(8,128)(2,1)}, bf16[128,1024]{1,0:T(8,128)(2,1)S(1)}, u32[]{:S(2)}, u32[]{:S(2)}) %collective-permute-start.50) | collective-permute-done | bytes 262176 | tf_op jit(solution)/shard_map/ppermute | solution.py:119
  215.6 3.9 feed_forward.3
  223.1 6.7 %collective-permute-done.52.refs_1_ = bf16[128,1024]{1,0:T(8,128)(2,1)S(1)} collective-permute-done((bf16[128,1024]{1,0:T(8,128)(2,1)S(1)}, bf16[128,1024]{1,0:T(8,128)(2,1)S(1)}, u32[]{:S(2)}, u32[]{:S(2)}) %collective-permute-start.52) | collective-permute-done | bytes 262176 | tf_op jit(solution)/shard_map/ppermute | solution.py:119
  229.8 2.5 collective-permute-done.53.refs_2_
  239.0 5.7 %collective-permute-done.55.refs_1_ = bf16[128,1024]{1,0:T(8,128)(2,1)S(1)} collective-permute-done((bf16[128,1024]{1,0:T(8,128)(2,1)S(1)}, bf16[128,1024]{1,0:T(8,128)(2,1)S(1)}, u32[]{:S(2)}, u32[]{:S(2)}) %collective-permute-start.55) | collective-permute-done | bytes 262176 | tf_op jit(solution)/shard_map/ppermute | solution.py:119
  244.6 4.9 collective-permute-done.56.refs_2_
  249.5 4.1 feed_backward.2
  253.7 2.0 feed_in_grads.2
  255.7 2.5 feed_out_grads.2
  262.7 6.1 %collective-permute-done.58.part_one = bf16[128,1024]{1,0:T(8,128)(2,1)S(1)} collective-permute-done((bf16[128,1024]{1,0:T(8,128)(2,1)S(1)}, bf16[128,1024]{1,0:T(8,128)(2,1)S(1)}, u32[]{:S(2)}, u32[]{:S(2)}) %collective-permute-start.58) | collective-permute-done | bytes 262176 | tf_op jit(solution)/shard_map/ppermute | solution.py:119
  268.8 4.8 collective-permute-done.59.part_two
  276.4 10.6 %convolve_back_start.1 = (f32[128,1024]{1,0:T(8,128)}, bf16[128,1024]{1,0:T(8,128)(2,1)}, f32[128,1024]{1,0:T(8,128)}, bf16[32,1024]{1,0:T(8,128)(2,1)}, f32[35,1024]{1,0:T(8,128)}) custom-call(s32[4]{0:T(128)} %copy-done.21, f32[128,1024]{1,0:T(8,128)} %copy-done.15, bf16[128,1024]{1,0:T(8,128)(2,1)} %copy-done.71, bf16[128,1024]{1,0:T(8,128)(2,1)} %copy-done.72, ...), custom_call_target="tpu_custom_call" | custom-call | flops 268435456 | bytes 11218944 | tf_op jit(solution)/shard_map/convolve_back_start/pallas_call | solution.py:86
  288.5 2.6 collective-permute-start.66
  292.0 6.9 %convolve_back_finish.1 = (f32[128,1024]{1,0:T(8,128)}, bf16[128,1024]{1,0:T(8,128)(2,1)}, bf16[128,2048]{1,0:T(8,128)(2,1)}, f32[3,1024]{1,0:T(4,128)}) custom-call(s32[4]{0:T(128)} %copy-done.21, f32[128,1024]{1,0:T(8,128)} %get-tuple-element.517.main_ref, bf16[32,1024]{1,0:T(8,128)(2,1)} %broadcast_select_fusion.late, ...), custom_call_target="tpu_custom_call" | custom-call | flops 536870912 | bytes 10498048 | tf_op jit(solution)/shard_map/convolve_back_finish/pallas_call | solution.py:86
  299.9 3.0 conv_grads.1
  308.6 5.0 collective-permute-done.68.refs_5_
  313.6 5.1 collective-permute-done.69.refs_3_
  322.9 2.1 collective-permute-start.78
  328.5 24.5 %attend_backward.1 = (bf16[1024,1024]{1,0:T(8,128)(2,1)S(1)}, bf16[1024,384]{1,0:T(8,128)(2,1)S(1)}, f32[512,128]{1,0:T(8,128)S(1)}, f32[8,128]{1,0:T(8,128)S(1)...) custom-call(s32[1]{0:T(128)} %bitcast.4.refs_0_, bf16[128,1024]{1,0:T(8,128)(2,1)S(1)} %copy-done.45, ...), custom_call_target="tpu_custom_call" | custom-call | flops 12884901888 | bytes 10883072 | tf_op jit(solution)/shard_map/attend_backward/pallas_call | solution.py:86
  353.0 8.3 %collective-permute-done.81.refs_5_ = bf16[512,768]{1,0:T(8,128)(2,1)S(1)} collective-permute-done((bf16[512,768]{1,0:T(8,128)(2,1)S(1)}, bf16[512,768]{1,0:T(8,128)(2,1)S(1)}, u32[]{:S(2)}, u32[]{:S(2)}) %collective-permute-start.81) | collective-permute-done | bytes 786464 | tf_op jit(solution)/shard_map/ppermute | solution.py:119
  365.6 4.1 collective-permute-done.82.refs_1_
  371.3 2.2 collective-permute-start.84
  376.6 10.0 %collective-permute-done.88.refs_5_ = bf16[64,1024]{1,0:T(8,128)(2,1)S(1)} collective-permute-done((bf16[64,1024]{1,0:T(8,128)(2,1)S(1)}, bf16[64,1024]{1,0:T(8,128)(2,1)S(1)}, u32[]{:S(2)}, u32[]{:S(2)}) %collective-permute-start.88) | collective-permute-done | bytes 131104 | tf_op jit(solution)/shard_map/ppermute | solution.py:119
  394.3 9.8 %collective-permute-done.92.refs_2_ = bf16[128,768]{1,0:T(8,128)(2,1)S(1)} collective-permute-done((bf16[128,768]{1,0:T(8,128)(2,1)S(1)}, bf16[128,768]{1,0:T(8,128)(2,1)S(1)}, u32[]{:S(2)}, u32[]{:S(2)}) %collective-permute-start.92) | collective-permute-done | bytes 196640 | tf_op jit(solution)/shard_map/ppermute | solution.py:119
  405.5 2.0 feed_out_grads.3
  407.7 2.6 collective-permute-done.94.refs_1_
  410.6 2.4 collective-permute-start.95
  413.4 5.2 %feed_backward.3 = (bf16[512,1024]{1,0:T(8,128)(2,1)}, bf16[512,1024]{1,0:T(8,128)(2,1)S(1)}, f32[1,1024]{1,0:T(1,128)S(1)}, f32[128,1024]{1,0:T(8,128)S(1)}, bf...) custom-call(s32[4]{0:T(128)S(1)} %copy-done.23, ...), custom_call_target="tpu_custom_call" | custom-call | flops 2147483648 | bytes 10752000 | tf_op jit(solution)/shard_map/feed_backward/pallas_call | solution.py:86
  418.5 5.0 collective-permute-done.95.refs_1_
  424.9 2.0 feed_in_grads.3
  432.9 3.3 collective-permute-done.100.refs_1_
  437.5 2.7 collective-permute-start.104
  444.2 10.1 %collective-permute-done.103.refs_1_ = bf16[128,1024]{1,0:T(8,128)(2,1)S(1)} collective-permute-done((bf16[128,1024]{1,0:T(8,128)(2,1)S(1)}, bf16[128,1024]{1,0:T(8,128)(2,1)S(1)}, u32[]{:S(2)}, u32[]{:S(2)}) %collective-permute-start.103) | collective-permute-done | bytes 262176 | tf_op jit(solution)/shard_map/ppermute | solution.py:119
  456.9 10.8 %collective-permute-done.106.refs_2_ = bf16[128,1024]{1,0:T(8,128)(2,1)S(1)} collective-permute-done((bf16[128,1024]{1,0:T(8,128)(2,1)S(1)}, bf16[128,1024]{1,0:T(8,128)(2,1)S(1)}, u32[]{:S(2)}, u32[]{:S(2)}) %collective-permute-start.106) | collective-permute-done | bytes 262176 | tf_op jit(solution)/shard_map/ppermute | solution.py:119
  474.1 5.6 %collective-permute-done.110.refs_4_ = bf16[64,1536]{1,0:T(8,128)(2,1)S(1)} collective-permute-done((bf16[64,1536]{1,0:T(8,128)(2,1)S(1)}, bf16[64,1536]{1,0:T(8,128)(2,1)S(1)}, u32[]{:S(2)}, u32[]{:S(2)}) %collective-permute-start.110) | collective-permute-done | bytes 196640 | tf_op jit(solution)/shard_map/ppermute | solution.py:119
  483.8 2.8 collective-permute-done.113.refs_2_
  489.1 3.6 all-to-all-start.1
  494.6 8.7 %collective-permute-done.115.refs_3_ = bf16[64,1024]{1,0:T(8,128)(2,1)S(1)} collective-permute-done((bf16[64,1024]{1,0:T(8,128)(2,1)S(1)}, bf16[64,1024]{1,0:T(8,128)(2,1)S(1)}, u32[]{:S(2)}, u32[]{:S(2)}) %collective-permute-start.115) | collective-permute-done | bytes 131104 | tf_op jit(solution)/shard_map/ppermute | solution.py:119
  503.4 2.9 feed_final.1
  506.2 5.2 %all-to-all-done.1.ref = bf16[32,80,128]{2,1,0:T(8,128)(2,1)S(1)} async-done(((bf16[32,80,128]{2,1,0:T(8,128)(2,1)}), bf16[32,80,128]{2,1,0:T(8,128)(2,1)S(1)}, u32[]{:S(2)}, u32[]{:S(2)}) %all-to-all-start.1) | async-done | bytes 655392 | tf_op jit(solution)/shard_map/all_to_all | solution.py:1640
  (435 shorter events, 163.1 us)
Async XLA Ops:
  10.5 25.5 %collective-permute-start.1 = (bf16[256,1024]{1,0:T(8,128)(2,1)S(1)}, bf16[256,1024]{1,0:T(8,128)(2,1)}, u32[]{:S(2)}, u32[]{:S(2)}) collective-permute-start(bf16[256,1024]{1,0:T(8,128)(2,1)S(1)} %pack_rows.3.refs_4_), channel_id=1, source_target_pairs={{0,8},{1,9},{2,10},{3,11},{4,12},{5,13},{6,14},{7,15},{8,0},{9,1},... | collective-permute-start | bytes 1572872 | tf_op jit(solution)/shard_map/ppermute | solution.py:119
  13.4 22.8 %collective-permute-start.2 = (bf16[256,1024]{1,0:T(8,128)(2,1)S(1)}, bf16[256,1024]{1,0:T(8,128)(2,1)}, u32[]{:S(2)}, u32[]{:S(2)}) collective-permute-start(bf16[256,1024]{1,0:T(8,128)(2,1)S(1)} %pack_rows.3.refs_4_), channel_id=1, source_target_pairs={{0,4},{1,5},{2,6},{3,7},{4,0},{5,1},{6,2},{7,3},{8,12},{9,13},{10,... | collective-permute-start | bytes 1572872 | tf_op jit(solution)/shard_map/ppermute | solution.py:119
  36.2 19.4 %collective-permute-start.8 = (bf16[256,1024]{1,0:T(8,128)(2,1)}, bf16[256,1024]{1,0:T(8,128)(2,1)}, u32[]{:S(2)}, u32[]{:S(2)}) collective-permute-start(bf16[256,1024]{1,0:T(8,128)(2,1)} %collective-permute-done.1.refs_6_), channel_id=1, source_target_pairs={{0,4},{1,5},{2,6},{3,7},{4,0},{5,1},{6,2},{7,3},{8,12},{9,13},{10,... | collective-permute-start | bytes 1572872 | tf_op jit(solution)/shard_map/ppermute | solution.py:119
  38.4 16.1 %all-to-all-start = ((bf16[16,2,1792]{2,1,0:T(2,128)(2,1)}), bf16[16,2,1792]{2,1,0:T(2,128)(2,1)}, u32[]{:S(2)}, u32[]{:S(2)}) async-start(bf16[16,2,1792]{2,1,0:T(2,128)(2,1)} %reshape.68), calls=%async_computation | async-start | bytes 229376 | tf_op jit(solution)/shard_map/all_to_all | solution.py:1528
  43.8 15.5 %collective-permute-start.9 = (bf16[256,1024]{1,0:T(8,128)(2,1)S(1)}, bf16[256,1024]{1,0:T(8,128)(2,1)}, u32[]{:S(2)}, u32[]{:S(2)}) collective-permute-start(bf16[256,1024]{1,0:T(8,128)(2,1)S(1)} %pack_rows.3.refs_4_), channel_id=1, source_target_pairs={{0,1},{1,0},{2,3},{3,2},{4,5},{5,4},{6,7},{7,6},{8,9},{9,8},{10,11... | collective-permute-start | bytes 1572872 | tf_op jit(solution)/shard_map/ppermute | solution.py:119
  44.2 17.3 %collective-permute-start.11 = (bf16[256,1024]{1,0:T(8,128)(2,1)}, bf16[256,1024]{1,0:T(8,128)(2,1)}, u32[]{:S(2)}, u32[]{:S(2)}) collective-permute-start(bf16[256,1024]{1,0:T(8,128)(2,1)} %collective-permute-done.1.refs_6_), channel_id=1, source_target_pairs={{0,1},{1,0},{2,3},{3,2},{4,5},{5,4},{6,7},{7,6},{8,9},{9,8},{10,11... | collective-permute-start | bytes 1572872 | tf_op jit(solution)/shard_map/ppermute | solution.py:119
  44.4 17.1 %collective-permute-start.10 = (bf16[256,1024]{1,0:T(8,128)(2,1)}, bf16[256,1024]{1,0:T(8,128)(2,1)}, u32[]{:S(2)}, u32[]{:S(2)}) collective-permute-start(bf16[256,1024]{1,0:T(8,128)(2,1)} %collective-permute-done.2.refs_5_), channel_id=1, source_target_pairs={{0,1},{1,0},{2,3},{3,2},{4,5},{5,4},{6,7},{7,6},{8,9},{9,8},{10,11... | collective-permute-start | bytes 1572872 | tf_op jit(solution)/shard_map/ppermute | solution.py:119
  59.1 28.4 %collective-permute-start.17 = (bf16[768,384]{1,0:T(8,128)(2,1)S(1)}, bf16[768,384]{1,0:T(8,128)(2,1)S(1)}, u32[]{:S(2)}, u32[]{:S(2)}) collective-permute-start(bf16[768,384]{1,0:T(8,128)(2,1)S(1)} %get-tuple-element.405), channel_id=1, source_target_pairs={{0,8},{1,9},{2,10},{3,11},{4,12},{5,13},{6,14},{7,15},{8,0},{9,1},... | collective-permute-start | bytes 1769480 | tf_op jit(solution)/shard_map/ppermute | solution.py:119
  59.3 21.9 %collective-permute-start.16 = (bf16[512,384]{1,0:T(8,128)(2,1)}, bf16[512,384]{1,0:T(8,128)(2,1)S(1)}, u32[]{:S(2)}, u32[]{:S(2)}) collective-permute-start(bf16[512,384]{1,0:T(8,128)(2,1)} %get-tuple-element.404), channel_id=1, source_target_pairs={{0,4},{1,5},{2,6},{3,7},{4,0},{5,1},{6,2},{7,3},{8,12},{9,13},{10,... | collective-permute-start | bytes 1179656 | tf_op jit(solution)/shard_map/ppermute | solution.py:119
  70.9 16.5 %collective-permute-start.13 = (bf16[128,1024]{1,0:T(8,128)(2,1)S(1)}, bf16[128,1024]{1,0:T(8,128)(2,1)S(1)}, u32[]{:S(2)}, u32[]{:S(2)}) collective-permute-start(bf16[128,1024]{1,0:T(8,128)(2,1)S(1)} %get-tuple-element.401), channel_id=1, source_target_pairs={{0,18},{1,19},{2,16},{3,17},{4,22},{5,23},{6,20},{7,21},{8,26},{9,... | collective-permute-start | bytes 786440 | tf_op jit(solution)/shard_map/ppermute | solution.py:119
  72.3 15.1 %collective-permute-start.14 = (bf16[128,1024]{1,0:T(8,128)(2,1)S(1)}, bf16[128,1024]{1,0:T(8,128)(2,1)S(1)}, u32[]{:S(2)}, u32[]{:S(2)}) collective-permute-start(bf16[128,1024]{1,0:T(8,128)(2,1)S(1)} %get-tuple-element.402), channel_id=1, source_target_pairs={{0,16},{1,17},{2,18},{3,19},{4,20},{5,21},{6,22},{7,23},{8,24},{9,... | collective-permute-start | bytes 786440 | tf_op jit(solution)/shard_map/ppermute | solution.py:119
  72.9 14.6 %collective-permute-start.15 = (bf16[128,1024]{1,0:T(8,128)(2,1)S(1)}, bf16[128,1024]{1,0:T(8,128)(2,1)S(1)}, u32[]{:S(2)}, u32[]{:S(2)}) collective-permute-start(bf16[128,1024]{1,0:T(8,128)(2,1)S(1)} %get-tuple-element.403), channel_id=1, source_target_pairs={{0,2},{1,3},{2,0},{3,1},{4,6},{5,7},{6,4},{7,5},{8,10},{9,11},{10,... | collective-permute-start | bytes 786440 | tf_op jit(solution)/shard_map/ppermute | solution.py:119
  87.9 15.2 %collective-permute-start.18 = (bf16[128,1024]{1,0:T(8,128)(2,1)S(1)}, bf16[128,1024]{1,0:T(8,128)(2,1)S(1)}, u32[]{:S(2)}, u32[]{:S(2)}) collective-permute-start(bf16[128,1024]{1,0:T(8,128)(2,1)S(1)} %get-tuple-element.414.refs_1_), channel_id=1, source_target_pairs={{0,4},{1,5},{2,6},{3,7},{4,0},{5,1},{6,2},{7,3},{8,12},{9,13},{10,... | collective-permute-start | bytes 786440 | tf_op jit(solution)/shard_map/ppermute | solution.py:119
  88.0 15.6 %collective-permute-start.19 = (bf16[128,1024]{1,0:T(8,128)(2,1)S(1)}, bf16[128,1024]{1,0:T(8,128)(2,1)S(1)}, u32[]{:S(2)}, u32[]{:S(2)}) collective-permute-start(bf16[128,1024]{1,0:T(8,128)(2,1)S(1)} %get-tuple-element.414.refs_1_), channel_id=1, source_target_pairs={{0,2},{1,3},{2,0},{3,1},{4,6},{5,7},{6,4},{7,5},{8,10},{9,11},{10,... | collective-permute-start | bytes 786440 | tf_op jit(solution)/shard_map/ppermute | solution.py:119
  88.5 17.0 %collective-permute-start.20 = (bf16[128,1024]{1,0:T(8,128)(2,1)S(1)}, bf16[128,1024]{1,0:T(8,128)(2,1)S(1)}, u32[]{:S(2)}, u32[]{:S(2)}) collective-permute-start(bf16[128,1024]{1,0:T(8,128)(2,1)S(1)} %get-tuple-element.414.refs_1_), channel_id=1, source_target_pairs={{0,6},{1,7},{2,4},{3,5},{4,2},{5,3},{6,0},{7,1},{8,14},{9,15},{10,... | collective-permute-start | bytes 786440 | tf_op jit(solution)/shard_map/ppermute | solution.py:119
  92.2 20.9 %collective-permute-start.25 = (bf16[512,384]{1,0:T(8,128)(2,1)S(1)}, bf16[512,384]{1,0:T(8,128)(2,1)S(1)}, u32[]{:S(2)}, u32[]{:S(2)}) collective-permute-start(bf16[512,384]{1,0:T(8,128)(2,1)S(1)} %slice.79), channel_id=1, source_target_pairs={{0,4},{1,5},{2,6},{3,7},{4,0},{5,1},{6,2},{7,3},{8,12},{9,13},{10,... | collective-permute-start | bytes 1179656 | tf_op jit(solution)/shard_map/ppermute | solution.py:119
  114.1 24.5 %collective-permute-start.28 = (bf16[1024,384]{1,0:T(8,128)(2,1)S(1)}, bf16[1024,384]{1,0:T(8,128)(2,1)}, u32[]{:S(2)}, u32[]{:S(2)}) collective-permute-start(bf16[1024,384]{1,0:T(8,128)(2,1)S(1)} %get-tuple-element.452.refs_6_.refs_0_), channel_id=1, source_target_pairs={{0,16},{1,17},{2,18},{3,19},{4,20},{5,21},{6,22},{7,23},{8,24},{9,... | collective-permute-start | bytes 2359304 | tf_op jit(solution)/shard_map/ppermute | solution.py:119
  115.7 22.9 %collective-permute-start.29 = (bf16[1024,384]{1,0:T(8,128)(2,1)S(1)}, bf16[1024,384]{1,0:T(8,128)(2,1)}, u32[]{:S(2)}, u32[]{:S(2)}) collective-permute-start(bf16[1024,384]{1,0:T(8,128)(2,1)S(1)} %get-tuple-element.452.refs_6_.refs_0_), channel_id=1, source_target_pairs={{0,2},{1,3},{2,0},{3,1},{4,6},{5,7},{6,4},{7,5},{8,10},{9,11},{10,... | collective-permute-start | bytes 2359304 | tf_op jit(solution)/shard_map/ppermute | solution.py:119
  115.9 26.0 %collective-permute-start.30 = (bf16[256,1024]{1,0:T(8,128)(2,1)S(1)}, bf16[256,1024]{1,0:T(8,128)(2,1)}, u32[]{:S(2)}, u32[]{:S(2)}) collective-permute-start(bf16[256,1024]{1,0:T(8,128)(2,1)S(1)} %pack_rows.4.refs_4_), channel_id=1, source_target_pairs={{0,8},{1,9},{2,10},{3,11},{4,12},{5,13},{6,14},{7,15},{8,0},{9,1},... | collective-permute-start | bytes 1572872 | tf_op jit(solution)/shard_map/ppermute | solution.py:119
  117.0 24.8 %collective-permute-start.31 = (bf16[256,1024]{1,0:T(8,128)(2,1)S(1)}, bf16[256,1024]{1,0:T(8,128)(2,1)S(1)}, u32[]{:S(2)}, u32[]{:S(2)}) collective-permute-start(bf16[256,1024]{1,0:T(8,128)(2,1)S(1)} %pack_rows.4.refs_4_), channel_id=1, source_target_pairs={{0,4},{1,5},{2,6},{3,7},{4,0},{5,1},{6,2},{7,3},{8,12},{9,13},{10,... | collective-permute-start | bytes 1572872 | tf_op jit(solution)/shard_map/ppermute | solution.py:119
  143.1 17.6 %collective-permute-start.36 = (bf16[512,384]{1,0:T(8,128)(2,1)S(1)}, bf16[512,384]{1,0:T(8,128)(2,1)S(1)}, u32[]{:S(2)}, u32[]{:S(2)}) collective-permute-start(bf16[512,384]{1,0:T(8,128)(2,1)S(1)} %slice.80), channel_id=1, source_target_pairs={{0,2},{1,3},{2,0},{3,1},{4,6},{5,7},{6,4},{7,5},{8,10},{9,11},{10,... | collective-permute-start | bytes 1179656 | tf_op jit(solution)/shard_map/ppermute | solution.py:119
  145.8 14.9 %collective-permute-start.37 = (bf16[512,384]{1,0:T(8,128)(2,1)S(1)}, bf16[512,384]{1,0:T(8,128)(2,1)S(1)}, u32[]{:S(2)}, u32[]{:S(2)}) collective-permute-start(bf16[512,384]{1,0:T(8,128)(2,1)S(1)} %slice.81), channel_id=1, source_target_pairs={{0,16},{1,17},{2,18},{3,19},{4,20},{5,21},{6,22},{7,23},{8,24},{9,... | collective-permute-start | bytes 1179656 | tf_op jit(solution)/shard_map/ppermute | solution.py:119
  149.0 13.4 %collective-permute-start.34 = (bf16[128,1024]{1,0:T(8,128)(2,1)S(1)}, bf16[128,1024]{1,0:T(8,128)(2,1)S(1)}, u32[]{:S(2)}, u32[]{:S(2)}) collective-permute-start(bf16[128,1024]{1,0:T(8,128)(2,1)S(1)} %get-tuple-element.441), channel_id=1, source_target_pairs={{0,4},{1,5},{2,6},{3,7},{4,0},{5,1},{6,2},{7,3},{8,12},{9,13},{10,... | collective-permute-start | bytes 786440 | tf_op jit(solution)/shard_map/ppermute | solution.py:119
  150.9 14.9 %collective-permute-start.35 = (bf16[128,1024]{1,0:T(8,128)(2,1)S(1)}, bf16[128,1024]{1,0:T(8,128)(2,1)S(1)}, u32[]{:S(2)}, u32[]{:S(2)}) collective-permute-start(bf16[128,1024]{1,0:T(8,128)(2,1)S(1)} %get-tuple-element.442), channel_id=1, source_target_pairs={{0,2},{1,3},{2,0},{3,1},{4,6},{5,7},{6,4},{7,5},{8,10},{9,11},{10,... | collective-permute-start | bytes 786440 | tf_op jit(solution)/shard_map/ppermute | solution.py:119
  169.5 14.2 %collective-permute-start.44 = (bf16[256,1024]{1,0:T(8,128)(2,1)}, bf16[256,1024]{1,0:T(8,128)(2,1)S(1)}, u32[]{:S(2)}, u32[]{:S(2)}) collective-permute-start(bf16[256,1024]{1,0:T(8,128)(2,1)} %collective-permute-done.30.refs_6_), channel_id=1, source_target_pairs={{0,4},{1,5},{2,6},{3,7},{4,0},{5,1},{6,2},{7,3},{8,12},{9,13},{10,... | collective-permute-start | bytes 1572872 | tf_op jit(solution)/shard_map/ppermute | solution.py:119
  195.9 14.1 %collective-permute-start.50 = (bf16[128,1024]{1,0:T(8,128)(2,1)}, bf16[128,1024]{1,0:T(8,128)(2,1)S(1)}, u32[]{:S(2)}, u32[]{:S(2)}) collective-permute-start(bf16[128,1024]{1,0:T(8,128)(2,1)} %get-tuple-element.468.refs_0_), channel_id=1, source_target_pairs={{0,2},{1,3},{2,0},{3,1},{4,6},{5,7},{6,4},{7,5},{8,10},{9,11},{10,... | collective-permute-start | bytes 786440 | tf_op jit(solution)/shard_map/ppermute | solution.py:119
  198.5 13.0 %collective-permute-start.51 = (bf16[128,1024]{1,0:T(8,128)(2,1)}, bf16[128,1024]{1,0:T(8,128)(2,1)S(1)}, u32[]{:S(2)}, u32[]{:S(2)}) collective-permute-start(bf16[128,1024]{1,0:T(8,128)(2,1)} %get-tuple-element.468.refs_0_), channel_id=1, source_target_pairs={{0,18},{1,19},{2,16},{3,17},{4,22},{5,23},{6,20},{7,21},{8,26},{9,... | collective-permute-start | bytes 786440 | tf_op jit(solution)/shard_map/ppermute | solution.py:119
  236.1 13.4 %collective-permute-start.56 = (bf16[128,1024]{1,0:T(8,128)(2,1)S(1)}, bf16[128,1024]{1,0:T(8,128)(2,1)S(1)}, u32[]{:S(2)}, u32[]{:S(2)}) collective-permute-start(bf16[128,1024]{1,0:T(8,128)(2,1)S(1)} %get-tuple-element.484.refs_0_), channel_id=1, source_target_pairs={{0,2},{1,3},{2,0},{3,1},{4,6},{5,7},{6,4},{7,5},{8,10},{9,11},{10,... | collective-permute-start | bytes 786440 | tf_op jit(solution)/shard_map/ppermute | solution.py:119
  237.5 12.0 %collective-permute-start.57 = (bf16[128,1024]{1,0:T(8,128)(2,1)S(1)}, bf16[128,1024]{1,0:T(8,128)(2,1)S(1)}, u32[]{:S(2)}, u32[]{:S(2)}) collective-permute-start(bf16[128,1024]{1,0:T(8,128)(2,1)S(1)} %get-tuple-element.484.refs_0_), channel_id=1, source_target_pairs={{0,18},{1,19},{2,16},{3,17},{4,22},{5,23},{6,20},{7,21},{8,26},{9,... | collective-permute-start | bytes 786440 | tf_op jit(solution)/shard_map/ppermute | solution.py:119
  260.0 13.6 %collective-permute-start.59 = (bf16[128,1024]{1,0:T(8,128)(2,1)S(1)}, bf16[128,1024]{1,0:T(8,128)(2,1)S(1)}, u32[]{:S(2)}, u32[]{:S(2)}) collective-permute-start(bf16[128,1024]{1,0:T(8,128)(2,1)S(1)} %get-tuple-element.497), channel_id=1, source_target_pairs={{0,16},{1,17},{2,18},{3,19},{4,20},{5,21},{6,22},{7,23},{8,24},{9,... | collective-permute-start | bytes 786440 | tf_op jit(solution)/shard_map/ppermute | solution.py:119
  274.4 16.8 %collective-permute-start.64 = (bf16[128,1024]{1,0:T(8,128)(2,1)S(1)}, bf16[128,1024]{1,0:T(8,128)(2,1)S(1)}, u32[]{:S(2)}, u32[]{:S(2)}) collective-permute-start(bf16[128,1024]{1,0:T(8,128)(2,1)S(1)} %get-tuple-element.520), channel_id=1, source_target_pairs={{0,4},{1,5},{2,6},{3,7},{4,0},{5,1},{6,2},{7,3},{8,12},{9,13},{10,... | collective-permute-start | bytes 786440 | tf_op jit(solution)/shard_map/ppermute | solution.py:119
  275.4 15.8 %collective-permute-start.65 = (bf16[128,1024]{1,0:T(8,128)(2,1)S(1)}, bf16[128,1024]{1,0:T(8,128)(2,1)S(1)}, u32[]{:S(2)}, u32[]{:S(2)}) collective-permute-start(bf16[128,1024]{1,0:T(8,128)(2,1)S(1)} %get-tuple-element.522), channel_id=1, source_target_pairs={{0,4},{1,5},{2,6},{3,7},{4,0},{5,1},{6,2},{7,3},{8,12},{9,13},{10,... | collective-permute-start | bytes 786440 | tf_op jit(solution)/shard_map/ppermute | solution.py:119
  288.5 14.4 %collective-permute-start.66 = (bf16[128,1024]{1,0:T(8,128)(2,1)S(1)}, bf16[128,1024]{1,0:T(8,128)(2,1)S(1)}, u32[]{:S(2)}, u32[]{:S(2)}) collective-permute-start(bf16[128,1024]{1,0:T(8,128)(2,1)S(1)} %get-tuple-element.538), channel_id=1, source_target_pairs={{0,4},{1,5},{2,6},{3,7},{4,0},{5,1},{6,2},{7,3},{8,12},{9,13},{10,... | collective-permute-start | bytes 786440 | tf_op jit(solution)/shard_map/ppermute | solution.py:119
  291.1 13.1 %collective-permute-start.67 = (bf16[128,1024]{1,0:T(8,128)(2,1)S(1)}, bf16[128,1024]{1,0:T(8,128)(2,1)S(1)}, u32[]{:S(2)}, u32[]{:S(2)}) collective-permute-start(bf16[128,1024]{1,0:T(8,128)(2,1)S(1)} %get-tuple-element.540), channel_id=1, source_target_pairs={{0,4},{1,5},{2,6},{3,7},{4,0},{5,1},{6,2},{7,3},{8,12},{9,13},{10,... | collective-permute-start | bytes 786440 | tf_op jit(solution)/shard_map/ppermute | solution.py:119
  304.3 16.2 %collective-permute-start.75 = (bf16[2048,768]{1,0:T(8,128)(2,1)S(1)}, bf16[2048,768]{1,0:T(8,128)(2,1)S(1)}, u32[]{:S(2)}, u32[]{:S(2)}) collective-permute-start(bf16[2048,768]{1,0:T(8,128)(2,1)S(1)} %get-tuple-element.543), channel_id=1, source_target_pairs={{0,1},{1,0},{2,3},{3,2},{4,5},{5,4},{6,7},{7,6},{8,9},{9,8},{10,11... | collective-permute-start | bytes 9437192 | tf_op jit(solution)/shard_map/ppermute | solution.py:119
  305.6 13.1 %collective-permute-start.69 = (bf16[128,1024]{1,0:T(8,128)(2,1)S(1)}, bf16[128,1024]{1,0:T(8,128)(2,1)S(1)}, u32[]{:S(2)}, u32[]{:S(2)}) collective-permute-start(bf16[128,1024]{1,0:T(8,128)(2,1)S(1)} %copy-done.45), channel_id=1, source_target_pairs={{0,2},{1,3},{2,0},{3,1},{4,6},{5,7},{6,4},{7,5},{8,10},{9,11},{10,... | collective-permute-start | bytes 786440 | tf_op jit(solution)/shard_map/ppermute | solution.py:119
  307.1 13.3 %collective-permute-start.70 = (bf16[128,1024]{1,0:T(8,128)(2,1)S(1)}, bf16[128,1024]{1,0:T(8,128)(2,1)S(1)}, u32[]{:S(2)}, u32[]{:S(2)}) collective-permute-start(bf16[128,1024]{1,0:T(8,128)(2,1)S(1)} %copy-done.45), channel_id=1, source_target_pairs={{0,6},{1,7},{2,4},{3,5},{4,2},{5,3},{6,0},{7,1},{8,14},{9,15},{10,... | collective-permute-start | bytes 786440 | tf_op jit(solution)/shard_map/ppermute | solution.py:119
  308.6 12.6 %collective-permute-start.71 = (bf16[128,1024]{1,0:T(8,128)(2,1)S(1)}, bf16[128,1024]{1,0:T(8,128)(2,1)S(1)}, u32[]{:S(2)}, u32[]{:S(2)}) collective-permute-start(bf16[128,1024]{1,0:T(8,128)(2,1)S(1)} %copy-done.45), channel_id=1, source_target_pairs={{0,1},{1,0},{2,3},{3,2},{4,5},{5,4},{6,7},{7,6},{8,9},{9,8},{10,11... | collective-permute-start | bytes 786440 | tf_op jit(solution)/shard_map/ppermute | solution.py:119
  322.0 30.9 %collective-permute-start.77 = (bf16[128,1024]{1,0:T(8,128)(2,1)S(1)}, bf16[128,1024]{1,0:T(8,128)(2,1)S(1)}, u32[]{:S(2)}, u32[]{:S(2)}) collective-permute-start(bf16[128,1024]{1,0:T(8,128)(2,1)S(1)} %plane_add.8), channel_id=1, source_target_pairs={{0,8},{1,9},{2,10},{3,11},{4,12},{5,13},{6,14},{7,15},{8,0},{9,1},... | collective-permute-start | bytes 786440 | tf_op jit(solution)/shard_map/ppermute | solution.py:119
  322.9 30.1 %collective-permute-start.78 = (bf16[128,1024]{1,0:T(8,128)(2,1)S(1)}, bf16[128,1024]{1,0:T(8,128)(2,1)S(1)}, u32[]{:S(2)}, u32[]{:S(2)}) collective-permute-start(bf16[128,1024]{1,0:T(8,128)(2,1)S(1)} %plane_add.9), channel_id=1, source_target_pairs={{0,8},{1,9},{2,10},{3,11},{4,12},{5,13},{6,14},{7,15},{8,0},{9,1},... | collective-permute-start | bytes 786440 | tf_op jit(solution)/shard_map/ppermute | solution.py:119
  324.9 28.0 %collective-permute-start.79 = (bf16[512,768]{1,0:T(8,128)(2,1)S(1)}, bf16[512,768]{1,0:T(8,128)(2,1)S(1)}, u32[]{:S(2)}, u32[]{:S(2)}) collective-permute-start(bf16[512,768]{1,0:T(8,128)(2,1)S(1)} %get-tuple-element.577), channel_id=1, source_target_pairs={{0,16},{1,17},{2,18},{3,19},{4,20},{5,21},{6,22},{7,23},{8,24},{9,... | collective-permute-start | bytes 2359304 | tf_op jit(solution)/shard_map/ppermute | solution.py:119
  325.1 27.9 %collective-permute-start.80 = (bf16[512,768]{1,0:T(8,128)(2,1)S(1)}, bf16[512,768]{1,0:T(8,128)(2,1)S(1)}, u32[]{:S(2)}, u32[]{:S(2)}) collective-permute-start(bf16[512,768]{1,0:T(8,128)(2,1)S(1)} %get-tuple-element.578), channel_id=1, source_target_pairs={{0,2},{1,3},{2,0},{3,1},{4,6},{5,7},{6,4},{7,5},{8,10},{9,11},{10,... | collective-permute-start | bytes 2359304 | tf_op jit(solution)/shard_map/ppermute | solution.py:119
  326.9 34.4 %collective-permute-start.81 = (bf16[512,768]{1,0:T(8,128)(2,1)S(1)}, bf16[512,768]{1,0:T(8,128)(2,1)S(1)}, u32[]{:S(2)}, u32[]{:S(2)}) collective-permute-start(bf16[512,768]{1,0:T(8,128)(2,1)S(1)} %get-tuple-element.579), channel_id=1, source_target_pairs={{0,18},{1,19},{2,16},{3,17},{4,22},{5,23},{6,20},{7,21},{8,26},{9,... | collective-permute-start | bytes 2359304 | tf_op jit(solution)/shard_map/ppermute | solution.py:119
  369.7 16.9 %collective-permute-start.87 = (bf16[256,1024]{1,0:T(8,128)(2,1)S(1)}, bf16[256,1024]{1,0:T(8,128)(2,1)S(1)}, u32[]{:S(2)}, u32[]{:S(2)}) collective-permute-start(bf16[256,1024]{1,0:T(8,128)(2,1)S(1)} %pack_rows.5), channel_id=1, source_target_pairs={{0,16},{1,17},{2,18},{3,19},{4,20},{5,21},{6,22},{7,23},{8,24},{9,... | collective-permute-start | bytes 1572872 | tf_op jit(solution)/shard_map/ppermute | solution.py:119
  371.3 15.3 %collective-permute-start.84 = (bf16[128,1024]{1,0:T(8,128)(2,1)S(1)}, bf16[128,1024]{1,0:T(8,128)(2,1)S(1)}, u32[]{:S(2)}, u32[]{:S(2)}) collective-permute-start(bf16[128,1024]{1,0:T(8,128)(2,1)S(1)} %get-tuple-element.584), channel_id=1, source_target_pairs={{0,6},{1,7},{2,4},{3,5},{4,2},{5,3},{6,0},{7,1},{8,14},{9,15},{10,... | collective-permute-start | bytes 786440 | tf_op jit(solution)/shard_map/ppermute | solution.py:119
  373.5 13.9 %collective-permute-start.85 = (bf16[128,1024]{1,0:T(8,128)(2,1)S(1)}, bf16[128,1024]{1,0:T(8,128)(2,1)S(1)}, u32[]{:S(2)}, u32[]{:S(2)}) collective-permute-start(bf16[128,1024]{1,0:T(8,128)(2,1)S(1)} %get-tuple-element.585), channel_id=1, source_target_pairs={{0,4},{1,5},{2,6},{3,7},{4,0},{5,1},{6,2},{7,3},{8,12},{9,13},{10,... | collective-permute-start | bytes 786440 | tf_op jit(solution)/shard_map/ppermute | solution.py:119
  373.9 13.5 %collective-permute-start.86 = (bf16[128,1024]{1,0:T(8,128)(2,1)S(1)}, bf16[128,1024]{1,0:T(8,128)(2,1)S(1)}, u32[]{:S(2)}, u32[]{:S(2)}) collective-permute-start(bf16[128,1024]{1,0:T(8,128)(2,1)S(1)} %get-tuple-element.586), channel_id=1, source_target_pairs={{0,2},{1,3},{2,0},{3,1},{4,6},{5,7},{6,4},{7,5},{8,10},{9,11},{10,... | collective-permute-start | bytes 786440 | tf_op jit(solution)/shard_map/ppermute | solution.py:119
  388.0 17.5 %collective-permute-start.93 = (bf16[384,768]{1,0:T(8,128)(2,1)S(1)}, bf16[384,768]{1,0:T(8,128)(2,1)S(1)}, u32[]{:S(2)}, u32[]{:S(2)}) collective-permute-start(bf16[384,768]{1,0:T(8,128)(2,1)S(1)} %get-tuple-element.619), channel_id=1, source_target_pairs={{0,4},{1,5},{2,6},{3,7},{4,0},{5,1},{6,2},{7,3},{8,12},{9,13},{10,... | collective-permute-start | bytes 1769480 | tf_op jit(solution)/shard_map/ppermute | solution.py:119
  389.4 14.6 %collective-permute-start.89 = (bf16[128,1024]{1,0:T(8,128)(2,1)S(1)}, bf16[128,1024]{1,0:T(8,128)(2,1)S(1)}, u32[]{:S(2)}, u32[]{:S(2)}) collective-permute-start(bf16[128,1024]{1,0:T(8,128)(2,1)S(1)} %get-tuple-element.631.refs_0_), channel_id=1, source_target_pairs={{0,16},{1,17},{2,18},{3,19},{4,20},{5,21},{6,22},{7,23},{8,24},{9,... | collective-permute-start | bytes 786440 | tf_op jit(solution)/shard_map/ppermute | solution.py:119
  390.7 13.3 %collective-permute-start.90 = (bf16[128,1024]{1,0:T(8,128)(2,1)S(1)}, bf16[128,1024]{1,0:T(8,128)(2,1)S(1)}, u32[]{:S(2)}, u32[]{:S(2)}) collective-permute-start(bf16[128,1024]{1,0:T(8,128)(2,1)S(1)} %get-tuple-element.631.refs_0_), channel_id=1, source_target_pairs={{0,2},{1,3},{2,0},{3,1},{4,6},{5,7},{6,4},{7,5},{8,10},{9,11},{10,... | collective-permute-start | bytes 786440 | tf_op jit(solution)/shard_map/ppermute | solution.py:119
  391.7 12.3 %collective-permute-start.91 = (bf16[128,1024]{1,0:T(8,128)(2,1)S(1)}, bf16[128,1024]{1,0:T(8,128)(2,1)S(1)}, u32[]{:S(2)}, u32[]{:S(2)}) collective-permute-start(bf16[128,1024]{1,0:T(8,128)(2,1)S(1)} %get-tuple-element.631.refs_0_), channel_id=1, source_target_pairs={{0,18},{1,19},{2,16},{3,17},{4,22},{5,23},{6,20},{7,21},{8,26},{9,... | collective-permute-start | bytes 786440 | tf_op jit(solution)/shard_map/ppermute | solution.py:119
  410.6 13.0 %collective-permute-start.95 = (bf16[128,1024]{1,0:T(8,128)(2,1)S(1)}, bf16[128,1024]{1,0:T(8,128)(2,1)S(1)}, u32[]{:S(2)}, u32[]{:S(2)}) collective-permute-start(bf16[128,1024]{1,0:T(8,128)(2,1)S(1)} %get-tuple-element.638), channel_id=1, source_target_pairs={{0,4},{1,5},{2,6},{3,7},{4,0},{5,1},{6,2},{7,3},{8,12},{9,13},{10,... | collective-permute-start | bytes 786440 | tf_op jit(solution)/shard_map/ppermute | solution.py:119
  429.1 13.0 %collective-permute-start.98 = (bf16[128,1024]{1,0:T(8,128)(2,1)S(1)}, bf16[128,1024]{1,0:T(8,128)(2,1)S(1)}, u32[]{:S(2)}, u32[]{:S(2)}) collective-permute-start(bf16[128,1024]{1,0:T(8,128)(2,1)S(1)} %get-tuple-element.650), channel_id=1, source_target_pairs={{0,16},{1,17},{2,18},{3,19},{4,20},{5,21},{6,22},{7,23},{8,24},{9,... | collective-permute-start | bytes 786440 | tf_op jit(solution)/shard_map/ppermute | solution.py:119
  430.1 12.8 %collective-permute-start.99 = (bf16[128,1024]{1,0:T(8,128)(2,1)S(1)}, bf16[128,1024]{1,0:T(8,128)(2,1)S(1)}, u32[]{:S(2)}, u32[]{:S(2)}) collective-permute-start(bf16[128,1024]{1,0:T(8,128)(2,1)S(1)} %get-tuple-element.651), channel_id=1, source_target_pairs={{0,2},{1,3},{2,0},{3,1},{4,6},{5,7},{6,4},{7,5},{8,10},{9,11},{10,... | collective-permute-start | bytes 786440 | tf_op jit(solution)/shard_map/ppermute | solution.py:119
  431.1 13.1 %collective-permute-start.102 = (bf16[128,1024]{1,0:T(8,128)(2,1)S(1)}, bf16[128,1024]{1,0:T(8,128)(2,1)S(1)}, u32[]{:S(2)}, u32[]{:S(2)}) collective-permute-start(bf16[128,1024]{1,0:T(8,128)(2,1)S(1)} %get-tuple-element.657), channel_id=1, source_target_pairs={{0,4},{1,5},{2,6},{3,7},{4,0},{5,1},{6,2},{7,3},{8,12},{9,13},{10,... | collective-permute-start | bytes 786440 | tf_op jit(solution)/shard_map/ppermute | solution.py:119
  436.2 18.1 %collective-permute-start.103 = (bf16[128,1024]{1,0:T(8,128)(2,1)S(1)}, bf16[128,1024]{1,0:T(8,128)(2,1)S(1)}, u32[]{:S(2)}, u32[]{:S(2)}) collective-permute-start(bf16[128,1024]{1,0:T(8,128)(2,1)S(1)} %get-tuple-element.659), channel_id=1, source_target_pairs={{0,4},{1,5},{2,6},{3,7},{4,0},{5,1},{6,2},{7,3},{8,12},{9,13},{10,... | collective-permute-start | bytes 786440 | tf_op jit(solution)/shard_map/ppermute | solution.py:119
  437.5 16.8 %collective-permute-start.104 = (bf16[128,768]{1,0:T(8,128)(2,1)S(1)}, bf16[128,768]{1,0:T(8,128)(2,1)S(1)}, u32[]{:S(2)}, u32[]{:S(2)}) collective-permute-start(bf16[128,768]{1,0:T(8,128)(2,1)S(1)} %get-tuple-element.661), channel_id=1, source_target_pairs={{0,12},{1,13},{2,14},{3,15},{4,8},{5,9},{6,10},{7,11},{8,4},{9,5},... | collective-permute-start | bytes 589832 | tf_op jit(solution)/shard_map/ppermute | solution.py:119
  442.1 25.6 %collective-permute-start.106 = (bf16[128,1024]{1,0:T(8,128)(2,1)S(1)}, bf16[128,1024]{1,0:T(8,128)(2,1)S(1)}, u32[]{:S(2)}, u32[]{:S(2)}) collective-permute-start(bf16[128,1024]{1,0:T(8,128)(2,1)S(1)} %plane_add.13), channel_id=1, source_target_pairs={{0,8},{1,9},{2,10},{3,11},{4,12},{5,13},{6,14},{7,15},{8,0},{9,1},... | collective-permute-start | bytes 786440 | tf_op jit(solution)/shard_map/ppermute | solution.py:119
  442.9 27.0 %collective-permute-start.112 = (bf16[128,768]{1,0:T(8,128)(2,1)S(1)}, bf16[128,768]{1,0:T(8,128)(2,1)S(1)}, u32[]{:S(2)}, u32[]{:S(2)}) collective-permute-start(bf16[128,768]{1,0:T(8,128)(2,1)S(1)} %conv_grads_sum.1.mine_ref), channel_id=1, source_target_pairs={{0,16},{1,17},{2,18},{3,19},{4,20},{5,21},{6,22},{7,23},{8,24},{9,... | collective-permute-start | bytes 589832 | tf_op jit(solution)/shard_map/ppermute | solution.py:119
  454.5 14.2 %collective-permute-start.107 = (bf16[64,1536]{1,0:T(8,128)(2,1)S(1)}, bf16[64,1536]{1,0:T(8,128)(2,1)S(1)}, u32[]{:S(2)}, u32[]{:S(2)}) collective-permute-start(bf16[64,1536]{1,0:T(8,128)(2,1)S(1)} %get-tuple-element.680), channel_id=1, source_target_pairs={{0,2},{1,3},{2,0},{3,1},{4,6},{5,7},{6,4},{7,5},{8,10},{9,11},{10,... | collective-permute-start | bytes 589832 | tf_op jit(solution)/shard_map/ppermute | solution.py:119
  454.7 26.8 %collective-permute-start.105 = (bf16[128,1024]{1,0:T(8,128)(2,1)S(1)}, bf16[128,1024]{1,0:T(8,128)(2,1)S(1)}, u32[]{:S(2)}, u32[]{:S(2)}) collective-permute-start(bf16[128,1024]{1,0:T(8,128)(2,1)S(1)} %plane_add.12), channel_id=1, source_target_pairs={{0,8},{1,9},{2,10},{3,11},{4,12},{5,13},{6,14},{7,15},{8,0},{9,1},... | collective-permute-start | bytes 786440 | tf_op jit(solution)/shard_map/ppermute | solution.py:119
  455.0 19.1 %collective-permute-start.109 = (bf16[64,1536]{1,0:T(8,128)(2,1)S(1)}, bf16[64,1536]{1,0:T(8,128)(2,1)S(1)}, u32[]{:S(2)}, u32[]{:S(2)}) collective-permute-start(bf16[64,1536]{1,0:T(8,128)(2,1)S(1)} %get-tuple-element.685.refs_0_), channel_id=1, source_target_pairs={{0,16},{1,17},{2,18},{3,19},{4,20},{5,21},{6,22},{7,23},{8,24},{9,... | collective-permute-start | bytes 589832 | tf_op jit(solution)/shard_map/ppermute | solution.py:119
  468.8 12.7 %collective-permute-start.108 = (bf16[128,1024]{1,0:T(8,128)(2,1)S(1)}, bf16[128,1024]{1,0:T(8,128)(2,1)S(1)}, u32[]{:S(2)}, u32[]{:S(2)}) collective-permute-start(bf16[128,1024]{1,0:T(8,128)(2,1)S(1)} %plane_add.14.refs_4_), channel_id=1, source_target_pairs={{0,16},{1,17},{2,18},{3,19},{4,20},{5,21},{6,22},{7,23},{8,24},{9,... | collective-permute-start | bytes 786440 | tf_op jit(solution)/shard_map/ppermute | solution.py:119
  489.1 22.3 %all-to-all-start.1 = ((bf16[32,80,128]{2,1,0:T(8,128)(2,1)}), bf16[32,80,128]{2,1,0:T(8,128)(2,1)S(1)}, u32[]{:S(2)}, u32[]{:S(2)}) async-start(bf16[32,80,128]{2,1,0:T(8,128)(2,1)} %small_pack.1), calls=%async_computation.1 | async-start | bytes 1310720 | tf_op jit(solution)/shard_map/all_to_all | solution.py:1640
  (140 other events, 1568.9 us)

commit v6 on v5

--- a/solution.py
+++ b/solution.py
@@ -545,7 +545,7 @@
     spot, pieces, rest = refs[0], refs[1 : 1 + SPAN], refs[1 + SPAN :]
     (mixed, table, peaks, weight_in, weight_out) = rest[:5]
     (branch, grad_mixed, grad_table, far, kept, sent) = rest[5:11]
-    keys, values, bias, grad_context, grad_keys, grad_values, slopes = rest[11:]
+    keys, values, bias, grad_context, grad_keys, grad_values, slopes, marked = rest[11:]
     length, width = grad_context.shape
     rows = length // SPAN
     head = table.shape[1] // 2
@@ -559,10 +559,14 @@
     grad_table[...] = jnp.zeros_like(grad_table)
     far[...] = jnp.zeros_like(far)
     lane = lax.broadcasted_iota(jnp.int32, (rows, width), 1)
-    padded = lax.broadcasted_iota(jnp.int32, (rows, length + 2 * rows), 1)
+    for which in range(2):
+        for block_id in range(SPAN):
+            own = slice(block_id * rows, (block_id + 1) * rows)
+            mark = jnp.where(lane % head == block_id, 1.0, 0.0).astype(BF)
+            marked[which, own, :] = jnp.where(lane // head == which, keys[own, :], mark)
     factor = head**-0.5
-    slopes[:, :rows] = jnp.zeros((rows, rows), F32)
-    slopes[:, rows + length :] = jnp.zeros((rows, rows), F32)
+    slopes[:, :rows] = jnp.zeros((rows, rows), BF)
+    slopes[:, rows + length :] = jnp.zeros((rows, rows), BF)
     mirror = (
         lax.broadcasted_iota(jnp.int32, (rows, rows), 0)
         + lax.broadcasted_iota(jnp.int32, (rows, rows), 1)
@@ -587,15 +591,15 @@
             grad_low = (probs * (grad_probs - shared)).astype(BF)
             grad_values[...] += dot_tn(probs.astype(BF), incoming)
             grad_keys[...] += dot_tn(grad_low, part)
-            slopes[:, rows : rows + length] = grad_low.astype(F32)
+            slopes[:, rows : rows + length] = grad_low
             window = slopes[:, pl.ds(place, 3 * rows)]
-            whole = slopes[...]
-            early = jnp.sum(jnp.where(padded < place, whole, 0.0), axis=1, keepdims=True)
-            late = jnp.sum(
-                jnp.where(padded >= place + 3 * rows, whole, 0.0), axis=1, keepdims=True
-            )
+            direct = dot_nn(grad_low, marked[which])
+            block_of = jnp.where(mine, SPAN, lane % head)
+            early = jnp.sum(jnp.where(block_of < index - 1, direct, 0.0), axis=1, keepdims=True)
+            after = (block_of > index + 1) & (block_of < SPAN)
+            late = jnp.sum(jnp.where(after, direct, 0.0), axis=1, keepdims=True)
             window = jnp.concatenate(
-                [jnp.zeros((rows, rows), F32), dot_nn(mirror, window.astype(BF))], axis=1
+                [jnp.zeros((rows, rows), F32), dot_nn(mirror, window)], axis=1
             )
             window = pltpu.roll(
                 window, 3 * rows + 1, axis=1, stride=1, stride_axis=0
@@ -611,7 +615,7 @@
                 precision=lax.Precision.HIGHEST,
             )
             results.append(
-                dot_nn(grad_low, keys[...])
+                direct
                 + close
                 + early * table[0:1, :].astype(F32)
                 + late * table[4 * rows - 1 :, :].astype(F32)
@@ -707,7 +711,8 @@
             pltpu.VMEM((length, width), BF),
             pltpu.VMEM((length, width), F32),
             pltpu.VMEM((length, width), F32),
-            pltpu.VMEM((rows, length + 2 * rows), F32),
+            pltpu.VMEM((rows, length + 2 * rows), BF),
+            pltpu.VMEM((2, length, width), BF),
         ],
         flops=96 * length * length * width,
     )
@@ -1055,7 +1060,14 @@
 def conv_relay(via_first, via_second, masks):
     first, second = masks
     half = via_first.shape[0] // 2
-    return flipped(via_first[:half], second), flipped(via_second[half:], first)
+    low, high = fused(
+        lambda one, two: (one[:half], two[half:]),
+        "conv_halves",
+        [shape_of(half, via_first.shape[1], BF)] * 2,
+        via_first,
+        via_second,
+    )
+    return flipped(low, second), flipped(high, first)
 
 
 def lay_conv(spot, refs, target, unit, first):
@@ -1079,14 +1091,22 @@
                 target[pl.ds(start, size), columns] = ref[source : source + size, own]
 
 
+def conv_whole_weights(pieces, model, place):
+    def kernel(spot, *refs):
+        w_in, w_out = refs[-2:]
+        lay_conv(spot, refs[:-2], w_in, place.unit, True)
+        lay_conv(spot, refs[:-2], w_out, place.unit, False)
+
+    outs = [shape_of(model, 2 * model, BF), shape_of(model, model, BF)]
+    return kernel_call(kernel, "conv_lay", outs, (place.spot, *pieces), scalars=1)
+
+
 def convolve_start(parts, before, wide, bias_row, weights, place):
     rows, model = before.shape
-    count = len(weights)
-
-    def kernel(spot, *refs):
-        part_refs, (base, small), weight_refs = refs[:4], refs[4:6], refs[6 : 6 + count]
-        current_ref, hidden_ref, doubled_ref, glued_ref, w_in = refs[6 + count :]
-        lay_conv(spot, weight_refs, w_in, place.unit, True)
+
+    def kernel(*refs):
+        part_refs, (base, small, w_in) = refs[:4], refs[4:7]
+        current_ref, hidden_ref, doubled_ref, glued_ref = refs[7:]
         parts_now = [ref[...] for ref in part_refs]
         current = base[...] + joined(parts_now) + small[bias_row : bias_row + 1, :]
         current_ref[...] = current
@@ -1106,10 +1126,7 @@
             shape_of(rows, 2 * model, F32),
             shape_of(rows, model, BF),
         ],
-        (place.spot, *parts, before, wide, *weights),
-        scalars=1,
-        scratch=[pltpu.VMEM((model, 2 * model), BF)],
-        limit=56,
+        (*parts, before, wide, weights[0]),
         flops=4 * rows * model * model,
     )
 
@@ -1118,10 +1135,10 @@
     rows, model = before.shape
     edge = border.shape[0]
 
-    def kernel(spot, glued_ref, border_ref, small, base, *refs):
-        weight_refs = refs[: len(weights)]
-        mixed_ref, rest_ref, current_ref, hidden_ref, padded, w_out = refs[len(weights) :]
-        lay_conv(spot, weight_refs, w_out, place.unit, False)
+    def kernel(
+        glued_ref, border_ref, small, base, w_out, mixed_ref, rest_ref, current_ref, hidden_ref,
+        padded,
+    ):
         padded[:edge, :] = border_ref[...].astype(F32)
         padded[edge:, :] = glued_ref[...].astype(F32)
         first, count = taps
@@ -1146,10 +1163,8 @@
         kernel,
         "convolve_finish",
         [shape_of(rows, model, dtype) for dtype in (F32, BF, F32, BF)],
-        (place.spot, glued, border, wide, before, *weights),
-        scalars=1,
-        scratch=[pltpu.VMEM((edge + rows, model), F32), pltpu.VMEM((model, model), BF)],
-        limit=56,
+        (glued, border, wide, before, weights[1]),
+        scratch=[pltpu.VMEM((edge + rows, model), F32)],
         flops=2 * rows * model * model,
     )
 
@@ -1160,13 +1175,10 @@
     first, count = taps
 
     def kernel(
-        spot, own, part_one, part_two, part_three, grad_ref, after_ref, mixed_ref, small,
-        glued_ref, border_ref, *refs,
+        own, part_one, part_two, part_three, grad_ref, after_ref, mixed_ref, small,
+        glued_ref, border_ref, w_out, grad_out, branch_ref, main_ref, halo_ref, sums,
+        padded, spread,
     ):
-        weight_refs = refs[: len(weights)]
-        grad_out, branch_ref, main_ref, halo_ref, sums = refs[len(weights) : -3]
-        padded, spread, w_out = refs[-3:]
-        lay_conv(spot, weight_refs, w_out, place.unit, False)
         incoming = joined((own[...], part_one[...], part_two[...], part_three[...]))
         slope, sum_gain, sum_shift = norm_back(after_ref[...], small[11:12, :], incoming)
         current = grad_ref[...] + slope
@@ -1213,15 +1225,10 @@
             shape_of(edge, model, BF),
             shape_of(count + 4, model, F32),
         ],
-        (
-            place.spot, *parts, grad, after, mixed, wide, glued, border,
-            *weights,
-        ),
-        scalars=1,
+        (*parts, grad, after, mixed, wide, glued, border, weights[1]),
         scratch=[
             pltpu.VMEM((edge + rows, model), F32),
             pltpu.VMEM((rows + 2 * edge, model), F32),
-            pltpu.VMEM((model, model), BF),
         ],
         limit=56,
         flops=2 * rows * model * model,
@@ -1231,11 +1238,11 @@
 def convolve_back_finish(main, incoming, doubled, weights, before, wide, grad, place):
     rows, model = before.shape
     edge = incoming.shape[0]
-    count = len(weights)
-
-    def kernel(spot, main_ref, late, both, base, small, grad_rows, *refs):
-        current_ref, branch_ref, slope_ref, sums, w_in = refs[count:]
-        lay_conv(spot, refs[:count], w_in, place.unit, True)
+
+    def kernel(
+        main_ref, late, both, base, small, grad_rows, w_in, current_ref, branch_ref, slope_ref,
+        sums,
+    ):
         last = main_ref[rows - edge :, :] + late[...].astype(F32)
         glued = jnp.concatenate([main_ref[: rows - edge, :], last], axis=0)
         glued = glued.astype(BF).astype(F32)
@@ -1261,13 +1268,7 @@
             shape_of(rows, 2 * model, BF),
             shape_of(3, model, F32),
         ],
-        (
-            place.spot, main, incoming, doubled, before, wide, grad,
-            *weights,
-        ),
-        scalars=1,
-        scratch=[pltpu.VMEM((model, 2 * model), BF)],
-        limit=56,
+        (main, incoming, doubled, before, wide, grad, weights[0]),
         flops=4 * rows * model * model,
     )
 
@@ -1775,15 +1776,19 @@
     if place.aligned:
         sent, via_first, via_second = tied(sent, via_first, via_second)
         low, high = conv_relay(via_first, via_second, place.feed_masks)
+        glue_far = [flipped(item, 1) for item in (glue, via_first, via_second)]
+        kept, *glue_far = tied(kept, *glue_far)
     sent, *second_far = tied(sent, *second_far)
     parts = group_reduce(kept, sent, place.span_masks)
     if place.aligned:
-        parts, glue, (second_pack, *second_far) = tied_lists(
-            parts, (glue, via_first, via_second, low, high), (second_pack, *second_far)
+        parts, (low, high), (second_pack, *second_far) = tied_lists(
+            parts, (low, high), (second_pack, *second_far)
         )
-        glue = [*glue, *(flipped(item, 1) for item in glue)]
+        glue = [glue, via_first, via_second, low, high]
+        glue += [*glue_far, flipped(low, 1), flipped(high, 1)]
     else:
         parts, (second_pack, *second_far) = tied_lists(parts, (second_pack, *second_far))
+    glue = conv_whole_weights(glue, model, place)
     second_near = plane_finish(second_pack, second_far, place)
     after_attend, conv_hidden, doubled, glued = convolve_start(
         parts, after_first, wide, count, glue, place
@@ -1849,18 +1854,16 @@
         kept, mix_swap = tied(kept, mix_swap)
         mix_swap = flipped(mix_swap, 1)
         kept, mix_swap = tied(kept, mix_swap)
-    kept, second_other = tied(kept, second_other)
-    second_pack = pack_rows((second_sums[0][:unit], second_other, second_sums[1]))
-    second_theirs = flipped(second_pack, place.shards)
     parts = group_reduce(kept, sent, place.span_masks)
     if place.aligned:
         mix_outs[1] = flipped(mix_outs[1], SPAN)
         planed = plane_pieces(mix_kept, mix_swap, conv_shares, place)
-        parts, (second_theirs, mix_outs[1]), planed = tied_lists(
-            parts, (second_theirs, mix_outs[1]), planed
+        parts, (second_other, mix_outs[1]), planed = tied_lists(
+            parts, (second_other, mix_outs[1]), planed
         )
     else:
-        parts, (second_theirs,) = tied_lists(parts, (second_theirs,))
+        parts, (second_other,) = tied_lists(parts, (second_other,))
+    second_pack = pack_rows((second_sums[0][:unit], second_other, second_sums[1]))
     grad_distance = distance_gradient(grad_table, table_far, rows)
     grad_first, branch, first_sums = attend_to_feed_back(parts, grad_attend, after_first, wide)
     if place.aligned:
@@ -1879,14 +1882,20 @@
         mix_grads = [item[None] for item in mix_grads]
     kept, sent = feed_out_grads(saved_first[2], pieces, place)
     out_split = plane_split(kept, flipped(sent, 1), place)
-    pieces, out_split = tied_lists(pieces, out_split)
+    pieces, out_split, (second_pack,) = tied_lists(pieces, out_split, (second_pack,))
+    second_theirs = flipped(second_pack, place.shards)
     out_lists = plane_early(out_split, place)
     result, branch, slope, first_bias = feed_back(pieces, first_packs, saved_first, place)
     slope, (out_top,) = tied_tops(slope, [out_lists], place)
+    slope, second_theirs = tied(slope, second_theirs)
     out_early = out_lists[0]
     if place.aligned:
-        slope, conv_last = tied(slope, conv_last)
-        conv_mine = conv_grads_sum(conv_zero, joint, conv_last)
+        slope, mix_three = tied(slope, mix_three)
+        mix_own, mix_other, mix_out_sum = attend_grads_sum(
+            (mix_zero, joint, mix_two, mix_three, *mix_outs), place
+        )
+        mix_arrived = flipped(mix_other, 2)
+        mix_theirs = [flipped(mix_own, place.shards), None, flipped(mix_out_sum, place.shards)]
     kept, sent = feed_in_grads(saved_first[0], slope, place)
     kept, *result = tied(kept, *result)
     in_swapped = flipped(sent, 1)
@@ -1895,21 +1904,27 @@
     out_last = plane_last(plane_total(out_top), place)
     parts, out_early, *in_lists = tied_lists(parts, out_early, *in_lists.values())
     in_early, in_top = in_lists[0], in_lists[-1]
-    in_last = plane_last(plane_total(in_top), place)
+    in_top = plane_total(in_top)
     if place.aligned:
-        parts[0], mix_three = tied(parts[0], mix_three)
-        mix_own, mix_other, mix_out_sum = attend_grads_sum(
-            (mix_zero, joint, mix_two, mix_three, *mix_outs), place
+        parts[0], in_top, mix_arrived, mix_theirs[0], mix_theirs[2], conv_last = tied(
+            parts[0], in_top, mix_arrived, mix_theirs[0], mix_theirs[2], conv_last
         )
-        mix_arrived = flipped(mix_other, 2)
-        mix_theirs = [flipped(mix_own, place.shards), None, flipped(mix_out_sum, place.shards)]
+        mix_theirs[1] = flipped(mix_arrived, place.shards)
+        conv_mine = conv_grads_sum(conv_zero, joint, conv_last)
         conv_theirs = flipped(conv_mine, place.shards)
+    in_last = plane_last(in_top, place)
     grad_input, input_sums = last_step(parts, grad_first, inputs, wide)
-    if place.aligned:
-        input_sums, out_last, mix_arrived = tied(input_sums, out_last, mix_arrived)
-        mix_theirs[1] = flipped(mix_arrived, place.shards)
+    input_sums, out_last = tied(input_sums, out_last)
     out_sum = plane_add([*out_early, out_last])
     out_theirs = flipped(out_sum, place.shards)
+    small_grads, bias_grads, grad_distance = small_reduce(
+        (input_sums, first_sums, attend_sums, conv_sums, last_sums),
+        mix_sums,
+        (first_bias, second_bias),
+        grad_distance,
+        (wide_rows, tap_count),
+        place,
+    )
     if place.aligned:
         mix_grads = attend_grads_final((mix_own, mix_arrived, mix_out_sum), mix_theirs, place)
         conv_grads = conv_grads_final(conv_mine, conv_theirs, place)
@@ -1919,22 +1934,13 @@
             conv_whole[2][None],
         )
 
-    (in_last, input_sums, out_theirs), mix_grads, conv_grads = tied_lists(
-        (in_last, input_sums, out_theirs), mix_grads, conv_grads
+    (in_last, small_grads, out_theirs), mix_grads, conv_grads = tied_lists(
+        (in_last, small_grads, out_theirs), mix_grads, conv_grads
     )
     in_sum = plane_add([*in_early, in_last])
     in_own, in_other = in_sum[:unit], flipped(in_sum[unit:], 2)
     in_theirs = flipped(in_own, place.shards)
-    input_sums, in_other, in_theirs = tied(input_sums, in_other, in_theirs)
     first_mine = [(in_own, in_theirs), (in_other, flipped(in_other, place.shards))]
-    small_grads, bias_grads, grad_distance = small_reduce(
-        (input_sums, first_sums, attend_sums, conv_sums, last_sums),
-        mix_sums,
-        (first_bias, second_bias),
-        grad_distance,
-        (wide_rows, tap_count),
-        place,
-    )
     first_mine = [*first_mine, (out_sum, out_theirs)]
     cuts = (0, unit, 2 * unit, 2 * unit + half)
     second_mine = [

time: 526 us -> 509 us (0.968); the launches traced: 516 us -> 506 us
  waiting for transfers between devices: 232 us -> 220 us
    ppermute x114, waiting for transfers between devices: 218 us -> 210 us  [flipped(): lax.ppermute(value, ('rep', 'shard'), [(i, i ^ mask) for i in range(total)])]
    unnamed x176 -> x222, local copies, waits for them, and re-layouts: 23.6 us -> 30.3 us
    pallas_call x54 -> x56, Pallas kernels: 126 us -> 123 us  [kernel_call(): pl.pallas_call(body, grid=(1,), in_specs=specs, out_specs=vmem(len(outs))...]
  transfers between devices with their start and end apart: 118 -> 118, of which waited for: 55 -> 55; matrix products, arithmetic and copies ran while one was open for 2% -> 1% of each run, Pallas kernels for 20% -> 19%
where the time goes in v6:
time: 509 us; the launch traced here: 506 us
  waiting for transfers between devices  220 us (43%)
  starting transfers between devices  125 us (25%)
  Pallas kernels  124 us (24%)
  local copies, waits for them, and re-layouts  33.2 us (7%)
    ppermute x114, waiting for transfers between devices, flipped(): lax.ppermute(value, ('rep', 'shard'), [(i, i ^ mask) for i in range(total)])  210 us
    pallas_call x56, Pallas kernels, kernel_call(): pl.pallas_call(body, grid=(1,), in_specs=specs, out_specs=vmem(len(outs))...  123 us
    ppermute x114, starting transfers between devices, flipped(): lax.ppermute(value, ('rep', 'shard'), [(i, i ^ mask) for i in range(total)])  114 us
    unnamed x222, local copies, waits for them, and re-layouts  30.3 us
  transfers between devices with their start and end apart: 118, of which 55 were waited for; matrix products, arithmetic and copies ran while one was open for 1% of the time, Pallas kernels for 19%

profile of v6, /device:TPU:0, one launch (start us, length us, event | category | flops | bytes accessed | tf_op | source)
XLA Modules:
  0.0 506.0 jit_solution(11623156309447336445)
XLA Ops:
  3.9 3.0 collective-permute-start
  6.9 3.5 collective-permute-done.refs_1_
  10.5 2.9 collective-permute-start.1
  20.0 3.8 collective-permute-done.3.refs_1_
  26.9 8.3 %collective-permute-done.6.refs_2_ = bf16[128,1024]{1,0:T(8,128)(2,1)S(1)} collective-permute-done((bf16[128,1024]{1,0:T(8,128)(2,1)S(1)}, bf16[128,1024]{1,0:T(8,128)(2,1)S(1)}, u32[]{:S(2)}, u32[]{:S(2)}) %collective-permute-start.6) | collective-permute-done | bytes 262176 | tf_op jit(solution)/shard_map/ppermute | solution.py:119
  38.4 4.7 all-to-all-start
  46.2 8.2 %all-to-all-done = bf16[16,2,1792]{2,1,0:T(2,128)(2,1)S(1)} async-done(((bf16[16,2,1792]{2,1,0:T(2,128)(2,1)}), bf16[16,2,1792]{2,1,0:T(2,128)(2,1)S(1)}, u32[]{:S(2)}, u32[]{:S(2)}) %all-to-all-start) | async-done | bytes 114720 | tf_op jit(solution)/shard_map/all_to_all | solution.py:1529
  57.8 2.2 collective-permute-start.16
  62.9 5.2 %feed_forward.2 = (bf16[512,1024]{1,0:T(8,128)(2,1)S(1)}, f32[512,1024]{1,0:T(8,128)S(1)}, bf16[512,1024]{1,0:T(8,128)(2,1)S(1)}, f32[128,1024]{1,0:T(8,128)S(1)...) custom-call(s32[4]{0:T(128)S(1)} %pad_add_fusion.spot.spot_ref, ...), custom_call_target="tpu_custom_call" | custom-call | flops 2147483648 | bytes 10948608 | tf_op jit(solution)/shard_map/feed_forward/pallas_call | solution.py:86
  74.0 5.7 %collective-permute-done.16.refs_2_ = bf16[512,384]{1,0:T(8,128)(2,1)S(1)} collective-permute-done((bf16[512,384]{1,0:T(8,128)(2,1)}, bf16[512,384]{1,0:T(8,128)(2,1)S(1)}, u32[]{:S(2)}, u32[]{:S(2)}) %collective-permute-start.16) | collective-permute-done | bytes 393248 | tf_op jit(solution)/shard_map/ppermute | solution.py:119
  79.7 6.3 %collective-permute-done.17.refs_3_ = bf16[768,384]{1,0:T(8,128)(2,1)S(1)} collective-permute-done((bf16[768,384]{1,0:T(8,128)(2,1)S(1)}, bf16[768,384]{1,0:T(8,128)(2,1)S(1)}, u32[]{:S(2)}, u32[]{:S(2)}) %collective-permute-start.17) | collective-permute-done | bytes 589856 | tf_op jit(solution)/shard_map/ppermute | solution.py:119
  87.6 3.0 collective-permute-start.20
  91.3 2.1 collective-permute-start.25
  93.4 8.9 %collective-permute-done.26.refs_1_ = bf16[64,1024]{1,0:T(8,128)(2,1)S(1)} collective-permute-done((bf16[64,1024]{1,0:T(8,128)(2,1)S(1)}, bf16[64,1024]{1,0:T(8,128)(2,1)S(1)}, u32[]{:S(2)}, u32[]{:S(2)}) %collective-permute-start.26) | collective-permute-done | bytes 131104 | tf_op jit(solution)/shard_map/ppermute | solution.py:119
  104.7 7.6 %collective-permute-done.25.refs_4_ = bf16[512,384]{1,0:T(8,128)(2,1)S(1)} collective-permute-done((bf16[512,384]{1,0:T(8,128)(2,1)S(1)}, bf16[512,384]{1,0:T(8,128)(2,1)S(1)}, u32[]{:S(2)}, u32[]{:S(2)}) %collective-permute-start.25) | collective-permute-done | bytes 393248 | tf_op jit(solution)/shard_map/ppermute | solution.py:119
  123.2 28.6 %attend_forward.1 = (bf16[1024,1024]{1,0:T(8,128)(2,1)}, bf16[1024,384]{1,0:T(8,128)(2,1)}, bf16[1024,128]{1,0:T(8,128)(2,1)}, f32[1024,128]{1,0:T(8,128)}, f32[...) custom-call(s32[1]{0:T(128)} %bitcast.4.refs_0_, bf16[128,1024]{1,0:T(8,128)(2,1)} %copy-done.73, ...), custom_call_target="tpu_custom_call" | custom-call | flops 6442450944 | bytes 10094080 | tf_op jit(solution)/shard_map/attend_forward/pallas_call | solution.py:86
  163.3 7.1 %collective-permute-done.39.refs_3_ = bf16[512,384]{1,0:T(8,128)(2,1)S(1)} collective-permute-done((bf16[512,384]{1,0:T(8,128)(2,1)S(1)}, bf16[512,384]{1,0:T(8,128)(2,1)S(1)}, u32[]{:S(2)}, u32[]{:S(2)}) %collective-permute-start.39) | collective-permute-done | bytes 393248 | tf_op jit(solution)/shard_map/ppermute | solution.py:119
  170.5 4.6 collective-permute-done.37.refs_2_
  183.8 2.0 collective-permute-start.43
  186.7 3.4 collective-permute-done.44.refs_7_
  191.2 3.4 convolve_finish.1
  199.6 5.7 %collective-permute-done.49.refs_1_ = bf16[128,1024]{1,0:T(8,128)(2,1)S(1)} collective-permute-done((bf16[128,1024]{1,0:T(8,128)(2,1)S(1)}, bf16[128,1024]{1,0:T(8,128)(2,1)S(1)}, u32[]{:S(2)}, u32[]{:S(2)}) %collective-permute-start.49) | collective-permute-done | bytes 262176 | tf_op jit(solution)/shard_map/ppermute | solution.py:119
  205.3 4.2 collective-permute-done.50.refs_2_
  211.2 4.0 feed_forward.3
  218.8 6.7 %collective-permute-done.52.refs_1_ = bf16[128,1024]{1,0:T(8,128)(2,1)S(1)} collective-permute-done((bf16[128,1024]{1,0:T(8,128)(2,1)S(1)}, bf16[128,1024]{1,0:T(8,128)(2,1)S(1)}, u32[]{:S(2)}, u32[]{:S(2)}) %collective-permute-start.52) | collective-permute-done | bytes 262176 | tf_op jit(solution)/shard_map/ppermute | solution.py:119
  225.5 2.6 collective-permute-done.53.refs_2_
  235.2 5.7 %collective-permute-done.55.refs_1_ = bf16[128,1024]{1,0:T(8,128)(2,1)S(1)} collective-permute-done((bf16[128,1024]{1,0:T(8,128)(2,1)S(1)}, bf16[128,1024]{1,0:T(8,128)(2,1)S(1)}, u32[]{:S(2)}, u32[]{:S(2)}) %collective-permute-start.55) | collective-permute-done | bytes 262176 | tf_op jit(solution)/shard_map/ppermute | solution.py:119
  240.9 4.8 collective-permute-done.56.refs_2_
  245.7 4.3 feed_backward.2
  250.0 2.0 feed_in_grads.2
  252.0 2.3 feed_out_grads.2
  260.8 4.1 collective-permute-done.58.part_one
  265.0 4.9 collective-permute-done.59.part_two
  272.0 9.4 %convolve_back_start.1 = (f32[128,1024]{1,0:T(8,128)}, bf16[128,1024]{1,0:T(8,128)(2,1)}, f32[128,1024]{1,0:T(8,128)}, bf16[32,1024]{1,0:T(8,128)(2,1)}, f32[35,1024]{1,0:T(8,128)}) custom-call(f32[128,1024]{1,0:T(8,128)} %copy-done.31, bf16[128,1024]{1,0:T(8,128)(2,1)} %copy-done.94, bf16[128,1024]{1,0:T(8,128)(2,1)} %copy-done.95, ...), custom_call_target="tpu_custom_call" | custom-call | flops 268435456 | bytes 7024640 | tf_op jit(solution)/shard_map/convolve_back_start/pallas_call | solution.py:86
  283.3 2.6 collective-permute-start.66
  286.2 2.2 copy-done.1
  292.2 3.0 conv_grads.1
  295.2 3.9 collective-permute-done.67.refs_1_
  302.7 5.6 %collective-permute-done.68.refs_5_ = bf16[128,1024]{1,0:T(8,128)(2,1)S(1)} collective-permute-done((bf16[128,1024]{1,0:T(8,128)(2,1)S(1)}, bf16[128,1024]{1,0:T(8,128)(2,1)S(1)}, u32[]{:S(2)}, u32[]{:S(2)}) %collective-permute-start.68) | collective-permute-done | bytes 262176 | tf_op jit(solution)/shard_map/ppermute | solution.py:119
  308.3 5.8 %collective-permute-done.69.refs_3_ = bf16[128,1024]{1,0:T(8,128)(2,1)S(1)} collective-permute-done((bf16[128,1024]{1,0:T(8,128)(2,1)S(1)}, bf16[128,1024]{1,0:T(8,128)(2,1)S(1)}, u32[]{:S(2)}, u32[]{:S(2)}) %collective-permute-start.69) | collective-permute-done | bytes 262176 | tf_op jit(solution)/shard_map/ppermute | solution.py:119
  316.1 2.0 collective-permute-start.77
  322.5 22.2 %attend_backward.1 = (bf16[1024,1024]{1,0:T(8,128)(2,1)S(1)}, bf16[1024,384]{1,0:T(8,128)(2,1)S(1)}, f32[512,128]{1,0:T(8,128)S(1)}, f32[8,128]{1,0:T(8,128)S(1)...) custom-call(s32[1]{0:T(128)} %bitcast.4.refs_0_, bf16[128,1024]{1,0:T(8,128)(2,1)S(1)} %get-tuple-element.561.refs_1_, ...), custom_call_target="tpu_custom_call" | custom-call | flops 12884901888 | bytes 10883072 | tf_op jit(solution)/shard_map/attend_backward/pallas_call | solution.py:86
  344.8 10.8 %collective-permute-done.80.refs_4_ = bf16[512,768]{1,0:T(8,128)(2,1)S(1)} collective-permute-done((bf16[512,768]{1,0:T(8,128)(2,1)S(1)}, bf16[512,768]{1,0:T(8,128)(2,1)S(1)}, u32[]{:S(2)}, u32[]{:S(2)}) %collective-permute-start.80) | collective-permute-done | bytes 786464 | tf_op jit(solution)/shard_map/ppermute | solution.py:119
  358.3 2.0 collective-permute-start.87
  367.6 10.4 %collective-permute-done.86.refs_1_ = bf16[64,1024]{1,0:T(8,128)(2,1)S(1)} collective-permute-done((bf16[64,1024]{1,0:T(8,128)(2,1)S(1)}, bf16[64,1024]{1,0:T(8,128)(2,1)S(1)}, u32[]{:S(2)}, u32[]{:S(2)}) %collective-permute-start.86) | collective-permute-done | bytes 131104 | tf_op jit(solution)/shard_map/ppermute | solution.py:119
  384.8 12.0 %collective-permute-done.91.refs_2_ = bf16[128,768]{1,0:T(8,128)(2,1)S(1)} collective-permute-done((bf16[128,768]{1,0:T(8,128)(2,1)S(1)}, bf16[128,768]{1,0:T(8,128)(2,1)S(1)}, u32[]{:S(2)}, u32[]{:S(2)}) %collective-permute-start.91) | collective-permute-done | bytes 196640 | tf_op jit(solution)/shard_map/ppermute | solution.py:119
  397.6 2.0 feed_out_grads.3
  399.9 2.5 collective-permute-done.93.refs_1_
  403.8 2.8 collective-permute-start.94
  407.7 5.2 %feed_backward.3 = (bf16[512,1024]{1,0:T(8,128)(2,1)}, bf16[512,1024]{1,0:T(8,128)(2,1)S(1)}, f32[1,1024]{1,0:T(1,128)S(1)}, f32[128,1024]{1,0:T(8,128)S(1)}, bf...) custom-call(s32[4]{0:T(128)S(1)} %pad_add_fusion.spot.spot_ref, ...), custom_call_target="tpu_custom_call" | custom-call | flops 2147483648 | bytes 10752000 | tf_op jit(solution)/shard_map/feed_backward/pallas_call | solution.py:86
  413.3 3.4 collective-permute-done.95
  418.0 2.0 feed_in_grads.3
  420.1 2.3 collective-permute-start.100
  426.4 3.1 collective-permute-done.100.refs_1_
  433.8 3.3 collective-permute-done.98.refs_2_
  439.0 3.7 collective-permute-done.102.refs_1_
  443.6 4.0 collective-permute-done.103.refs_1_
  448.8 5.5 %collective-permute-done.107.refs_2_ = bf16[128,768]{1,0:T(8,128)(2,1)S(1)} collective-permute-done((bf16[128,768]{1,0:T(8,128)(2,1)S(1)}, bf16[128,768]{1,0:T(8,128)(2,1)S(1)}, u32[]{:S(2)}, u32[]{:S(2)}) %collective-permute-start.107) | collective-permute-done | bytes 196640 | tf_op jit(solution)/shard_map/ppermute | solution.py:119
  457.4 2.9 all-to-all-start.1
  460.4 2.7 collective-permute-start.108
  467.1 17.1 %collective-permute-done.112.theirs_ref = bf16[128,768]{1,0:T(8,128)(2,1)S(1)} collective-permute-done((bf16[128,768]{1,0:T(8,128)(2,1)S(1)}, bf16[128,768]{1,0:T(8,128)(2,1)S(1)}, u32[]{:S(2)}, u32[]{:S(2)}) %collective-permute-start.112) | collective-permute-done | bytes 196640 | tf_op jit(solution)/shard_map/ppermute | solution.py:119
  485.7 2.2 attend_final.1
  499.2 3.8 collective-permute-done.115.refs_3_
  503.0 2.8 feed_final.1
  (481 shorter events, 164.8 us)
Async XLA Ops:
  10.5 25.5 %collective-permute-start.1 = (bf16[256,1024]{1,0:T(8,128)(2,1)S(1)}, bf16[256,1024]{1,0:T(8,128)(2,1)}, u32[]{:S(2)}, u32[]{:S(2)}) collective-permute-start(bf16[256,1024]{1,0:T(8,128)(2,1)S(1)} %pack_rows.3.refs_4_), channel_id=1, source_target_pairs={{0,8},{1,9},{2,10},{3,11},{4,12},{5,13},{6,14},{7,15},{8,0},{9,1},... | collective-permute-start | bytes 1572872 | tf_op jit(solution)/shard_map/ppermute | solution.py:119
  13.4 22.8 %collective-permute-start.2 = (bf16[256,1024]{1,0:T(8,128)(2,1)S(1)}, bf16[256,1024]{1,0:T(8,128)(2,1)}, u32[]{:S(2)}, u32[]{:S(2)}) collective-permute-start(bf16[256,1024]{1,0:T(8,128)(2,1)S(1)} %pack_rows.3.refs_4_), channel_id=1, source_target_pairs={{0,4},{1,5},{2,6},{3,7},{4,0},{5,1},{6,2},{7,3},{8,12},{9,13},{10,... | collective-permute-start | bytes 1572872 | tf_op jit(solution)/shard_map/ppermute | solution.py:119
  36.2 18.4 %collective-permute-start.8 = (bf16[256,1024]{1,0:T(8,128)(2,1)}, bf16[256,1024]{1,0:T(8,128)(2,1)}, u32[]{:S(2)}, u32[]{:S(2)}) collective-permute-start(bf16[256,1024]{1,0:T(8,128)(2,1)} %collective-permute-done.1.refs_6_), channel_id=1, source_target_pairs={{0,4},{1,5},{2,6},{3,7},{4,0},{5,1},{6,2},{7,3},{8,12},{9,13},{10,... | collective-permute-start | bytes 1572872 | tf_op jit(solution)/shard_map/ppermute | solution.py:119
  38.4 16.0 %all-to-all-start = ((bf16[16,2,1792]{2,1,0:T(2,128)(2,1)}), bf16[16,2,1792]{2,1,0:T(2,128)(2,1)S(1)}, u32[]{:S(2)}, u32[]{:S(2)}) async-start(bf16[16,2,1792]{2,1,0:T(2,128)(2,1)} %reshape.68), calls=%async_computation | async-start | bytes 229376 | tf_op jit(solution)/shard_map/all_to_all | solution.py:1529
  43.8 14.0 %collective-permute-start.9 = (bf16[256,1024]{1,0:T(8,128)(2,1)S(1)}, bf16[256,1024]{1,0:T(8,128)(2,1)}, u32[]{:S(2)}, u32[]{:S(2)}) collective-permute-start(bf16[256,1024]{1,0:T(8,128)(2,1)S(1)} %pack_rows.3.refs_4_), channel_id=1, source_target_pairs={{0,1},{1,0},{2,3},{3,2},{4,5},{5,4},{6,7},{7,6},{8,9},{9,8},{10,11... | collective-permute-start | bytes 1572872 | tf_op jit(solution)/shard_map/ppermute | solution.py:119
  44.3 15.8 %collective-permute-start.11 = (bf16[256,1024]{1,0:T(8,128)(2,1)}, bf16[256,1024]{1,0:T(8,128)(2,1)}, u32[]{:S(2)}, u32[]{:S(2)}) collective-permute-start(bf16[256,1024]{1,0:T(8,128)(2,1)} %collective-permute-done.1.refs_6_), channel_id=1, source_target_pairs={{0,1},{1,0},{2,3},{3,2},{4,5},{5,4},{6,7},{7,6},{8,9},{9,8},{10,11... | collective-permute-start | bytes 1572872 | tf_op jit(solution)/shard_map/ppermute | solution.py:119
  44.4 15.6 %collective-permute-start.10 = (bf16[256,1024]{1,0:T(8,128)(2,1)}, bf16[256,1024]{1,0:T(8,128)(2,1)}, u32[]{:S(2)}, u32[]{:S(2)}) collective-permute-start(bf16[256,1024]{1,0:T(8,128)(2,1)} %collective-permute-done.2.refs_5_), channel_id=1, source_target_pairs={{0,1},{1,0},{2,3},{3,2},{4,5},{5,4},{6,7},{7,6},{8,9},{9,8},{10,11... | collective-permute-start | bytes 1572872 | tf_op jit(solution)/shard_map/ppermute | solution.py:119
  57.5 28.4 %collective-permute-start.17 = (bf16[768,384]{1,0:T(8,128)(2,1)S(1)}, bf16[768,384]{1,0:T(8,128)(2,1)S(1)}, u32[]{:S(2)}, u32[]{:S(2)}) collective-permute-start(bf16[768,384]{1,0:T(8,128)(2,1)S(1)} %get-tuple-element.411), channel_id=1, source_target_pairs={{0,8},{1,9},{2,10},{3,11},{4,12},{5,13},{6,14},{7,15},{8,0},{9,1},... | collective-permute-start | bytes 1769480 | tf_op jit(solution)/shard_map/ppermute | solution.py:119
  57.8 21.9 %collective-permute-start.16 = (bf16[512,384]{1,0:T(8,128)(2,1)}, bf16[512,384]{1,0:T(8,128)(2,1)S(1)}, u32[]{:S(2)}, u32[]{:S(2)}) collective-permute-start(bf16[512,384]{1,0:T(8,128)(2,1)} %copy-done.66), channel_id=1, source_target_pairs={{0,4},{1,5},{2,6},{3,7},{4,0},{5,1},{6,2},{7,3},{8,12},{9,13},{10,... | collective-permute-start | bytes 1179656 | tf_op jit(solution)/shard_map/ppermute | solution.py:119
  70.5 15.5 %collective-permute-start.13 = (bf16[128,1024]{1,0:T(8,128)(2,1)S(1)}, bf16[128,1024]{1,0:T(8,128)(2,1)S(1)}, u32[]{:S(2)}, u32[]{:S(2)}) collective-permute-start(bf16[128,1024]{1,0:T(8,128)(2,1)S(1)} %get-tuple-element.407), channel_id=1, source_target_pairs={{0,18},{1,19},{2,16},{3,17},{4,22},{5,23},{6,20},{7,21},{8,26},{9,... | collective-permute-start | bytes 786440 | tf_op jit(solution)/shard_map/ppermute | solution.py:119
  71.9 14.1 %collective-permute-start.14 = (bf16[128,1024]{1,0:T(8,128)(2,1)S(1)}, bf16[128,1024]{1,0:T(8,128)(2,1)S(1)}, u32[]{:S(2)}, u32[]{:S(2)}) collective-permute-start(bf16[128,1024]{1,0:T(8,128)(2,1)S(1)} %get-tuple-element.408), channel_id=1, source_target_pairs={{0,16},{1,17},{2,18},{3,19},{4,20},{5,21},{6,22},{7,23},{8,24},{9,... | collective-permute-start | bytes 786440 | tf_op jit(solution)/shard_map/ppermute | solution.py:119
  72.4 13.6 %collective-permute-start.15 = (bf16[128,1024]{1,0:T(8,128)(2,1)S(1)}, bf16[128,1024]{1,0:T(8,128)(2,1)S(1)}, u32[]{:S(2)}, u32[]{:S(2)}) collective-permute-start(bf16[128,1024]{1,0:T(8,128)(2,1)S(1)} %get-tuple-element.409), channel_id=1, source_target_pairs={{0,2},{1,3},{2,0},{3,1},{4,6},{5,7},{6,4},{7,5},{8,10},{9,11},{10,... | collective-permute-start | bytes 786440 | tf_op jit(solution)/shard_map/ppermute | solution.py:119
  87.2 15.1 %collective-permute-start.18 = (bf16[128,1024]{1,0:T(8,128)(2,1)S(1)}, bf16[128,1024]{1,0:T(8,128)(2,1)S(1)}, u32[]{:S(2)}, u32[]{:S(2)}) collective-permute-start(bf16[128,1024]{1,0:T(8,128)(2,1)S(1)} %get-tuple-element.420.refs_1_), channel_id=1, source_target_pairs={{0,4},{1,5},{2,6},{3,7},{4,0},{5,1},{6,2},{7,3},{8,12},{9,13},{10,... | collective-permute-start | bytes 786440 | tf_op jit(solution)/shard_map/ppermute | solution.py:119
  87.2 15.6 %collective-permute-start.19 = (bf16[128,1024]{1,0:T(8,128)(2,1)S(1)}, bf16[128,1024]{1,0:T(8,128)(2,1)S(1)}, u32[]{:S(2)}, u32[]{:S(2)}) collective-permute-start(bf16[128,1024]{1,0:T(8,128)(2,1)S(1)} %get-tuple-element.420.refs_1_), channel_id=1, source_target_pairs={{0,2},{1,3},{2,0},{3,1},{4,6},{5,7},{6,4},{7,5},{8,10},{9,11},{10,... | collective-permute-start | bytes 786440 | tf_op jit(solution)/shard_map/ppermute | solution.py:119
  87.6 17.1 %collective-permute-start.20 = (bf16[128,1024]{1,0:T(8,128)(2,1)S(1)}, bf16[128,1024]{1,0:T(8,128)(2,1)S(1)}, u32[]{:S(2)}, u32[]{:S(2)}) collective-permute-start(bf16[128,1024]{1,0:T(8,128)(2,1)S(1)} %get-tuple-element.420.refs_1_), channel_id=1, source_target_pairs={{0,6},{1,7},{2,4},{3,5},{4,2},{5,3},{6,0},{7,1},{8,14},{9,15},{10,... | collective-permute-start | bytes 786440 | tf_op jit(solution)/shard_map/ppermute | solution.py:119
  91.3 21.0 %collective-permute-start.25 = (bf16[512,384]{1,0:T(8,128)(2,1)S(1)}, bf16[512,384]{1,0:T(8,128)(2,1)S(1)}, u32[]{:S(2)}, u32[]{:S(2)}) collective-permute-start(bf16[512,384]{1,0:T(8,128)(2,1)S(1)} %slice.73), channel_id=1, source_target_pairs={{0,4},{1,5},{2,6},{3,7},{4,0},{5,1},{6,2},{7,3},{8,12},{9,13},{10,... | collective-permute-start | bytes 1179656 | tf_op jit(solution)/shard_map/ppermute | solution.py:119
  114.1 37.8 %collective-permute-start.29 = (bf16[1024,384]{1,0:T(8,128)(2,1)S(1)}, bf16[1024,384]{1,0:T(8,128)(2,1)S(1)}, u32[]{:S(2)}, u32[]{:S(2)}) collective-permute-start(bf16[1024,384]{1,0:T(8,128)(2,1)S(1)} %get-tuple-element.440.refs_0_), channel_id=1, source_target_pairs={{0,16},{1,17},{2,18},{3,19},{4,20},{5,21},{6,22},{7,23},{8,24},{9,... | collective-permute-start | bytes 2359304 | tf_op jit(solution)/shard_map/ppermute | solution.py:119
  115.6 36.2 %collective-permute-start.30 = (bf16[1024,384]{1,0:T(8,128)(2,1)S(1)}, bf16[1024,384]{1,0:T(8,128)(2,1)S(1)}, u32[]{:S(2)}, u32[]{:S(2)}) collective-permute-start(bf16[1024,384]{1,0:T(8,128)(2,1)S(1)} %get-tuple-element.440.refs_0_), channel_id=1, source_target_pairs={{0,2},{1,3},{2,0},{3,1},{4,6},{5,7},{6,4},{7,5},{8,10},{9,11},{10,... | collective-permute-start | bytes 2359304 | tf_op jit(solution)/shard_map/ppermute | solution.py:119
  115.8 36.1 %collective-permute-start.33 = (bf16[256,1024]{1,0:T(8,128)(2,1)S(1)}, bf16[256,1024]{1,0:T(8,128)(2,1)}, u32[]{:S(2)}, u32[]{:S(2)}) collective-permute-start(bf16[256,1024]{1,0:T(8,128)(2,1)S(1)} %pack_rows.4.refs_4_), channel_id=1, source_target_pairs={{0,8},{1,9},{2,10},{3,11},{4,12},{5,13},{6,14},{7,15},{8,0},{9,1},... | collective-permute-start | bytes 1572872 | tf_op jit(solution)/shard_map/ppermute | solution.py:119
  116.9 35.0 %collective-permute-start.34 = (bf16[256,1024]{1,0:T(8,128)(2,1)S(1)}, bf16[256,1024]{1,0:T(8,128)(2,1)S(1)}, u32[]{:S(2)}, u32[]{:S(2)}) collective-permute-start(bf16[256,1024]{1,0:T(8,128)(2,1)S(1)} %pack_rows.4.refs_4_), channel_id=1, source_target_pairs={{0,4},{1,5},{2,6},{3,7},{4,0},{5,1},{6,2},{7,3},{8,12},{9,13},{10,... | collective-permute-start | bytes 1572872 | tf_op jit(solution)/shard_map/ppermute | solution.py:119
  153.1 17.4 %collective-permute-start.39 = (bf16[512,384]{1,0:T(8,128)(2,1)S(1)}, bf16[512,384]{1,0:T(8,128)(2,1)S(1)}, u32[]{:S(2)}, u32[]{:S(2)}) collective-permute-start(bf16[512,384]{1,0:T(8,128)(2,1)S(1)} %get-tuple-element.452), channel_id=1, source_target_pairs={{0,2},{1,3},{2,0},{3,1},{4,6},{5,7},{6,4},{7,5},{8,10},{9,11},{10,... | collective-permute-start | bytes 1179656 | tf_op jit(solution)/shard_map/ppermute | solution.py:119
  155.8 14.7 %collective-permute-start.40 = (bf16[512,384]{1,0:T(8,128)(2,1)S(1)}, bf16[512,384]{1,0:T(8,128)(2,1)S(1)}, u32[]{:S(2)}, u32[]{:S(2)}) collective-permute-start(bf16[512,384]{1,0:T(8,128)(2,1)S(1)} %get-tuple-element.453), channel_id=1, source_target_pairs={{0,16},{1,17},{2,18},{3,19},{4,20},{5,21},{6,22},{7,23},{8,24},{9,... | collective-permute-start | bytes 1179656 | tf_op jit(solution)/shard_map/ppermute | solution.py:119
  161.3 13.7 %collective-permute-start.37 = (bf16[128,1024]{1,0:T(8,128)(2,1)S(1)}, bf16[128,1024]{1,0:T(8,128)(2,1)S(1)}, u32[]{:S(2)}, u32[]{:S(2)}) collective-permute-start(bf16[128,1024]{1,0:T(8,128)(2,1)S(1)} %get-tuple-element.450), channel_id=1, source_target_pairs={{0,4},{1,5},{2,6},{3,7},{4,0},{5,1},{6,2},{7,3},{8,12},{9,13},{10,... | collective-permute-start | bytes 786440 | tf_op jit(solution)/shard_map/ppermute | solution.py:119
  163.0 12.4 %collective-permute-start.38 = (bf16[128,1024]{1,0:T(8,128)(2,1)S(1)}, bf16[128,1024]{1,0:T(8,128)(2,1)S(1)}, u32[]{:S(2)}, u32[]{:S(2)}) collective-permute-start(bf16[128,1024]{1,0:T(8,128)(2,1)S(1)} %get-tuple-element.451), channel_id=1, source_target_pairs={{0,2},{1,3},{2,0},{3,1},{4,6},{5,7},{6,4},{7,5},{8,10},{9,11},{10,... | collective-permute-start | bytes 786440 | tf_op jit(solution)/shard_map/ppermute | solution.py:119
  176.0 14.1 %collective-permute-start.44 = (bf16[256,1024]{1,0:T(8,128)(2,1)}, bf16[256,1024]{1,0:T(8,128)(2,1)}, u32[]{:S(2)}, u32[]{:S(2)}) collective-permute-start(bf16[256,1024]{1,0:T(8,128)(2,1)} %collective-permute-done.33.refs_6_), channel_id=1, source_target_pairs={{0,4},{1,5},{2,6},{3,7},{4,0},{5,1},{6,2},{7,3},{8,12},{9,13},{10,... | collective-permute-start | bytes 1572872 | tf_op jit(solution)/shard_map/ppermute | solution.py:119
  196.7 12.8 %collective-permute-start.50 = (bf16[128,1024]{1,0:T(8,128)(2,1)S(1)}, bf16[128,1024]{1,0:T(8,128)(2,1)S(1)}, u32[]{:S(2)}, u32[]{:S(2)}) collective-permute-start(bf16[128,1024]{1,0:T(8,128)(2,1)S(1)} %get-tuple-element.479.refs_0_), channel_id=1, source_target_pairs={{0,2},{1,3},{2,0},{3,1},{4,6},{5,7},{6,4},{7,5},{8,10},{9,11},{10,... | collective-permute-start | bytes 786440 | tf_op jit(solution)/shard_map/ppermute | solution.py:119
  198.4 12.7 %collective-permute-start.51 = (bf16[128,1024]{1,0:T(8,128)(2,1)S(1)}, bf16[128,1024]{1,0:T(8,128)(2,1)S(1)}, u32[]{:S(2)}, u32[]{:S(2)}) collective-permute-start(bf16[128,1024]{1,0:T(8,128)(2,1)S(1)} %get-tuple-element.479.refs_0_), channel_id=1, source_target_pairs={{0,18},{1,19},{2,16},{3,17},{4,22},{5,23},{6,20},{7,21},{8,26},{9,... | collective-permute-start | bytes 786440 | tf_op jit(solution)/shard_map/ppermute | solution.py:119
  232.3 13.3 %collective-permute-start.56 = (bf16[128,1024]{1,0:T(8,128)(2,1)S(1)}, bf16[128,1024]{1,0:T(8,128)(2,1)S(1)}, u32[]{:S(2)}, u32[]{:S(2)}) collective-permute-start(bf16[128,1024]{1,0:T(8,128)(2,1)S(1)} %get-tuple-element.495.refs_0_), channel_id=1, source_target_pairs={{0,2},{1,3},{2,0},{3,1},{4,6},{5,7},{6,4},{7,5},{8,10},{9,11},{10,... | collective-permute-start | bytes 786440 | tf_op jit(solution)/shard_map/ppermute | solution.py:119
  256.3 13.7 %collective-permute-start.59 = (bf16[128,1024]{1,0:T(8,128)(2,1)S(1)}, bf16[128,1024]{1,0:T(8,128)(2,1)S(1)}, u32[]{:S(2)}, u32[]{:S(2)}) collective-permute-start(bf16[128,1024]{1,0:T(8,128)(2,1)S(1)} %get-tuple-element.508), channel_id=1, source_target_pairs={{0,16},{1,17},{2,18},{3,19},{4,20},{5,21},{6,22},{7,23},{8,24},{9,... | collective-permute-start | bytes 786440 | tf_op jit(solution)/shard_map/ppermute | solution.py:119
  258.0 11.9 %collective-permute-start.60 = (bf16[128,1024]{1,0:T(8,128)(2,1)S(1)}, bf16[128,1024]{1,0:T(8,128)(2,1)S(1)}, u32[]{:S(2)}, u32[]{:S(2)}) collective-permute-start(bf16[128,1024]{1,0:T(8,128)(2,1)S(1)} %get-tuple-element.509), channel_id=1, source_target_pairs={{0,2},{1,3},{2,0},{3,1},{4,6},{5,7},{6,4},{7,5},{8,10},{9,11},{10,... | collective-permute-start | bytes 786440 | tf_op jit(solution)/shard_map/ppermute | solution.py:119
  269.9 16.0 %collective-permute-start.64 = (bf16[128,1024]{1,0:T(8,128)(2,1)}, bf16[128,1024]{1,0:T(8,128)(2,1)S(1)}, u32[]{:S(2)}, u32[]{:S(2)}) collective-permute-start(bf16[128,1024]{1,0:T(8,128)(2,1)} %get-tuple-element.531), channel_id=1, source_target_pairs={{0,4},{1,5},{2,6},{3,7},{4,0},{5,1},{6,2},{7,3},{8,12},{9,13},{10,... | collective-permute-start | bytes 786440 | tf_op jit(solution)/shard_map/ppermute | solution.py:119
  271.4 14.5 %collective-permute-start.65 = (bf16[128,1024]{1,0:T(8,128)(2,1)}, bf16[128,1024]{1,0:T(8,128)(2,1)S(1)}, u32[]{:S(2)}, u32[]{:S(2)}) collective-permute-start(bf16[128,1024]{1,0:T(8,128)(2,1)} %get-tuple-element.533), channel_id=1, source_target_pairs={{0,4},{1,5},{2,6},{3,7},{4,0},{5,1},{6,2},{7,3},{8,12},{9,13},{10,... | collective-permute-start | bytes 786440 | tf_op jit(solution)/shard_map/ppermute | solution.py:119
  285.9 13.2 %collective-permute-start.67 = (bf16[128,1024]{1,0:T(8,128)(2,1)}, bf16[128,1024]{1,0:T(8,128)(2,1)S(1)}, u32[]{:S(2)}, u32[]{:S(2)}) collective-permute-start(bf16[128,1024]{1,0:T(8,128)(2,1)} %copy-done.81), channel_id=1, source_target_pairs={{0,4},{1,5},{2,6},{3,7},{4,0},{5,1},{6,2},{7,3},{8,12},{9,13},{10,... | collective-permute-start | bytes 786440 | tf_op jit(solution)/shard_map/ppermute | solution.py:119
  299.1 15.6 %collective-permute-start.75 = (bf16[2048,768]{1,0:T(8,128)(2,1)S(1)}, bf16[2048,768]{1,0:T(8,128)(2,1)S(1)}, u32[]{:S(2)}, u32[]{:S(2)}) collective-permute-start(bf16[2048,768]{1,0:T(8,128)(2,1)S(1)} %get-tuple-element.554), channel_id=1, source_target_pairs={{0,1},{1,0},{2,3},{3,2},{4,5},{5,4},{6,7},{7,6},{8,9},{9,8},{10,11... | collective-permute-start | bytes 9437192 | tf_op jit(solution)/shard_map/ppermute | solution.py:119
  300.2 14.0 %collective-permute-start.69 = (bf16[128,1024]{1,0:T(8,128)(2,1)S(1)}, bf16[128,1024]{1,0:T(8,128)(2,1)S(1)}, u32[]{:S(2)}, u32[]{:S(2)}) collective-permute-start(bf16[128,1024]{1,0:T(8,128)(2,1)S(1)} %get-tuple-element.561.refs_1_), channel_id=1, source_target_pairs={{0,2},{1,3},{2,0},{3,1},{4,6},{5,7},{6,4},{7,5},{8,10},{9,11},{10,... | collective-permute-start | bytes 786440 | tf_op jit(solution)/shard_map/ppermute | solution.py:119
  300.8 13.3 %collective-permute-start.70 = (bf16[128,1024]{1,0:T(8,128)(2,1)S(1)}, bf16[128,1024]{1,0:T(8,128)(2,1)S(1)}, u32[]{:S(2)}, u32[]{:S(2)}) collective-permute-start(bf16[128,1024]{1,0:T(8,128)(2,1)S(1)} %get-tuple-element.561.refs_1_), channel_id=1, source_target_pairs={{0,6},{1,7},{2,4},{3,5},{4,2},{5,3},{6,0},{7,1},{8,14},{9,15},{10,... | collective-permute-start | bytes 786440 | tf_op jit(solution)/shard_map/ppermute | solution.py:119
  302.7 12.7 %collective-permute-start.71 = (bf16[128,1024]{1,0:T(8,128)(2,1)S(1)}, bf16[128,1024]{1,0:T(8,128)(2,1)S(1)}, u32[]{:S(2)}, u32[]{:S(2)}) collective-permute-start(bf16[128,1024]{1,0:T(8,128)(2,1)S(1)} %get-tuple-element.561.refs_1_), channel_id=1, source_target_pairs={{0,1},{1,0},{2,3},{3,2},{4,5},{5,4},{6,7},{7,6},{8,9},{9,8},{10,11... | collective-permute-start | bytes 786440 | tf_op jit(solution)/shard_map/ppermute | solution.py:119
  316.1 28.7 %collective-permute-start.77 = (bf16[128,1024]{1,0:T(8,128)(2,1)S(1)}, bf16[128,1024]{1,0:T(8,128)(2,1)S(1)}, u32[]{:S(2)}, u32[]{:S(2)}) collective-permute-start(bf16[128,1024]{1,0:T(8,128)(2,1)S(1)} %plane_add.8), channel_id=1, source_target_pairs={{0,8},{1,9},{2,10},{3,11},{4,12},{5,13},{6,14},{7,15},{8,0},{9,1},... | collective-permute-start | bytes 786440 | tf_op jit(solution)/shard_map/ppermute | solution.py:119
  318.0 26.7 %collective-permute-start.78 = (bf16[128,1024]{1,0:T(8,128)(2,1)S(1)}, bf16[128,1024]{1,0:T(8,128)(2,1)S(1)}, u32[]{:S(2)}, u32[]{:S(2)}) collective-permute-start(bf16[128,1024]{1,0:T(8,128)(2,1)S(1)} %plane_add.9), channel_id=1, source_target_pairs={{0,8},{1,9},{2,10},{3,11},{4,12},{5,13},{6,14},{7,15},{8,0},{9,1},... | collective-permute-start | bytes 786440 | tf_op jit(solution)/shard_map/ppermute | solution.py:119
  319.0 25.8 %collective-permute-start.79 = (bf16[512,768]{1,0:T(8,128)(2,1)S(1)}, bf16[512,768]{1,0:T(8,128)(2,1)S(1)}, u32[]{:S(2)}, u32[]{:S(2)}) collective-permute-start(bf16[512,768]{1,0:T(8,128)(2,1)S(1)} %get-tuple-element.586), channel_id=1, source_target_pairs={{0,16},{1,17},{2,18},{3,19},{4,20},{5,21},{6,22},{7,23},{8,24},{9,... | collective-permute-start | bytes 2359304 | tf_op jit(solution)/shard_map/ppermute | solution.py:119
  319.9 35.6 %collective-permute-start.80 = (bf16[512,768]{1,0:T(8,128)(2,1)S(1)}, bf16[512,768]{1,0:T(8,128)(2,1)S(1)}, u32[]{:S(2)}, u32[]{:S(2)}) collective-permute-start(bf16[512,768]{1,0:T(8,128)(2,1)S(1)} %get-tuple-element.587), channel_id=1, source_target_pairs={{0,2},{1,3},{2,0},{3,1},{4,6},{5,7},{6,4},{7,5},{8,10},{9,11},{10,... | collective-permute-start | bytes 2359304 | tf_op jit(solution)/shard_map/ppermute | solution.py:119
  321.3 34.2 %collective-permute-start.81 = (bf16[512,768]{1,0:T(8,128)(2,1)S(1)}, bf16[512,768]{1,0:T(8,128)(2,1)S(1)}, u32[]{:S(2)}, u32[]{:S(2)}) collective-permute-start(bf16[512,768]{1,0:T(8,128)(2,1)S(1)} %get-tuple-element.588), channel_id=1, source_target_pairs={{0,18},{1,19},{2,16},{3,17},{4,22},{5,23},{6,20},{7,21},{8,26},{9,... | collective-permute-start | bytes 2359304 | tf_op jit(solution)/shard_map/ppermute | solution.py:119
  360.6 17.4 %collective-permute-start.83 = (bf16[128,1024]{1,0:T(8,128)(2,1)S(1)}, bf16[128,1024]{1,0:T(8,128)(2,1)S(1)}, u32[]{:S(2)}, u32[]{:S(2)}) collective-permute-start(bf16[128,1024]{1,0:T(8,128)(2,1)S(1)} %get-tuple-element.591), channel_id=1, source_target_pairs={{0,6},{1,7},{2,4},{3,5},{4,2},{5,3},{6,0},{7,1},{8,14},{9,15},{10,... | collective-permute-start | bytes 786440 | tf_op jit(solution)/shard_map/ppermute | solution.py:119
  361.6 16.4 %collective-permute-start.84 = (bf16[128,1024]{1,0:T(8,128)(2,1)S(1)}, bf16[128,1024]{1,0:T(8,128)(2,1)S(1)}, u32[]{:S(2)}, u32[]{:S(2)}) collective-permute-start(bf16[128,1024]{1,0:T(8,128)(2,1)S(1)} %get-tuple-element.592), channel_id=1, source_target_pairs={{0,4},{1,5},{2,6},{3,7},{4,0},{5,1},{6,2},{7,3},{8,12},{9,13},{10,... | collective-permute-start | bytes 786440 | tf_op jit(solution)/shard_map/ppermute | solution.py:119
  363.5 14.5 %collective-permute-start.85 = (bf16[128,1024]{1,0:T(8,128)(2,1)S(1)}, bf16[128,1024]{1,0:T(8,128)(2,1)S(1)}, u32[]{:S(2)}, u32[]{:S(2)}) collective-permute-start(bf16[128,1024]{1,0:T(8,128)(2,1)S(1)} %get-tuple-element.593), channel_id=1, source_target_pairs={{0,2},{1,3},{2,0},{3,1},{4,6},{5,7},{6,4},{7,5},{8,10},{9,11},{10,... | collective-permute-start | bytes 786440 | tf_op jit(solution)/shard_map/ppermute | solution.py:119
  364.2 13.8 %collective-permute-start.86 = (bf16[64,1024]{1,0:T(8,128)(2,1)S(1)}, bf16[64,1024]{1,0:T(8,128)(2,1)S(1)}, u32[]{:S(2)}, u32[]{:S(2)}) collective-permute-start(bf16[64,1024]{1,0:T(8,128)(2,1)S(1)} %get-tuple-element.764), channel_id=1, source_target_pairs={{0,2},{1,3},{2,0},{3,1},{4,6},{5,7},{6,4},{7,5},{8,10},{9,11},{10,... | collective-permute-start | bytes 393224 | tf_op jit(solution)/shard_map/ppermute | solution.py:119
  378.6 19.0 %collective-permute-start.92 = (bf16[384,768]{1,0:T(8,128)(2,1)S(1)}, bf16[384,768]{1,0:T(8,128)(2,1)S(1)}, u32[]{:S(2)}, u32[]{:S(2)}) collective-permute-start(bf16[384,768]{1,0:T(8,128)(2,1)S(1)} %get-tuple-element.625), channel_id=1, source_target_pairs={{0,4},{1,5},{2,6},{3,7},{4,0},{5,1},{6,2},{7,3},{8,12},{9,13},{10,... | collective-permute-start | bytes 1769480 | tf_op jit(solution)/shard_map/ppermute | solution.py:119
  380.5 16.3 %collective-permute-start.88 = (bf16[128,1024]{1,0:T(8,128)(2,1)S(1)}, bf16[128,1024]{1,0:T(8,128)(2,1)S(1)}, u32[]{:S(2)}, u32[]{:S(2)}) collective-permute-start(bf16[128,1024]{1,0:T(8,128)(2,1)S(1)} %get-tuple-element.641.refs_0_), channel_id=1, source_target_pairs={{0,16},{1,17},{2,18},{3,19},{4,20},{5,21},{6,22},{7,23},{8,24},{9,... | collective-permute-start | bytes 786440 | tf_op jit(solution)/shard_map/ppermute | solution.py:119
  381.3 15.6 %collective-permute-start.89 = (bf16[128,1024]{1,0:T(8,128)(2,1)S(1)}, bf16[128,1024]{1,0:T(8,128)(2,1)S(1)}, u32[]{:S(2)}, u32[]{:S(2)}) collective-permute-start(bf16[128,1024]{1,0:T(8,128)(2,1)S(1)} %get-tuple-element.641.refs_0_), channel_id=1, source_target_pairs={{0,2},{1,3},{2,0},{3,1},{4,6},{5,7},{6,4},{7,5},{8,10},{9,11},{10,... | collective-permute-start | bytes 786440 | tf_op jit(solution)/shard_map/ppermute | solution.py:119
  382.6 14.3 %collective-permute-start.90 = (bf16[128,1024]{1,0:T(8,128)(2,1)S(1)}, bf16[128,1024]{1,0:T(8,128)(2,1)S(1)}, u32[]{:S(2)}, u32[]{:S(2)}) collective-permute-start(bf16[128,1024]{1,0:T(8,128)(2,1)S(1)} %get-tuple-element.641.refs_0_), channel_id=1, source_target_pairs={{0,18},{1,19},{2,16},{3,17},{4,22},{5,23},{6,20},{7,21},{8,26},{9,... | collective-permute-start | bytes 786440 | tf_op jit(solution)/shard_map/ppermute | solution.py:119
  384.0 12.9 %collective-permute-start.91 = (bf16[128,768]{1,0:T(8,128)(2,1)S(1)}, bf16[128,768]{1,0:T(8,128)(2,1)S(1)}, u32[]{:S(2)}, u32[]{:S(2)}) collective-permute-start(bf16[128,768]{1,0:T(8,128)(2,1)S(1)} %get-tuple-element.623), channel_id=1, source_target_pairs={{0,8},{1,9},{2,10},{3,11},{4,12},{5,13},{6,14},{7,15},{8,0},{9,1},... | collective-permute-start | bytes 589832 | tf_op jit(solution)/shard_map/ppermute | solution.py:119
  402.7 14.0 %collective-permute-start.95 = (bf16[256,1024]{1,0:T(8,128)(2,1)S(1)}, bf16[256,1024]{1,0:T(8,128)(2,1)S(1)}, u32[]{:S(2)}, u32[]{:S(2)}) collective-permute-start(bf16[256,1024]{1,0:T(8,128)(2,1)S(1)} %pack_rows.5), channel_id=1, source_target_pairs={{0,16},{1,17},{2,18},{3,19},{4,20},{5,21},{6,22},{7,23},{8,24},{9,... | collective-permute-start | bytes 1572872 | tf_op jit(solution)/shard_map/ppermute | solution.py:119
  424.1 13.0 %collective-permute-start.98 = (bf16[128,1024]{1,0:T(8,128)(2,1)S(1)}, bf16[128,1024]{1,0:T(8,128)(2,1)S(1)}, u32[]{:S(2)}, u32[]{:S(2)}) collective-permute-start(bf16[128,1024]{1,0:T(8,128)(2,1)S(1)} %get-tuple-element.661), channel_id=1, source_target_pairs={{0,16},{1,17},{2,18},{3,19},{4,20},{5,21},{6,22},{7,23},{8,24},{9,... | collective-permute-start | bytes 786440 | tf_op jit(solution)/shard_map/ppermute | solution.py:119
  425.2 12.8 %collective-permute-start.99 = (bf16[128,1024]{1,0:T(8,128)(2,1)S(1)}, bf16[128,1024]{1,0:T(8,128)(2,1)S(1)}, u32[]{:S(2)}, u32[]{:S(2)}) collective-permute-start(bf16[128,1024]{1,0:T(8,128)(2,1)S(1)} %get-tuple-element.662), channel_id=1, source_target_pairs={{0,2},{1,3},{2,0},{3,1},{4,6},{5,7},{6,4},{7,5},{8,10},{9,11},{10,... | collective-permute-start | bytes 786440 | tf_op jit(solution)/shard_map/ppermute | solution.py:119
  426.3 16.4 %collective-permute-start.102 = (bf16[128,1024]{1,0:T(8,128)(2,1)S(1)}, bf16[128,1024]{1,0:T(8,128)(2,1)S(1)}, u32[]{:S(2)}, u32[]{:S(2)}) collective-permute-start(bf16[128,1024]{1,0:T(8,128)(2,1)S(1)} %get-tuple-element.668), channel_id=1, source_target_pairs={{0,4},{1,5},{2,6},{3,7},{4,0},{5,1},{6,2},{7,3},{8,12},{9,13},{10,... | collective-permute-start | bytes 786440 | tf_op jit(solution)/shard_map/ppermute | solution.py:119
  429.5 18.1 %collective-permute-start.103 = (bf16[128,1024]{1,0:T(8,128)(2,1)S(1)}, bf16[128,1024]{1,0:T(8,128)(2,1)S(1)}, u32[]{:S(2)}, u32[]{:S(2)}) collective-permute-start(bf16[128,1024]{1,0:T(8,128)(2,1)S(1)} %get-tuple-element.670), channel_id=1, source_target_pairs={{0,4},{1,5},{2,6},{3,7},{4,0},{5,1},{6,2},{7,3},{8,12},{9,13},{10,... | collective-permute-start | bytes 786440 | tf_op jit(solution)/shard_map/ppermute | solution.py:119
  432.6 23.1 %collective-permute-start.109 = (bf16[128,1024]{1,0:T(8,128)(2,1)S(1)}, bf16[128,1024]{1,0:T(8,128)(2,1)S(1)}, u32[]{:S(2)}, u32[]{:S(2)}) collective-permute-start(bf16[128,1024]{1,0:T(8,128)(2,1)S(1)} %plane_add.13), channel_id=1, source_target_pairs={{0,8},{1,9},{2,10},{3,11},{4,12},{5,13},{6,14},{7,15},{8,0},{9,1},... | collective-permute-start | bytes 786440 | tf_op jit(solution)/shard_map/ppermute | solution.py:119
  437.1 17.2 %collective-permute-start.107 = (bf16[128,768]{1,0:T(8,128)(2,1)S(1)}, bf16[128,768]{1,0:T(8,128)(2,1)S(1)}, u32[]{:S(2)}, u32[]{:S(2)}) collective-permute-start(bf16[128,768]{1,0:T(8,128)(2,1)S(1)} %conv_grads_top.1), channel_id=1, source_target_pairs={{0,8},{1,9},{2,10},{3,11},{4,12},{5,13},{6,14},{7,15},{8,0},{9,1},... | collective-permute-start | bytes 589832 | tf_op jit(solution)/shard_map/ppermute | solution.py:119
  438.0 16.3 %collective-permute-start.104 = (bf16[64,1536]{1,0:T(8,128)(2,1)S(1)}, bf16[64,1536]{1,0:T(8,128)(2,1)}, u32[]{:S(2)}, u32[]{:S(2)}) collective-permute-start(bf16[64,1536]{1,0:T(8,128)(2,1)S(1)} %get-tuple-element.680), channel_id=1, source_target_pairs={{0,2},{1,3},{2,0},{3,1},{4,6},{5,7},{6,4},{7,5},{8,10},{9,11},{10,... | collective-permute-start | bytes 589832 | tf_op jit(solution)/shard_map/ppermute | solution.py:119
  457.4 30.5 %all-to-all-start.1 = ((bf16[32,80,128]{2,1,0:T(8,128)(2,1)}), bf16[32,80,128]{2,1,0:T(8,128)(2,1)S(1)}, u32[]{:S(2)}, u32[]{:S(2)}) async-start(bf16[32,80,128]{2,1,0:T(8,128)(2,1)} %small_pack.1), calls=%async_computation.1 | async-start | bytes 1310720 | tf_op jit(solution)/shard_map/all_to_all | solution.py:1641
  460.4 29.1 %collective-permute-start.108 = (bf16[128,1024]{1,0:T(8,128)(2,1)S(1)}, bf16[128,1024]{1,0:T(8,128)(2,1)}, u32[]{:S(2)}, u32[]{:S(2)}) collective-permute-start(bf16[128,1024]{1,0:T(8,128)(2,1)S(1)} %plane_add.12), channel_id=1, source_target_pairs={{0,8},{1,9},{2,10},{3,11},{4,12},{5,13},{6,14},{7,15},{8,0},{9,1},... | collective-permute-start | bytes 786440 | tf_op jit(solution)/shard_map/ppermute | solution.py:119
  463.2 26.2 %collective-permute-start.110 = (bf16[128,1024]{1,0:T(8,128)(2,1)S(1)}, bf16[128,1024]{1,0:T(8,128)(2,1)S(1)}, u32[]{:S(2)}, u32[]{:S(2)}) collective-permute-start(bf16[128,1024]{1,0:T(8,128)(2,1)S(1)} %plane_add.14.refs_4_), channel_id=1, source_target_pairs={{0,16},{1,17},{2,18},{3,19},{4,20},{5,21},{6,22},{7,23},{8,24},{9,... | collective-permute-start | bytes 786440 | tf_op jit(solution)/shard_map/ppermute | solution.py:119
  464.9 20.8 %collective-permute-start.111 = (bf16[64,1536]{1,0:T(8,128)(2,1)}, bf16[64,1536]{1,0:T(8,128)(2,1)S(1)}, u32[]{:S(2)}, u32[]{:S(2)}) collective-permute-start(bf16[64,1536]{1,0:T(8,128)(2,1)} %collective-permute-done.104.refs_1_), channel_id=1, source_target_pairs={{0,16},{1,17},{2,18},{3,19},{4,20},{5,21},{6,22},{7,23},{8,24},{9,... | collective-permute-start | bytes 589832 | tf_op jit(solution)/shard_map/ppermute | solution.py:119
  465.6 18.6 %collective-permute-start.112 = (bf16[128,768]{1,0:T(8,128)(2,1)S(1)}, bf16[128,768]{1,0:T(8,128)(2,1)S(1)}, u32[]{:S(2)}, u32[]{:S(2)}) collective-permute-start(bf16[128,768]{1,0:T(8,128)(2,1)S(1)} %conv_grads_sum.1.mine_ref), channel_id=1, source_target_pairs={{0,16},{1,17},{2,18},{3,19},{4,20},{5,21},{6,22},{7,23},{8,24},{9,... | collective-permute-start | bytes 589832 | tf_op jit(solution)/shard_map/ppermute | solution.py:119
  (163 other events, 1978.2 us)

commit v7 on v6

--- a/solution.py
+++ b/solution.py
@@ -1564,10 +1564,10 @@
         for bit in range((2 * shards).bit_length() - 1):
             distance = distance + flipped(distance, 1 << bit)
         return total[:rows], total[rows:].reshape(2, 2 * half), distance
-    extent = -(-(rows + 8) // 32) * 32
+    table_rows = distance.shape[0]
+    share = -(-table_rows // shards)
+    extent = -(-(rows + 8 + share) // 32) * 32
     size = extent // 2
-    table_rows = distance.shape[0]
-    fold = -(-table_rows // 32) * 16
 
     def pack(spot, in_ref, first, attend_ref, conv, last, mix, bias_one, bias_two, table, out, wide):
         plane, second, core, rep = spot[0], spot[1], spot[2], spot[3]
@@ -1612,11 +1612,14 @@
                         wide[line : line + 1, pl.ds(start, LANES)] = jnp.where(
                             rep == side, value, 0.0
                         )
-        rest = jnp.concatenate(
-            [table[fold:, :], jnp.zeros((2 * fold - table_rows, unit), F32)], axis=0
+        whole = jnp.concatenate(
+            [table[...], jnp.zeros((share * shards - table_rows, unit), F32)], axis=0
         )
-        folded = jnp.concatenate([table[:fold, :], rest], axis=1)
-        folded = folded.astype(BF)
+        for pair in range(shards // 2):
+            start = 2 * pair * share
+            wide[rows + 8 : rows + 8 + share, pair * LANES : (pair + 1) * LANES] = jnp.concatenate(
+                [whole[start : start + share], whole[start + share : start + 2 * share]], axis=1
+            )
         wide_lane = lax.broadcasted_iota(jnp.int32, (size, LANES), 1)
         for pair in range(shards // 2):
             block = wide[:, pair * LANES : (pair + 1) * LANES]
@@ -1627,13 +1630,12 @@
             )
             for side in range(2):
                 for target in (2 * pair + side, 2 * pair + side + shards):
-                    out[target, :size, :] = both[side].astype(BF)
-                    out[target, size:, :] = folded
+                    out[target] = both[side].astype(BF)
 
     packed = kernel_call(
         pack,
         "small_pack",
-        [jax.ShapeDtypeStruct((2 * shards, size + fold, LANES), BF)],
+        [jax.ShapeDtypeStruct((2 * shards, size, LANES), BF)],
         (place.spot, *sums, mix_sums, *biases, distance),
         scalars=1,
         scratch=[pltpu.VMEM((extent, model), F32)],
@@ -1645,10 +1647,9 @@
         for index in range(1, 2 * shards):
             total = total + ref[index].astype(F32)
         moved = pltpu.roll(total, unit, axis=1)
-        table[:fold, :] = total[size:, :unit]
-        table[fold:, :] = moved[size : size + table_rows - fold, :unit]
         both = jnp.concatenate([total[:size, :unit], moved[:size, :unit]], axis=0)
         wide[...] = both[:rows]
+        table[...] = both[rows + 8 : rows + 8 + share]
         for module in range(2):
             for side in range(2):
                 line = rows + (module * 2 + side) * 2
@@ -1656,13 +1657,16 @@
                     [both[line : line + 1], both[line + 1 : line + 2]], axis=1
                 )
 
-    return kernel_call(
+    wide, bias, table = kernel_call(
         unpack,
         "small_sum",
-        [shape_of(rows, unit, F32), shape_of(2, 2 * half, F32), shape_of(*distance.shape, F32)],
+        [shape_of(rows, unit, F32), shape_of(2, 2 * half, F32), shape_of(share, unit, F32)],
         (place.spot, packed),
         scalars=1,
     )
+    table = jnp.broadcast_to(table[None], (shards, share, unit))
+    table = lax.all_to_all(table, "shard", 0, 0, tiled=True)
+    return wide, bias, table.reshape(shards * share, unit)[:table_rows]
 
 
 class Place:
@@ -1925,23 +1929,30 @@
         (wide_rows, tap_count),
         place,
     )
+    waited = [*mix_theirs, conv_theirs] if place.aligned else []
+    (in_last, out_theirs), waited = tied_lists((in_last, out_theirs), waited)
+    in_sum = plane_add([*in_early, in_last])
+    in_own, in_other = in_sum[:unit], flipped(in_sum[unit:], 2)
+    in_theirs = flipped(in_own, place.shards)
+    first_mine = [(in_own, in_theirs), (in_other, flipped(in_other, place.shards))]
     if place.aligned:
-        mix_grads = attend_grads_final((mix_own, mix_arrived, mix_out_sum), mix_theirs, place)
-        conv_grads = conv_grads_final(conv_mine, conv_theirs, place)
+        mix_grads = attend_grads_final((mix_own, mix_arrived, mix_out_sum), waited[:3], place)
+        conv_grads = conv_grads_final(conv_mine, waited[3], place)
     else:
         conv_grads = (
             jnp.concatenate([conv_whole[0], conv_whole[1]], axis=1)[None],
             conv_whole[2][None],
         )
-
-    (in_last, small_grads, out_theirs), mix_grads, conv_grads = tied_lists(
-        (in_last, small_grads, out_theirs), mix_grads, conv_grads
-    )
-    in_sum = plane_add([*in_early, in_last])
-    in_own, in_other = in_sum[:unit], flipped(in_sum[unit:], 2)
-    in_theirs = flipped(in_own, place.shards)
-    first_mine = [(in_own, in_theirs), (in_other, flipped(in_other, place.shards))]
-    first_mine = [*first_mine, (out_sum, out_theirs)]
+    in_last_theirs = first_mine[1][1]
+    small_outs = [
+        bias_grads[None],
+        small_grads[count + 1 :][None],
+        grad_distance[None],
+        small_grads[:count][None],
+        small_grads[count : count + 1],
+    ]
+    in_last_theirs, *small_outs = tied(in_last_theirs, *small_outs)
+    first_mine = [first_mine[0], (in_other, in_last_theirs), (out_sum, out_theirs)]
     cuts = (0, unit, 2 * unit, 2 * unit + half)
     second_mine = [
         (second_pack[cuts[i] : cuts[i + 1]], second_theirs[cuts[i] : cuts[i + 1]])
@@ -1952,13 +1963,10 @@
         output,
         grad_input,
         *feed_grads,
-        bias_grads[None],
+        small_outs[0],
         *mix_grads,
         *conv_grads,
-        small_grads[count + 1 :][None],
-        grad_distance[None],
-        small_grads[:count][None],
-        small_grads[count : count + 1],
+        *small_outs[1:],
     )
 
 

time: 509 us -> 504 us (level)
  waiting for transfers between devices: 220 us -> 208 us
    ppermute x114, waiting for transfers between devices: 210 us -> 195 us  [flipped(): lax.ppermute(value, ('rep', 'shard'), [(i, i ^ mask) for i in range(total)])]
    all_to_all x0 -> x1, waiting for transfers between devices: none -> 5.45 us  [small_reduce(): table = lax.all_to_all(table, 'shard', 0, 0, tiled=True)]
    unnamed x222 -> x202, local copies, waits for them, and re-layouts: 30.3 us -> 31.1 us
  transfers between devices with their start and end apart: 118 -> 119, of which waited for: 55 -> 54; matrix products, arithmetic and copies ran while one was open for 1% -> 2% of each run, Pallas kernels for 19% -> 20%
where the time goes in v7:
time: 504 us; the launch traced here: 500 us
  waiting for transfers between devices  208 us (41%)
  starting transfers between devices  127 us (25%)
  Pallas kernels  124 us (25%)
  local copies, waits for them, and re-layouts  37.3 us (7%)
    ppermute x114, waiting for transfers between devices, flipped(): lax.ppermute(value, ('rep', 'shard'), [(i, i ^ mask) for i in range(total)])  195 us
    pallas_call x56, Pallas kernels, kernel_call(): pl.pallas_call(body, grid=(1,), in_specs=specs, out_specs=vmem(len(outs))...  122 us
    ppermute x114, starting transfers between devices, flipped(): lax.ppermute(value, ('rep', 'shard'), [(i, i ^ mask) for i in range(total)])  112 us
    unnamed x202, local copies, waits for them, and re-layouts  31.1 us
  transfers between devices with their start and end apart: 119, of which 54 were waited for; matrix products, arithmetic and copies ran while one was open for 2% of the time, Pallas kernels for 20%

profile of v7, /device:TPU:0, one launch (start us, length us, event | category | flops | bytes accessed | tf_op | source)
XLA Modules:
  0.0 500.3 jit_solution(12301275282252279471)
XLA Ops:
  3.9 3.0 collective-permute-start
  6.9 3.5 collective-permute-done.refs_1_
  10.5 2.9 collective-permute-start.1
  20.0 3.8 collective-permute-done.3.refs_1_
  26.9 8.3 %collective-permute-done.6.refs_2_ = bf16[128,1024]{1,0:T(8,128)(2,1)S(1)} collective-permute-done((bf16[128,1024]{1,0:T(8,128)(2,1)S(1)}, bf16[128,1024]{1,0:T(8,128)(2,1)S(1)}, u32[]{:S(2)}, u32[]{:S(2)}) %collective-permute-start.6) | collective-permute-done | bytes 262176 | tf_op jit(solution)/shard_map/ppermute | solution.py:119
  40.0 4.7 all-to-all-start
  47.8 6.6 %all-to-all-done = bf16[16,2,1792]{2,1,0:T(2,128)(2,1)S(1)} async-done(((bf16[16,2,1792]{2,1,0:T(2,128)(2,1)}), bf16[16,2,1792]{2,1,0:T(2,128)(2,1)S(1)}, u32[]{:S(2)}, u32[]{:S(2)}) %all-to-all-start) | async-done | bytes 114720 | tf_op jit(solution)/shard_map/all_to_all | solution.py:1529
  58.3 2.2 collective-permute-start.16
  62.4 5.2 %feed_forward.2 = (bf16[512,1024]{1,0:T(8,128)(2,1)S(1)}, f32[512,1024]{1,0:T(8,128)S(1)}, bf16[512,1024]{1,0:T(8,128)(2,1)S(1)}, f32[128,1024]{1,0:T(8,128)S(1)...) custom-call(s32[4]{0:T(128)S(1)} %pad_add_fusion.spot.spot_ref, ...), custom_call_target="tpu_custom_call" | custom-call | flops 2147483648 | bytes 10948608 | tf_op jit(solution)/shard_map/feed_forward/pallas_call | solution.py:86
  73.4 6.8 %collective-permute-done.16.refs_2_ = bf16[512,384]{1,0:T(8,128)(2,1)S(1)} collective-permute-done((bf16[512,384]{1,0:T(8,128)(2,1)}, bf16[512,384]{1,0:T(8,128)(2,1)S(1)}, u32[]{:S(2)}, u32[]{:S(2)}) %collective-permute-start.16) | collective-permute-done | bytes 393248 | tf_op jit(solution)/shard_map/ppermute | solution.py:119
  80.2 6.3 %collective-permute-done.17.refs_3_ = bf16[768,384]{1,0:T(8,128)(2,1)S(1)} collective-permute-done((bf16[768,384]{1,0:T(8,128)(2,1)S(1)}, bf16[768,384]{1,0:T(8,128)(2,1)S(1)}, u32[]{:S(2)}, u32[]{:S(2)}) %collective-permute-start.17) | collective-permute-done | bytes 589856 | tf_op jit(solution)/shard_map/ppermute | solution.py:119
  88.1 3.0 collective-permute-start.20
  91.8 2.1 collective-permute-start.25
  93.9 8.9 %collective-permute-done.26.refs_1_ = bf16[64,1024]{1,0:T(8,128)(2,1)S(1)} collective-permute-done((bf16[64,1024]{1,0:T(8,128)(2,1)S(1)}, bf16[64,1024]{1,0:T(8,128)(2,1)S(1)}, u32[]{:S(2)}, u32[]{:S(2)}) %collective-permute-start.26) | collective-permute-done | bytes 131104 | tf_op jit(solution)/shard_map/ppermute | solution.py:119
  105.2 7.6 %collective-permute-done.25.refs_4_ = bf16[512,384]{1,0:T(8,128)(2,1)S(1)} collective-permute-done((bf16[512,384]{1,0:T(8,128)(2,1)S(1)}, bf16[512,384]{1,0:T(8,128)(2,1)S(1)}, u32[]{:S(2)}, u32[]{:S(2)}) %collective-permute-start.25) | collective-permute-done | bytes 393248 | tf_op jit(solution)/shard_map/ppermute | solution.py:119
  124.3 28.6 %attend_forward.1 = (bf16[1024,1024]{1,0:T(8,128)(2,1)}, bf16[1024,384]{1,0:T(8,128)(2,1)}, bf16[1024,128]{1,0:T(8,128)(2,1)}, f32[1024,128]{1,0:T(8,128)}, f32[...) custom-call(s32[1]{0:T(128)} %bitcast.4.refs_0_, bf16[128,1024]{1,0:T(8,128)(2,1)} %copy-done.65, ...), custom_call_target="tpu_custom_call" | custom-call | flops 6442450944 | bytes 10094080 | tf_op jit(solution)/shard_map/attend_forward/pallas_call | solution.py:86
  164.4 7.1 %collective-permute-done.39.refs_3_ = bf16[512,384]{1,0:T(8,128)(2,1)S(1)} collective-permute-done((bf16[512,384]{1,0:T(8,128)(2,1)S(1)}, bf16[512,384]{1,0:T(8,128)(2,1)S(1)}, u32[]{:S(2)}, u32[]{:S(2)}) %collective-permute-start.39) | collective-permute-done | bytes 393248 | tf_op jit(solution)/shard_map/ppermute | solution.py:119
  171.5 4.6 collective-permute-done.37.refs_2_
  184.8 2.0 collective-permute-start.43
  187.8 3.4 collective-permute-done.44.refs_7_
  192.2 3.4 convolve_finish.1
  200.7 5.7 %collective-permute-done.49.refs_1_ = bf16[128,1024]{1,0:T(8,128)(2,1)S(1)} collective-permute-done((bf16[128,1024]{1,0:T(8,128)(2,1)S(1)}, bf16[128,1024]{1,0:T(8,128)(2,1)S(1)}, u32[]{:S(2)}, u32[]{:S(2)}) %collective-permute-start.49) | collective-permute-done | bytes 262176 | tf_op jit(solution)/shard_map/ppermute | solution.py:119
  206.3 4.2 collective-permute-done.50.refs_2_
  212.2 4.0 feed_forward.3
  219.8 6.7 %collective-permute-done.52.refs_1_ = bf16[128,1024]{1,0:T(8,128)(2,1)S(1)} collective-permute-done((bf16[128,1024]{1,0:T(8,128)(2,1)S(1)}, bf16[128,1024]{1,0:T(8,128)(2,1)S(1)}, u32[]{:S(2)}, u32[]{:S(2)}) %collective-permute-start.52) | collective-permute-done | bytes 262176 | tf_op jit(solution)/shard_map/ppermute | solution.py:119
  226.5 2.6 collective-permute-done.53.refs_2_
  236.2 5.7 %collective-permute-done.55.refs_1_ = bf16[128,1024]{1,0:T(8,128)(2,1)S(1)} collective-permute-done((bf16[128,1024]{1,0:T(8,128)(2,1)S(1)}, bf16[128,1024]{1,0:T(8,128)(2,1)S(1)}, u32[]{:S(2)}, u32[]{:S(2)}) %collective-permute-start.55) | collective-permute-done | bytes 262176 | tf_op jit(solution)/shard_map/ppermute | solution.py:119
  241.9 4.8 collective-permute-done.56.refs_2_
  246.7 4.3 feed_backward.2
  251.0 2.0 feed_in_grads.2
  253.0 2.3 feed_out_grads.2
  261.9 4.1 collective-permute-done.58.part_one
  266.0 4.9 collective-permute-done.59.part_two
  273.0 9.5 %convolve_back_start.1 = (f32[128,1024]{1,0:T(8,128)}, bf16[128,1024]{1,0:T(8,128)(2,1)}, f32[128,1024]{1,0:T(8,128)}, bf16[32,1024]{1,0:T(8,128)(2,1)}, f32[35,1024]{1,0:T(8,128)}) custom-call(f32[128,1024]{1,0:T(8,128)} %copy-done.31, bf16[128,1024]{1,0:T(8,128)(2,1)} %copy-done.83, bf16[128,1024]{1,0:T(8,128)(2,1)} %copy-done.84, ...), custom_call_target="tpu_custom_call" | custom-call | flops 268435456 | bytes 7024640 | tf_op jit(solution)/shard_map/convolve_back_start/pallas_call | solution.py:86
  284.3 2.6 collective-permute-start.66
  287.2 2.2 copy-done.1
  293.2 3.0 conv_grads.1
  296.2 3.9 collective-permute-done.67.refs_1_
  303.7 5.6 %collective-permute-done.68.refs_5_ = bf16[128,1024]{1,0:T(8,128)(2,1)S(1)} collective-permute-done((bf16[128,1024]{1,0:T(8,128)(2,1)S(1)}, bf16[128,1024]{1,0:T(8,128)(2,1)S(1)}, u32[]{:S(2)}, u32[]{:S(2)}) %collective-permute-start.68) | collective-permute-done | bytes 262176 | tf_op jit(solution)/shard_map/ppermute | solution.py:119
  309.4 5.8 %collective-permute-done.69.refs_3_ = bf16[128,1024]{1,0:T(8,128)(2,1)S(1)} collective-permute-done((bf16[128,1024]{1,0:T(8,128)(2,1)S(1)}, bf16[128,1024]{1,0:T(8,128)(2,1)S(1)}, u32[]{:S(2)}, u32[]{:S(2)}) %collective-permute-start.69) | collective-permute-done | bytes 262176 | tf_op jit(solution)/shard_map/ppermute | solution.py:119
  317.1 2.0 collective-permute-start.77
  323.5 22.2 %attend_backward.1 = (bf16[1024,1024]{1,0:T(8,128)(2,1)S(1)}, bf16[1024,384]{1,0:T(8,128)(2,1)S(1)}, f32[512,128]{1,0:T(8,128)S(1)}, f32[8,128]{1,0:T(8,128)S(1)...) custom-call(s32[1]{0:T(128)} %bitcast.4.refs_0_, bf16[128,1024]{1,0:T(8,128)(2,1)S(1)} %get-tuple-element.566.refs_1_, ...), custom_call_target="tpu_custom_call" | custom-call | flops 12884901888 | bytes 10883072 | tf_op jit(solution)/shard_map/attend_backward/pallas_call | solution.py:86
  345.8 10.8 %collective-permute-done.80.refs_4_ = bf16[512,768]{1,0:T(8,128)(2,1)S(1)} collective-permute-done((bf16[512,768]{1,0:T(8,128)(2,1)S(1)}, bf16[512,768]{1,0:T(8,128)(2,1)S(1)}, u32[]{:S(2)}, u32[]{:S(2)}) %collective-permute-start.80) | collective-permute-done | bytes 786464 | tf_op jit(solution)/shard_map/ppermute | solution.py:119
  368.7 10.4 %collective-permute-done.86.refs_1_ = bf16[64,1024]{1,0:T(8,128)(2,1)S(1)} collective-permute-done((bf16[64,1024]{1,0:T(8,128)(2,1)S(1)}, bf16[64,1024]{1,0:T(8,128)(2,1)S(1)}, u32[]{:S(2)}, u32[]{:S(2)}) %collective-permute-start.86) | collective-permute-done | bytes 131104 | tf_op jit(solution)/shard_map/ppermute | solution.py:119
  385.9 12.0 %collective-permute-done.91.refs_2_ = bf16[128,768]{1,0:T(8,128)(2,1)S(1)} collective-permute-done((bf16[128,768]{1,0:T(8,128)(2,1)S(1)}, bf16[128,768]{1,0:T(8,128)(2,1)S(1)}, u32[]{:S(2)}, u32[]{:S(2)}) %collective-permute-start.91) | collective-permute-done | bytes 196640 | tf_op jit(solution)/shard_map/ppermute | solution.py:119
  398.6 2.0 feed_out_grads.3
  400.9 2.5 collective-permute-done.93.refs_1_
  404.8 2.8 collective-permute-start.94
  408.8 5.2 %feed_backward.3 = (bf16[512,1024]{1,0:T(8,128)(2,1)}, bf16[512,1024]{1,0:T(8,128)(2,1)S(1)}, f32[1,1024]{1,0:T(1,128)S(1)}, f32[128,1024]{1,0:T(8,128)S(1)}, bf...) custom-call(s32[4]{0:T(128)S(1)} %pad_add_fusion.spot.spot_ref, ...), custom_call_target="tpu_custom_call" | custom-call | flops 2147483648 | bytes 10752000 | tf_op jit(solution)/shard_map/feed_backward/pallas_call | solution.py:86
  414.3 3.4 collective-permute-done.95
  419.0 2.0 feed_in_grads.3
  421.1 2.3 collective-permute-start.100
  427.3 3.3 collective-permute-done.100.refs_1_
  434.5 3.6 collective-permute-done.98.refs_2_
  441.8 5.8 %collective-permute-done.103.refs_1_ = bf16[128,1024]{1,0:T(8,128)(2,1)S(1)} collective-permute-done((bf16[128,1024]{1,0:T(8,128)(2,1)S(1)}, bf16[128,1024]{1,0:T(8,128)(2,1)S(1)}, u32[]{:S(2)}, u32[]{:S(2)}) %collective-permute-start.103) | collective-permute-done | bytes 262176 | tf_op jit(solution)/shard_map/ppermute | solution.py:119
  448.7 3.9 collective-permute-done.106.refs_5_
  452.8 2.0 collective-permute-start.108
  456.2 7.0 %collective-permute-done.109.refs_2_ = bf16[128,1024]{1,0:T(8,128)(2,1)S(1)} collective-permute-done((bf16[128,1024]{1,0:T(8,128)(2,1)S(1)}, bf16[128,1024]{1,0:T(8,128)(2,1)S(1)}, u32[]{:S(2)}, u32[]{:S(2)}) %collective-permute-start.109) | collective-permute-done | bytes 262176 | tf_op jit(solution)/shard_map/ppermute | solution.py:119
  468.2 2.6 all-to-all-start.1
  472.0 2.4 collective-permute-done.112.theirs_ref
  478.9 2.3 attend_final.1
  484.0 3.9 all-to-all-start.2
  489.1 5.5 %all-to-all-done.2 = f32[16,1,320]{2,1,0:T(1,128)S(1)} async-done(((f32[16,1,320]{2,1,0:T(1,128)}), f32[16,1,320]{2,1,0:T(1,128)S(1)}, u32[]{:S(2)}, u32[]{:S(2)}) %all-to-all-start.2) | async-done | bytes 20512 | tf_op jit(solution)/shard_map/all_to_all | solution.py:1668
  497.2 2.9 feed_final.1
  (468 shorter events, 167.6 us)
Async XLA Ops:
  10.5 25.5 %collective-permute-start.1 = (bf16[256,1024]{1,0:T(8,128)(2,1)S(1)}, bf16[256,1024]{1,0:T(8,128)(2,1)}, u32[]{:S(2)}, u32[]{:S(2)}) collective-permute-start(bf16[256,1024]{1,0:T(8,128)(2,1)S(1)} %pack_rows.3.refs_4_), channel_id=1, source_target_pairs={{0,8},{1,9},{2,10},{3,11},{4,12},{5,13},{6,14},{7,15},{8,0},{9,1},... | collective-permute-start | bytes 1572872 | tf_op jit(solution)/shard_map/ppermute | solution.py:119
  13.4 22.8 %collective-permute-start.2 = (bf16[256,1024]{1,0:T(8,128)(2,1)S(1)}, bf16[256,1024]{1,0:T(8,128)(2,1)}, u32[]{:S(2)}, u32[]{:S(2)}) collective-permute-start(bf16[256,1024]{1,0:T(8,128)(2,1)S(1)} %pack_rows.3.refs_4_), channel_id=1, source_target_pairs={{0,4},{1,5},{2,6},{3,7},{4,0},{5,1},{6,2},{7,3},{8,12},{9,13},{10,... | collective-permute-start | bytes 1572872 | tf_op jit(solution)/shard_map/ppermute | solution.py:119
  36.2 18.4 %collective-permute-start.8 = (bf16[256,1024]{1,0:T(8,128)(2,1)}, bf16[256,1024]{1,0:T(8,128)(2,1)}, u32[]{:S(2)}, u32[]{:S(2)}) collective-permute-start(bf16[256,1024]{1,0:T(8,128)(2,1)} %collective-permute-done.1.refs_6_), channel_id=1, source_target_pairs={{0,4},{1,5},{2,6},{3,7},{4,0},{5,1},{6,2},{7,3},{8,12},{9,13},{10,... | collective-permute-start | bytes 1572872 | tf_op jit(solution)/shard_map/ppermute | solution.py:119
  40.0 14.4 %all-to-all-start = ((bf16[16,2,1792]{2,1,0:T(2,128)(2,1)}), bf16[16,2,1792]{2,1,0:T(2,128)(2,1)S(1)}, u32[]{:S(2)}, u32[]{:S(2)}) async-start(bf16[16,2,1792]{2,1,0:T(2,128)(2,1)} %reshape.73), calls=%async_computation | async-start | bytes 229376 | tf_op jit(solution)/shard_map/all_to_all | solution.py:1529
  45.4 12.9 %collective-permute-start.9 = (bf16[256,1024]{1,0:T(8,128)(2,1)S(1)}, bf16[256,1024]{1,0:T(8,128)(2,1)}, u32[]{:S(2)}, u32[]{:S(2)}) collective-permute-start(bf16[256,1024]{1,0:T(8,128)(2,1)S(1)} %pack_rows.3.refs_4_), channel_id=1, source_target_pairs={{0,1},{1,0},{2,3},{3,2},{4,5},{5,4},{6,7},{7,6},{8,9},{9,8},{10,11... | collective-permute-start | bytes 1572872 | tf_op jit(solution)/shard_map/ppermute | solution.py:119
  45.9 14.6 %collective-permute-start.11 = (bf16[256,1024]{1,0:T(8,128)(2,1)}, bf16[256,1024]{1,0:T(8,128)(2,1)}, u32[]{:S(2)}, u32[]{:S(2)}) collective-permute-start(bf16[256,1024]{1,0:T(8,128)(2,1)} %collective-permute-done.1.refs_6_), channel_id=1, source_target_pairs={{0,1},{1,0},{2,3},{3,2},{4,5},{5,4},{6,7},{7,6},{8,9},{9,8},{10,11... | collective-permute-start | bytes 1572872 | tf_op jit(solution)/shard_map/ppermute | solution.py:119
  46.0 14.5 %collective-permute-start.10 = (bf16[256,1024]{1,0:T(8,128)(2,1)}, bf16[256,1024]{1,0:T(8,128)(2,1)}, u32[]{:S(2)}, u32[]{:S(2)}) collective-permute-start(bf16[256,1024]{1,0:T(8,128)(2,1)} %collective-permute-done.2.refs_5_), channel_id=1, source_target_pairs={{0,1},{1,0},{2,3},{3,2},{4,5},{5,4},{6,7},{7,6},{8,9},{9,8},{10,11... | collective-permute-start | bytes 1572872 | tf_op jit(solution)/shard_map/ppermute | solution.py:119
  58.1 28.4 %collective-permute-start.17 = (bf16[768,384]{1,0:T(8,128)(2,1)S(1)}, bf16[768,384]{1,0:T(8,128)(2,1)S(1)}, u32[]{:S(2)}, u32[]{:S(2)}) collective-permute-start(bf16[768,384]{1,0:T(8,128)(2,1)S(1)} %get-tuple-element.416), channel_id=1, source_target_pairs={{0,8},{1,9},{2,10},{3,11},{4,12},{5,13},{6,14},{7,15},{8,0},{9,1},... | collective-permute-start | bytes 1769480 | tf_op jit(solution)/shard_map/ppermute | solution.py:119
  58.3 21.9 %collective-permute-start.16 = (bf16[512,384]{1,0:T(8,128)(2,1)}, bf16[512,384]{1,0:T(8,128)(2,1)S(1)}, u32[]{:S(2)}, u32[]{:S(2)}) collective-permute-start(bf16[512,384]{1,0:T(8,128)(2,1)} %copy-done.58), channel_id=1, source_target_pairs={{0,4},{1,5},{2,6},{3,7},{4,0},{5,1},{6,2},{7,3},{8,12},{9,13},{10,... | collective-permute-start | bytes 1179656 | tf_op jit(solution)/shard_map/ppermute | solution.py:119
  69.9 16.5 %collective-permute-start.13 = (bf16[128,1024]{1,0:T(8,128)(2,1)S(1)}, bf16[128,1024]{1,0:T(8,128)(2,1)S(1)}, u32[]{:S(2)}, u32[]{:S(2)}) collective-permute-start(bf16[128,1024]{1,0:T(8,128)(2,1)S(1)} %get-tuple-element.412), channel_id=1, source_target_pairs={{0,18},{1,19},{2,16},{3,17},{4,22},{5,23},{6,20},{7,21},{8,26},{9,... | collective-permute-start | bytes 786440 | tf_op jit(solution)/shard_map/ppermute | solution.py:119
  71.4 15.1 %collective-permute-start.14 = (bf16[128,1024]{1,0:T(8,128)(2,1)S(1)}, bf16[128,1024]{1,0:T(8,128)(2,1)S(1)}, u32[]{:S(2)}, u32[]{:S(2)}) collective-permute-start(bf16[128,1024]{1,0:T(8,128)(2,1)S(1)} %get-tuple-element.413), channel_id=1, source_target_pairs={{0,16},{1,17},{2,18},{3,19},{4,20},{5,21},{6,22},{7,23},{8,24},{9,... | collective-permute-start | bytes 786440 | tf_op jit(solution)/shard_map/ppermute | solution.py:119
  71.9 14.6 %collective-permute-start.15 = (bf16[128,1024]{1,0:T(8,128)(2,1)S(1)}, bf16[128,1024]{1,0:T(8,128)(2,1)S(1)}, u32[]{:S(2)}, u32[]{:S(2)}) collective-permute-start(bf16[128,1024]{1,0:T(8,128)(2,1)S(1)} %get-tuple-element.414), channel_id=1, source_target_pairs={{0,2},{1,3},{2,0},{3,1},{4,6},{5,7},{6,4},{7,5},{8,10},{9,11},{10,... | collective-permute-start | bytes 786440 | tf_op jit(solution)/shard_map/ppermute | solution.py:119
  87.6 15.1 %collective-permute-start.18 = (bf16[128,1024]{1,0:T(8,128)(2,1)S(1)}, bf16[128,1024]{1,0:T(8,128)(2,1)S(1)}, u32[]{:S(2)}, u32[]{:S(2)}) collective-permute-start(bf16[128,1024]{1,0:T(8,128)(2,1)S(1)} %get-tuple-element.425.refs_1_), channel_id=1, source_target_pairs={{0,4},{1,5},{2,6},{3,7},{4,0},{5,1},{6,2},{7,3},{8,12},{9,13},{10,... | collective-permute-start | bytes 786440 | tf_op jit(solution)/shard_map/ppermute | solution.py:119
  87.6 15.6 %collective-permute-start.19 = (bf16[128,1024]{1,0:T(8,128)(2,1)S(1)}, bf16[128,1024]{1,0:T(8,128)(2,1)S(1)}, u32[]{:S(2)}, u32[]{:S(2)}) collective-permute-start(bf16[128,1024]{1,0:T(8,128)(2,1)S(1)} %get-tuple-element.425.refs_1_), channel_id=1, source_target_pairs={{0,2},{1,3},{2,0},{3,1},{4,6},{5,7},{6,4},{7,5},{8,10},{9,11},{10,... | collective-permute-start | bytes 786440 | tf_op jit(solution)/shard_map/ppermute | solution.py:119
  88.1 17.1 %collective-permute-start.20 = (bf16[128,1024]{1,0:T(8,128)(2,1)S(1)}, bf16[128,1024]{1,0:T(8,128)(2,1)S(1)}, u32[]{:S(2)}, u32[]{:S(2)}) collective-permute-start(bf16[128,1024]{1,0:T(8,128)(2,1)S(1)} %get-tuple-element.425.refs_1_), channel_id=1, source_target_pairs={{0,6},{1,7},{2,4},{3,5},{4,2},{5,3},{6,0},{7,1},{8,14},{9,15},{10,... | collective-permute-start | bytes 786440 | tf_op jit(solution)/shard_map/ppermute | solution.py:119
  91.8 21.0 %collective-permute-start.25 = (bf16[512,384]{1,0:T(8,128)(2,1)S(1)}, bf16[512,384]{1,0:T(8,128)(2,1)S(1)}, u32[]{:S(2)}, u32[]{:S(2)}) collective-permute-start(bf16[512,384]{1,0:T(8,128)(2,1)S(1)} %slice.76), channel_id=1, source_target_pairs={{0,4},{1,5},{2,6},{3,7},{4,0},{5,1},{6,2},{7,3},{8,12},{9,13},{10,... | collective-permute-start | bytes 1179656 | tf_op jit(solution)/shard_map/ppermute | solution.py:119
  115.1 37.7 %collective-permute-start.29 = (bf16[1024,384]{1,0:T(8,128)(2,1)S(1)}, bf16[1024,384]{1,0:T(8,128)(2,1)S(1)}, u32[]{:S(2)}, u32[]{:S(2)}) collective-permute-start(bf16[1024,384]{1,0:T(8,128)(2,1)S(1)} %get-tuple-element.445.refs_0_), channel_id=1, source_target_pairs={{0,16},{1,17},{2,18},{3,19},{4,20},{5,21},{6,22},{7,23},{8,24},{9,... | collective-permute-start | bytes 2359304 | tf_op jit(solution)/shard_map/ppermute | solution.py:119
  116.7 36.2 %collective-permute-start.30 = (bf16[1024,384]{1,0:T(8,128)(2,1)S(1)}, bf16[1024,384]{1,0:T(8,128)(2,1)S(1)}, u32[]{:S(2)}, u32[]{:S(2)}) collective-permute-start(bf16[1024,384]{1,0:T(8,128)(2,1)S(1)} %get-tuple-element.445.refs_0_), channel_id=1, source_target_pairs={{0,2},{1,3},{2,0},{3,1},{4,6},{5,7},{6,4},{7,5},{8,10},{9,11},{10,... | collective-permute-start | bytes 2359304 | tf_op jit(solution)/shard_map/ppermute | solution.py:119
  116.9 36.1 %collective-permute-start.33 = (bf16[256,1024]{1,0:T(8,128)(2,1)S(1)}, bf16[256,1024]{1,0:T(8,128)(2,1)}, u32[]{:S(2)}, u32[]{:S(2)}) collective-permute-start(bf16[256,1024]{1,0:T(8,128)(2,1)S(1)} %pack_rows.4.refs_4_), channel_id=1, source_target_pairs={{0,8},{1,9},{2,10},{3,11},{4,12},{5,13},{6,14},{7,15},{8,0},{9,1},... | collective-permute-start | bytes 1572872 | tf_op jit(solution)/shard_map/ppermute | solution.py:119
  118.0 34.9 %collective-permute-start.34 = (bf16[256,1024]{1,0:T(8,128)(2,1)S(1)}, bf16[256,1024]{1,0:T(8,128)(2,1)S(1)}, u32[]{:S(2)}, u32[]{:S(2)}) collective-permute-start(bf16[256,1024]{1,0:T(8,128)(2,1)S(1)} %pack_rows.4.refs_4_), channel_id=1, source_target_pairs={{0,4},{1,5},{2,6},{3,7},{4,0},{5,1},{6,2},{7,3},{8,12},{9,13},{10,... | collective-permute-start | bytes 1572872 | tf_op jit(solution)/shard_map/ppermute | solution.py:119
  154.1 17.4 %collective-permute-start.39 = (bf16[512,384]{1,0:T(8,128)(2,1)S(1)}, bf16[512,384]{1,0:T(8,128)(2,1)S(1)}, u32[]{:S(2)}, u32[]{:S(2)}) collective-permute-start(bf16[512,384]{1,0:T(8,128)(2,1)S(1)} %get-tuple-element.457), channel_id=1, source_target_pairs={{0,2},{1,3},{2,0},{3,1},{4,6},{5,7},{6,4},{7,5},{8,10},{9,11},{10,... | collective-permute-start | bytes 1179656 | tf_op jit(solution)/shard_map/ppermute | solution.py:119
  156.8 14.7 %collective-permute-start.40 = (bf16[512,384]{1,0:T(8,128)(2,1)S(1)}, bf16[512,384]{1,0:T(8,128)(2,1)S(1)}, u32[]{:S(2)}, u32[]{:S(2)}) collective-permute-start(bf16[512,384]{1,0:T(8,128)(2,1)S(1)} %get-tuple-element.458), channel_id=1, source_target_pairs={{0,16},{1,17},{2,18},{3,19},{4,20},{5,21},{6,22},{7,23},{8,24},{9,... | collective-permute-start | bytes 1179656 | tf_op jit(solution)/shard_map/ppermute | solution.py:119
  162.4 13.7 %collective-permute-start.37 = (bf16[128,1024]{1,0:T(8,128)(2,1)S(1)}, bf16[128,1024]{1,0:T(8,128)(2,1)S(1)}, u32[]{:S(2)}, u32[]{:S(2)}) collective-permute-start(bf16[128,1024]{1,0:T(8,128)(2,1)S(1)} %get-tuple-element.455), channel_id=1, source_target_pairs={{0,4},{1,5},{2,6},{3,7},{4,0},{5,1},{6,2},{7,3},{8,12},{9,13},{10,... | collective-permute-start | bytes 786440 | tf_op jit(solution)/shard_map/ppermute | solution.py:119
  164.1 12.4 %collective-permute-start.38 = (bf16[128,1024]{1,0:T(8,128)(2,1)S(1)}, bf16[128,1024]{1,0:T(8,128)(2,1)S(1)}, u32[]{:S(2)}, u32[]{:S(2)}) collective-permute-start(bf16[128,1024]{1,0:T(8,128)(2,1)S(1)} %get-tuple-element.456), channel_id=1, source_target_pairs={{0,2},{1,3},{2,0},{3,1},{4,6},{5,7},{6,4},{7,5},{8,10},{9,11},{10,... | collective-permute-start | bytes 786440 | tf_op jit(solution)/shard_map/ppermute | solution.py:119
  177.0 14.1 %collective-permute-start.44 = (bf16[256,1024]{1,0:T(8,128)(2,1)}, bf16[256,1024]{1,0:T(8,128)(2,1)}, u32[]{:S(2)}, u32[]{:S(2)}) collective-permute-start(bf16[256,1024]{1,0:T(8,128)(2,1)} %collective-permute-done.33.refs_6_), channel_id=1, source_target_pairs={{0,4},{1,5},{2,6},{3,7},{4,0},{5,1},{6,2},{7,3},{8,12},{9,13},{10,... | collective-permute-start | bytes 1572872 | tf_op jit(solution)/shard_map/ppermute | solution.py:119
  197.7 12.8 %collective-permute-start.50 = (bf16[128,1024]{1,0:T(8,128)(2,1)S(1)}, bf16[128,1024]{1,0:T(8,128)(2,1)S(1)}, u32[]{:S(2)}, u32[]{:S(2)}) collective-permute-start(bf16[128,1024]{1,0:T(8,128)(2,1)S(1)} %get-tuple-element.484.refs_0_), channel_id=1, source_target_pairs={{0,2},{1,3},{2,0},{3,1},{4,6},{5,7},{6,4},{7,5},{8,10},{9,11},{10,... | collective-permute-start | bytes 786440 | tf_op jit(solution)/shard_map/ppermute | solution.py:119
  199.4 12.7 %collective-permute-start.51 = (bf16[128,1024]{1,0:T(8,128)(2,1)S(1)}, bf16[128,1024]{1,0:T(8,128)(2,1)S(1)}, u32[]{:S(2)}, u32[]{:S(2)}) collective-permute-start(bf16[128,1024]{1,0:T(8,128)(2,1)S(1)} %get-tuple-element.484.refs_0_), channel_id=1, source_target_pairs={{0,18},{1,19},{2,16},{3,17},{4,22},{5,23},{6,20},{7,21},{8,26},{9,... | collective-permute-start | bytes 786440 | tf_op jit(solution)/shard_map/ppermute | solution.py:119
  233.3 13.3 %collective-permute-start.56 = (bf16[128,1024]{1,0:T(8,128)(2,1)S(1)}, bf16[128,1024]{1,0:T(8,128)(2,1)S(1)}, u32[]{:S(2)}, u32[]{:S(2)}) collective-permute-start(bf16[128,1024]{1,0:T(8,128)(2,1)S(1)} %get-tuple-element.500.refs_0_), channel_id=1, source_target_pairs={{0,2},{1,3},{2,0},{3,1},{4,6},{5,7},{6,4},{7,5},{8,10},{9,11},{10,... | collective-permute-start | bytes 786440 | tf_op jit(solution)/shard_map/ppermute | solution.py:119
  234.7 11.9 %collective-permute-start.57 = (bf16[128,1024]{1,0:T(8,128)(2,1)S(1)}, bf16[128,1024]{1,0:T(8,128)(2,1)S(1)}, u32[]{:S(2)}, u32[]{:S(2)}) collective-permute-start(bf16[128,1024]{1,0:T(8,128)(2,1)S(1)} %get-tuple-element.500.refs_0_), channel_id=1, source_target_pairs={{0,18},{1,19},{2,16},{3,17},{4,22},{5,23},{6,20},{7,21},{8,26},{9,... | collective-permute-start | bytes 786440 | tf_op jit(solution)/shard_map/ppermute | solution.py:119
  257.2 13.7 %collective-permute-start.59 = (bf16[128,1024]{1,0:T(8,128)(2,1)S(1)}, bf16[128,1024]{1,0:T(8,128)(2,1)S(1)}, u32[]{:S(2)}, u32[]{:S(2)}) collective-permute-start(bf16[128,1024]{1,0:T(8,128)(2,1)S(1)} %get-tuple-element.513), channel_id=1, source_target_pairs={{0,16},{1,17},{2,18},{3,19},{4,20},{5,21},{6,22},{7,23},{8,24},{9,... | collective-permute-start | bytes 786440 | tf_op jit(solution)/shard_map/ppermute | solution.py:119
  270.9 16.1 %collective-permute-start.64 = (bf16[128,1024]{1,0:T(8,128)(2,1)}, bf16[128,1024]{1,0:T(8,128)(2,1)S(1)}, u32[]{:S(2)}, u32[]{:S(2)}) collective-permute-start(bf16[128,1024]{1,0:T(8,128)(2,1)} %get-tuple-element.536), channel_id=1, source_target_pairs={{0,4},{1,5},{2,6},{3,7},{4,0},{5,1},{6,2},{7,3},{8,12},{9,13},{10,... | collective-permute-start | bytes 786440 | tf_op jit(solution)/shard_map/ppermute | solution.py:119
  272.4 14.6 %collective-permute-start.65 = (bf16[128,1024]{1,0:T(8,128)(2,1)}, bf16[128,1024]{1,0:T(8,128)(2,1)S(1)}, u32[]{:S(2)}, u32[]{:S(2)}) collective-permute-start(bf16[128,1024]{1,0:T(8,128)(2,1)} %get-tuple-element.538), channel_id=1, source_target_pairs={{0,4},{1,5},{2,6},{3,7},{4,0},{5,1},{6,2},{7,3},{8,12},{9,13},{10,... | collective-permute-start | bytes 786440 | tf_op jit(solution)/shard_map/ppermute | solution.py:119
  286.9 13.2 %collective-permute-start.67 = (bf16[128,1024]{1,0:T(8,128)(2,1)}, bf16[128,1024]{1,0:T(8,128)(2,1)S(1)}, u32[]{:S(2)}, u32[]{:S(2)}) collective-permute-start(bf16[128,1024]{1,0:T(8,128)(2,1)} %copy-done.71), channel_id=1, source_target_pairs={{0,4},{1,5},{2,6},{3,7},{4,0},{5,1},{6,2},{7,3},{8,12},{9,13},{10,... | collective-permute-start | bytes 786440 | tf_op jit(solution)/shard_map/ppermute | solution.py:119
  300.1 15.6 %collective-permute-start.75 = (bf16[2048,768]{1,0:T(8,128)(2,1)S(1)}, bf16[2048,768]{1,0:T(8,128)(2,1)S(1)}, u32[]{:S(2)}, u32[]{:S(2)}) collective-permute-start(bf16[2048,768]{1,0:T(8,128)(2,1)S(1)} %get-tuple-element.559), channel_id=1, source_target_pairs={{0,1},{1,0},{2,3},{3,2},{4,5},{5,4},{6,7},{7,6},{8,9},{9,8},{10,11... | collective-permute-start | bytes 9437192 | tf_op jit(solution)/shard_map/ppermute | solution.py:119
  301.2 14.0 %collective-permute-start.69 = (bf16[128,1024]{1,0:T(8,128)(2,1)S(1)}, bf16[128,1024]{1,0:T(8,128)(2,1)S(1)}, u32[]{:S(2)}, u32[]{:S(2)}) collective-permute-start(bf16[128,1024]{1,0:T(8,128)(2,1)S(1)} %get-tuple-element.566.refs_1_), channel_id=1, source_target_pairs={{0,2},{1,3},{2,0},{3,1},{4,6},{5,7},{6,4},{7,5},{8,10},{9,11},{10,... | collective-permute-start | bytes 786440 | tf_op jit(solution)/shard_map/ppermute | solution.py:119
  301.8 13.3 %collective-permute-start.70 = (bf16[128,1024]{1,0:T(8,128)(2,1)S(1)}, bf16[128,1024]{1,0:T(8,128)(2,1)S(1)}, u32[]{:S(2)}, u32[]{:S(2)}) collective-permute-start(bf16[128,1024]{1,0:T(8,128)(2,1)S(1)} %get-tuple-element.566.refs_1_), channel_id=1, source_target_pairs={{0,6},{1,7},{2,4},{3,5},{4,2},{5,3},{6,0},{7,1},{8,14},{9,15},{10,... | collective-permute-start | bytes 786440 | tf_op jit(solution)/shard_map/ppermute | solution.py:119
  303.7 12.7 %collective-permute-start.71 = (bf16[128,1024]{1,0:T(8,128)(2,1)S(1)}, bf16[128,1024]{1,0:T(8,128)(2,1)S(1)}, u32[]{:S(2)}, u32[]{:S(2)}) collective-permute-start(bf16[128,1024]{1,0:T(8,128)(2,1)S(1)} %get-tuple-element.566.refs_1_), channel_id=1, source_target_pairs={{0,1},{1,0},{2,3},{3,2},{4,5},{5,4},{6,7},{7,6},{8,9},{9,8},{10,11... | collective-permute-start | bytes 786440 | tf_op jit(solution)/shard_map/ppermute | solution.py:119
  317.1 28.7 %collective-permute-start.77 = (bf16[128,1024]{1,0:T(8,128)(2,1)S(1)}, bf16[128,1024]{1,0:T(8,128)(2,1)S(1)}, u32[]{:S(2)}, u32[]{:S(2)}) collective-permute-start(bf16[128,1024]{1,0:T(8,128)(2,1)S(1)} %plane_add.8), channel_id=1, source_target_pairs={{0,8},{1,9},{2,10},{3,11},{4,12},{5,13},{6,14},{7,15},{8,0},{9,1},... | collective-permute-start | bytes 786440 | tf_op jit(solution)/shard_map/ppermute | solution.py:119
  319.1 26.7 %collective-permute-start.78 = (bf16[128,1024]{1,0:T(8,128)(2,1)S(1)}, bf16[128,1024]{1,0:T(8,128)(2,1)S(1)}, u32[]{:S(2)}, u32[]{:S(2)}) collective-permute-start(bf16[128,1024]{1,0:T(8,128)(2,1)S(1)} %plane_add.9), channel_id=1, source_target_pairs={{0,8},{1,9},{2,10},{3,11},{4,12},{5,13},{6,14},{7,15},{8,0},{9,1},... | collective-permute-start | bytes 786440 | tf_op jit(solution)/shard_map/ppermute | solution.py:119
  320.0 25.8 %collective-permute-start.79 = (bf16[512,768]{1,0:T(8,128)(2,1)S(1)}, bf16[512,768]{1,0:T(8,128)(2,1)S(1)}, u32[]{:S(2)}, u32[]{:S(2)}) collective-permute-start(bf16[512,768]{1,0:T(8,128)(2,1)S(1)} %get-tuple-element.591), channel_id=1, source_target_pairs={{0,16},{1,17},{2,18},{3,19},{4,20},{5,21},{6,22},{7,23},{8,24},{9,... | collective-permute-start | bytes 2359304 | tf_op jit(solution)/shard_map/ppermute | solution.py:119
  321.0 35.6 %collective-permute-start.80 = (bf16[512,768]{1,0:T(8,128)(2,1)S(1)}, bf16[512,768]{1,0:T(8,128)(2,1)S(1)}, u32[]{:S(2)}, u32[]{:S(2)}) collective-permute-start(bf16[512,768]{1,0:T(8,128)(2,1)S(1)} %get-tuple-element.592), channel_id=1, source_target_pairs={{0,2},{1,3},{2,0},{3,1},{4,6},{5,7},{6,4},{7,5},{8,10},{9,11},{10,... | collective-permute-start | bytes 2359304 | tf_op jit(solution)/shard_map/ppermute | solution.py:119
  322.3 34.2 %collective-permute-start.81 = (bf16[512,768]{1,0:T(8,128)(2,1)S(1)}, bf16[512,768]{1,0:T(8,128)(2,1)S(1)}, u32[]{:S(2)}, u32[]{:S(2)}) collective-permute-start(bf16[512,768]{1,0:T(8,128)(2,1)S(1)} %get-tuple-element.593), channel_id=1, source_target_pairs={{0,18},{1,19},{2,16},{3,17},{4,22},{5,23},{6,20},{7,21},{8,26},{9,... | collective-permute-start | bytes 2359304 | tf_op jit(solution)/shard_map/ppermute | solution.py:119
  361.7 17.4 %collective-permute-start.83 = (bf16[128,1024]{1,0:T(8,128)(2,1)S(1)}, bf16[128,1024]{1,0:T(8,128)(2,1)S(1)}, u32[]{:S(2)}, u32[]{:S(2)}) collective-permute-start(bf16[128,1024]{1,0:T(8,128)(2,1)S(1)} %get-tuple-element.596), channel_id=1, source_target_pairs={{0,6},{1,7},{2,4},{3,5},{4,2},{5,3},{6,0},{7,1},{8,14},{9,15},{10,... | collective-permute-start | bytes 786440 | tf_op jit(solution)/shard_map/ppermute | solution.py:119
  362.6 16.5 %collective-permute-start.84 = (bf16[128,1024]{1,0:T(8,128)(2,1)S(1)}, bf16[128,1024]{1,0:T(8,128)(2,1)S(1)}, u32[]{:S(2)}, u32[]{:S(2)}) collective-permute-start(bf16[128,1024]{1,0:T(8,128)(2,1)S(1)} %get-tuple-element.597), channel_id=1, source_target_pairs={{0,4},{1,5},{2,6},{3,7},{4,0},{5,1},{6,2},{7,3},{8,12},{9,13},{10,... | collective-permute-start | bytes 786440 | tf_op jit(solution)/shard_map/ppermute | solution.py:119
  364.6 14.5 %collective-permute-start.85 = (bf16[128,1024]{1,0:T(8,128)(2,1)S(1)}, bf16[128,1024]{1,0:T(8,128)(2,1)S(1)}, u32[]{:S(2)}, u32[]{:S(2)}) collective-permute-start(bf16[128,1024]{1,0:T(8,128)(2,1)S(1)} %get-tuple-element.598), channel_id=1, source_target_pairs={{0,2},{1,3},{2,0},{3,1},{4,6},{5,7},{6,4},{7,5},{8,10},{9,11},{10,... | collective-permute-start | bytes 786440 | tf_op jit(solution)/shard_map/ppermute | solution.py:119
  365.2 13.8 %collective-permute-start.86 = (bf16[64,1024]{1,0:T(8,128)(2,1)S(1)}, bf16[64,1024]{1,0:T(8,128)(2,1)S(1)}, u32[]{:S(2)}, u32[]{:S(2)}) collective-permute-start(bf16[64,1024]{1,0:T(8,128)(2,1)S(1)} %get-tuple-element.774), channel_id=1, source_target_pairs={{0,2},{1,3},{2,0},{3,1},{4,6},{5,7},{6,4},{7,5},{8,10},{9,11},{10,... | collective-permute-start | bytes 393224 | tf_op jit(solution)/shard_map/ppermute | solution.py:119
  379.7 19.0 %collective-permute-start.92 = (bf16[384,768]{1,0:T(8,128)(2,1)S(1)}, bf16[384,768]{1,0:T(8,128)(2,1)S(1)}, u32[]{:S(2)}, u32[]{:S(2)}) collective-permute-start(bf16[384,768]{1,0:T(8,128)(2,1)S(1)} %get-tuple-element.630), channel_id=1, source_target_pairs={{0,4},{1,5},{2,6},{3,7},{4,0},{5,1},{6,2},{7,3},{8,12},{9,13},{10,... | collective-permute-start | bytes 1769480 | tf_op jit(solution)/shard_map/ppermute | solution.py:119
  381.6 16.3 %collective-permute-start.88 = (bf16[128,1024]{1,0:T(8,128)(2,1)S(1)}, bf16[128,1024]{1,0:T(8,128)(2,1)S(1)}, u32[]{:S(2)}, u32[]{:S(2)}) collective-permute-start(bf16[128,1024]{1,0:T(8,128)(2,1)S(1)} %get-tuple-element.646.refs_0_), channel_id=1, source_target_pairs={{0,16},{1,17},{2,18},{3,19},{4,20},{5,21},{6,22},{7,23},{8,24},{9,... | collective-permute-start | bytes 786440 | tf_op jit(solution)/shard_map/ppermute | solution.py:119
  382.3 15.6 %collective-permute-start.89 = (bf16[128,1024]{1,0:T(8,128)(2,1)S(1)}, bf16[128,1024]{1,0:T(8,128)(2,1)S(1)}, u32[]{:S(2)}, u32[]{:S(2)}) collective-permute-start(bf16[128,1024]{1,0:T(8,128)(2,1)S(1)} %get-tuple-element.646.refs_0_), channel_id=1, source_target_pairs={{0,2},{1,3},{2,0},{3,1},{4,6},{5,7},{6,4},{7,5},{8,10},{9,11},{10,... | collective-permute-start | bytes 786440 | tf_op jit(solution)/shard_map/ppermute | solution.py:119
  383.6 14.3 %collective-permute-start.90 = (bf16[128,1024]{1,0:T(8,128)(2,1)S(1)}, bf16[128,1024]{1,0:T(8,128)(2,1)S(1)}, u32[]{:S(2)}, u32[]{:S(2)}) collective-permute-start(bf16[128,1024]{1,0:T(8,128)(2,1)S(1)} %get-tuple-element.646.refs_0_), channel_id=1, source_target_pairs={{0,18},{1,19},{2,16},{3,17},{4,22},{5,23},{6,20},{7,21},{8,26},{9,... | collective-permute-start | bytes 786440 | tf_op jit(solution)/shard_map/ppermute | solution.py:119
  385.0 12.9 %collective-permute-start.91 = (bf16[128,768]{1,0:T(8,128)(2,1)S(1)}, bf16[128,768]{1,0:T(8,128)(2,1)S(1)}, u32[]{:S(2)}, u32[]{:S(2)}) collective-permute-start(bf16[128,768]{1,0:T(8,128)(2,1)S(1)} %get-tuple-element.628), channel_id=1, source_target_pairs={{0,8},{1,9},{2,10},{3,11},{4,12},{5,13},{6,14},{7,15},{8,0},{9,1},... | collective-permute-start | bytes 589832 | tf_op jit(solution)/shard_map/ppermute | solution.py:119
  403.7 14.0 %collective-permute-start.95 = (bf16[256,1024]{1,0:T(8,128)(2,1)S(1)}, bf16[256,1024]{1,0:T(8,128)(2,1)S(1)}, u32[]{:S(2)}, u32[]{:S(2)}) collective-permute-start(bf16[256,1024]{1,0:T(8,128)(2,1)S(1)} %pack_rows.5), channel_id=1, source_target_pairs={{0,16},{1,17},{2,18},{3,19},{4,20},{5,21},{6,22},{7,23},{8,24},{9,... | collective-permute-start | bytes 1572872 | tf_op jit(solution)/shard_map/ppermute | solution.py:119
  425.0 13.0 %collective-permute-start.98 = (bf16[128,1024]{1,0:T(8,128)(2,1)S(1)}, bf16[128,1024]{1,0:T(8,128)(2,1)S(1)}, u32[]{:S(2)}, u32[]{:S(2)}) collective-permute-start(bf16[128,1024]{1,0:T(8,128)(2,1)S(1)} %get-tuple-element.666), channel_id=1, source_target_pairs={{0,16},{1,17},{2,18},{3,19},{4,20},{5,21},{6,22},{7,23},{8,24},{9,... | collective-permute-start | bytes 786440 | tf_op jit(solution)/shard_map/ppermute | solution.py:119
  426.0 12.9 %collective-permute-start.99 = (bf16[128,1024]{1,0:T(8,128)(2,1)S(1)}, bf16[128,1024]{1,0:T(8,128)(2,1)S(1)}, u32[]{:S(2)}, u32[]{:S(2)}) collective-permute-start(bf16[128,1024]{1,0:T(8,128)(2,1)S(1)} %get-tuple-element.667), channel_id=1, source_target_pairs={{0,2},{1,3},{2,0},{3,1},{4,6},{5,7},{6,4},{7,5},{8,10},{9,11},{10,... | collective-permute-start | bytes 786440 | tf_op jit(solution)/shard_map/ppermute | solution.py:119
  427.1 13.5 %collective-permute-start.102 = (bf16[128,1024]{1,0:T(8,128)(2,1)S(1)}, bf16[128,1024]{1,0:T(8,128)(2,1)S(1)}, u32[]{:S(2)}, u32[]{:S(2)}) collective-permute-start(bf16[128,1024]{1,0:T(8,128)(2,1)S(1)} %get-tuple-element.673), channel_id=1, source_target_pairs={{0,4},{1,5},{2,6},{3,7},{4,0},{5,1},{6,2},{7,3},{8,12},{9,13},{10,... | collective-permute-start | bytes 786440 | tf_op jit(solution)/shard_map/ppermute | solution.py:119
  430.5 17.1 %collective-permute-start.103 = (bf16[128,1024]{1,0:T(8,128)(2,1)S(1)}, bf16[128,1024]{1,0:T(8,128)(2,1)S(1)}, u32[]{:S(2)}, u32[]{:S(2)}) collective-permute-start(bf16[128,1024]{1,0:T(8,128)(2,1)S(1)} %get-tuple-element.675), channel_id=1, source_target_pairs={{0,4},{1,5},{2,6},{3,7},{4,0},{5,1},{6,2},{7,3},{8,12},{9,13},{10,... | collective-permute-start | bytes 786440 | tf_op jit(solution)/shard_map/ppermute | solution.py:119
  433.5 15.2 %collective-permute-start.107 = (bf16[128,768]{1,0:T(8,128)(2,1)S(1)}, bf16[128,768]{1,0:T(8,128)(2,1)S(1)}, u32[]{:S(2)}, u32[]{:S(2)}) collective-permute-start(bf16[128,768]{1,0:T(8,128)(2,1)S(1)} %conv_grads_top.1), channel_id=1, source_target_pairs={{0,8},{1,9},{2,10},{3,11},{4,12},{5,13},{6,14},{7,15},{8,0},{9,1},... | collective-permute-start | bytes 589832 | tf_op jit(solution)/shard_map/ppermute | solution.py:119
  438.0 25.2 %collective-permute-start.109 = (bf16[128,1024]{1,0:T(8,128)(2,1)S(1)}, bf16[128,1024]{1,0:T(8,128)(2,1)S(1)}, u32[]{:S(2)}, u32[]{:S(2)}) collective-permute-start(bf16[128,1024]{1,0:T(8,128)(2,1)S(1)} %plane_add.13), channel_id=1, source_target_pairs={{0,8},{1,9},{2,10},{3,11},{4,12},{5,13},{6,14},{7,15},{8,0},{9,1},... | collective-permute-start | bytes 786440 | tf_op jit(solution)/shard_map/ppermute | solution.py:119
  439.0 13.6 %collective-permute-start.104 = (bf16[64,1536]{1,0:T(8,128)(2,1)S(1)}, bf16[64,1536]{1,0:T(8,128)(2,1)}, u32[]{:S(2)}, u32[]{:S(2)}) collective-permute-start(bf16[64,1536]{1,0:T(8,128)(2,1)S(1)} %get-tuple-element.685), channel_id=1, source_target_pairs={{0,2},{1,3},{2,0},{3,1},{4,6},{5,7},{6,4},{7,5},{8,10},{9,11},{10,... | collective-permute-start | bytes 589832 | tf_op jit(solution)/shard_map/ppermute | solution.py:119
  440.6 11.9 %collective-permute-start.105 = (bf16[64,1536]{1,0:T(8,128)(2,1)S(1)}, bf16[64,1536]{1,0:T(8,128)(2,1)S(1)}, u32[]{:S(2)}, u32[]{:S(2)}) collective-permute-start(bf16[64,1536]{1,0:T(8,128)(2,1)S(1)} %get-tuple-element.686.refs_0_), channel_id=1, source_target_pairs={{0,16},{1,17},{2,18},{3,19},{4,20},{5,21},{6,22},{7,23},{8,24},{9,... | collective-permute-start | bytes 589832 | tf_op jit(solution)/shard_map/ppermute | solution.py:119
  452.8 21.6 %collective-permute-start.108 = (bf16[128,1024]{1,0:T(8,128)(2,1)S(1)}, bf16[128,1024]{1,0:T(8,128)(2,1)S(1)}, u32[]{:S(2)}, u32[]{:S(2)}) collective-permute-start(bf16[128,1024]{1,0:T(8,128)(2,1)S(1)} %plane_add.12), channel_id=1, source_target_pairs={{0,8},{1,9},{2,10},{3,11},{4,12},{5,13},{6,14},{7,15},{8,0},{9,1},... | collective-permute-start | bytes 786440 | tf_op jit(solution)/shard_map/ppermute | solution.py:119
  468.2 13.8 %all-to-all-start.1 = ((bf16[32,32,128]{2,1,0:T(8,128)(2,1)}), bf16[32,32,128]{2,1,0:T(8,128)(2,1)S(1)}, u32[]{:S(2)}, u32[]{:S(2)}) async-start(bf16[32,32,128]{2,1,0:T(8,128)(2,1)} %small_pack.1), calls=%async_computation.1 | async-start | bytes 524288 | tf_op jit(solution)/shard_map/all_to_all | solution.py:1643
  475.8 21.4 %collective-permute-start.113 = (bf16[64,1024]{1,0:T(8,128)(2,1)S(1)}, bf16[64,1024]{1,0:T(8,128)(2,1)S(1)}, u32[]{:S(2)}, u32[]{:S(2)}) collective-permute-start(bf16[64,1024]{1,0:T(8,128)(2,1)S(1)} %get-tuple-element.772.refs_0_), channel_id=1, source_target_pairs={{0,16},{1,17},{2,18},{3,19},{4,20},{5,21},{6,22},{7,23},{8,24},{9,... | collective-permute-start | bytes 393224 | tf_op jit(solution)/shard_map/ppermute | solution.py:119
  481.2 14.7 %collective-permute-start.115 = (bf16[64,1024]{1,0:T(8,128)(2,1)S(1)}, bf16[64,1024]{1,0:T(8,128)(2,1)S(1)}, u32[]{:S(2)}, u32[]{:S(2)}) collective-permute-start(bf16[64,1024]{1,0:T(8,128)(2,1)S(1)} %collective-permute-done.114.refs_2_), channel_id=1, source_target_pairs={{0,16},{1,17},{2,18},{3,19},{4,20},{5,21},{6,22},{7,23},{8,24},{9,... | collective-permute-start | bytes 393224 | tf_op jit(solution)/shard_map/ppermute | solution.py:119
  (153 other events, 1831.4 us)
